TPU v7x, 128 devices: a whole 4x4x4 slice. The times are simulated.
128 devices in a mesh: vtx: 32 (over y, x, core), edg: 4 (over z).
Axes of the slice: x: 4, y: 4, z: 4, core: 2. Of those that a mesh axis runs over, the one named last changes fastest.
Arguments:
- sketch_cols: bfloat16 [524288, 128], P(('vtx', 'edg')), may hold values from -6 to 6
- edge_weight: float32 [524288], P(('vtx', 'edg')), may hold values from 0.25 to 4
- ground: float32 [65536], P('vtx'), may hold values from 0.05 to 0.5
- src_local: int32 [524288], P(('vtx', 'edg')), may hold values from 0 to 2047
- dst_index: int32 [524288], P(('vtx', 'edg')), may hold values from 0 to 3583
- send_rows: int32 [128, 32, 48], P(('vtx', 'edg')), may hold values from 0 to 2047
- edge_count: int32 [128], P(('vtx', 'edg')), may hold values from 512 to 4096, as said below
Outputs:
- solution: float32 [65536, 128], P('vtx')
- resistance: float32 [524288], P(('vtx', 'edg'))
Inputs may be any that keep to these rules, and one draw needn't show every extreme that they name: `edge_count`: edge slots of a device at positions of its count or beyond are unused. In every draw some device has all 4096 slots live.
All inputs are finite; a program needn't handle non-finite values.
Results may differ from a plain program's by a relative error of at most 0.0003.
Values sent between devices are 32-bit elements; how exact they have to be, the bound alone decides.
No kernel may reach another device: no remote copies, remote signals or barrier semaphores. Data moves between devices by JAX's collectives and lax.ppermute only.
A program may use at most 64 MiB of HBM per device.

v0:
```python
import math

import jax
import jax.numpy as jnp
from jax import lax
from jax.sharding import PartitionSpec as P

ITERS = 3


lam_low = 0.05
lam_high = 2.0


def side_by_side(arrays, axis, split_dim, concat_dim, along):
    columns = [a.reshape(*a.shape[:along], -1) for a in arrays]
    both = jnp.concatenate(columns, axis=along)
    out, at, gathered = (
        lax.all_to_all(both, axis, split_axis=split_dim, concat_axis=concat_dim, tiled=True),
        0,
        [],
    )
    for a, column in zip(arrays, columns):
        section = out[..., at : at + column.shape[along]]
        gathered.append(section.reshape(*section.shape[:along], *a.shape[along:]))
        at += column.shape[along]
    return tuple(gathered)


def in_blocks(shard, dim, length):
    dims = shard.shape
    tiles = shard.reshape(*dims[:dim], length, dims[dim] // length, *dims[dim + 1 :])
    return jnp.moveaxis(tiles, dim, 0)


def summed_on_arrival(shard, axis, dim):
    tiles = in_blocks(shard, dim, lax.axis_size(axis))
    arrived = lax.all_to_all(tiles, axis, split_axis=0, concat_axis=0, tiled=True)
    return arrived.sum(axis=0)


def in_one_piece(arrays, axis, dim, along):
    widths = [math.prod(a.shape[along:]) for a in arrays]
    both = jnp.concatenate(
        [a.reshape(*a.shape[:along], w) for a, w in zip(arrays, widths)], axis=along
    )
    out = summed_on_arrival(both, axis, dim)
    tiles = jnp.split(out, [sum(widths[:k]) for k in range(1, len(widths))], axis=along)
    return tuple((b.reshape(*out.shape[:along], *a.shape[along:]) for a, b in zip(arrays, tiles)))


def joined_along(tiles, dim):
    tiles = jnp.moveaxis(tiles, 0, dim)
    dims = tiles.shape
    return tiles.reshape(*dims[:dim], dims[dim] * dims[dim + 1], *dims[dim + 2 :])


def sent_to_all(shard, axis):
    length = lax.axis_size(axis)
    return lax.all_to_all(
        jnp.broadcast_to(shard[None], (length, *shard.shape)), axis, 0, 0, tiled=True
    )


def gathered_copies(shard, axis, dim):
    return joined_along(sent_to_all(shard, axis), dim)


def chebyshev_terms(steps):
    centre = (lam_high + lam_low) / 2.0
    half_width = (lam_high - lam_low) / 2.0
    sigma_val = centre / half_width
    rho_prev = 1.0 / sigma_val
    pairs = []
    for count_idx in range(steps - 1):
        rho_next = 1.0 / (2.0 * sigma_val - rho_prev)
        pairs.append((rho_next * rho_prev, 2.0 * rho_next / half_width))
        rho_prev = rho_next
    return (1.0 / centre, pairs)


def fetch(field_in, list_table):
    listed = field_in[list_table]
    arrived = lax.all_to_all(listed, "vtx", split_axis=0, concat_axis=0, tiled=True)
    return jnp.concatenate([field_in, arrived.reshape(-1, field_in.shape[1])], axis=0)


def edge_part(field_in, list_table, flat_rows, sources, targets, weights):
    num_rows = field_in.shape[0]
    extended = fetch(field_in, list_table)
    edge_diffs = weights[:, None] * (field_in[sources] - extended[targets])
    summed = jnp.zeros(extended.shape, jnp.float32)
    summed = summed.at[sources].add(edge_diffs).at[targets].add(-edge_diffs)
    outgoing = summed[num_rows:].reshape(list_table.shape + (field_in.shape[1],))
    returned = lax.all_to_all(outgoing, "vtx", split_axis=0, concat_axis=0, tiled=True)
    return summed[:num_rows].at[flat_rows].add(returned.reshape(-1, field_in.shape[1]))


def local(sketch_cols, edge_weight, ground, src_local, dst_index, send_rows, edge_count):
    blocks = lax.axis_size("vtx")
    num_rows = ground.shape[0]
    num_edges = edge_weight.shape[0]
    slot_width = send_rows.shape[2]
    columns = sketch_cols.shape[1]
    halo_len = blocks * slot_width
    row_lists = send_rows[0]
    flat_list = row_lists.reshape(-1)
    own_table = row_lists[:, None, :]
    live_mask = (jnp.arange(num_edges, dtype=jnp.int32) < edge_count[0]).astype(jnp.float32)
    weight_live = edge_weight * live_mask
    root_live = jnp.sqrt(edge_weight) * live_mask
    edge_terms = root_live[:, None] * sketch_cols.astype(jnp.float32)
    summed = jnp.zeros((num_rows + halo_len, columns), jnp.float32)
    summed = summed.at[src_local].add(edge_terms).at[dst_index].add(-edge_terms)
    degrees = jnp.zeros((num_rows + halo_len,), jnp.float32)
    degrees = degrees.at[src_local].add(weight_live).at[dst_index].add(weight_live)
    back_terms, back_degree = side_by_side(
        (
            summed[num_rows:].reshape(blocks, slot_width, columns),
            degrees[num_rows:].reshape(blocks, slot_width),
        ),
        "vtx",
        0,
        0,
        2,
    )
    local_side = summed[:num_rows].at[flat_list].add(back_terms.reshape(halo_len, columns))
    local_degree = degrees[:num_rows].at[flat_list].add(back_degree.reshape(halo_len))
    first, pairs = chebyshev_terms(ITERS)
    lanes = lax.axis_size("edg")
    share = num_rows // lanes
    start = lax.axis_index("edg") * share
    right_share, degree_share = in_one_piece((local_side, local_degree), "edg", 0, 1)
    ground_share = lax.dynamic_slice_in_dim(ground, start, share)
    inverse = (1.0 / (degree_share + ground_share))[:, None]
    residual_now = right_share
    dir_share = first * inverse * right_share
    sol_share = jnp.zeros_like(right_share)
    for step_idx in range(ITERS):
        sol_share = sol_share + dir_share
        if step_idx + 1 < ITERS:
            dir_full = gathered_copies(dir_share, "edg", 0)
            flows = summed_on_arrival(
                edge_part(dir_full, own_table, flat_list, src_local, dst_index, weight_live),
                "edg",
                0,
            )
            residual_now = residual_now - (ground_share[:, None] * dir_share + flows)
            keep_coef, push_coef = pairs[step_idx]
            dir_share = keep_coef * dir_share + push_coef * inverse * residual_now
    solution = gathered_copies(sol_share, "edg", 0)
    extended = fetch(solution, own_table)
    gaps = solution[src_local] - extended[dst_index]
    resistance = live_mask * jnp.sum(gaps * gaps, axis=1) / columns
    return (solution, resistance)


def solution(mesh):
    in_specs = (
        P(("vtx", "edg"), None),
        P(("vtx", "edg")),
        P("vtx"),
        P(("vtx", "edg")),
        P(("vtx", "edg")),
        P(("vtx", "edg"), None, None),
        P(("vtx", "edg")),
    )
    out_specs = (P("vtx", None), P(("vtx", "edg")))
    return jax.shard_map(local, mesh=mesh, in_specs=in_specs, out_specs=out_specs, check_vma=False)
```

profile of v0, /device:TPU:1, one launch (start us, length us, event | category | flops | bytes accessed | tf_op | source)
XLA Modules:
  0.0 564.7 jit_solution(7875823565702120226)
XLA Ops:
  3.5 22.0 %scatter_custom_fusion.2 = f32[3584]{0:T(1024)S(1)} fusion(s32[4096]{0:T(1024)S(1)} %get-tuple-element.8, f32[4096]{0:T(1024)S(1)} %get-tuple-element.10, f32[]{:T(128)} %constant.14.clone.1), kind=kCustom, calls=%fused_computation.61 | custom fusion | flops 4096 | bytes 14340 | tf_op jit(solution)/shard_map/scatter-add | solution.py:116
  25.5 22.4 %scatter_fusion = f32[3584]{0:T(1024)S(1)} fusion(f32[3584]{0:T(1024)S(1)} %scatter_custom_fusion.2, s32[4096]{0:T(1024)S(1)} %get-tuple-element.6, f32[4096]{0:T(1024)S(1)} %get-tuple-element.10), kind=kCustom, calls=%fused_computation.12 | custom fusion | flops 4096 | bytes 65536 | tf_op jit(solution)/shard_map/scatter-add | solution.py:116
  49.4 24.8 %scatter_custom_fusion = f32[3584,128]{1,0:T(8,128)S(1)} fusion(s32[4096]{0:T(1024)S(1)} %get-tuple-element.8, bf16[4096,128]{1,0:T(8,128)(2,1)S(1)} %copy-done.4, f32[4096]{0:T(1024)S(1)} %get-tuple-element.9, f32[]{:T(128)} %constant.14.clone.1), kind=kCustom, calls=%fused_computation.31 | custom fusion | flops 1572864 | bytes 2899972 | tf_op jit(solution)/shard_map/scatter-add | solution.py:114
  74.2 25.1 %scatter_custom_fusion.1 = f32[3584,128]{1,0:T(8,128)S(1)} fusion(f32[3584,128]{1,0:T(8,128)S(1)} %scatter_custom_fusion, s32[4096]{0:T(1024)S(1)} %get-tuple-element.6, bf16[4096,128]{1,0:T(8,128)(2,1)S(1)} %copy-done.4, f32[4096]{0:T(1024)S(1)} %get-tuple-element.9), kind=kCustom, calls=%fused_computation.28 | custom fusion | flops 2097152 | bytes 2899968 | tf_op jit(solution)/shard_map/scatter-add | solution.py:114
  110.8 22.0 %all-to-all-done = f32[32,48,129]{2,1,0:T(8,128)} async-done(((f32[32,48,129]{2,1,0:T(8,128)}), f32[32,48,129]{2,1,0:T(8,128)}, u32[]{:S(2)}, u32[]{:S(2)}) %all-to-all-start) | async-done | bytes 792608 | tf_op jit(solution)/shard_map/all_to_all | solution.py:19
  159.9 13.5 %all-to-all-done.1 = f32[4,512,129]{1,2,0:T(8,128)S(1)} async-done(((f32[4,512,129]{1,2,0:T(8,128)}), f32[4,512,129]{1,2,0:T(8,128)S(1)}, u32[]{:S(2)}, u32[]{:S(2)}) %all-to-all-start.1) | async-done | bytes 1056800 | tf_op jit(solution)/shard_map/all_to_all | solution.py:38
  179.3 11.5 %all-to-all-done.2 = f32[4,512,128]{2,1,0:T(8,128)S(1)} async-done(((f32[4,512,128]{2,1,0:T(8,128)}), f32[4,512,128]{2,1,0:T(8,128)S(1)}, u32[]{:S(2)}, u32[]{:S(2)}) %all-to-all-start.2) | async-done | bytes 1048608 | tf_op jit(solution)/shard_map/all_to_all | solution.py:60
  194.5 11.6 %all-to-all-start.3 = ((f32[32,1,48,128]{3,2,1,0:T(8,128)}), f32[32,1,48,128]{3,2,1,0:T(8,128)S(1)}, u32[]{:S(2)}, u32[]{:S(2)}) async-start(f32[32,1,48,128]{3,2,1,0:T(8,128)} %bitcast.8), calls=%async_computation.3 | async-start | bytes 1572864 | tf_op jit(solution)/shard_map/all_to_all | solution.py:84
  206.0 14.1 %gather_fusion = f32[4096,128]{1,0:T(8,128)} fusion(f32[2048,128]{1,0:T(8,128)S(1)} %bitcast.45, s32[4096]{0:T(1024)S(1)} %get-tuple-element.7), kind=kCustom, calls=%fused_computation | custom fusion | bytes 4210688 | tf_op jit(solution)/shard_map/gather | solution.py:91
  222.4 14.1 %gather_fusion.2 = f32[4096,128]{1,0:T(8,128)} fusion(f32[3584,128]{1,0:T(8,128)S(1)} %pad_maximum_fusion, s32[4096]{0:T(1024)S(1)} %get-tuple-element.5), kind=kCustom, calls=%fused_computation.2 | custom fusion | bytes 4210688 | tf_op jit(solution)/shard_map/gather | solution.py:91
  236.5 26.3 %scatter_custom_fusion.6 = f32[3584,128]{1,0:T(8,128)} fusion(s32[4096]{0:T(1024)S(1)} %get-tuple-element.8, f32[]{:T(128)} %constant.14.clone.1, f32[4096,128]{1,0:T(8,128)} %gather_fusion, f32[4096,128]{1,0:T(8,128)} %gather_fusion.2, f32[4096]{0:T(1024)S(1)} %get-tuple-element.10), kind=kCustom, calls=%fused_computation.41 | custom fusion | flops 1572864 | bytes 6045700 | tf_op jit(solution)/shard_map/scatter-add | solution.py:93
  262.8 27.5 %scatter_custom_fusion.7 = f32[3584,128]{1,0:T(8,128)} fusion(f32[3584,128]{1,0:T(8,128)} %scatter_custom_fusion.6, s32[4096]{0:T(1024)S(1)} %get-tuple-element.6, f32[4096,128]{1,0:T(8,128)S(1)} %copy-done.1, f32[4096,128]{1,0:T(8,128)} %gather_fusion.2, f32[4096]{0:T(1024)S(1)} %get-tuple-element.10), kind=kCustom, calls=%fused_computation.25 | custom fusion | flops 2097152 | bytes 6045696 | tf_op jit(solution)/shard_map/scatter-add | solution.py:93
  299.8 14.2 %all-to-all-done.4 = f32[32,1,48,128]{3,2,1,0:T(8,128)} async-done(((f32[32,1,48,128]{3,2,1,0:T(8,128)}), f32[32,1,48,128]{3,2,1,0:T(8,128)}, u32[]{:S(2)}, u32[]{:S(2)}) %all-to-all-start.4) | async-done | bytes 786464 | tf_op jit(solution)/shard_map/all_to_all | solution.py:95
  323.6 17.0 %all_to_all.60 = f32[4,512,128]{2,1,0:T(8,128)S(1)} all-to-all(f32[4,512,128]{2,1,0:T(8,128)S(1)} %bitcast.52), channel_id=1, replica_groups=mesh['vtx'=32,'edg'=4] {'edg'}, dimensions={0} | all-to-all | bytes 2097152 | tf_op jit(solution)/shard_map/all_to_all | solution.py:38
  341.0 15.8 %all_to_all.61 = f32[4,512,128]{2,1,0:T(8,128)S(1)} all-to-all(f32[4,512,128]{2,1,0:T(8,128)S(1)} %broadcast_in_dim.19), channel_id=1, replica_groups=mesh['vtx'=32,'edg'=4] {'edg'}, dimensions={0} | all-to-all | bytes 2097152 | tf_op jit(solution)/shard_map/all_to_all | solution.py:60
  367.9 14.1 %gather_fusion.3 = f32[4096,128]{1,0:T(8,128)} fusion(f32[2048,128]{1,0:T(8,128)S(1)} %bitcast.48, s32[4096]{0:T(1024)S(1)} %get-tuple-element.7), kind=kCustom, calls=%fused_computation.3 | custom fusion | bytes 4210688 | tf_op jit(solution)/shard_map/gather | solution.py:91
  384.3 14.1 %gather_fusion.5 = f32[4096,128]{1,0:T(8,128)} fusion(f32[3584,128]{1,0:T(8,128)S(1)} %pad_maximum_fusion.1, s32[4096]{0:T(1024)S(1)} %get-tuple-element.5), kind=kCustom, calls=%fused_computation.5 | custom fusion | bytes 4210688 | tf_op jit(solution)/shard_map/gather | solution.py:91
  398.3 26.3 %scatter_custom_fusion.9 = f32[3584,128]{1,0:T(8,128)} fusion(s32[4096]{0:T(1024)S(1)} %get-tuple-element.8, f32[]{:T(128)} %constant.14.clone.1, f32[4096,128]{1,0:T(8,128)} %gather_fusion.3, f32[4096,128]{1,0:T(8,128)} %gather_fusion.5, f32[4096]{0:T(1024)S(1)} %get-tuple-element.10), kind=kCustom, calls=%fused_computation.39 | custom fusion | flops 1572864 | bytes 6045700 | tf_op jit(solution)/shard_map/scatter-add | solution.py:93
  424.7 27.5 %scatter_custom_fusion.10 = f32[3584,128]{1,0:T(8,128)} fusion(f32[3584,128]{1,0:T(8,128)} %scatter_custom_fusion.9, s32[4096]{0:T(1024)S(1)} %get-tuple-element.6, f32[4096,128]{1,0:T(8,128)S(1)} %copy-done, f32[4096,128]{1,0:T(8,128)} %gather_fusion.5, f32[4096]{0:T(1024)S(1)} %get-tuple-element.10), kind=kCustom, calls=%fused_computation.22 | custom fusion | flops 2097152 | bytes 6045696 | tf_op jit(solution)/shard_map/scatter-add | solution.py:93
  461.7 14.2 %all-to-all-done.8 = f32[32,1,48,128]{3,2,1,0:T(8,128)} async-done(((f32[32,1,48,128]{3,2,1,0:T(8,128)}), f32[32,1,48,128]{3,2,1,0:T(8,128)}, u32[]{:S(2)}, u32[]{:S(2)}) %all-to-all-start.8) | async-done | bytes 786464 | tf_op jit(solution)/shard_map/all_to_all | solution.py:95
  485.5 17.0 %all_to_all.62 = f32[4,512,128]{2,1,0:T(8,128)S(1)} all-to-all(f32[4,512,128]{2,1,0:T(8,128)S(1)} %bitcast.51), channel_id=1, replica_groups=mesh['vtx'=32,'edg'=4] {'edg'}, dimensions={0} | all-to-all | bytes 2097152 | tf_op jit(solution)/shard_map/all_to_all | solution.py:38
  503.0 15.8 %all_to_all.63 = f32[4,512,128]{2,1,0:T(8,128)S(1)} all-to-all(f32[4,512,128]{2,1,0:T(8,128)S(1)} %broadcast_in_dim.20), channel_id=1, replica_groups=mesh['vtx'=32,'edg'=4] {'edg'}, dimensions={0} | all-to-all | bytes 2097152 | tf_op jit(solution)/shard_map/all_to_all | solution.py:60
  529.8 14.1 %gather_fusion.6 = f32[4096,128]{1,0:T(8,128)} fusion(f32[2048,128]{1,0:T(8,128)S(1)} %bitcast.41, s32[4096]{0:T(1024)S(1)} %get-tuple-element.7), kind=kCustom, calls=%fused_computation.6 | custom fusion | bytes 4210688 | tf_op jit(solution)/shard_map/gather | solution.py:153
  546.2 14.1 %gather_fusion.8 = f32[4096,128]{1,0:T(8,128)} fusion(f32[3584,128]{1,0:T(8,128)S(1)} %pad_maximum_fusion.2, s32[4096]{0:T(1024)S(1)} %get-tuple-element.5), kind=kCustom, calls=%fused_computation.8 | custom fusion | bytes 4210688 | tf_op jit(solution)/shard_map/gather | solution.py:153
  (80 shorter events, 124.0 us)
Async XLA Ops:
  25.5 23.9 %copy-start.4 = (bf16[4096,128]{1,0:T(8,128)(2,1)S(1)}, bf16[4096,128]{1,0:T(8,128)(2,1)}, u32[]{:S(2)}) copy-start(bf16[4096,128]{1,0:T(8,128)(2,1)} %param.7) | copy-start | bytes 3145732
  99.3 1.1 copy-start.8
  101.7 8.9 %copy-start.9 = (s32[1,32,48]{2,1,0:T(8,128)S(1)}, s32[1,32,48]{2,1,0:T(8,128)}, u32[]{:S(2)}) copy-start(s32[1,32,48]{2,1,0:T(8,128)} %param.12) | copy-start | bytes 18436
  101.7 31.1 %all-to-all-start = ((f32[32,48,129]{2,1,0:T(8,128)}), f32[32,48,129]{2,1,0:T(8,128)}, u32[]{:S(2)}, u32[]{:S(2)}) async-start(f32[32,48,129]{2,1,0:T(8,128)} %pad_maximum_fusion.3), calls=%async_computation | async-start | bytes 3145728 | tf_op jit(solution)/shard_map/all_to_all | solution.py:19
  154.9 18.5 %all-to-all-start.1 = ((f32[4,512,129]{1,2,0:T(8,128)}), f32[4,512,129]{1,2,0:T(8,128)S(1)}, u32[]{:S(2)}, u32[]{:S(2)}) async-start(f32[4,512,129]{1,2,0:T(8,128)} %pad_maximum_fusion.4), calls=%async_computation.1 | async-start | bytes 2228224 | tf_op jit(solution)/shard_map/all_to_all | solution.py:38
  175.7 15.1 %all-to-all-start.2 = ((f32[4,512,128]{2,1,0:T(8,128)}), f32[4,512,128]{2,1,0:T(8,128)S(1)}, u32[]{:S(2)}, u32[]{:S(2)}) async-start(f32[4,512,128]{2,1,0:T(8,128)} %broadcast_in_dim.17), calls=%async_computation.2 | async-start | bytes 2097152 | tf_op jit(solution)/shard_map/all_to_all | solution.py:60
  194.5 25.8 %all-to-all-start.3 = ((f32[32,1,48,128]{3,2,1,0:T(8,128)}), f32[32,1,48,128]{3,2,1,0:T(8,128)S(1)}, u32[]{:S(2)}, u32[]{:S(2)}) async-start(f32[32,1,48,128]{3,2,1,0:T(8,128)} %bitcast.8), calls=%async_computation.3 | async-start | bytes 1572864 | tf_op jit(solution)/shard_map/all_to_all | solution.py:84
  220.2 0.9 copy-start.5
  236.5 26.3 %copy-start.1 = (f32[4096,128]{1,0:T(8,128)S(1)}, f32[4096,128]{1,0:T(8,128)}, u32[]{:S(2)}) copy-start(f32[4096,128]{1,0:T(8,128)} %gather_fusion) | copy-start | bytes 6291460
  290.2 9.5 %copy-start.3 = (f32[3584,128]{1,0:T(8,128)S(1)}, f32[3584,128]{1,0:T(8,128)}, u32[]{:S(2)}) copy-start(f32[3584,128]{1,0:T(8,128)} %scatter_custom_fusion.7) | copy-start | bytes 5505028
  292.4 21.6 %all-to-all-start.4 = ((f32[32,1,48,128]{3,2,1,0:T(8,128)}), f32[32,1,48,128]{3,2,1,0:T(8,128)}, u32[]{:S(2)}, u32[]{:S(2)}) async-start(f32[32,1,48,128]{3,2,1,0:T(8,128)} %bitcast.11), calls=%async_computation.4 | async-start | bytes 1572864 | tf_op jit(solution)/shard_map/all_to_all | solution.py:95
  360.6 21.6 %all-to-all-start.7 = ((f32[32,1,48,128]{3,2,1,0:T(8,128)}), f32[32,1,48,128]{3,2,1,0:T(8,128)S(1)}, u32[]{:S(2)}, u32[]{:S(2)}) async-start(f32[32,1,48,128]{3,2,1,0:T(8,128)} %bitcast.16), calls=%async_computation.7 | async-start | bytes 1572864 | tf_op jit(solution)/shard_map/all_to_all | solution.py:84
  382.1 0.9 copy-start.6
  398.3 26.3 %copy-start = (f32[4096,128]{1,0:T(8,128)S(1)}, f32[4096,128]{1,0:T(8,128)}, u32[]{:S(2)}) copy-start(f32[4096,128]{1,0:T(8,128)} %gather_fusion.3) | copy-start | bytes 6291460
  452.1 9.5 %copy-start.2 = (f32[3584,128]{1,0:T(8,128)S(1)}, f32[3584,128]{1,0:T(8,128)}, u32[]{:S(2)}) copy-start(f32[3584,128]{1,0:T(8,128)} %scatter_custom_fusion.10) | copy-start | bytes 5505028
  454.3 21.6 %all-to-all-start.8 = ((f32[32,1,48,128]{3,2,1,0:T(8,128)}), f32[32,1,48,128]{3,2,1,0:T(8,128)}, u32[]{:S(2)}, u32[]{:S(2)}) async-start(f32[32,1,48,128]{3,2,1,0:T(8,128)} %bitcast.19), calls=%async_computation.8 | async-start | bytes 1572864 | tf_op jit(solution)/shard_map/all_to_all | solution.py:95
  522.5 21.6 %all-to-all-start.11 = ((f32[32,1,48,128]{3,2,1,0:T(8,128)}), f32[32,1,48,128]{3,2,1,0:T(8,128)S(1)}, u32[]{:S(2)}, u32[]{:S(2)}) async-start(f32[32,1,48,128]{3,2,1,0:T(8,128)} %bitcast.24), calls=%async_computation.11 | async-start | bytes 1572864 | tf_op jit(solution)/shard_map/all_to_all | solution.py:84
  544.1 0.9 copy-start.7
where the time goes:
time: 566 us; the launch traced here: 565 us
  other arithmetic  252 us (45%)
  local copies, waits for them, and re-layouts  111 us (20%)
  waiting for transfers between devices  75.8 us (13%)
  blocking collectives  65.8 us (12%)
  starting transfers between devices  58.2 us (10%)
    scatter-add x4, other arithmetic, edge_part(): summed = summed.at[sources].add(edge_diffs).at[targets].add(-edge_diffs)  108 us
    gather x4, local copies, waits for them, and re-layouts, edge_part(): edge_diffs = weights[:, None] * (field_in[sources] - extended[targets])  56.4 us
    scatter-add x2, other arithmetic, local(): summed = summed.at[src_local].add(edge_terms).at[dst_index].add(-edge_terms)  49.8 us
    scatter-add x2, other arithmetic, local(): degrees.at[src_local].add(weight_live).at[dst_index].add(weight_live)  44.5 us
    all_to_all x2, blocking collectives, summed_on_arrival(): lax.all_to_all(tiles, axis, split_axis=0, concat_axis=0, tiled=True)  34.1 us
    all_to_all x2, blocking collectives, sent_to_all(): lax.all_to_all(jnp.broadcast_to(shard[None], (length, *shard.shape)), axi...  31.7 us
    all_to_all x2, waiting for transfers between devices, edge_part(): lax.all_to_all(outgoing, 'vtx', split_axis=0, concat_axis=0, tiled=True)  28.4 us
    gather x2, local copies, waits for them, and re-layouts, local(): gaps = solution[src_local] - extended[dst_index]  28.2 us
  transfers between devices with their start and end apart: 8, of which 8 were waited for; matrix products, arithmetic and copies ran while one was open for 8% of the time, Pallas kernels for 0%

commit v1 on v0

v1 whole, which is shorter than its diff:
```python
import functools

import jax
import jax.numpy as jnp
from jax import lax
from jax.experimental import pallas as pl
from jax.experimental.pallas import tpu as pltpu
from jax.sharding import PartitionSpec as P

ITERS = 3
LANES = 128
UNROLL = 16
BANKS = 4

lam_low = 0.05
lam_high = 2.0

SMEM = pl.BlockSpec(memory_space=pltpu.SMEM)
VMEM = pl.BlockSpec(memory_space=pltpu.VMEM)
LIMIT = 48 * 2**20


def chebyshev_terms(steps):
    centre = (lam_high + lam_low) / 2.0
    half_width = (lam_high - lam_low) / 2.0
    sigma_val = centre / half_width
    rho_prev = 1.0 / sigma_val
    pairs = []
    for count_idx in range(steps - 1):
        rho_next = 1.0 / (2.0 * sigma_val - rho_prev)
        pairs.append((rho_next * rho_prev, 2.0 * rho_next / half_width))
        rho_prev = rho_next
    return (1.0 / centre, pairs)


def call(kernel, outs, ins, scratch, name, flops=0, moved=2**22):
    return pl.pallas_call(
        kernel,
        out_shape=[jax.ShapeDtypeStruct(shape, dtype) for shape, dtype, _ in outs],
        in_specs=ins,
        out_specs=[space for _, _, space in outs],
        scratch_shapes=scratch,
        compiler_params=pltpu.CompilerParams(vmem_limit_bytes=LIMIT),
        cost_estimate=pl.CostEstimate(flops=flops, bytes_accessed=moved, transcendentals=0),
        name=name,
    )


def split(x):
    high = x.astype(jnp.bfloat16)
    return high, (x - high.astype(jnp.float32)).astype(jnp.bfloat16)


def put_split(ref, rows, x):
    high, low = split(x)
    ref[rows, :LANES] = high
    ref[rows, LANES:] = low


def halves(x):
    return x[:, :LANES] + x[:, LANES:]


def one_hot(row, height, base):
    place = lax.broadcasted_iota(jnp.int32, (height, row.shape[1]), 0) + base
    return jnp.where(place == row, 1.0, 0.0)


def factored(pick, groups, high_of, low_of, weight_of, height):
    total = jnp.zeros((2 * height, LANES), jnp.float32)
    for k0 in range(0, groups, pick):
        left, right = [], []
        for k in range(k0, k0 + pick):
            member = one_hot(high_of(k), height, 0) * weight_of(k)
            high, low = split(member)
            left.append(jnp.concatenate([high, low], axis=0))
            right.append(one_hot(low_of(k), LANES, 0).astype(jnp.bfloat16))
        total = total + lax.dot_general(
            jnp.concatenate(left, axis=1),
            jnp.concatenate(right, axis=1),
            (((1,), (1,)), ((), ())),
            preferred_element_type=jnp.float32,
        )
    return total[:height] + total[height:]


def halo_side_kernel(rows, slots, width, terms, target, weight, out, both, hot):
    groups = target.shape[0]
    edges = terms.shape[0]
    put_split(both, slice(None), terms[...])
    tall = hot.shape[0]
    per = tall // width

    def chunk(i, _):
        base = rows + i * tall
        for k in range(groups):
            hot[:, k * LANES : (k + 1) * LANES] = one_hot(target[k : k + 1, :], tall, base).astype(jnp.bfloat16)
        got = halves(jnp.dot(hot[...], both[...], preferred_element_type=jnp.float32))
        for c in range(per):
            out[i * per + c, :width, :] = -got[c * width : (c + 1) * width]
        return 0

    lax.fori_loop(0, slots // tall, chunk, 0)
    blocks = slots // width

    def slot(k):
        return target[k : k + 1, :] - rows

    def block_of(k):
        return jnp.where(slot(k) < 0, -1, lax.shift_right_arithmetic(slot(k) * 1366, 16))

    def within(k):
        return slot(k) - block_of(k) * width

    deg = factored(4, groups, block_of, within, lambda k: weight[k : k + 1, :], blocks)
    for c in range(blocks):
        out[c, width : width + 8, :] = jnp.broadcast_to(deg[c : c + 1, :], (8, LANES))


def own_side_kernel(terms, source, target, weight, out, degree, both, hot):
    groups = target.shape[0]
    rows = out.shape[0]
    put_split(both, slice(None), terms[...])
    tall = hot.shape[0]

    def chunk(i, _):
        base = i * tall
        for k in range(groups):
            plus = one_hot(source[k : k + 1, :], tall, base)
            minus = one_hot(target[k : k + 1, :], tall, base)
            hot[:, k * LANES : (k + 1) * LANES] = (plus - minus).astype(jnp.bfloat16)
        out[pl.ds(pl.multiple_of(i * tall, tall), tall), :] = halves(
            jnp.dot(hot[...], both[...], preferred_element_type=jnp.float32)
        )
        return 0

    lax.fori_loop(0, rows // tall, chunk, 0)

    def total(ref):
        return factored(
            4,
            groups,
            lambda k: lax.shift_right_logical(ref[k : k + 1, :], 7),
            lambda k: ref[k : k + 1, :] & (LANES - 1),
            lambda k: weight[k : k + 1, :],
            rows // LANES,
        )

    degree[...] = total(source) + total(target)


def scatter_back(ret_both, listed, hot, emit, rows):
    tall = hot.shape[0]
    groups = listed.shape[0]

    def chunk(i, _):
        base = i * tall
        for k in range(groups):
            hot[:, k * LANES : (k + 1) * LANES] = one_hot(listed[k : k + 1, :], tall, base).astype(jnp.bfloat16)
        emit(i, halves(jnp.dot(hot[...], ret_both[...], preferred_element_type=jnp.float32)))
        return 0

    lax.fori_loop(0, rows // tall, chunk, 0)


def side_join_kernel(lane, returned, listed, padded, own, own_degree, *refs):
    lanes = 4
    outs, (acc, ret_both, hot) = refs[:lanes], refs[lanes:]
    blocks = returned.shape[0]
    rows = own.shape[0]
    width = listed.shape[0] * LANES // blocks
    share = rows // lanes
    for c in range(blocks):
        put_split(ret_both, slice(c * width, (c + 1) * width), returned[c, :width, :])

    def emit(i, got):
        at = pl.ds(pl.multiple_of(i * hot.shape[0], hot.shape[0]), hot.shape[0])
        acc[at, :] = own[at, :] + got

    scatter_back(ret_both, listed, hot, emit, rows)
    deg = own_degree[...] + factored(
        4,
        blocks,
        lambda k: lax.shift_right_arithmetic(padded[k : k + 1, :], 7),
        lambda k: padded[k : k + 1, :] & (LANES - 1),
        lambda k: returned[k, width : width + 1, :],
        rows // LANES,
    )
    deg_rows = share // LANES
    for s in range(lanes):
        q = lax.rem(lane[0] + s, lanes)
        outs[s][:share, :] = acc[pl.ds(pl.multiple_of(q * share, share), share), :]
        row = jnp.zeros((8, LANES), jnp.float32)
        place = lax.broadcasted_iota(jnp.int32, (8, LANES), 0)
        for p in range(lanes):
            for d in range(deg_rows):
                one = jnp.broadcast_to(deg[p * deg_rows + d : p * deg_rows + d + 1, :], (8, LANES))
                row = jnp.where((place == d) & (q == p), one, row)
        outs[s][share : share + 8, :] = row


def partition_kernel(rows, count, source, target, weight, order, heavy, edge, sizes):
    second = order.shape[0] // 2

    def step(i, at):
        near, far = at
        for u in range(8):
            e = i * 8 + u
            t = target[e]
            away = (t >= rows).astype(jnp.int32)
            pos = jnp.where(away == 1, far + second, near)
            order[pos] = source[e] | ((t - away * rows) << 12)
            heavy[pos] = weight[e]
            edge[pos] = e
            near, far = near + 1 - away, far + away
        return near, far

    near, far = lax.fori_loop(0, (count[0] + 7) // 8, step, (0, 0))
    for u in range(UNROLL):
        for pos in (near + u, far + second + u):
            order[pos] = 0
            heavy[pos] = 0.0
            edge[pos] = 0
    sizes[0] = near
    sizes[1] = far


def trips(n):
    return lax.div(n + UNROLL - 1, UNROLL)


def clear(banks):
    for a in banks:
        a[...] = jnp.zeros_like(a)


def field_kernel(lane, sizes, order, heavy, lists, *refs):
    lanes = 4
    shares, (field, out), banks = refs[:lanes], refs[lanes : lanes + 2], refs[lanes + 2 :]
    share = shares[0].shape[0]
    blocks, both, _ = out.shape
    width = both // 2
    second = order.shape[0] // 2
    for s in range(lanes):
        q = lax.rem(lane[0] - s + lanes, lanes)
        field[pl.ds(pl.multiple_of(q * share, share), share), :] = shares[s][...]

    def pack(c, _):
        for r in range(width):
            out[c, pl.ds(r, 1), :] = field[pl.ds(lists[c * width + r], 1), :]
        return 0

    lax.fori_loop(0, blocks, pack, 0)
    clear(banks)

    def step(i, _):
        for u in range(0, UNROLL, BANKS):
            at = second + i * UNROLL + u
            code = [order[at + k] for k in range(BANKS)]
            rows = [field[pl.ds(code[k] & 4095, 1), :] * heavy[at + k] for k in range(BANKS)]
            to = [pl.ds(code[k] >> 12, 1) for k in range(BANKS)]
            new = [banks[k][to[k], :] + rows[k] for k in range(BANKS)]
            for k in range(BANKS):
                banks[k][to[k], :] = new[k]
        return 0

    lax.fori_loop(0, trips(sizes[1]), step, 0)
    total = banks[0][...]
    for a in banks[1:]:
        total = total + a[...]
    for c in range(blocks):
        out[c, width:, :] = total[c * width : (c + 1) * width]


def near_kernel(sizes, order, heavy, field, out, *banks):
    clear(banks)

    def step(i, _):
        for u in range(0, UNROLL, BANKS):
            at = i * UNROLL + u
            code = [order[at + k] for k in range(BANKS)]
            mass = [heavy[at + k] for k in range(BANKS)]
            one = [pl.ds(code[k] & 4095, 1) for k in range(BANKS)]
            two = [pl.ds(code[k] >> 12, 1) for k in range(BANKS)]
            from_one = [field[one[k], :] * mass[k] for k in range(BANKS)]
            from_two = [field[two[k], :] * mass[k] for k in range(BANKS)]
            new = [banks[k][one[k], :] + from_two[k] for k in range(BANKS)]
            for k in range(BANKS):
                banks[k][one[k], :] = new[k]
            new = [banks[k][two[k], :] + from_one[k] for k in range(BANKS)]
            for k in range(BANKS):
                banks[k][two[k], :] = new[k]
        return 0

    lax.fori_loop(0, trips(sizes[0]), step, 0)
    total = banks[0][...]
    for a in banks[1:]:
        total = total + a[...]
    out[...] = total


def flow_join_kernel(lane, sizes, order, heavy, listed, near, arrived, *refs):
    lanes = 4
    outs, ret_both, hot, banks = refs[:lanes], refs[lanes], refs[lanes + 1], refs[lanes + 2 :]
    blocks, both, _ = arrived.shape
    width = both // 2
    rows = near.shape[0]
    share = rows // lanes
    second = order.shape[0] // 2
    halo = banks[-1]
    banks = banks[:-1]
    for c in range(blocks):
        halo[c * width : (c + 1) * width, :] = arrived[c, :width, :]
        put_split(ret_both, slice(c * width, (c + 1) * width), arrived[c, width:, :])

    def emit(i, got):
        at = pl.ds(pl.multiple_of(i * hot.shape[0], hot.shape[0]), hot.shape[0])
        banks[0][at, :] = near[at, :] + got

    scatter_back(ret_both, listed, hot, emit, rows)
    clear(banks[1:])

    def step(i, _):
        for u in range(0, UNROLL, BANKS):
            at = second + i * UNROLL + u
            code = [order[at + k] for k in range(BANKS)]
            got = [halo[pl.ds(code[k] >> 12, 1), :] * heavy[at + k] for k in range(BANKS)]
            to = [pl.ds(code[k] & 4095, 1) for k in range(BANKS)]
            new = [banks[k][to[k], :] + got[k] for k in range(BANKS)]
            for k in range(BANKS):
                banks[k][to[k], :] = new[k]
        return 0

    lax.fori_loop(0, trips(sizes[1]), step, 0)
    for s in range(lanes):
        q = lax.rem(lane[0] + s, lanes)
        at = pl.ds(pl.multiple_of(q * share, share), share)
        total = banks[0][at, :]
        for a in banks[1:]:
            total = total + a[at, :]
        outs[s][...] = total


def solution_kernel(lane, lists, *refs):
    lanes = 4
    shares, (field, out) = refs[:lanes], refs[lanes:]
    share = shares[0].shape[0]
    blocks, width, _ = out.shape
    for s in range(lanes):
        q = lax.rem(lane[0] - s + lanes, lanes)
        field[pl.ds(pl.multiple_of(q * share, share), share), :] = shares[s][...]

    def pack(c, _):
        for r in range(width):
            out[c, pl.ds(r, 1), :] = field[pl.ds(lists[c * width + r], 1), :]
        return 0

    lax.fori_loop(0, blocks, pack, 0)


def near_gap_kernel(count, source, target, field, gaps, more):
    rows = field.shape[0]
    more[:rows, :] = field[...]
    more[rows:, :] = jnp.zeros((more.shape[0] - rows, LANES), jnp.float32)

    def step(i, _):
        for u in range(UNROLL):
            e = i * UNROLL + u
            t = jnp.minimum(target[e], rows)
            gaps[pl.ds(e, 1), :] = field[pl.ds(source[e], 1), :] - more[pl.ds(t, 1), :]
        return 0

    lax.fori_loop(0, trips(count[0]), step, 0)


def far_gap_kernel(sizes, order, edge, near_gaps, halo, live, out, gaps):
    second = order.shape[0] // 2
    edges = near_gaps.shape[0]
    groups = edges // LANES
    gaps[:edges, :] = near_gaps[...]

    def step(i, _):
        left = sizes[1] - i * UNROLL
        for u in range(0, UNROLL, BANKS):
            at = second + i * UNROLL + u
            to = [pl.ds(jnp.where(u + k < left, edge[at + k], edges), 1) for k in range(BANKS)]
            new = [gaps[to[k], :] - halo[pl.ds(order[at + k] >> 12, 1), :] for k in range(BANKS)]
            for k in range(BANKS):
                gaps[to[k], :] = new[k]
        return 0

    lax.fori_loop(0, trips(sizes[1]), step, 0)
    for k in range(groups):
        gap = gaps[k * LANES : (k + 1) * LANES, :]
        total = jnp.sum((gap * gap).T, axis=0, keepdims=True)
        alive = live[k : k + 1, :]
        out[k : k + 1, :] = jnp.where(alive > 0, total * (alive / LANES), 0.0)


def passed_round(blocks, lanes, sign):
    return [blocks[0]] + [
        lax.ppermute(blocks[s], "edg", [(i, (i + sign * s) % lanes) for i in range(lanes)]) for s in (2, 1, 3)
    ]


def summed(blocks, lanes):
    got = passed_round(blocks, lanes, 1)
    return got[0] + got[1] + got[2] + got[3]


def to_all(mine, lanes):
    home, two, one, three = passed_round([mine] * lanes, lanes, 1)
    return [home, one, two, three]


def across(x):
    return lax.all_to_all(x, "vtx", split_axis=0, concat_axis=0, tiled=True)


def local(sketch_cols, edge_weight, ground, src_local, dst_index, send_rows, edge_count):
    blocks = lax.axis_size("vtx")
    lanes = lax.axis_size("edg")
    rows = ground.shape[0]
    edges = edge_weight.shape[0]
    width = send_rows.shape[2]
    slots = blocks * width
    share = rows // lanes
    groups = edges // LANES
    f32, i32, bf16 = jnp.float32, jnp.int32, jnp.bfloat16
    lane = lax.axis_index("edg").astype(i32).reshape(1)
    lists = send_rows[0].reshape(-1)
    listed = lists.reshape(slots // LANES, LANES)
    padded = jnp.pad(send_rows[0], ((0, 0), (0, LANES - width)), constant_values=-1)
    live = (jnp.arange(edges, dtype=i32) < edge_count[0]).astype(f32)
    weight = edge_weight * live
    root = jnp.sqrt(edge_weight) * live
    terms = root[:, None] * sketch_cols.astype(f32)
    live_rows = live.reshape(groups, LANES)
    weight_rows = weight.reshape(groups, LANES)
    source_rows = src_local.reshape(groups, LANES)
    target_rows = dst_index.reshape(groups, LANES)

    outgoing = call(
        functools.partial(halo_side_kernel, rows, slots, width),
        [((blocks, width + 8, LANES), f32, VMEM)],
        [VMEM] * 3,
        [pltpu.VMEM((edges, 2 * LANES), bf16), pltpu.VMEM((8 * width, edges), bf16)],
        "halo_side",
        flops=2 * slots * edges * 2 * LANES,
    )(terms, target_rows, weight_rows)[0]
    returned = across(outgoing)
    own, own_degree = call(
        own_side_kernel,
        [((rows, LANES), f32, VMEM), ((rows // LANES, LANES), f32, VMEM)],
        [VMEM] * 4,
        [pltpu.VMEM((edges, 2 * LANES), bf16), pltpu.VMEM((256, edges), bf16)],
        "own_side",
        flops=2 * rows * edges * 2 * LANES,
    )(terms, source_rows, target_rows, weight_rows)
    room = edges + LANES
    order, heavy, edge, sizes = call(
        functools.partial(partition_kernel, rows),
        [((2 * room,), i32, SMEM), ((2 * room,), f32, SMEM), ((2 * room,), i32, SMEM), ((2,), i32, SMEM)],
        [SMEM] * 4,
        [],
        "partition",
        moved=2**25,
    )(edge_count, src_local, dst_index, weight)
    sides = call(
        side_join_kernel,
        [((share + 8, LANES), f32, VMEM)] * lanes,
        [SMEM] + [VMEM] * 5,
        [pltpu.VMEM((rows, LANES), f32), pltpu.VMEM((slots, 2 * LANES), bf16), pltpu.VMEM((256, slots), bf16)],
        "side_join",
        flops=2 * rows * slots * 2 * LANES,
    )(lane, returned, listed, padded, own, own_degree)
    side = summed(sides, lanes)
    right_share = side[:share]
    degree_share = side[share : share + share // LANES].reshape(share)
    ground_share = lax.dynamic_slice_in_dim(ground, lane[0] * share, share)
    diagonal = (degree_share + ground_share)[:, None]
    inverse = 1.0 / diagonal

    first, pairs = chebyshev_terms(ITERS)
    residual = right_share
    direction = first * inverse * right_share
    solution_share = direction
    for keep, push in pairs:
        field, message = call(
            field_kernel,
            [((rows, LANES), f32, VMEM), ((blocks, 2 * width, LANES), f32, VMEM)],
            [SMEM] * 5 + [VMEM] * lanes,
            [pltpu.VMEM((slots, LANES), f32)] * BANKS,
            "field",
        )(lane, sizes, order, heavy, lists, *to_all(direction, lanes))
        arrived = across(message)
        near = call(
            near_kernel,
            [((rows, LANES), f32, VMEM)],
            [SMEM] * 3 + [VMEM],
            [pltpu.VMEM((rows, LANES), f32)] * BANKS,
            "near",
            moved=2**25,
        )(sizes, order, heavy, field)[0]
        flows = call(
            flow_join_kernel,
            [((share, LANES), f32, VMEM)] * lanes,
            [SMEM] * 4 + [VMEM] * 3,
            [pltpu.VMEM((slots, 2 * LANES), bf16), pltpu.VMEM((256, slots), bf16)]
            + [pltpu.VMEM((rows, LANES), f32)] * BANKS
            + [pltpu.VMEM((slots, LANES), f32)],
            "flow_join",
            flops=2 * rows * slots * 2 * LANES,
        )(lane, sizes, order, heavy, listed, near, arrived)
        residual = residual - (diagonal * direction - summed(flows, lanes))
        direction = keep * direction + push * inverse * residual
        solution_share = solution_share + direction
    field, message = call(
        solution_kernel,
        [((rows, LANES), f32, VMEM), ((blocks, width, LANES), f32, VMEM)],
        [SMEM] * 2 + [VMEM] * lanes,
        [],
        "solution_rows",
    )(lane, lists, *to_all(solution_share, lanes))
    halo = across(message)
    gaps = call(
        near_gap_kernel,
        [((edges, LANES), f32, VMEM)],
        [SMEM] * 3 + [VMEM],
        [pltpu.VMEM((rows + 8, LANES), f32)],
        "near_gap",
        moved=2**25,
    )(edge_count, src_local, dst_index, field)[0]
    resistance = call(
        far_gap_kernel,
        [((groups, LANES), f32, VMEM)],
        [SMEM] * 3 + [VMEM] * 3,
        [pltpu.VMEM((edges + 8, LANES), f32)],
        "far_gap",
    )(sizes, order, edge, gaps, halo.reshape(slots, LANES), live_rows)[0]
    return (field, resistance.reshape(edges))


def solution(mesh):
    in_specs = (
        P(("vtx", "edg"), None),
        P(("vtx", "edg")),
        P("vtx"),
        P(("vtx", "edg")),
        P(("vtx", "edg")),
        P(("vtx", "edg"), None, None),
        P(("vtx", "edg")),
    )
    out_specs = (P("vtx", None), P(("vtx", "edg")))
    return jax.shard_map(local, mesh=mesh, in_specs=in_specs, out_specs=out_specs, check_vma=False)
```

time: 566 us -> 278 us (0.49)
  other arithmetic: 252 us -> 4.88 us
  local copies, waits for them, and re-layouts: 111 us -> 8.92 us
  blocking collectives: 65.8 us -> 0 us
  Pallas kernels: 0 us -> 65 us
  waiting for transfers between devices: 75.8 us -> 112 us
  starting transfers between devices: 58.2 us -> 82.6 us
    scatter-add x12 -> x0, other arithmetic: 239 us -> none  [the longest x4 108 us: edge_part(): summed = summed.at[sources].add(edge_diffs).at[targets].add(-edge_diffs)]
    gather x9 -> x0, local copies, waits for them, and re-layouts: 95.6 us -> none  [the longest x4 56.4 us: edge_part(): edge_diffs = weights[:, None] * (field_in[sources] - extended[targets])]
    all_to_all x4 -> x0, blocking collectives: 65.8 us -> none  [the longest x2 34.1 us: summed_on_arrival(): lax.all_to_all(tiles, axis, split_axis=0, concat_axis=0, tiled=True)]
    pallas_call x0 -> x13, Pallas kernels: none -> 65 us  [the longest x1 12 us: local(): call(own_side_kernel, [((rows, LANES), f32, VMEM), ((rows // LANES, LANES...]
    ppermute x0 -> x18, waiting for transfers between devices: none -> 62.2 us  [passed_round(): lax.ppermute(blocks[s], 'edg', [(i, (i + sign * s) % lanes) for i in rang...]
    ppermute x0 -> x18, starting transfers between devices: none -> 26.8 us  [passed_round(): lax.ppermute(blocks[s], 'edg', [(i, (i + sign * s) % lanes) for i in rang...]
    all_to_all x8 -> x4, waiting for transfers between devices: 75.8 us -> 49.7 us  [across(): return lax.all_to_all(x, 'vtx', split_axis=0, concat_axis=0, tiled=True)]
    slice x10 -> x0, local copies, waits for them, and re-layouts: 7.26 us -> none  [the longest x2 4.39 us: edge_part(): summed[num_rows:].reshape(list_table.shape + (field_in.shape[1],))]
  transfers between devices with their start and end apart: 8 -> 22, of which waited for: 8 -> 16; matrix products, arithmetic and copies ran while one was open for 8% -> 0% of each run, Pallas kernels for 0% -> 10%
where the time goes in v1:
time: 278 us; the launch traced here: 275 us
  waiting for transfers between devices  112 us (40%)
  starting transfers between devices  82.6 us (30%)
  Pallas kernels  65 us (23%)
  local copies, waits for them, and re-layouts  8.92 us (3%)
  other arithmetic  4.88 us (2%)
    ppermute x18, waiting for transfers between devices, passed_round(): lax.ppermute(blocks[s], 'edg', [(i, (i + sign * s) % lanes) for i in rang...  62.2 us
    all_to_all x4, starting transfers between devices, across(): return lax.all_to_all(x, 'vtx', split_axis=0, concat_axis=0, tiled=True)  55.9 us
    all_to_all x4, waiting for transfers between devices, across(): return lax.all_to_all(x, 'vtx', split_axis=0, concat_axis=0, tiled=True)  49.7 us
    ppermute x18, starting transfers between devices, passed_round(): lax.ppermute(blocks[s], 'edg', [(i, (i + sign * s) % lanes) for i in rang...  26.8 us
    pallas_call x1, Pallas kernels, local(): call(own_side_kernel, [((rows, LANES), f32, VMEM), ((rows // LANES, LANES...  12 us
    pallas_call x2, Pallas kernels, local(): call(flow_join_kernel, [((share, LANES), f32, VMEM)] * lanes, [SMEM] * 4...  11.6 us
    pallas_call x2, Pallas kernels, local(): call(field_kernel, [((rows, LANES), f32, VMEM), ((blocks, 2 * width, LANE...  10.6 us
    unnamed x24, local copies, waits for them, and re-layouts  8.77 us
  transfers between devices with their start and end apart: 22, of which 16 were waited for; matrix products, arithmetic and copies ran while one was open for 0% of the time, Pallas kernels for 10%

profile of v1, /device:TPU:1, one launch (start us, length us, event | category | flops | bytes accessed | tf_op | source)
XLA Modules:
  0.0 274.9 jit_solution(299663459568244615)
XLA Ops:
  3.9 5.1 %halo_side.1 = f32[32,56,128]{2,1,0:T(8,128)S(1)} custom-call(f32[4096,128]{1,0:T(8,128)S(1)} %convert_multiply_fusion.terms, s32[32,128]{1,0:T(8,128)S(1)} %bitcast.16, f32[32,128]{1,0:T(8,128)S(1)} %bitcast.19), custom_call_target="tpu_custom_call" | custom-call | flops 3221225472 | bytes 4194304 | tf_op jit(solution)/shard_map/halo_side/pallas_call | solution.py:443
  10.0 8.6 %all-to-all-start = ((f32[32,56,128]{2,1,0:T(8,128)}), f32[32,56,128]{2,1,0:T(8,128)S(1)}, u32[]{:S(2)}, u32[]{:S(2)}) async-start(f32[32,56,128]{2,1,0:T(8,128)} %copy-done.5), calls=%async_computation | async-start | bytes 1835008 | tf_op jit(solution)/shard_map/all_to_all | solution.py:417
  18.7 12.0 %own_side.1 = (f32[2048,128]{1,0:T(8,128)S(1)}, f32[16,128]{1,0:T(8,128)S(1)}) custom-call(f32[4096,128]{1,0:T(8,128)S(1)} %convert_multiply_fusion.terms, s32[32,128]{1,0:T(8,128)S(1)} %bitcast.18, s32[32,128]{1,0:T(8,128)S(1)} %bitcast.17, f32[32,128]{1,0:T(8,128)S(1)} %bitcast.20), custom_call_target="tpu_custom_call" | custom-call | flops 4294967296 | bytes 4194304 | tf_op jit(solution)/shard_map/own_side/pallas_call | solution.py:452
  35.6 3.6 %side_join.1 = (f32[520,128]{1,0:T(8,128)S(1)}, f32[520,128]{1,0:T(8,128)S(1)}, f32[520,128]{1,0:T(8,128)S(1)}, f32[520,128]{1,0:T(8,128)S(1)}) custom-call(s32[1]{0:T(128)} %bitcast.lane, f32[32,56,128]{2,1,0:T(8,128)S(1)} %all-to-all-done.returned, s32[12,128]{1,0:T(8,128)S(1)} %reshape_reshape_squeeze.3.listed, s32[32,128]{1,0:T(8,128)S(1)} %pad.4.padded, ...), custom_call_target="tpu_custom_call" | custom-call | flops 1610612736 | bytes 4194304 | tf_op jit(solution)/shard_map/side_join/pallas_call | solution.py:469
  39.2 3.8 %collective-permute-start.2 = (f32[520,128]{1,0:T(8,128)S(1)}, f32[520,128]{1,0:T(8,128)S(1)}, u32[]{:S(2)}, u32[]{:S(2)}) collective-permute-start(f32[520,128]{1,0:T(8,128)S(1)} %get-tuple-element.31), channel_id=1, source_target_pairs={{0,3},{1,0},{2,1},{3,2},{4,7},{5,4},{6,5},{7,6},{8,11},{9,8},{10,9... | collective-permute-start | bytes 798728 | tf_op jit(solution)/shard_map/ppermute | solution.py:402
  44.3 9.8 %collective-permute-done.2 = f32[520,128]{1,0:T(8,128)S(1)} collective-permute-done((f32[520,128]{1,0:T(8,128)S(1)}, f32[520,128]{1,0:T(8,128)S(1)}, u32[]{:S(2)}, u32[]{:S(2)}) %collective-permute-start.2) | collective-permute-done | bytes 266272 | tf_op jit(solution)/shard_map/ppermute | solution.py:402
  61.0 7.0 %partition.1 = (s32[8448]{0:T(1024)S(1)}, f32[8448]{0:T(1024)S(1)}, s32[8448]{0:T(1024)S(1)}, s32[2]{0:T(128)S(1)}) custom-call(s32[1]{0:T(128)} %copy.9.count, s32[4096]{0:T(1024)S(1)} %copy-done.7, s32[4096]{0:T(1024)S(1)} %copy-done.6, f32[4096]{0:T(1024)S(1)} %get-tuple-element.54.weight), custom_call_target="tpu_custom_call" | custom-call | bytes 33554432 | tf_op jit(solution)/shard_map/partition/pallas_call | solution.py:461
  72.2 5.3 %field.2 = (f32[2048,128]{1,0:T(8,128)S(1)}, f32[32,96,128]{2,1,0:T(8,128)}) custom-call(s32[1]{0:T(128)} %bitcast.lane, s32[2]{0:T(128)S(1)} %get-tuple-element.32.sizes, s32[8448]{0:T(1024)S(1)} %get-tuple-element.33.order, f32[8448]{0:T(1024)S(1)} %get-tuple-element.34.heavy, s32[1536]{0:T(1024)S(1)} %reshape_squeeze.3.lists, ...), custom_call_target="tpu_custom_call" | custom-call | bytes 4194304 | tf_op jit(solution)/shard_map/field/pallas_call | solution.py:489
  77.5 29.4 %all-to-all-start.1 = ((f32[32,96,128]{2,1,0:T(8,128)}), f32[32,96,128]{2,1,0:T(8,128)S(1)}, u32[]{:S(2)}, u32[]{:S(2)}) async-start(f32[32,96,128]{2,1,0:T(8,128)} %get-tuple-element.36), calls=%async_computation.1 | async-start | bytes 3145728 | tf_op jit(solution)/shard_map/all_to_all | solution.py:417
  110.9 18.2 %all-to-all-done.1.arrived = f32[32,96,128]{2,1,0:T(8,128)S(1)} async-done(((f32[32,96,128]{2,1,0:T(8,128)}), f32[32,96,128]{2,1,0:T(8,128)S(1)}, u32[]{:S(2)}, u32[]{:S(2)}) %all-to-all-start.1) | async-done | bytes 1572896 | tf_op jit(solution)/shard_map/all_to_all | solution.py:417
  130.4 5.8 %flow_join.2 = (f32[512,128]{1,0:T(8,128)S(1)}, f32[512,128]{1,0:T(8,128)S(1)}, f32[512,128]{1,0:T(8,128)S(1)}, f32[512,128]{1,0:T(8,128)S(1)}) custom-call(s32[1]{0:T(128)} %bitcast.lane, s32[2]{0:T(128)S(1)} %get-tuple-element.32.sizes, s32[8448]{0:T(1024)S(1)} %get-tuple-element.33.order, f32[8448]{0:T(1024)S(1)} %get-tuple-element.34.heavy, ...), custom_call_target="tpu_custom_call" | custom-call | flops 1610612736 | bytes 4194304 | tf_op jit(solution)/shard_map/flow_join/pallas_call | solution.py:505
  137.7 6.0 %collective-permute-start.6 = (f32[512,128]{1,0:T(8,128)S(1)}, f32[512,128]{1,0:T(8,128)S(1)}, u32[]{:S(2)}, u32[]{:S(2)}) collective-permute-start(f32[512,128]{1,0:T(8,128)S(1)} %get-tuple-element.38), channel_id=1, source_target_pairs={{0,2},{1,3},{2,0},{3,1},{4,6},{5,7},{6,4},{7,5},{8,10},{9,11},{10,... | collective-permute-start | bytes 786440 | tf_op jit(solution)/shard_map/ppermute | solution.py:402
  143.8 5.4 %collective-permute-done.7 = f32[512,128]{1,0:T(8,128)S(1)} collective-permute-done((f32[512,128]{1,0:T(8,128)S(1)}, f32[512,128]{1,0:T(8,128)S(1)}, u32[]{:S(2)}, u32[]{:S(2)}) %collective-permute-start.7) | collective-permute-done | bytes 262176 | tf_op jit(solution)/shard_map/ppermute | solution.py:402
  149.2 6.5 %collective-permute-done.6 = f32[512,128]{1,0:T(8,128)S(1)} collective-permute-done((f32[512,128]{1,0:T(8,128)S(1)}, f32[512,128]{1,0:T(8,128)S(1)}, u32[]{:S(2)}, u32[]{:S(2)}) %collective-permute-start.6) | collective-permute-done | bytes 262176 | tf_op jit(solution)/shard_map/ppermute | solution.py:402
  159.3 10.9 %collective-permute-done.9.refs_1_ = f32[512,128]{1,0:T(8,128)S(1)} collective-permute-done((f32[512,128]{1,0:T(8,128)S(1)}, f32[512,128]{1,0:T(8,128)S(1)}, u32[]{:S(2)}, u32[]{:S(2)}) %collective-permute-start.9) | collective-permute-done | bytes 262176 | tf_op jit(solution)/shard_map/ppermute | solution.py:402
  170.6 5.3 %field.3 = (f32[2048,128]{1,0:T(8,128)S(1)}, f32[32,96,128]{2,1,0:T(8,128)}) custom-call(s32[1]{0:T(128)} %bitcast.lane, s32[2]{0:T(128)S(1)} %get-tuple-element.32.sizes, s32[8448]{0:T(1024)S(1)} %get-tuple-element.33.order, f32[8448]{0:T(1024)S(1)} %get-tuple-element.34.heavy, s32[1536]{0:T(1024)S(1)} %reshape_squeeze.3.lists, ...), custom_call_target="tpu_custom_call" | custom-call | bytes 4194304 | tf_op jit(solution)/shard_map/field/pallas_call | solution.py:489
  176.9 9.1 %all-to-all-start.2 = ((f32[32,96,128]{2,1,0:T(8,128)}), f32[32,96,128]{2,1,0:T(8,128)S(1)}, u32[]{:S(2)}, u32[]{:S(2)}) async-start(f32[32,96,128]{2,1,0:T(8,128)} %get-tuple-element.42), calls=%async_computation.2 | async-start | bytes 3145728 | tf_op jit(solution)/shard_map/all_to_all | solution.py:417
  190.2 18.0 %all-to-all-done.2.arrived = f32[32,96,128]{2,1,0:T(8,128)S(1)} async-done(((f32[32,96,128]{2,1,0:T(8,128)}), f32[32,96,128]{2,1,0:T(8,128)S(1)}, u32[]{:S(2)}, u32[]{:S(2)}) %all-to-all-start.2) | async-done | bytes 1572896 | tf_op jit(solution)/shard_map/all_to_all | solution.py:417
  208.2 5.8 %flow_join.3 = (f32[512,128]{1,0:T(8,128)S(1)}, f32[512,128]{1,0:T(8,128)S(1)}, f32[512,128]{1,0:T(8,128)S(1)}, f32[512,128]{1,0:T(8,128)S(1)}) custom-call(s32[1]{0:T(128)} %bitcast.lane, s32[2]{0:T(128)S(1)} %get-tuple-element.32.sizes, s32[8448]{0:T(1024)S(1)} %get-tuple-element.33.order, f32[8448]{0:T(1024)S(1)} %get-tuple-element.34.heavy, ...), custom_call_target="tpu_custom_call" | custom-call | flops 1610612736 | bytes 4194304 | tf_op jit(solution)/shard_map/flow_join/pallas_call | solution.py:505
  214.0 3.8 %collective-permute-start.14 = (f32[512,128]{1,0:T(8,128)S(1)}, f32[512,128]{1,0:T(8,128)S(1)}, u32[]{:S(2)}, u32[]{:S(2)}) collective-permute-start(f32[512,128]{1,0:T(8,128)S(1)} %get-tuple-element.46), channel_id=1, source_target_pairs={{0,3},{1,0},{2,1},{3,2},{4,7},{5,4},{6,5},{7,6},{8,11},{9,8},{10,9... | collective-permute-start | bytes 786440 | tf_op jit(solution)/shard_map/ppermute | solution.py:402
  224.2 6.4 %collective-permute-done.12 = f32[512,128]{1,0:T(8,128)S(1)} collective-permute-done((f32[512,128]{1,0:T(8,128)S(1)}, f32[512,128]{1,0:T(8,128)S(1)}, u32[]{:S(2)}, u32[]{:S(2)}) %collective-permute-start.12) | collective-permute-done | bytes 262176 | tf_op jit(solution)/shard_map/ppermute | solution.py:402
  233.8 11.3 %collective-permute-done.15.refs_1_ = f32[512,128]{1,0:T(8,128)S(1)} collective-permute-done((f32[512,128]{1,0:T(8,128)S(1)}, f32[512,128]{1,0:T(8,128)S(1)}, u32[]{:S(2)}, u32[]{:S(2)}) %collective-permute-start.15) | collective-permute-done | bytes 262176 | tf_op jit(solution)/shard_map/ppermute | solution.py:402
  248.3 8.7 %all-to-all-start.3 = ((f32[32,48,128]{2,1,0:T(8,128)}), f32[32,48,128]{2,1,0:T(8,128)S(1)}, u32[]{:S(2)}, u32[]{:S(2)}) async-start(f32[32,48,128]{2,1,0:T(8,128)} %get-tuple-element.49), calls=%async_computation.3 | async-start | bytes 1572864 | tf_op jit(solution)/shard_map/all_to_all | solution.py:417
  260.5 10.7 %all-to-all-done.3 = f32[32,48,128]{2,1,0:T(8,128)S(1)} async-done(((f32[32,48,128]{2,1,0:T(8,128)}), f32[32,48,128]{2,1,0:T(8,128)S(1)}, u32[]{:S(2)}, u32[]{:S(2)}) %all-to-all-start.3) | async-done | bytes 786464 | tf_op jit(solution)/shard_map/all_to_all | solution.py:417
  (69 shorter events, 56.7 us)
Async XLA Ops:
  3.9 14.8 %copy-start.7 = (s32[4096]{0:T(1024)S(1)}, s32[4096]{0:T(1024)}, u32[]{:S(2)}) copy-start(s32[4096]{0:T(1024)} %source.3) | copy-start | bytes 49156
  10.0 24.4 %all-to-all-start = ((f32[32,56,128]{2,1,0:T(8,128)}), f32[32,56,128]{2,1,0:T(8,128)S(1)}, u32[]{:S(2)}, u32[]{:S(2)}) async-start(f32[32,56,128]{2,1,0:T(8,128)} %copy-done.5), calls=%async_computation | async-start | bytes 1835008 | tf_op jit(solution)/shard_map/all_to_all | solution.py:417
  39.2 14.9 %collective-permute-start.2 = (f32[520,128]{1,0:T(8,128)S(1)}, f32[520,128]{1,0:T(8,128)S(1)}, u32[]{:S(2)}, u32[]{:S(2)}) collective-permute-start(f32[520,128]{1,0:T(8,128)S(1)} %get-tuple-element.31), channel_id=1, source_target_pairs={{0,3},{1,0},{2,1},{3,2},{4,7},{5,4},{6,5},{7,6},{8,11},{9,8},{10,9... | collective-permute-start | bytes 798728 | tf_op jit(solution)/shard_map/ppermute | solution.py:402
  43.0 14.2 %collective-permute-start.1 = (f32[520,128]{1,0:T(8,128)S(1)}, f32[520,128]{1,0:T(8,128)S(1)}, u32[]{:S(2)}, u32[]{:S(2)}) collective-permute-start(f32[520,128]{1,0:T(8,128)S(1)} %get-tuple-element.30), channel_id=1, source_target_pairs={{0,1},{1,2},{2,3},{3,0},{4,5},{5,6},{6,7},{7,4},{8,9},{9,10},{10,1... | collective-permute-start | bytes 798728 | tf_op jit(solution)/shard_map/ppermute | solution.py:402
  43.0 14.2 %collective-permute-start = (f32[520,128]{1,0:T(8,128)S(1)}, f32[520,128]{1,0:T(8,128)S(1)}, u32[]{:S(2)}, u32[]{:S(2)}) collective-permute-start(f32[520,128]{1,0:T(8,128)S(1)} %get-tuple-element.29), channel_id=1, source_target_pairs={{0,2},{1,3},{2,0},{3,1},{4,6},{5,7},{6,4},{7,5},{8,10},{9,11},{10,... | collective-permute-start | bytes 798728 | tf_op jit(solution)/shard_map/ppermute | solution.py:402
  58.2 9.9 %collective-permute-start.3 = (f32[512,128]{1,0:T(8,128)S(1)}, f32[512,128]{1,0:T(8,128)S(1)}, u32[]{:S(2)}, u32[]{:S(2)}) collective-permute-start(f32[512,128]{1,0:T(8,128)S(1)} %slice_multiply_fusion.refs_0_), channel_id=1, source_target_pairs={{0,1},{1,2},{2,3},{3,0},{4,5},{5,6},{6,7},{7,4},{8,9},{9,10},{10,1... | collective-permute-start | bytes 786440 | tf_op jit(solution)/shard_map/ppermute | solution.py:402
  58.3 12.2 %collective-permute-start.4 = (f32[512,128]{1,0:T(8,128)S(1)}, f32[512,128]{1,0:T(8,128)S(1)}, u32[]{:S(2)}, u32[]{:S(2)}) collective-permute-start(f32[512,128]{1,0:T(8,128)S(1)} %slice_multiply_fusion.refs_0_), channel_id=1, source_target_pairs={{0,2},{1,3},{2,0},{3,1},{4,6},{5,7},{6,4},{7,5},{8,10},{9,11},{10,... | collective-permute-start | bytes 786440 | tf_op jit(solution)/shard_map/ppermute | solution.py:402
  59.8 12.5 %collective-permute-start.5 = (f32[512,128]{1,0:T(8,128)S(1)}, f32[512,128]{1,0:T(8,128)S(1)}, u32[]{:S(2)}, u32[]{:S(2)}) collective-permute-start(f32[512,128]{1,0:T(8,128)S(1)} %slice_multiply_fusion.refs_0_), channel_id=1, source_target_pairs={{0,3},{1,0},{2,1},{3,2},{4,7},{5,4},{6,5},{7,6},{8,11},{9,8},{10,9... | collective-permute-start | bytes 786440 | tf_op jit(solution)/shard_map/ppermute | solution.py:402
  77.5 51.6 %all-to-all-start.1 = ((f32[32,96,128]{2,1,0:T(8,128)}), f32[32,96,128]{2,1,0:T(8,128)S(1)}, u32[]{:S(2)}, u32[]{:S(2)}) async-start(f32[32,96,128]{2,1,0:T(8,128)} %get-tuple-element.36), calls=%async_computation.1 | async-start | bytes 3145728 | tf_op jit(solution)/shard_map/all_to_all | solution.py:417
  136.2 7.6 %collective-permute-start.8 = (f32[512,128]{1,0:T(8,128)S(1)}, f32[512,128]{1,0:T(8,128)S(1)}, u32[]{:S(2)}, u32[]{:S(2)}) collective-permute-start(f32[512,128]{1,0:T(8,128)S(1)} %get-tuple-element.40), channel_id=1, source_target_pairs={{0,3},{1,0},{2,1},{3,2},{4,7},{5,4},{6,5},{7,6},{8,11},{9,8},{10,9... | collective-permute-start | bytes 786440 | tf_op jit(solution)/shard_map/ppermute | solution.py:402
  137.3 11.8 %collective-permute-start.7 = (f32[512,128]{1,0:T(8,128)S(1)}, f32[512,128]{1,0:T(8,128)S(1)}, u32[]{:S(2)}, u32[]{:S(2)}) collective-permute-start(f32[512,128]{1,0:T(8,128)S(1)} %get-tuple-element.39), channel_id=1, source_target_pairs={{0,1},{1,2},{2,3},{3,0},{4,5},{5,6},{6,7},{7,4},{8,9},{9,10},{10,1... | collective-permute-start | bytes 786440 | tf_op jit(solution)/shard_map/ppermute | solution.py:402
  137.7 17.9 %collective-permute-start.6 = (f32[512,128]{1,0:T(8,128)S(1)}, f32[512,128]{1,0:T(8,128)S(1)}, u32[]{:S(2)}, u32[]{:S(2)}) collective-permute-start(f32[512,128]{1,0:T(8,128)S(1)} %get-tuple-element.38), channel_id=1, source_target_pairs={{0,2},{1,3},{2,0},{3,1},{4,6},{5,7},{6,4},{7,5},{8,10},{9,11},{10,... | collective-permute-start | bytes 786440 | tf_op jit(solution)/shard_map/ppermute | solution.py:402
  156.6 13.6 %collective-permute-start.9 = (f32[512,128]{1,0:T(8,128)S(1)}, f32[512,128]{1,0:T(8,128)S(1)}, u32[]{:S(2)}, u32[]{:S(2)}) collective-permute-start(f32[512,128]{1,0:T(8,128)S(1)} %get-tuple-element.52.refs_0_), channel_id=1, source_target_pairs={{0,1},{1,2},{2,3},{3,0},{4,5},{5,6},{6,7},{7,4},{8,9},{9,10},{10,1... | collective-permute-start | bytes 786440 | tf_op jit(solution)/shard_map/ppermute | solution.py:402
  156.6 13.6 %collective-permute-start.10 = (f32[512,128]{1,0:T(8,128)S(1)}, f32[512,128]{1,0:T(8,128)S(1)}, u32[]{:S(2)}, u32[]{:S(2)}) collective-permute-start(f32[512,128]{1,0:T(8,128)S(1)} %get-tuple-element.52.refs_0_), channel_id=1, source_target_pairs={{0,2},{1,3},{2,0},{3,1},{4,6},{5,7},{6,4},{7,5},{8,10},{9,11},{10,... | collective-permute-start | bytes 786440 | tf_op jit(solution)/shard_map/ppermute | solution.py:402
  157.0 13.6 %collective-permute-start.11 = (f32[512,128]{1,0:T(8,128)S(1)}, f32[512,128]{1,0:T(8,128)S(1)}, u32[]{:S(2)}, u32[]{:S(2)}) collective-permute-start(f32[512,128]{1,0:T(8,128)S(1)} %get-tuple-element.52.refs_0_), channel_id=1, source_target_pairs={{0,3},{1,0},{2,1},{3,2},{4,7},{5,4},{6,5},{7,6},{8,11},{9,8},{10,9... | collective-permute-start | bytes 786440 | tf_op jit(solution)/shard_map/ppermute | solution.py:402
  176.9 31.3 %all-to-all-start.2 = ((f32[32,96,128]{2,1,0:T(8,128)}), f32[32,96,128]{2,1,0:T(8,128)S(1)}, u32[]{:S(2)}, u32[]{:S(2)}) async-start(f32[32,96,128]{2,1,0:T(8,128)} %get-tuple-element.42), calls=%async_computation.2 | async-start | bytes 3145728 | tf_op jit(solution)/shard_map/all_to_all | solution.py:417
  208.2 22.5 %copy-start.10 = (f32[512,128]{1,0:T(8,128)S(1)}, f32[512,128]{1,0:T(8,128)}, u32[]{:S(2)}) copy-start(f32[512,128]{1,0:T(8,128)} %get-tuple-element.53) | copy-start | bytes 786436
  214.0 7.3 %collective-permute-start.14 = (f32[512,128]{1,0:T(8,128)S(1)}, f32[512,128]{1,0:T(8,128)S(1)}, u32[]{:S(2)}, u32[]{:S(2)}) collective-permute-start(f32[512,128]{1,0:T(8,128)S(1)} %get-tuple-element.46), channel_id=1, source_target_pairs={{0,3},{1,0},{2,1},{3,2},{4,7},{5,4},{6,5},{7,6},{8,11},{9,8},{10,9... | collective-permute-start | bytes 786440 | tf_op jit(solution)/shard_map/ppermute | solution.py:402
  217.8 6.4 %collective-permute-start.13 = (f32[512,128]{1,0:T(8,128)S(1)}, f32[512,128]{1,0:T(8,128)S(1)}, u32[]{:S(2)}, u32[]{:S(2)}) collective-permute-start(f32[512,128]{1,0:T(8,128)S(1)} %get-tuple-element.45), channel_id=1, source_target_pairs={{0,1},{1,2},{2,3},{3,0},{4,5},{5,6},{6,7},{7,4},{8,9},{9,10},{10,1... | collective-permute-start | bytes 786440 | tf_op jit(solution)/shard_map/ppermute | solution.py:402
  217.8 12.9 %collective-permute-start.12 = (f32[512,128]{1,0:T(8,128)S(1)}, f32[512,128]{1,0:T(8,128)S(1)}, u32[]{:S(2)}, u32[]{:S(2)}) collective-permute-start(f32[512,128]{1,0:T(8,128)S(1)} %get-tuple-element.44), channel_id=1, source_target_pairs={{0,2},{1,3},{2,0},{3,1},{4,6},{5,7},{6,4},{7,5},{8,10},{9,11},{10,... | collective-permute-start | bytes 786440 | tf_op jit(solution)/shard_map/ppermute | solution.py:402
  231.0 14.0 %collective-permute-start.15 = (f32[512,128]{1,0:T(8,128)S(1)}, f32[512,128]{1,0:T(8,128)S(1)}, u32[]{:S(2)}, u32[]{:S(2)}) collective-permute-start(f32[512,128]{1,0:T(8,128)S(1)} %add_add_fusion.1.refs_0_), channel_id=1, source_target_pairs={{0,1},{1,2},{2,3},{3,0},{4,5},{5,6},{6,7},{7,4},{8,9},{9,10},{10,1... | collective-permute-start | bytes 786440 | tf_op jit(solution)/shard_map/ppermute | solution.py:402
  231.1 13.9 %collective-permute-start.16 = (f32[512,128]{1,0:T(8,128)S(1)}, f32[512,128]{1,0:T(8,128)S(1)}, u32[]{:S(2)}, u32[]{:S(2)}) collective-permute-start(f32[512,128]{1,0:T(8,128)S(1)} %add_add_fusion.1.refs_0_), channel_id=1, source_target_pairs={{0,2},{1,3},{2,0},{3,1},{4,6},{5,7},{6,4},{7,5},{8,10},{9,11},{10,... | collective-permute-start | bytes 786440 | tf_op jit(solution)/shard_map/ppermute | solution.py:402
  231.2 13.8 %collective-permute-start.17 = (f32[512,128]{1,0:T(8,128)S(1)}, f32[512,128]{1,0:T(8,128)S(1)}, u32[]{:S(2)}, u32[]{:S(2)}) collective-permute-start(f32[512,128]{1,0:T(8,128)S(1)} %add_add_fusion.1.refs_0_), channel_id=1, source_target_pairs={{0,3},{1,0},{2,1},{3,2},{4,7},{5,4},{6,5},{7,6},{8,11},{9,8},{10,9... | collective-permute-start | bytes 786440 | tf_op jit(solution)/shard_map/ppermute | solution.py:402
  248.3 23.0 %all-to-all-start.3 = ((f32[32,48,128]{2,1,0:T(8,128)}), f32[32,48,128]{2,1,0:T(8,128)S(1)}, u32[]{:S(2)}, u32[]{:S(2)}) async-start(f32[32,48,128]{2,1,0:T(8,128)} %get-tuple-element.49), calls=%async_computation.3 | async-start | bytes 1572864 | tf_op jit(solution)/shard_map/all_to_all | solution.py:417
  (10 other events, 26.7 us)

commit v2 on v1

--- a/solution.py
+++ b/solution.py
@@ -17,7 +17,7 @@
 
 SMEM = pl.BlockSpec(memory_space=pltpu.SMEM)
 VMEM = pl.BlockSpec(memory_space=pltpu.VMEM)
-LIMIT = 48 * 2**20
+LIMIT = 40 * 2**20
 
 
 def chebyshev_terms(steps):
@@ -199,32 +199,6 @@
         outs[s][share : share + 8, :] = row
 
 
-def partition_kernel(rows, count, source, target, weight, order, heavy, edge, sizes):
-    second = order.shape[0] // 2
-
-    def step(i, at):
-        near, far = at
-        for u in range(8):
-            e = i * 8 + u
-            t = target[e]
-            away = (t >= rows).astype(jnp.int32)
-            pos = jnp.where(away == 1, far + second, near)
-            order[pos] = source[e] | ((t - away * rows) << 12)
-            heavy[pos] = weight[e]
-            edge[pos] = e
-            near, far = near + 1 - away, far + away
-        return near, far
-
-    near, far = lax.fori_loop(0, (count[0] + 7) // 8, step, (0, 0))
-    for u in range(UNROLL):
-        for pos in (near + u, far + second + u):
-            order[pos] = 0
-            heavy[pos] = 0.0
-            edge[pos] = 0
-    sizes[0] = near
-    sizes[1] = far
-
-
 def trips(n):
     return lax.div(n + UNROLL - 1, UNROLL)
 
@@ -234,45 +208,89 @@
         a[...] = jnp.zeros_like(a)
 
 
-def field_kernel(lane, sizes, order, heavy, lists, *refs):
-    lanes = 4
-    shares, (field, out), banks = refs[:lanes], refs[lanes : lanes + 2], refs[lanes + 2 :]
+def matrix_kernel(count, place, mass, high, low, acc):
+    flat = acc.shape[0]
+    chunk = 2048
+
+    def wipe(i, _):
+        acc[pl.ds(pl.multiple_of(i * chunk, chunk), chunk), :] = jnp.zeros((chunk, LANES), jnp.float32)
+        return 0
+
+    lax.fori_loop(0, flat // chunk, wipe, 0)
+    column = lax.broadcasted_iota(jnp.int32, (1, LANES), 1)
+
+    def step(i, _):
+        for u in range(0, UNROLL, 2):
+            e = i * UNROLL + u
+            p, q = place[e], place[e + 1]
+            rp, rq = lax.shift_right_logical(p, 7), lax.shift_right_logical(q, 7)
+            one = jnp.where(column == (p & (LANES - 1)), mass[e], 0.0)
+            two = jnp.where(column == (q & (LANES - 1)), mass[e + 1], 0.0)
+            two = two + one * (rp == rq).astype(jnp.float32)
+            one = one + acc[pl.ds(rp, 1), :]
+            two = two + acc[pl.ds(rq, 1), :]
+            acc[pl.ds(rp, 1), :] = one
+            acc[pl.ds(rq, 1), :] = two
+        return 0
+
+    lax.fori_loop(0, trips(count[0]), step, 0)
+    slots = high.shape[1]
+
+    def part(i, _):
+        top, rest = split(acc[pl.ds(pl.multiple_of(i * slots, slots), slots), :])
+        high[i] = top
+        low[i] = rest
+        return 0
+
+    lax.fori_loop(0, high.shape[0], part, 0)
+
+
+def send_kernel(shifts, first, lanes, lane, high, low, wanted, *refs):
+    shares = refs[: len(shifts)]
+    before, (out, both) = (None, refs[-2:]) if first else (refs[len(shifts)], refs[-2:])
+    blocks, wide, _ = out.shape
+    width = wide // 2
     share = shares[0].shape[0]
-    blocks, both, _ = out.shape
-    width = both // 2
-    second = order.shape[0] // 2
+    tiles = share // LANES
+    tall = 8 * width
+    for n, (s, mine) in enumerate(zip(shifts, shares)):
+        q = lax.rem(lane[0] - s + lanes, lanes)
+        put_split(both, slice(None), mine[...])
+
+        def chunk(i, _):
+            at = pl.ds(pl.multiple_of(i * tall, tall), tall)
+            want = wanted[at, :] - q * share
+            column = lax.broadcasted_iota(jnp.int32, (tall, LANES), 1)
+            hot = jnp.concatenate(
+                [jnp.where(want == column + k * LANES, 1.0, 0.0).astype(jnp.bfloat16) for k in range(tiles)], axis=1
+            )
+            top = jnp.concatenate([high[q * tiles + k, at, :] for k in range(tiles)], axis=1)
+            rest = jnp.concatenate([low[q * tiles + k, at, :] for k in range(tiles)], axis=1)
+            rows = both[...]
+            copied = halves(jnp.dot(hot, rows, preferred_element_type=jnp.float32))
+            summed_at = halves(
+                jnp.dot(top, rows, preferred_element_type=jnp.float32)
+                + jnp.dot(rest, rows, preferred_element_type=jnp.float32)
+            )
+            old = out if n else before
+            for c in range(8):
+                a, b = copied[c * width : (c + 1) * width], summed_at[c * width : (c + 1) * width]
+                if old is not None:
+                    a = a + old[i * 8 + c, :width, :]
+                    b = b + old[i * 8 + c, width:, :]
+                out[i * 8 + c, :width, :] = a
+                out[i * 8 + c, width:, :] = b
+            return 0
+
+        lax.fori_loop(0, blocks // 8, chunk, 0)
+
+
+def near_kernel(lanes, lane, count, order, heavy, *refs):
+    shares, (out, field), banks = refs[:lanes], refs[lanes : lanes + 2], refs[lanes + 2 :]
+    share = shares[0].shape[0]
     for s in range(lanes):
         q = lax.rem(lane[0] - s + lanes, lanes)
         field[pl.ds(pl.multiple_of(q * share, share), share), :] = shares[s][...]
-
-    def pack(c, _):
-        for r in range(width):
-            out[c, pl.ds(r, 1), :] = field[pl.ds(lists[c * width + r], 1), :]
-        return 0
-
-    lax.fori_loop(0, blocks, pack, 0)
-    clear(banks)
-
-    def step(i, _):
-        for u in range(0, UNROLL, BANKS):
-            at = second + i * UNROLL + u
-            code = [order[at + k] for k in range(BANKS)]
-            rows = [field[pl.ds(code[k] & 4095, 1), :] * heavy[at + k] for k in range(BANKS)]
-            to = [pl.ds(code[k] >> 12, 1) for k in range(BANKS)]
-            new = [banks[k][to[k], :] + rows[k] for k in range(BANKS)]
-            for k in range(BANKS):
-                banks[k][to[k], :] = new[k]
-        return 0
-
-    lax.fori_loop(0, trips(sizes[1]), step, 0)
-    total = banks[0][...]
-    for a in banks[1:]:
-        total = total + a[...]
-    for c in range(blocks):
-        out[c, width:, :] = total[c * width : (c + 1) * width]
-
-
-def near_kernel(sizes, order, heavy, field, out, *banks):
     clear(banks)
 
     def step(i, _):
@@ -281,7 +299,7 @@
             code = [order[at + k] for k in range(BANKS)]
             mass = [heavy[at + k] for k in range(BANKS)]
             one = [pl.ds(code[k] & 4095, 1) for k in range(BANKS)]
-            two = [pl.ds(code[k] >> 12, 1) for k in range(BANKS)]
+            two = [pl.ds(lax.shift_right_logical(code[k], 12), 1) for k in range(BANKS)]
             from_one = [field[one[k], :] * mass[k] for k in range(BANKS)]
             from_two = [field[two[k], :] * mass[k] for k in range(BANKS)]
             new = [banks[k][one[k], :] + from_two[k] for k in range(BANKS)]
@@ -292,53 +310,52 @@
                 banks[k][two[k], :] = new[k]
         return 0
 
-    lax.fori_loop(0, trips(sizes[0]), step, 0)
+    lax.fori_loop(0, trips(count[0]), step, 0)
     total = banks[0][...]
     for a in banks[1:]:
         total = total + a[...]
     out[...] = total
 
 
-def flow_join_kernel(lane, sizes, order, heavy, listed, near, arrived, *refs):
-    lanes = 4
-    outs, ret_both, hot, banks = refs[:lanes], refs[lanes], refs[lanes + 1], refs[lanes + 2 :]
-    blocks, both, _ = arrived.shape
-    width = both // 2
-    rows = near.shape[0]
-    share = rows // lanes
-    second = order.shape[0] // 2
-    halo = banks[-1]
-    banks = banks[:-1]
+def land_kernel(arrived, turned, ret_both, halo):
+    blocks, wide, _ = arrived.shape
+    width = wide // 2
     for c in range(blocks):
         halo[c * width : (c + 1) * width, :] = arrived[c, :width, :]
         put_split(ret_both, slice(c * width, (c + 1) * width), arrived[c, width:, :])
-
-    def emit(i, got):
-        at = pl.ds(pl.multiple_of(i * hot.shape[0], hot.shape[0]), hot.shape[0])
-        banks[0][at, :] = near[at, :] + got
-
-    scatter_back(ret_both, listed, hot, emit, rows)
-    clear(banks[1:])
-
-    def step(i, _):
-        for u in range(0, UNROLL, BANKS):
-            at = second + i * UNROLL + u
-            code = [order[at + k] for k in range(BANKS)]
-            got = [halo[pl.ds(code[k] >> 12, 1), :] * heavy[at + k] for k in range(BANKS)]
-            to = [pl.ds(code[k] & 4095, 1) for k in range(BANKS)]
-            new = [banks[k][to[k], :] + got[k] for k in range(BANKS)]
-            for k in range(BANKS):
-                banks[k][to[k], :] = new[k]
-        return 0
-
-    lax.fori_loop(0, trips(sizes[1]), step, 0)
-    for s in range(lanes):
-        q = lax.rem(lane[0] + s, lanes)
-        at = pl.ds(pl.multiple_of(q * share, share), share)
-        total = banks[0][at, :]
-        for a in banks[1:]:
-            total = total + a[at, :]
-        outs[s][...] = total
+    for k in range(halo.shape[0] // LANES):
+        at = slice(k * LANES, (k + 1) * LANES)
+        top, rest = split(halo[at, :].T)
+        turned[:LANES, at] = top
+        turned[LANES:, at] = rest
+
+
+def join(q, high, low, listed, near, turned, ret_both, out, hot):
+    share = out.shape[0]
+    tiles = share // LANES
+    for k in range(listed.shape[0]):
+        hot[:, k * LANES : (k + 1) * LANES] = one_hot(listed[k : k + 1, :], share, q * share).astype(jnp.bfloat16)
+    got = halves(jnp.dot(hot[...], ret_both[...], preferred_element_type=jnp.float32))
+    top = jnp.concatenate([high[q * tiles + k] for k in range(tiles)], axis=1)
+    rest = jnp.concatenate([low[q * tiles + k] for k in range(tiles)], axis=1)
+    sides = jnp.dot(turned[...], top, preferred_element_type=jnp.float32)
+    more = jnp.dot(turned[:LANES, :], rest, preferred_element_type=jnp.float32)
+    back = sides[:LANES] + sides[LANES:] + more
+    for k in range(tiles):
+        at = pl.ds(pl.multiple_of(q * share + k * LANES, LANES), LANES)
+        part = slice(k * LANES, (k + 1) * LANES)
+        out[part, :] = near[at, :] + got[part] + back[:, part].T
+
+
+def first_join_kernel(shift, lanes, lane, high, low, listed, near, arrived, out, turned, ret_both, halo, hot):
+    land_kernel(arrived, turned, ret_both, halo)
+    join(lax.rem(lane[0] + shift, lanes), high, low, listed, near, turned, ret_both, out, hot)
+
+
+def join_kernel(shifts, lanes, lane, high, low, listed, near, turned, ret_both, *refs):
+    outs, hot = refs[:-1], refs[-1]
+    for s, out in zip(shifts, outs):
+        join(lax.rem(lane[0] + s, lanes), high, low, listed, near, turned, ret_both, out, hot)
 
 
 def solution_kernel(lane, lists, *refs):
@@ -358,7 +375,7 @@
     lax.fori_loop(0, blocks, pack, 0)
 
 
-def near_gap_kernel(count, source, target, field, gaps, more):
+def near_gap_kernel(count, order, field, gaps, more):
     rows = field.shape[0]
     more[:rows, :] = field[...]
     more[rows:, :] = jnp.zeros((more.shape[0] - rows, LANES), jnp.float32)
@@ -366,32 +383,31 @@
     def step(i, _):
         for u in range(UNROLL):
             e = i * UNROLL + u
-            t = jnp.minimum(target[e], rows)
-            gaps[pl.ds(e, 1), :] = field[pl.ds(source[e], 1), :] - more[pl.ds(t, 1), :]
+            code = order[e]
+            gaps[pl.ds(e, 1), :] = (
+                field[pl.ds(code & 4095, 1), :] - more[pl.ds(lax.shift_right_logical(code, 12), 1), :]
+            )
         return 0
 
     lax.fori_loop(0, trips(count[0]), step, 0)
 
 
-def far_gap_kernel(sizes, order, edge, near_gaps, halo, live, out, gaps):
-    second = order.shape[0] // 2
-    edges = near_gaps.shape[0]
-    groups = edges // LANES
-    gaps[:edges, :] = near_gaps[...]
+def far_gap_kernel(count, slot, gaps, halo, live, out, more, taken):
+    slots = halo.shape[0]
+    groups = live.shape[0]
+    more[:slots, :] = halo[...]
+    more[slots:, :] = jnp.zeros((more.shape[0] - slots, LANES), jnp.float32)
 
     def step(i, _):
-        left = sizes[1] - i * UNROLL
-        for u in range(0, UNROLL, BANKS):
-            at = second + i * UNROLL + u
-            to = [pl.ds(jnp.where(u + k < left, edge[at + k], edges), 1) for k in range(BANKS)]
-            new = [gaps[to[k], :] - halo[pl.ds(order[at + k] >> 12, 1), :] for k in range(BANKS)]
-            for k in range(BANKS):
-                gaps[to[k], :] = new[k]
-        return 0
-
-    lax.fori_loop(0, trips(sizes[1]), step, 0)
+        for u in range(UNROLL):
+            e = i * UNROLL + u
+            taken[pl.ds(e, 1), :] = more[pl.ds(slot[e], 1), :]
+        return 0
+
+    lax.fori_loop(0, trips(count[0]), step, 0)
     for k in range(groups):
-        gap = gaps[k * LANES : (k + 1) * LANES, :]
+        at = slice(k * LANES, (k + 1) * LANES)
+        gap = gaps[at, :] - taken[at, :]
         total = jnp.sum((gap * gap).T, axis=0, keepdims=True)
         alive = live[k : k + 1, :]
         out[k : k + 1, :] = jnp.where(alive > 0, total * (alive / LANES), 0.0)
@@ -410,7 +426,7 @@
 
 def to_all(mine, lanes):
     home, two, one, three = passed_round([mine] * lanes, lanes, 1)
-    return [home, one, two, three]
+    return (home, one, two, three)
 
 
 def across(x):
@@ -457,15 +473,6 @@
         "own_side",
         flops=2 * rows * edges * 2 * LANES,
     )(terms, source_rows, target_rows, weight_rows)
-    room = edges + LANES
-    order, heavy, edge, sizes = call(
-        functools.partial(partition_kernel, rows),
-        [((2 * room,), i32, SMEM), ((2 * room,), f32, SMEM), ((2 * room,), i32, SMEM), ((2,), i32, SMEM)],
-        [SMEM] * 4,
-        [],
-        "partition",
-        moved=2**25,
-    )(edge_count, src_local, dst_index, weight)
     sides = call(
         side_join_kernel,
         [((share + 8, LANES), f32, VMEM)] * lanes,
@@ -481,38 +488,82 @@
     diagonal = (degree_share + ground_share)[:, None]
     inverse = 1.0 / diagonal
 
+    away = dst_index >= rows
+    slot = jnp.where(away, dst_index - rows, 0)
+    place = (lax.shift_right_logical(src_local, 7) * slots + slot) * LANES + (src_local & (LANES - 1))
+    place = jnp.where(away, place, 0)
+    far_weight = jnp.where(away, weight, 0.0)
+    near_weight = jnp.where(away, 0.0, weight)
+    near_order = src_local | (jnp.where(away, 0, dst_index) << 12)
+    gap_order = src_local | (jnp.minimum(dst_index, rows) << 12)
+    gap_slot = jnp.where(away, dst_index - rows, slots)
+    wanted = jnp.broadcast_to(lists[:, None], (slots, LANES))
+    tiles = rows // LANES
+    high, low = call(
+        matrix_kernel,
+        [((tiles, slots, LANES), bf16, VMEM)] * 2,
+        [SMEM] * 3,
+        [pltpu.VMEM((tiles * slots, LANES), f32)],
+        "matrix",
+        moved=2**25,
+    )(edge_count, place, far_weight)
+
     first, pairs = chebyshev_terms(ITERS)
     residual = right_share
     direction = first * inverse * right_share
     solution_share = direction
+    message_shape = ((blocks, 2 * width, LANES), f32, VMEM)
+
+    def send(shifts, before, parts):
+        return call(
+            functools.partial(send_kernel, shifts, before is None, lanes),
+            [message_shape],
+            [SMEM] + [VMEM] * (3 + len(parts) + (before is not None)),
+            [pltpu.VMEM((share, 2 * LANES), bf16)],
+            "send",
+            flops=6 * slots * share * 2 * LANES * len(parts),
+        )(lane, high, low, wanted, *parts, *(() if before is None else (before,)))[0]
+
     for keep, push in pairs:
-        field, message = call(
-            field_kernel,
-            [((rows, LANES), f32, VMEM), ((blocks, 2 * width, LANES), f32, VMEM)],
-            [SMEM] * 5 + [VMEM] * lanes,
-            [pltpu.VMEM((slots, LANES), f32)] * BANKS,
-            "field",
-        )(lane, sizes, order, heavy, lists, *to_all(direction, lanes))
+        parts = to_all(direction, lanes)
+        message = send((0,), None, parts[:1])
+        message = send((1, 3), message, (parts[1], parts[3]))
+        message = send((2,), message, parts[2:3])
         arrived = across(message)
         near = call(
-            near_kernel,
+            functools.partial(near_kernel, lanes),
             [((rows, LANES), f32, VMEM)],
-            [SMEM] * 3 + [VMEM],
-            [pltpu.VMEM((rows, LANES), f32)] * BANKS,
+            [SMEM] * 4 + [VMEM] * lanes,
+            [pltpu.VMEM((rows, LANES), f32)] * (1 + BANKS),
             "near",
             moved=2**25,
-        )(sizes, order, heavy, field)[0]
-        flows = call(
-            flow_join_kernel,
-            [((share, LANES), f32, VMEM)] * lanes,
-            [SMEM] * 4 + [VMEM] * 3,
-            [pltpu.VMEM((slots, 2 * LANES), bf16), pltpu.VMEM((256, slots), bf16)]
-            + [pltpu.VMEM((rows, LANES), f32)] * BANKS
-            + [pltpu.VMEM((slots, LANES), f32)],
-            "flow_join",
-            flops=2 * rows * slots * 2 * LANES,
-        )(lane, sizes, order, heavy, listed, near, arrived)
-        residual = residual - (diagonal * direction - summed(flows, lanes))
+        )(lane, edge_count, near_order, near_weight, *parts)[0]
+        two, turned, ret_both = call(
+            functools.partial(first_join_kernel, 2, lanes),
+            [((share, LANES), f32, VMEM), ((2 * LANES, slots), bf16, VMEM), ((slots, 2 * LANES), bf16, VMEM)],
+            [SMEM] + [VMEM] * 5,
+            [pltpu.VMEM((slots, LANES), f32), pltpu.VMEM((share, slots), bf16)],
+            "join_two",
+            flops=6 * share * slots * 2 * LANES,
+        )(lane, high, low, listed, near, arrived)
+        one, three = call(
+            functools.partial(join_kernel, (1, 3), lanes),
+            [((share, LANES), f32, VMEM)] * 2,
+            [SMEM] + [VMEM] * 6,
+            [pltpu.VMEM((share, slots), bf16)],
+            "join_one_three",
+            flops=12 * share * slots * 2 * LANES,
+        )(lane, high, low, listed, near, turned, ret_both)
+        home = call(
+            functools.partial(join_kernel, (0,), lanes),
+            [((share, LANES), f32, VMEM)],
+            [SMEM] + [VMEM] * 6,
+            [pltpu.VMEM((share, slots), bf16)],
+            "join_home",
+            flops=6 * share * slots * 2 * LANES,
+        )(lane, high, low, listed, near, turned, ret_both)[0]
+        flows = summed((home, one, two, three), lanes)
+        residual = residual - (diagonal * direction - flows)
         direction = keep * direction + push * inverse * residual
         solution_share = solution_share + direction
     field, message = call(
@@ -526,18 +577,18 @@
     gaps = call(
         near_gap_kernel,
         [((edges, LANES), f32, VMEM)],
-        [SMEM] * 3 + [VMEM],
+        [SMEM] * 2 + [VMEM],
         [pltpu.VMEM((rows + 8, LANES), f32)],
         "near_gap",
         moved=2**25,
-    )(edge_count, src_local, dst_index, field)[0]
+    )(edge_count, gap_order, field)[0]
     resistance = call(
         far_gap_kernel,
         [((groups, LANES), f32, VMEM)],
-        [SMEM] * 3 + [VMEM] * 3,
-        [pltpu.VMEM((edges + 8, LANES), f32)],
+        [SMEM] * 2 + [VMEM] * 3,
+        [pltpu.VMEM((slots + 8, LANES), f32), pltpu.VMEM((edges, LANES), f32)],
         "far_gap",
-    )(sizes, order, edge, gaps, halo.reshape(slots, LANES), live_rows)[0]
+    )(edge_count, gap_slot, gaps, halo.reshape(slots, LANES), live_rows)[0]
     return (field, resistance.reshape(edges))
 
 

time: 278 us -> 289 us (1.040)
  Pallas kernels: 65 us -> 102 us
  waiting for transfers between devices: 112 us -> 78.9 us
  local copies, waits for them, and re-layouts: 8.92 us -> 21.5 us
  starting transfers between devices: 82.6 us -> 75.7 us
    pallas_call x9 -> x17, Pallas kernels: 41 us -> 78.3 us  [the longest x6 33.5 us: send(): call(functools.partial(send_kernel, shifts, before is None, lanes), [mess...]
    ppermute x18, waiting for transfers between devices: 62.2 us -> 32.2 us  [passed_round(): lax.ppermute(blocks[s], 'edg', [(i, (i + sign * s) % lanes) for i in rang...]
    unnamed x24 -> x58, local copies, waits for them, and re-layouts: 8.77 us -> 21.1 us
    all_to_all x4, starting transfers between devices: 55.9 us -> 52.4 us  [across(): return lax.all_to_all(x, 'vtx', split_axis=0, concat_axis=0, tiled=True)]
    ppermute x18, starting transfers between devices: 26.8 us -> 23.4 us  [passed_round(): lax.ppermute(blocks[s], 'edg', [(i, (i + sign * s) % lanes) for i in rang...]
  transfers between devices with their start and end apart: 22 -> 22, of which waited for: 16 -> 16; matrix products, arithmetic and copies ran while one was open for 0% -> 0% of each run, Pallas kernels for 10% -> 12%
where the time goes in v2:
time: 289 us; the launch traced here: 285 us
  Pallas kernels  102 us (35%)
  waiting for transfers between devices  78.9 us (27%)
  starting transfers between devices  75.7 us (26%)
  local copies, waits for them, and re-layouts  21.5 us (7%)
  other arithmetic  4.98 us (2%)
    all_to_all x4, starting transfers between devices, across(): return lax.all_to_all(x, 'vtx', split_axis=0, concat_axis=0, tiled=True)  52.4 us
    all_to_all x4, waiting for transfers between devices, across(): return lax.all_to_all(x, 'vtx', split_axis=0, concat_axis=0, tiled=True)  46.8 us
    pallas_call x6, Pallas kernels, send(): call(functools.partial(send_kernel, shifts, before is None, lanes), [mess...  33.5 us
    ppermute x18, waiting for transfers between devices, passed_round(): lax.ppermute(blocks[s], 'edg', [(i, (i + sign * s) % lanes) for i in rang...  32.2 us
    ppermute x18, starting transfers between devices, passed_round(): lax.ppermute(blocks[s], 'edg', [(i, (i + sign * s) % lanes) for i in rang...  23.4 us
    unnamed x58, local copies, waits for them, and re-layouts  21.1 us
    pallas_call x1, Pallas kernels, local(): call(own_side_kernel, [((rows, LANES), f32, VMEM), ((rows // LANES, LANES...  12 us
    pallas_call x2, Pallas kernels, local(): call(functools.partial(join_kernel, (1, 3), lanes), [((share, LANES), f32...  11.1 us
  transfers between devices with their start and end apart: 22, of which 16 were waited for; matrix products, arithmetic and copies ran while one was open for 0% of the time, Pallas kernels for 12%

profile of v2, /device:TPU:1, one launch (start us, length us, event | category | flops | bytes accessed | tf_op | source)
XLA Modules:
  0.0 285.3 jit_solution(15425781338798748528)
XLA Ops:
  3.9 5.2 %halo_side.1 = f32[32,56,128]{2,1,0:T(8,128)S(1)} custom-call(f32[4096,128]{1,0:T(8,128)S(1)} %convert_multiply_fusion.terms, s32[32,128]{1,0:T(8,128)S(1)} %bitcast.19, f32[32,128]{1,0:T(8,128)S(1)} %get-tuple-element.52.weight), custom_call_target="tpu_custom_call" | custom-call | flops 3221225472 | bytes 4194304 | tf_op jit(solution)/shard_map/halo_side/pallas_call | solution.py:459
  10.0 8.7 %all-to-all-start = ((f32[32,56,128]{2,1,0:T(8,128)}), f32[32,56,128]{2,1,0:T(8,128)S(1)}, u32[]{:S(2)}, u32[]{:S(2)}) async-start(f32[32,56,128]{2,1,0:T(8,128)} %copy-done.17), calls=%async_computation | async-start | bytes 1835008 | tf_op jit(solution)/shard_map/all_to_all | solution.py:433
  18.9 12.0 %own_side.1 = (f32[2048,128]{1,0:T(8,128)S(1)}, f32[16,128]{1,0:T(8,128)S(1)}) custom-call(f32[4096,128]{1,0:T(8,128)S(1)} %convert_multiply_fusion.terms, s32[32,128]{1,0:T(8,128)S(1)} %bitcast.21, s32[32,128]{1,0:T(8,128)S(1)} %bitcast.20, f32[32,128]{1,0:T(8,128)S(1)} %get-tuple-element.52.weight), custom_call_target="tpu_custom_call" | custom-call | flops 4294967296 | bytes 4194304 | tf_op jit(solution)/shard_map/own_side/pallas_call | solution.py:468
  49.6 6.1 %collective-permute-done.1 = f32[520,128]{1,0:T(8,128)S(1)} collective-permute-done((f32[520,128]{1,0:T(8,128)S(1)}, f32[520,128]{1,0:T(8,128)S(1)}, u32[]{:S(2)}, u32[]{:S(2)}) %collective-permute-start.1) | collective-permute-done | bytes 266272 | tf_op jit(solution)/shard_map/ppermute | solution.py:418
  60.1 5.6 %matrix.1 = (bf16[16,1536,128]{2,1,0:T(8,128)(2,1)S(1)}, bf16[16,1536,128]{2,1,0:T(8,128)(2,1)S(1)}) custom-call(s32[1]{0:T(128)} %copy.9.count, s32[4096]{0:T(1024)S(1)} %get-tuple-element.47.place, f32[4096]{0:T(1024)S(1)} %get-tuple-element.50.mass), custom_call_target="tpu_custom_call" | custom-call | bytes 33554432 | tf_op jit(solution)/shard_map/matrix/pallas_call | solution.py:502
  69.8 5.5 %send.6.refs_2_ = f32[32,96,128]{2,1,0:T(8,128)S(1)} custom-call(s32[1]{0:T(128)} %bitcast.lane, bf16[16,1536,128]{2,1,0:T(8,128)(2,1)S(1)} %get-tuple-element.28.high, bf16[16,1536,128]{2,1,0:T(8,128)(2,1)} %copy-done.3, s32[1536,128]{1,0:T(8,128)S(1)} %broadcast_in_dim.20.wanted, f32[512,128]{1,0:T(8,128)S(1)} %slice_multiply_fusion.refs_0_), custom_call_target="tpu_custom_call" | custom-call | flops 1207959552 | bytes 4194304 | tf_op jit(solution)/shard_map/send/pallas_call | solution.py:518
  76.0 6.9 %send.7.refs_1_ = f32[32,96,128]{2,1,0:T(8,128)S(1)} custom-call(s32[1]{0:T(128)} %bitcast.lane, bf16[16,1536,128]{2,1,0:T(8,128)(2,1)S(1)} %get-tuple-element.28.high, bf16[16,1536,128]{2,1,0:T(8,128)(2,1)} %copy-done.3, s32[1536,128]{1,0:T(8,128)S(1)} %broadcast_in_dim.20.wanted, f32[512,128]{1,0:T(8,128)S(1)} %collective-permute-done.3.refs_1_.refs_0_, ...), custom_call_target="tpu_custom_call" | custom-call | flops 2415919104 | bytes 4194304 | tf_op jit(solution)/shard_map/send/pallas_call | solution.py:518
  83.0 4.8 %send.8 = f32[32,96,128]{2,1,0:T(8,128)S(1)} custom-call(s32[1]{0:T(128)} %bitcast.lane, bf16[16,1536,128]{2,1,0:T(8,128)(2,1)S(1)} %get-tuple-element.28.high, bf16[16,1536,128]{2,1,0:T(8,128)(2,1)} %copy-done.3, s32[1536,128]{1,0:T(8,128)S(1)} %broadcast_in_dim.20.wanted, f32[512,128]{1,0:T(8,128)S(1)} %collective-permute-done.4.refs_2_.refs_0_, ...), custom_call_target="tpu_custom_call" | custom-call | flops 1207959552 | bytes 4194304 | tf_op jit(solution)/shard_map/send/pallas_call | solution.py:518
  89.6 17.8 %all-to-all-start.1 = ((f32[32,96,128]{2,1,0:T(8,128)}), f32[32,96,128]{2,1,0:T(8,128)S(1)}, u32[]{:S(2)}, u32[]{:S(2)}) async-start(f32[32,96,128]{2,1,0:T(8,128)} %copy-done.5), calls=%async_computation.1 | async-start | bytes 3145728 | tf_op jit(solution)/shard_map/all_to_all | solution.py:433
  114.5 15.1 %all-to-all-done.1.arrived = f32[32,96,128]{2,1,0:T(8,128)S(1)} async-done(((f32[32,96,128]{2,1,0:T(8,128)}), f32[32,96,128]{2,1,0:T(8,128)S(1)}, u32[]{:S(2)}, u32[]{:S(2)}) %all-to-all-start.1) | async-done | bytes 1572896 | tf_op jit(solution)/shard_map/all_to_all | solution.py:433
  132.4 4.2 %join_two.2 = (f32[512,128]{1,0:T(8,128)S(1)}, bf16[256,1536]{1,0:T(8,128)(2,1)S(1)}, bf16[1536,256]{1,0:T(8,128)(2,1)S(1)}) custom-call(s32[1]{0:T(128)} %bitcast.lane, bf16[16,1536,128]{2,1,0:T(8,128)(2,1)S(1)} %copy-done.1, bf16[16,1536,128]{2,1,0:T(8,128)(2,1)} %copy-done.3, s32[12,128]{1,0:T(8,128)S(1)} %reshape_reshape_squeeze.3.listed, ...), custom_call_target="tpu_custom_call" | custom-call | flops 1207959552 | bytes 4194304 | tf_op jit(solution)/shard_map/join_two/pallas_call | solution.py:541
  136.6 5.6 %join_one_three.2 = (f32[512,128]{1,0:T(8,128)S(1)}, f32[512,128]{1,0:T(8,128)S(1)}) custom-call(s32[1]{0:T(128)} %bitcast.lane, bf16[16,1536,128]{2,1,0:T(8,128)(2,1)S(1)} %copy-done.1, bf16[16,1536,128]{2,1,0:T(8,128)(2,1)} %copy-done.3, s32[12,128]{1,0:T(8,128)S(1)} %reshape_reshape_squeeze.3.listed, f32[2048,128]{1,0:T(8,128)S(1)} %near.2, ...), custom_call_target="tpu_custom_call" | custom-call | flops 2415919104 | bytes 4194304 | tf_op jit(solution)/shard_map/join_one_three/pallas_call | solution.py:549
  145.0 4.3 %join_home.2 = f32[512,128]{1,0:T(8,128)S(1)} custom-call(s32[1]{0:T(128)} %bitcast.lane, bf16[16,1536,128]{2,1,0:T(8,128)(2,1)S(1)} %copy-done.1, bf16[16,1536,128]{2,1,0:T(8,128)(2,1)} %copy-done.3, s32[12,128]{1,0:T(8,128)S(1)} %reshape_reshape_squeeze.3.listed, f32[2048,128]{1,0:T(8,128)S(1)} %near.2, bf16[256,1536]{1,0:T(8,128)(2,1)S(1)} %get-tuple-element.30.turned, ...), custom_call_target="tpu_custom_call" | custom-call | flops 1207959552 | bytes 4194304 | tf_op jit(solution)/shard_map/join_home/pallas_call | solution.py:557
  149.9 4.3 %collective-permute-done.6 = f32[512,128]{1,0:T(8,128)S(1)} collective-permute-done((f32[512,128]{1,0:T(8,128)S(1)}, f32[512,128]{1,0:T(8,128)S(1)}, u32[]{:S(2)}, u32[]{:S(2)}) %collective-permute-start.6) | collective-permute-done | bytes 262176 | tf_op jit(solution)/shard_map/ppermute | solution.py:418
  158.3 4.7 %send.9.refs_2_ = f32[32,96,128]{2,1,0:T(8,128)S(1)} custom-call(s32[1]{0:T(128)} %bitcast.lane, bf16[16,1536,128]{2,1,0:T(8,128)(2,1)S(1)} %bitcast.17, bf16[16,1536,128]{2,1,0:T(8,128)(2,1)} %copy-done.3, s32[1536,128]{1,0:T(8,128)S(1)} %broadcast_in_dim.20.wanted, f32[512,128]{1,0:T(8,128)S(1)} %get-tuple-element.44.refs_0_), custom_call_target="tpu_custom_call" | custom-call | flops 1207959552 | bytes 4194304 | tf_op jit(solution)/shard_map/send/pallas_call | solution.py:518
  167.2 6.7 %send.10.refs_1_ = f32[32,96,128]{2,1,0:T(8,128)S(1)} custom-call(s32[1]{0:T(128)} %bitcast.lane, bf16[16,1536,128]{2,1,0:T(8,128)(2,1)S(1)} %bitcast.17, bf16[16,1536,128]{2,1,0:T(8,128)(2,1)} %copy-done.3, s32[1536,128]{1,0:T(8,128)S(1)} %broadcast_in_dim.20.wanted, f32[512,128]{1,0:T(8,128)S(1)} %collective-permute-done.9.refs_1_.refs_0_, ...), custom_call_target="tpu_custom_call" | custom-call | flops 2415919104 | bytes 4194304 | tf_op jit(solution)/shard_map/send/pallas_call | solution.py:518
  173.9 4.8 %send.11 = f32[32,96,128]{2,1,0:T(8,128)S(1)} custom-call(s32[1]{0:T(128)} %bitcast.lane, bf16[16,1536,128]{2,1,0:T(8,128)(2,1)S(1)} %bitcast.17, bf16[16,1536,128]{2,1,0:T(8,128)(2,1)} %copy-done.3, s32[1536,128]{1,0:T(8,128)S(1)} %broadcast_in_dim.20.wanted, f32[512,128]{1,0:T(8,128)S(1)} %collective-permute-done.10.refs_2_.refs_0_, ...), custom_call_target="tpu_custom_call" | custom-call | flops 1207959552 | bytes 4194304 | tf_op jit(solution)/shard_map/send/pallas_call | solution.py:518
  179.9 13.7 %all-to-all-start.2 = ((f32[32,96,128]{2,1,0:T(8,128)}), f32[32,96,128]{2,1,0:T(8,128)S(1)}, u32[]{:S(2)}, u32[]{:S(2)}) async-start(f32[32,96,128]{2,1,0:T(8,128)} %copy-done.4), calls=%async_computation.2 | async-start | bytes 3145728 | tf_op jit(solution)/shard_map/all_to_all | solution.py:433
  198.0 17.9 %all-to-all-done.2.arrived = f32[32,96,128]{2,1,0:T(8,128)S(1)} async-done(((f32[32,96,128]{2,1,0:T(8,128)}), f32[32,96,128]{2,1,0:T(8,128)S(1)}, u32[]{:S(2)}, u32[]{:S(2)}) %all-to-all-start.2) | async-done | bytes 1572896 | tf_op jit(solution)/shard_map/all_to_all | solution.py:433
  218.6 4.2 %join_two.3 = (f32[512,128]{1,0:T(8,128)S(1)}, bf16[256,1536]{1,0:T(8,128)(2,1)S(1)}, bf16[1536,256]{1,0:T(8,128)(2,1)S(1)}) custom-call(s32[1]{0:T(128)} %bitcast.lane, bf16[16,1536,128]{2,1,0:T(8,128)(2,1)S(1)} %copy-done.2, bf16[16,1536,128]{2,1,0:T(8,128)(2,1)} %copy-done.3, s32[12,128]{1,0:T(8,128)S(1)} %reshape_reshape_squeeze.3.listed, ...), custom_call_target="tpu_custom_call" | custom-call | flops 1207959552 | bytes 4194304 | tf_op jit(solution)/shard_map/join_two/pallas_call | solution.py:541
  222.9 5.6 %join_one_three.3 = (f32[512,128]{1,0:T(8,128)S(1)}, f32[512,128]{1,0:T(8,128)S(1)}) custom-call(s32[1]{0:T(128)} %bitcast.lane, bf16[16,1536,128]{2,1,0:T(8,128)(2,1)S(1)} %copy-done.2, bf16[16,1536,128]{2,1,0:T(8,128)(2,1)} %copy-done.3, s32[12,128]{1,0:T(8,128)S(1)} %reshape_reshape_squeeze.3.listed, f32[2048,128]{1,0:T(8,128)S(1)} %near.3, ...), custom_call_target="tpu_custom_call" | custom-call | flops 2415919104 | bytes 4194304 | tf_op jit(solution)/shard_map/join_one_three/pallas_call | solution.py:549
  247.2 4.2 %collective-permute-done.16.refs_2_ = f32[512,128]{1,0:T(8,128)S(1)} collective-permute-done((f32[512,128]{1,0:T(8,128)S(1)}, f32[512,128]{1,0:T(8,128)S(1)}, u32[]{:S(2)}, u32[]{:S(2)}) %collective-permute-start.16) | collective-permute-done | bytes 262176 | tf_op jit(solution)/shard_map/ppermute | solution.py:418
  256.4 12.1 %all-to-all-start.3 = ((f32[32,48,128]{2,1,0:T(8,128)}), f32[32,48,128]{2,1,0:T(8,128)S(1)}, u32[]{:S(2)}, u32[]{:S(2)}) async-start(f32[32,48,128]{2,1,0:T(8,128)} %get-tuple-element.41), calls=%async_computation.3 | async-start | bytes 1572864 | tf_op jit(solution)/shard_map/all_to_all | solution.py:433
  271.6 11.1 %all-to-all-done.3 = f32[32,48,128]{2,1,0:T(8,128)S(1)} async-done(((f32[32,48,128]{2,1,0:T(8,128)}), f32[32,48,128]{2,1,0:T(8,128)S(1)}, u32[]{:S(2)}, u32[]{:S(2)}) %all-to-all-start.3) | async-done | bytes 786464 | tf_op jit(solution)/shard_map/all_to_all | solution.py:433
  (114 shorter events, 92.4 us)
Async XLA Ops:
  10.0 24.5 %all-to-all-start = ((f32[32,56,128]{2,1,0:T(8,128)}), f32[32,56,128]{2,1,0:T(8,128)S(1)}, u32[]{:S(2)}, u32[]{:S(2)}) async-start(f32[32,56,128]{2,1,0:T(8,128)} %copy-done.17), calls=%async_computation | async-start | bytes 1835008 | tf_op jit(solution)/shard_map/all_to_all | solution.py:433
  39.5 10.2 %collective-permute-start = (f32[520,128]{1,0:T(8,128)S(1)}, f32[520,128]{1,0:T(8,128)S(1)}, u32[]{:S(2)}, u32[]{:S(2)}) collective-permute-start(f32[520,128]{1,0:T(8,128)S(1)} %get-tuple-element.25), channel_id=1, source_target_pairs={{0,2},{1,3},{2,0},{3,1},{4,6},{5,7},{6,4},{7,5},{8,10},{9,11},{10,... | collective-permute-start | bytes 798728 | tf_op jit(solution)/shard_map/ppermute | solution.py:418
  43.2 12.6 %collective-permute-start.1 = (f32[520,128]{1,0:T(8,128)S(1)}, f32[520,128]{1,0:T(8,128)S(1)}, u32[]{:S(2)}, u32[]{:S(2)}) collective-permute-start(f32[520,128]{1,0:T(8,128)S(1)} %get-tuple-element.26), channel_id=1, source_target_pairs={{0,1},{1,2},{2,3},{3,0},{4,5},{5,6},{6,7},{7,4},{8,9},{9,10},{10,1... | collective-permute-start | bytes 798728 | tf_op jit(solution)/shard_map/ppermute | solution.py:418
  43.9 11.9 %collective-permute-start.2 = (f32[520,128]{1,0:T(8,128)S(1)}, f32[520,128]{1,0:T(8,128)S(1)}, u32[]{:S(2)}, u32[]{:S(2)}) collective-permute-start(f32[520,128]{1,0:T(8,128)S(1)} %get-tuple-element.27), channel_id=1, source_target_pairs={{0,3},{1,0},{2,1},{3,2},{4,7},{5,4},{6,5},{7,6},{8,11},{9,8},{10,9... | collective-permute-start | bytes 798728 | tf_op jit(solution)/shard_map/ppermute | solution.py:418
  56.8 19.2 %collective-permute-start.3 = (f32[512,128]{1,0:T(8,128)S(1)}, f32[512,128]{1,0:T(8,128)S(1)}, u32[]{:S(2)}, u32[]{:S(2)}) collective-permute-start(f32[512,128]{1,0:T(8,128)S(1)} %slice_multiply_fusion.refs_0_), channel_id=1, source_target_pairs={{0,1},{1,2},{2,3},{3,0},{4,5},{5,6},{6,7},{7,4},{8,9},{9,10},{10,1... | collective-permute-start | bytes 786440 | tf_op jit(solution)/shard_map/ppermute | solution.py:418
  57.9 18.1 %collective-permute-start.5 = (f32[512,128]{1,0:T(8,128)S(1)}, f32[512,128]{1,0:T(8,128)S(1)}, u32[]{:S(2)}, u32[]{:S(2)}) collective-permute-start(f32[512,128]{1,0:T(8,128)S(1)} %slice_multiply_fusion.refs_0_), channel_id=1, source_target_pairs={{0,3},{1,0},{2,1},{3,2},{4,7},{5,4},{6,5},{7,6},{8,11},{9,8},{10,9... | collective-permute-start | bytes 786440 | tf_op jit(solution)/shard_map/ppermute | solution.py:418
  68.4 14.6 %copy-start = (bf16[16,1536,128]{2,1,0:T(8,128)(2,1)}, bf16[16,1536,128]{2,1,0:T(8,128)(2,1)S(1)}, u32[]{:S(2)}) copy-start(bf16[16,1536,128]{2,1,0:T(8,128)(2,1)S(1)} %get-tuple-element.28.high) | copy-start | bytes 18874372
  68.4 14.6 %collective-permute-start.4 = (f32[512,128]{1,0:T(8,128)S(1)}, f32[512,128]{1,0:T(8,128)S(1)}, u32[]{:S(2)}, u32[]{:S(2)}) collective-permute-start(f32[512,128]{1,0:T(8,128)S(1)} %slice_multiply_fusion.refs_0_), channel_id=1, source_target_pairs={{0,2},{1,3},{2,0},{3,1},{4,6},{5,7},{6,4},{7,5},{8,10},{9,11},{10,... | collective-permute-start | bytes 786440 | tf_op jit(solution)/shard_map/ppermute | solution.py:418
  89.6 40.0 %all-to-all-start.1 = ((f32[32,96,128]{2,1,0:T(8,128)}), f32[32,96,128]{2,1,0:T(8,128)S(1)}, u32[]{:S(2)}, u32[]{:S(2)}) async-start(f32[32,96,128]{2,1,0:T(8,128)} %copy-done.5), calls=%async_computation.1 | async-start | bytes 3145728 | tf_op jit(solution)/shard_map/all_to_all | solution.py:433
  142.2 7.2 %collective-permute-start.7 = (f32[512,128]{1,0:T(8,128)S(1)}, f32[512,128]{1,0:T(8,128)S(1)}, u32[]{:S(2)}, u32[]{:S(2)}) collective-permute-start(f32[512,128]{1,0:T(8,128)S(1)} %get-tuple-element.33), channel_id=1, source_target_pairs={{0,1},{1,2},{2,3},{3,0},{4,5},{5,6},{6,7},{7,4},{8,9},{9,10},{10,1... | collective-permute-start | bytes 786440 | tf_op jit(solution)/shard_map/ppermute | solution.py:418
  142.2 7.7 %collective-permute-start.8 = (f32[512,128]{1,0:T(8,128)S(1)}, f32[512,128]{1,0:T(8,128)S(1)}, u32[]{:S(2)}, u32[]{:S(2)}) collective-permute-start(f32[512,128]{1,0:T(8,128)S(1)} %get-tuple-element.34), channel_id=1, source_target_pairs={{0,3},{1,0},{2,1},{3,2},{4,7},{5,4},{6,5},{7,6},{8,11},{9,8},{10,9... | collective-permute-start | bytes 786440 | tf_op jit(solution)/shard_map/ppermute | solution.py:418
  144.9 13.4 %slice-start = ((s8[6291456]{0:T(1024)(128)(4,1)}), s8[4194304]{0:T(1024)(128)(4,1)S(1)}, s32[]{:S(2)}) async-start(s8[6291456]{0:T(1024)(128)(4,1)} %bitcast.16), calls=%async_computation.4 | async-start | bytes 8388608
  144.9 9.3 %collective-permute-start.6 = (f32[512,128]{1,0:T(8,128)S(1)}, f32[512,128]{1,0:T(8,128)S(1)}, u32[]{:S(2)}, u32[]{:S(2)}) collective-permute-start(f32[512,128]{1,0:T(8,128)S(1)} %get-tuple-element.32), channel_id=1, source_target_pairs={{0,2},{1,3},{2,0},{3,1},{4,6},{5,7},{6,4},{7,5},{8,10},{9,11},{10,... | collective-permute-start | bytes 786440 | tf_op jit(solution)/shard_map/ppermute | solution.py:418
  155.1 7.9 %collective-permute-start.11 = (f32[512,128]{1,0:T(8,128)S(1)}, f32[512,128]{1,0:T(8,128)S(1)}, u32[]{:S(2)}, u32[]{:S(2)}) collective-permute-start(f32[512,128]{1,0:T(8,128)S(1)} %get-tuple-element.44.refs_0_), channel_id=1, source_target_pairs={{0,3},{1,0},{2,1},{3,2},{4,7},{5,4},{6,5},{7,6},{8,11},{9,8},{10,9... | collective-permute-start | bytes 786440 | tf_op jit(solution)/shard_map/ppermute | solution.py:418
  157.1 10.0 %collective-permute-start.9 = (f32[512,128]{1,0:T(8,128)S(1)}, f32[512,128]{1,0:T(8,128)S(1)}, u32[]{:S(2)}, u32[]{:S(2)}) collective-permute-start(f32[512,128]{1,0:T(8,128)S(1)} %get-tuple-element.44.refs_0_), channel_id=1, source_target_pairs={{0,1},{1,2},{2,3},{3,0},{4,5},{5,6},{6,7},{7,4},{8,9},{9,10},{10,1... | collective-permute-start | bytes 786440 | tf_op jit(solution)/shard_map/ppermute | solution.py:418
  157.1 16.7 %collective-permute-start.10 = (f32[512,128]{1,0:T(8,128)S(1)}, f32[512,128]{1,0:T(8,128)S(1)}, u32[]{:S(2)}, u32[]{:S(2)}) collective-permute-start(f32[512,128]{1,0:T(8,128)S(1)} %get-tuple-element.44.refs_0_), channel_id=1, source_target_pairs={{0,2},{1,3},{2,0},{3,1},{4,6},{5,7},{6,4},{7,5},{8,10},{9,11},{10,... | collective-permute-start | bytes 786440 | tf_op jit(solution)/shard_map/ppermute | solution.py:418
  179.9 35.9 %all-to-all-start.2 = ((f32[32,96,128]{2,1,0:T(8,128)}), f32[32,96,128]{2,1,0:T(8,128)S(1)}, u32[]{:S(2)}, u32[]{:S(2)}) async-start(f32[32,96,128]{2,1,0:T(8,128)} %copy-done.4), calls=%async_computation.2 | async-start | bytes 3145728 | tf_op jit(solution)/shard_map/all_to_all | solution.py:433
  228.4 7.2 %collective-permute-start.13 = (f32[512,128]{1,0:T(8,128)S(1)}, f32[512,128]{1,0:T(8,128)S(1)}, u32[]{:S(2)}, u32[]{:S(2)}) collective-permute-start(f32[512,128]{1,0:T(8,128)S(1)} %get-tuple-element.38), channel_id=1, source_target_pairs={{0,1},{1,2},{2,3},{3,0},{4,5},{5,6},{6,7},{7,4},{8,9},{9,10},{10,1... | collective-permute-start | bytes 786440 | tf_op jit(solution)/shard_map/ppermute | solution.py:418
  228.5 7.7 %collective-permute-start.14 = (f32[512,128]{1,0:T(8,128)S(1)}, f32[512,128]{1,0:T(8,128)S(1)}, u32[]{:S(2)}, u32[]{:S(2)}) collective-permute-start(f32[512,128]{1,0:T(8,128)S(1)} %get-tuple-element.39), channel_id=1, source_target_pairs={{0,3},{1,0},{2,1},{3,2},{4,7},{5,4},{6,5},{7,6},{8,11},{9,8},{10,9... | collective-permute-start | bytes 786440 | tf_op jit(solution)/shard_map/ppermute | solution.py:418
  231.2 9.1 %collective-permute-start.12 = (f32[512,128]{1,0:T(8,128)S(1)}, f32[512,128]{1,0:T(8,128)S(1)}, u32[]{:S(2)}, u32[]{:S(2)}) collective-permute-start(f32[512,128]{1,0:T(8,128)S(1)} %get-tuple-element.37), channel_id=1, source_target_pairs={{0,2},{1,3},{2,0},{3,1},{4,6},{5,7},{6,4},{7,5},{8,10},{9,11},{10,... | collective-permute-start | bytes 786440 | tf_op jit(solution)/shard_map/ppermute | solution.py:418
  240.7 6.5 %collective-permute-start.15 = (f32[512,128]{1,0:T(8,128)S(1)}, f32[512,128]{1,0:T(8,128)S(1)}, u32[]{:S(2)}, u32[]{:S(2)}) collective-permute-start(f32[512,128]{1,0:T(8,128)S(1)} %add_add_fusion.1.refs_0_), channel_id=1, source_target_pairs={{0,1},{1,2},{2,3},{3,0},{4,5},{5,6},{6,7},{7,4},{8,9},{9,10},{10,1... | collective-permute-start | bytes 786440 | tf_op jit(solution)/shard_map/ppermute | solution.py:418
  242.2 9.2 %collective-permute-start.16 = (f32[512,128]{1,0:T(8,128)S(1)}, f32[512,128]{1,0:T(8,128)S(1)}, u32[]{:S(2)}, u32[]{:S(2)}) collective-permute-start(f32[512,128]{1,0:T(8,128)S(1)} %add_add_fusion.1.refs_0_), channel_id=1, source_target_pairs={{0,2},{1,3},{2,0},{3,1},{4,6},{5,7},{6,4},{7,5},{8,10},{9,11},{10,... | collective-permute-start | bytes 786440 | tf_op jit(solution)/shard_map/ppermute | solution.py:418
  244.0 9.0 %collective-permute-start.17 = (f32[512,128]{1,0:T(8,128)S(1)}, f32[512,128]{1,0:T(8,128)S(1)}, u32[]{:S(2)}, u32[]{:S(2)}) collective-permute-start(f32[512,128]{1,0:T(8,128)S(1)} %add_add_fusion.1.refs_0_), channel_id=1, source_target_pairs={{0,3},{1,0},{2,1},{3,2},{4,7},{5,4},{6,5},{7,6},{8,11},{9,8},{10,9... | collective-permute-start | bytes 786440 | tf_op jit(solution)/shard_map/ppermute | solution.py:418
  256.4 26.3 %all-to-all-start.3 = ((f32[32,48,128]{2,1,0:T(8,128)}), f32[32,48,128]{2,1,0:T(8,128)S(1)}, u32[]{:S(2)}, u32[]{:S(2)}) async-start(f32[32,48,128]{2,1,0:T(8,128)} %get-tuple-element.41), calls=%async_computation.3 | async-start | bytes 1572864 | tf_op jit(solution)/shard_map/all_to_all | solution.py:433
  (27 other events, 101.0 us)

commit v3 on v1

v3 whole, which is shorter than its diff:
```python
import functools

import jax
import jax.numpy as jnp
from jax import lax
from jax.experimental import pallas as pl
from jax.experimental.pallas import tpu as pltpu
from jax.sharding import PartitionSpec as P

ITERS = 3
LANES = 128
UNROLL = 16
BANKS = 4

lam_low = 0.05
lam_high = 2.0

SMEM = pl.BlockSpec(memory_space=pltpu.SMEM)
VMEM = pl.BlockSpec(memory_space=pltpu.VMEM)
ANY = pl.BlockSpec(memory_space=pl.ANY)
LIMIT = 24 * 2**20


def chebyshev_terms(steps):
    centre = (lam_high + lam_low) / 2.0
    half_width = (lam_high - lam_low) / 2.0
    sigma_val = centre / half_width
    rho_prev = 1.0 / sigma_val
    pairs = []
    for count_idx in range(steps - 1):
        rho_next = 1.0 / (2.0 * sigma_val - rho_prev)
        pairs.append((rho_next * rho_prev, 2.0 * rho_next / half_width))
        rho_prev = rho_next
    return (1.0 / centre, pairs)


def call(kernel, outs, ins, scratch, name, flops=0, moved=2**22):
    return pl.pallas_call(
        kernel,
        out_shape=[jax.ShapeDtypeStruct(shape, dtype) for shape, dtype, _ in outs],
        in_specs=ins,
        out_specs=[space for _, _, space in outs],
        scratch_shapes=scratch,
        compiler_params=pltpu.CompilerParams(vmem_limit_bytes=LIMIT),
        cost_estimate=pl.CostEstimate(flops=flops, bytes_accessed=moved, transcendentals=0),
        name=name,
    )


def split(x):
    high = x.astype(jnp.bfloat16)
    return high, (x - high.astype(jnp.float32)).astype(jnp.bfloat16)


def put_split(ref, rows, x):
    high, low = split(x)
    ref[rows, :LANES] = high
    ref[rows, LANES:] = low


def halves(x):
    return x[:, :LANES] + x[:, LANES:]


def one_hot(row, height, base):
    place = lax.broadcasted_iota(jnp.int32, (height, row.shape[1]), 0) + base
    return jnp.where(place == row, 1.0, 0.0)


def factored(pick, groups, high_of, low_of, weight_of, height):
    total = jnp.zeros((2 * height, LANES), jnp.float32)
    for k0 in range(0, groups, pick):
        left, right = [], []
        for k in range(k0, k0 + pick):
            member = one_hot(high_of(k), height, 0) * weight_of(k)
            high, low = split(member)
            left.append(jnp.concatenate([high, low], axis=0))
            right.append(one_hot(low_of(k), LANES, 0).astype(jnp.bfloat16))
        total = total + lax.dot_general(
            jnp.concatenate(left, axis=1),
            jnp.concatenate(right, axis=1),
            (((1,), (1,)), ((), ())),
            preferred_element_type=jnp.float32,
        )
    return total[:height] + total[height:]


def halo_side_kernel(rows, slots, width, terms, target, weight, sent, both, hot, out, leave):
    groups = target.shape[0]
    edges = terms.shape[0]
    put_split(both, slice(None), terms[...])
    tall = hot.shape[0]
    per = tall // width

    def chunk(i, _):
        base = rows + i * tall
        for k in range(groups):
            hot[:, k * LANES : (k + 1) * LANES] = one_hot(target[k : k + 1, :], tall, base).astype(jnp.bfloat16)
        got = halves(jnp.dot(hot[...], both[...], preferred_element_type=jnp.float32))
        for c in range(per):
            out[i * per + c, :width, :] = -got[c * width : (c + 1) * width]
        return 0

    lax.fori_loop(0, slots // tall, chunk, 0)
    blocks = slots // width

    def slot(k):
        return target[k : k + 1, :] - rows

    def block_of(k):
        return jnp.where(slot(k) < 0, -1, lax.shift_right_arithmetic(slot(k) * 1366, 16))

    def within(k):
        return slot(k) - block_of(k) * width

    deg = factored(4, groups, block_of, within, lambda k: weight[k : k + 1, :], blocks)
    for c in range(blocks):
        out[c, width : width + 8, :] = jnp.broadcast_to(deg[c : c + 1, :], (8, LANES))
    go = pltpu.make_async_copy(out, sent, leave)
    go.start()
    go.wait()


def own_side_kernel(terms, source, target, weight, out, degree, both, hot):
    groups = target.shape[0]
    rows = out.shape[0]
    put_split(both, slice(None), terms[...])
    tall = hot.shape[0]

    def chunk(i, _):
        base = i * tall
        for k in range(groups):
            plus = one_hot(source[k : k + 1, :], tall, base)
            minus = one_hot(target[k : k + 1, :], tall, base)
            hot[:, k * LANES : (k + 1) * LANES] = (plus - minus).astype(jnp.bfloat16)
        out[pl.ds(pl.multiple_of(i * tall, tall), tall), :] = halves(
            jnp.dot(hot[...], both[...], preferred_element_type=jnp.float32)
        )
        return 0

    lax.fori_loop(0, rows // tall, chunk, 0)

    def total(ref):
        return factored(
            4,
            groups,
            lambda k: lax.shift_right_logical(ref[k : k + 1, :], 7),
            lambda k: ref[k : k + 1, :] & (LANES - 1),
            lambda k: weight[k : k + 1, :],
            rows // LANES,
        )

    degree[...] = total(source) + total(target)


def scatter_back(ret_both, listed, hot, emit, rows):
    tall = hot.shape[0]
    groups = listed.shape[0]

    def chunk(i, _):
        base = i * tall
        for k in range(groups):
            hot[:, k * LANES : (k + 1) * LANES] = one_hot(listed[k : k + 1, :], tall, base).astype(jnp.bfloat16)
        emit(i, halves(jnp.dot(hot[...], ret_both[...], preferred_element_type=jnp.float32)))
        return 0

    lax.fori_loop(0, rows // tall, chunk, 0)


def side_join_kernel(lane, returned, listed, padded, own, own_degree, *refs):
    lanes = 4
    outs, (acc, ret_both, hot, landed, arrival) = refs[:lanes], refs[lanes:]
    come = pltpu.make_async_copy(returned, landed, arrival)
    come.start()
    blocks = returned.shape[0]
    rows = own.shape[0]
    width = listed.shape[0] * LANES // blocks
    share = rows // lanes
    come.wait()
    for c in range(blocks):
        put_split(ret_both, slice(c * width, (c + 1) * width), landed[c, :width, :])

    def emit(i, got):
        at = pl.ds(pl.multiple_of(i * hot.shape[0], hot.shape[0]), hot.shape[0])
        acc[at, :] = own[at, :] + got

    scatter_back(ret_both, listed, hot, emit, rows)
    deg = own_degree[...] + factored(
        4,
        blocks,
        lambda k: lax.shift_right_arithmetic(padded[k : k + 1, :], 7),
        lambda k: padded[k : k + 1, :] & (LANES - 1),
        lambda k: landed[k, width : width + 1, :],
        rows // LANES,
    )
    deg_rows = share // LANES
    for s in range(lanes):
        q = lax.rem(lane[0] + s, lanes)
        outs[s][:share, :] = acc[pl.ds(pl.multiple_of(q * share, share), share), :]
        row = jnp.zeros((8, LANES), jnp.float32)
        place = lax.broadcasted_iota(jnp.int32, (8, LANES), 0)
        for p in range(lanes):
            for d in range(deg_rows):
                one = jnp.broadcast_to(deg[p * deg_rows + d : p * deg_rows + d + 1, :], (8, LANES))
                row = jnp.where((place == d) & (q == p), one, row)
        outs[s][share : share + 8, :] = row


def far_list_kernel(begin, end, count, order, mass, code, heavy, size):
    def step(i, at):
        e = begin + i * 8
        given = [order[e + u] for u in range(8)]
        loads = [mass[e + u] for u in range(8)]
        for u in range(8):
            code[at] = given[u]
            heavy[at] = loads[u]
            at = at + 1 + lax.shift_right_arithmetic(given[u], 31)
        return at

    live = jnp.clip(count[0] - begin, 0, end - begin)
    at = lax.fori_loop(0, lax.div(live + 7, 8), step, 0)
    for u in range(UNROLL):
        code[at + u] = 0
        heavy[at + u] = 0.0
    size[0] = at


def trips(n):
    return lax.div(n + UNROLL - 1, UNROLL)


def clear(banks):
    for a in banks:
        a[...] = jnp.zeros_like(a)


def far_rows(lists, take, give, banks):
    for code, heavy, size in lists:

        def step(i, _):
            for u in range(0, UNROLL, BANKS):
                at = i * UNROLL + u
                given = [code[at + k] for k in range(BANKS)]
                rows = [take(given[k]) * heavy[at + k] for k in range(BANKS)]
                to = [pl.ds(give(given[k]), 1) for k in range(BANKS)]
                new = [banks[k][to[k], :] + rows[k] for k in range(BANKS)]
                for k in range(BANKS):
                    banks[k][to[k], :] = new[k]
            return 0

        lax.fori_loop(0, trips(size[0]), step, 0)


def source_of(given):
    return given & 4095


def target_of(given):
    return lax.shift_right_logical(given, 12)


def assemble(lane, lanes, shares, field):
    share = shares[0].shape[0]
    for s in range(lanes):
        q = lax.rem(lane[0] - s + lanes, lanes)
        field[pl.ds(pl.multiple_of(q * share, share), share), :] = shares[s][...]


def pack(lists, field, out, width):
    def step(c, _):
        for r in range(width):
            out[c, pl.ds(r, 1), :] = field[pl.ds(lists[c * width + r], 1), :]
        return 0

    lax.fori_loop(0, out.shape[0], step, 0)


def field_kernel(lane, rows_a, mass_a, size_a, rows_b, mass_b, size_b, lists, *refs):
    lanes = 4
    shares, (field, sent), refs = refs[:lanes], refs[lanes : lanes + 2], refs[lanes + 2 :]
    out, sums, leave, leave_more = refs[:4]
    banks = refs[4:]
    blocks, width, _ = out.shape
    assemble(lane, lanes, shares, field)
    pack(lists, field, out, width)
    go = pltpu.make_async_copy(out, sent.at[:, :width, :], leave)
    go.start()
    clear(banks)
    far_rows(
        ((rows_a, mass_a, size_a), (rows_b, mass_b, size_b)),
        lambda given: field[pl.ds(source_of(given), 1), :],
        target_of,
        banks,
    )
    total = banks[0][...]
    for a in banks[1:]:
        total = total + a[...]
    for c in range(blocks):
        sums[c] = total[c * width : (c + 1) * width]
    more = pltpu.make_async_copy(sums, sent.at[:, width:, :], leave_more)
    more.start()
    go.wait()
    more.wait()


def near_kernel(count, order, heavy, field, out, *banks):
    clear(banks)

    def step(i, _):
        for u in range(0, UNROLL, BANKS):
            at = i * UNROLL + u
            code = [order[at + k] for k in range(BANKS)]
            mass = [heavy[at + k] for k in range(BANKS)]
            one = [pl.ds(source_of(code[k]), 1) for k in range(BANKS)]
            two = [pl.ds(target_of(code[k]), 1) for k in range(BANKS)]
            from_one = [field[one[k], :] * mass[k] for k in range(BANKS)]
            from_two = [field[two[k], :] * mass[k] for k in range(BANKS)]
            new = [banks[k][one[k], :] + from_two[k] for k in range(BANKS)]
            for k in range(BANKS):
                banks[k][one[k], :] = new[k]
            new = [banks[k][two[k], :] + from_one[k] for k in range(BANKS)]
            for k in range(BANKS):
                banks[k][two[k], :] = new[k]
        return 0

    lax.fori_loop(0, trips(count[0]), step, 0)
    total = banks[0][...]
    for a in banks[1:]:
        total = total + a[...]
    out[...] = total


def share_block(q, listed, far, ret_both, hot, out):
    share = out.shape[0]
    for k in range(listed.shape[0]):
        hot[:, k * LANES : (k + 1) * LANES] = one_hot(listed[k : k + 1, :], share, q * share).astype(jnp.bfloat16)
    got = halves(jnp.dot(hot[...], ret_both[...], preferred_element_type=jnp.float32))
    out[...] = far[pl.ds(pl.multiple_of(q * share, share), share), :] + got


def first_join_kernel(
    shift, lanes, lane, rows_a, mass_a, size_a, rows_b, mass_b, size_b, listed, near, arrived, *refs
):
    out, far, ret_both, hot, halo, ret, come_halo, come_ret = refs[:8]
    banks = refs[8:]
    blocks, width, _ = halo.shape
    first = pltpu.make_async_copy(arrived.at[:, :width, :], halo, come_halo)
    second = pltpu.make_async_copy(arrived.at[:, width:, :], ret, come_ret)
    first.start()
    second.start()
    clear(banks)
    first.wait()
    flat = halo.reshape(blocks * width, LANES)
    far_rows(
        ((rows_a, mass_a, size_a), (rows_b, mass_b, size_b)),
        lambda given: flat[pl.ds(target_of(given), 1), :],
        source_of,
        banks,
    )
    total = near[...]
    for a in banks:
        total = total + a[...]
    far[...] = total
    second.wait()
    for c in range(blocks):
        put_split(ret_both, slice(c * width, (c + 1) * width), ret[c])
    share_block(lax.rem(lane[0] + shift, lanes), listed, far, ret_both, hot, out)


def join_kernel(shifts, lanes, lane, listed, far, ret_both, *refs):
    outs, hot = refs[:-1], refs[-1]
    for s, out in zip(shifts, outs):
        share_block(lax.rem(lane[0] + s, lanes), listed, far, ret_both, hot, out)


def solution_kernel(lane, lists, *refs):
    lanes = 4
    shares, (field, sent, out, leave) = refs[:lanes], refs[lanes:]
    assemble(lane, lanes, shares, field)
    pack(lists, field, out, out.shape[1])
    go = pltpu.make_async_copy(out, sent, leave)
    go.start()
    go.wait()


def near_gap_kernel(count, order, field, gaps, more):
    rows = field.shape[0]
    more[:rows, :] = field[...]
    more[rows:, :] = jnp.zeros((more.shape[0] - rows, LANES), jnp.float32)

    def step(i, _):
        for u in range(UNROLL):
            e = i * UNROLL + u
            code = order[e]
            gaps[pl.ds(e, 1), :] = (
                field[pl.ds(code & 4095, 1), :] - more[pl.ds(lax.shift_right_logical(code, 12), 1), :]
            )
        return 0

    lax.fori_loop(0, trips(count[0]), step, 0)


def far_gap_kernel(count, slot, gaps, arrived, live, out, halo, taken, come):
    blocks, width, _ = arrived.shape
    groups = live.shape[0]
    first = pltpu.make_async_copy(arrived, halo.at[:blocks], come)
    first.start()
    halo[blocks] = jnp.zeros((width, LANES), jnp.float32)
    first.wait()
    flat = halo.reshape((blocks + 1) * width, LANES)

    def step(i, _):
        for u in range(4 * UNROLL):
            e = i * 4 * UNROLL + u
            taken[pl.ds(e, 1), :] = flat[pl.ds(slot[e], 1), :]
        return 0

    lax.fori_loop(0, lax.div(count[0] + 4 * UNROLL - 1, 4 * UNROLL), step, 0)
    for k in range(groups):
        at = slice(k * LANES, (k + 1) * LANES)
        gap = gaps[at, :] - taken[at, :]
        total = jnp.sum((gap * gap).T, axis=0, keepdims=True)
        alive = live[k : k + 1, :]
        out[k : k + 1, :] = jnp.where(alive > 0, total * (alive / LANES), 0.0)


def passed_round(blocks, lanes, sign):
    return [blocks[0]] + [
        lax.ppermute(blocks[s], "edg", [(i, (i + sign * s) % lanes) for i in range(lanes)]) for s in (2, 1, 3)
    ]


def summed(blocks, lanes):
    home, two, one, three = passed_round(blocks, lanes, 1)
    return (home + one) + (two + three)


def to_all(mine, lanes):
    home, two, one, three = passed_round([mine] * lanes, lanes, 1)
    return [home, one, two, three]


def across(x):
    return lax.all_to_all(x, "vtx", split_axis=0, concat_axis=0, tiled=True)


def local(sketch_cols, edge_weight, ground, src_local, dst_index, send_rows, edge_count):
    blocks = lax.axis_size("vtx")
    lanes = lax.axis_size("edg")
    rows = ground.shape[0]
    edges = edge_weight.shape[0]
    width = send_rows.shape[2]
    slots = blocks * width
    share = rows // lanes
    groups = edges // LANES
    f32, i32, bf16 = jnp.float32, jnp.int32, jnp.bfloat16
    lane = lax.axis_index("edg").astype(i32).reshape(1)
    lists = send_rows[0].reshape(-1)
    listed = lists.reshape(slots // LANES, LANES)
    padded = jnp.pad(send_rows[0], ((0, 0), (0, LANES - width)), constant_values=-1)
    live = (jnp.arange(edges, dtype=i32) < edge_count[0]).astype(f32)
    weight = edge_weight * live
    root = jnp.sqrt(edge_weight) * live
    terms = root[:, None] * sketch_cols.astype(f32)
    live_rows = live.reshape(groups, LANES)
    weight_rows = weight.reshape(groups, LANES)
    source_rows = src_local.reshape(groups, LANES)
    target_rows = dst_index.reshape(groups, LANES)

    outgoing = call(
        functools.partial(halo_side_kernel, rows, slots, width),
        [((blocks, width + 8, LANES), f32, ANY)],
        [VMEM] * 3,
        [pltpu.VMEM((edges, 2 * LANES), bf16), pltpu.VMEM((8 * width, edges), bf16)]
        + [pltpu.VMEM((blocks, width + 8, LANES), f32), pltpu.SemaphoreType.DMA],
        "halo_side",
        flops=2 * slots * edges * 2 * LANES,
    )(terms, target_rows, weight_rows)[0]
    returned = across(outgoing)
    own, own_degree = call(
        own_side_kernel,
        [((rows, LANES), f32, VMEM), ((rows // LANES, LANES), f32, VMEM)],
        [VMEM] * 4,
        [pltpu.VMEM((edges, 2 * LANES), bf16), pltpu.VMEM((256, edges), bf16)],
        "own_side",
        flops=2 * rows * edges * 2 * LANES,
    )(terms, source_rows, target_rows, weight_rows)
    sides = call(
        side_join_kernel,
        [((share + 8, LANES), f32, VMEM)] * lanes,
        [SMEM, ANY] + [VMEM] * 4,
        [pltpu.VMEM((rows, LANES), f32), pltpu.VMEM((slots, 2 * LANES), bf16), pltpu.VMEM((256, slots), bf16)]
        + [pltpu.VMEM((blocks, width + 8, LANES), f32), pltpu.SemaphoreType.DMA],
        "side_join",
        flops=2 * rows * slots * 2 * LANES,
    )(lane, returned, listed, padded, own, own_degree)
    begin, *sides = lax.optimization_barrier((edge_count, *sides))
    away = dst_index >= rows
    near_weight = jnp.where(away, 0.0, weight)
    near_order = src_local | (jnp.where(away, 0, dst_index) << 12)
    gap_order = src_local | (jnp.minimum(dst_index, rows) << 12)
    gap_slot = jnp.where(away, dst_index - rows, slots)
    far_order = jnp.where(away, src_local | ((dst_index - rows) << 12), -1)

    def far_list(start, stop, count):
        room = stop - start + LANES
        return call(
            functools.partial(far_list_kernel, start, stop),
            [((room,), i32, SMEM), ((room,), f32, SMEM), ((1,), i32, SMEM)],
            [SMEM] * 3,
            [],
            "far_list",
            moved=2**25,
        )(count, far_order, weight)

    middle = edges // 2
    list_a = far_list(0, middle, begin)
    side = summed(sides, lanes)
    side, size_a = lax.optimization_barrier((side, list_a[2]))
    later, side = lax.optimization_barrier((edge_count, side))
    list_b = far_list(middle, edges, later)
    far = (list_a[0], list_a[1], size_a, *list_b)
    right_share = side[:share]
    degree_share = side[share : share + share // LANES].reshape(share)
    ground_share = lax.dynamic_slice_in_dim(ground, lane[0] * share, share)
    diagonal = (degree_share + ground_share)[:, None]
    inverse = 1.0 / diagonal

    first, pairs = chebyshev_terms(ITERS)
    residual = right_share
    direction = first * inverse * right_share
    solution_share = direction
    for keep, push in pairs:
        field, message = call(
            field_kernel,
            [((rows, LANES), f32, VMEM), ((blocks, 2 * width, LANES), f32, ANY)],
            [SMEM] * 8 + [VMEM] * lanes,
            [pltpu.VMEM((blocks, width, LANES), f32)] * 2
            + [pltpu.SemaphoreType.DMA] * 2
            + [pltpu.VMEM((slots, LANES), f32)] * BANKS,
            "field",
        )(lane, *far, lists, *to_all(direction, lanes))
        arrived = across(message)
        near = call(
            near_kernel,
            [((rows, LANES), f32, VMEM)],
            [SMEM] * 3 + [VMEM],
            [pltpu.VMEM((rows, LANES), f32)] * BANKS,
            "near",
            moved=2**25,
        )(edge_count, near_order, near_weight, field)[0]
        two, sums, ret_both = call(
            functools.partial(first_join_kernel, 2, lanes),
            [((share, LANES), f32, VMEM), ((rows, LANES), f32, VMEM), ((slots, 2 * LANES), bf16, VMEM)],
            [SMEM] * 7 + [VMEM, VMEM, ANY],
            [pltpu.VMEM((share, slots), bf16)]
            + [pltpu.VMEM((blocks, width, LANES), f32)] * 2
            + [pltpu.SemaphoreType.DMA] * 2
            + [pltpu.VMEM((rows, LANES), f32)] * BANKS,
            "join_two",
        )(lane, *far, listed, near, arrived)
        one, three = call(
            functools.partial(join_kernel, (1, 3), lanes),
            [((share, LANES), f32, VMEM)] * 2,
            [SMEM] + [VMEM] * 3,
            [pltpu.VMEM((share, slots), bf16)],
            "join_one_three",
        )(lane, listed, sums, ret_both)
        home = call(
            functools.partial(join_kernel, (0,), lanes),
            [((share, LANES), f32, VMEM)],
            [SMEM] + [VMEM] * 3,
            [pltpu.VMEM((share, slots), bf16)],
            "join_home",
            moved=2**25,
        )(lane, listed, sums, ret_both)[0]
        flows = summed((home, one, two, three), lanes)
        residual = residual - (diagonal * direction - flows)
        direction = keep * direction + push * inverse * residual
        solution_share = solution_share + direction
    field, message = call(
        solution_kernel,
        [((rows, LANES), f32, VMEM), ((blocks, width, LANES), f32, ANY)],
        [SMEM] * 2 + [VMEM] * lanes,
        [pltpu.VMEM((blocks, width, LANES), f32), pltpu.SemaphoreType.DMA],
        "solution_rows",
    )(lane, lists, *to_all(solution_share, lanes))
    halo = across(message)
    gaps = call(
        near_gap_kernel,
        [((edges, LANES), f32, VMEM)],
        [SMEM] * 2 + [VMEM],
        [pltpu.VMEM((rows + 8, LANES), f32)],
        "near_gap",
        moved=2**25,
    )(edge_count, gap_order, field)[0]
    resistance = call(
        far_gap_kernel,
        [((groups, LANES), f32, VMEM)],
        [SMEM] * 2 + [VMEM, ANY, VMEM],
        [pltpu.VMEM((blocks + 1, width, LANES), f32), pltpu.VMEM((edges, LANES), f32), pltpu.SemaphoreType.DMA],
        "far_gap",
    )(edge_count, gap_slot, gaps, halo, live_rows)[0]
    return (field, resistance.reshape(edges))


def solution(mesh):
    in_specs = (
        P(("vtx", "edg"), None),
        P(("vtx", "edg")),
        P("vtx"),
        P(("vtx", "edg")),
        P(("vtx", "edg")),
        P(("vtx", "edg"), None, None),
        P(("vtx", "edg")),
    )
    out_specs = (P("vtx", None), P(("vtx", "edg")))
    return jax.shard_map(local, mesh=mesh, in_specs=in_specs, out_specs=out_specs, check_vma=False)
```

time: 278 us -> 257 us (0.924)
  waiting for transfers between devices: 112 us -> 95.1 us
  starting transfers between devices: 82.6 us -> 78.8 us
    ppermute x18, waiting for transfers between devices: 62.2 us -> 45.5 us  [passed_round(): lax.ppermute(blocks[s], 'edg', [(i, (i + sign * s) % lanes) for i in rang...]
    all_to_all x4, starting transfers between devices: 55.9 us -> 48.1 us  [across(): return lax.all_to_all(x, 'vtx', split_axis=0, concat_axis=0, tiled=True)]
    ppermute x18, starting transfers between devices: 26.8 us -> 30.7 us  [passed_round(): lax.ppermute(blocks[s], 'edg', [(i, (i + sign * s) % lanes) for i in rang...]
    pallas_call x6 -> x11, Pallas kernels: 28.1 us -> 27.3 us  [the longest x2 8.93 us: local(): call(functools.partial(first_join_kernel, 2, lanes), [((share, LANES), f3...]
  transfers between devices with their start and end apart: 22 -> 22, of which waited for: 16 -> 18; matrix products, arithmetic and copies ran while one was open for 0% -> 0% of each run, Pallas kernels for 10% -> 11%
where the time goes in v3:
time: 257 us; the launch traced here: 256 us
  waiting for transfers between devices  95.1 us (37%)
  starting transfers between devices  78.8 us (31%)
  Pallas kernels  66.4 us (26%)
  local copies, waits for them, and re-layouts  8.93 us (3%)
  other arithmetic  4.9 us (2%)
    all_to_all x4, waiting for transfers between devices, across(): return lax.all_to_all(x, 'vtx', split_axis=0, concat_axis=0, tiled=True)  49.6 us
    all_to_all x4, starting transfers between devices, across(): return lax.all_to_all(x, 'vtx', split_axis=0, concat_axis=0, tiled=True)  48.1 us
    ppermute x18, waiting for transfers between devices, passed_round(): lax.ppermute(blocks[s], 'edg', [(i, (i + sign * s) % lanes) for i in rang...  45.5 us
    ppermute x18, starting transfers between devices, passed_round(): lax.ppermute(blocks[s], 'edg', [(i, (i + sign * s) % lanes) for i in rang...  30.7 us
    pallas_call x1, Pallas kernels, local(): call(own_side_kernel, [((rows, LANES), f32, VMEM), ((rows // LANES, LANES...  12 us
    pallas_call x2, Pallas kernels, local(): call(field_kernel, [((rows, LANES), f32, VMEM), ((blocks, 2 * width, LANE...  11.7 us
    pallas_call x2, Pallas kernels, local(): call(functools.partial(first_join_kernel, 2, lanes), [((share, LANES), f3...  8.93 us
    unnamed x24, local copies, waits for them, and re-layouts  8.77 us
  transfers between devices with their start and end apart: 22, of which 18 were waited for; matrix products, arithmetic and copies ran while one was open for 0% of the time, Pallas kernels for 11%

profile of v3, /device:TPU:1, one launch (start us, length us, event | category | flops | bytes accessed | tf_op | source)
XLA Modules:
  0.0 255.8 jit_solution(43640378554621386)
XLA Ops:
  3.9 5.4 %halo_side.1 = f32[32,56,128]{2,1,0:T(8,128)S(1)} custom-call(f32[4096,128]{1,0:T(8,128)S(1)} %convert_multiply_fusion.terms, s32[32,128]{1,0:T(8,128)S(1)} %bitcast.14, f32[32,128]{1,0:T(8,128)S(1)} %bitcast.12), custom_call_target="tpu_custom_call" | custom-call | flops 3221225472 | bytes 4194304 | tf_op jit(solution)/shard_map/halo_side/pallas_call | solution.py:470
  10.3 8.6 %all-to-all-start = ((f32[32,56,128]{2,1,0:T(8,128)}), f32[32,56,128]{2,1,0:T(8,128)S(1)}, u32[]{:S(2)}, u32[]{:S(2)}) async-start(f32[32,56,128]{2,1,0:T(8,128)} %copy-done.5), calls=%async_computation | async-start | bytes 1835008 | tf_op jit(solution)/shard_map/all_to_all | solution.py:444
  19.0 12.0 %own_side.1 = (f32[2048,128]{1,0:T(8,128)S(1)}, f32[16,128]{1,0:T(8,128)S(1)}) custom-call(f32[4096,128]{1,0:T(8,128)S(1)} %convert_multiply_fusion.terms, s32[32,128]{1,0:T(8,128)S(1)} %bitcast.16, s32[32,128]{1,0:T(8,128)S(1)} %bitcast.15, f32[32,128]{1,0:T(8,128)S(1)} %bitcast.13), custom_call_target="tpu_custom_call" | custom-call | flops 4294967296 | bytes 4194304 | tf_op jit(solution)/shard_map/own_side/pallas_call | solution.py:480
  35.9 3.9 %side_join.1 = (f32[520,128]{1,0:T(8,128)S(1)}, f32[520,128]{1,0:T(8,128)S(1)}, f32[520,128]{1,0:T(8,128)S(1)}, f32[520,128]{1,0:T(8,128)S(1)}) custom-call(s32[1]{0:T(128)} %bitcast.lane, f32[32,56,128]{2,1,0:T(8,128)S(1)} %all-to-all-done.returned, s32[12,128]{1,0:T(8,128)S(1)} %reshape_reshape_squeeze.3.listed, s32[32,128]{1,0:T(8,128)S(1)} %pad.4.padded, ...), custom_call_target="tpu_custom_call" | custom-call | flops 1610612736 | bytes 4194304 | tf_op jit(solution)/shard_map/side_join/pallas_call | solution.py:488
  45.6 4.3 %far_list.2 = (s32[2176]{0:T(1024)S(1)}, f32[2176]{0:T(1024)S(1)}, s32[1]{0:T(128)}) custom-call(s32[1]{0:T(128)} %copy.9.count, s32[4096]{0:T(1024)S(1)} %get-tuple-element.83.order, f32[4096]{0:T(1024)S(1)} %get-tuple-element.81.mass), custom_call_target="tpu_custom_call" | custom-call | bytes 33554432 | tf_op jit(solution)/shard_map/far_list/pallas_call | solution.py:507
  50.1 6.6 %collective-permute-done.1 = f32[520,128]{1,0:T(8,128)S(1)} collective-permute-done((f32[520,128]{1,0:T(8,128)S(1)}, f32[520,128]{1,0:T(8,128)S(1)}, u32[]{:S(2)}, u32[]{:S(2)}) %collective-permute-start.1) | collective-permute-done | bytes 266272 | tf_op jit(solution)/shard_map/ppermute | solution.py:429
  65.5 7.5 %collective-permute-done.4.refs_2_ = f32[512,128]{1,0:T(8,128)S(1)} collective-permute-done((f32[512,128]{1,0:T(8,128)S(1)}, f32[512,128]{1,0:T(8,128)S(1)}, u32[]{:S(2)}, u32[]{:S(2)}) %collective-permute-start.4) | collective-permute-done | bytes 262176 | tf_op jit(solution)/shard_map/ppermute | solution.py:429
  73.1 5.8 %field.2 = (f32[2048,128]{1,0:T(8,128)S(1)}, f32[32,96,128]{2,1,0:T(8,128)}) custom-call(s32[1]{0:T(128)} %bitcast.lane, s32[2176]{0:T(1024)S(1)} %get-tuple-element.53.rows_a, f32[2176]{0:T(1024)S(1)} %get-tuple-element.54.mass_a, s32[1]{0:T(128)} %get-tuple-element.55.size_a, s32[2176]{0:T(1024)S(1)} %get-tuple-element.57.rows_b, ...), custom_call_target="tpu_custom_call" | custom-call | bytes 4194304 | tf_op jit(solution)/shard_map/field/pallas_call | solution.py:534
  79.9 9.7 %all-to-all-start.1 = ((f32[32,96,128]{2,1,0:T(8,128)}), f32[32,96,128]{2,1,0:T(8,128)S(1)}, u32[]{:S(2)}, u32[]{:S(2)}) async-start(f32[32,96,128]{2,1,0:T(8,128)} %get-tuple-element.61), calls=%async_computation.1 | async-start | bytes 3145728 | tf_op jit(solution)/shard_map/all_to_all | solution.py:444
  93.9 17.9 %all-to-all-done.1.arrived = f32[32,96,128]{2,1,0:T(8,128)S(1)} async-done(((f32[32,96,128]{2,1,0:T(8,128)}), f32[32,96,128]{2,1,0:T(8,128)S(1)}, u32[]{:S(2)}, u32[]{:S(2)}) %all-to-all-start.1) | async-done | bytes 1572896 | tf_op jit(solution)/shard_map/all_to_all | solution.py:444
  111.7 4.6 %join_two.2 = (f32[512,128]{1,0:T(8,128)S(1)}, f32[2048,128]{1,0:T(8,128)S(1)}, bf16[1536,256]{1,0:T(8,128)(2,1)S(1)}) custom-call(s32[1]{0:T(128)} %bitcast.lane, s32[2176]{0:T(1024)S(1)} %get-tuple-element.53.rows_a, f32[2176]{0:T(1024)S(1)} %get-tuple-element.54.mass_a, s32[1]{0:T(128)} %get-tuple-element.55.size_a, s32[2176]{0:T(1024)S(1)} %get-tuple-element.57.rows_b, ...), custom_call_target="tpu_custom_call" | custom-call | bytes 4194304 | tf_op jit(solution)/shard_map/join_two/pallas_call | solution.py:552
  124.1 3.8 %collective-permute-done.8 = f32[512,128]{1,0:T(8,128)S(1)} collective-permute-done((f32[512,128]{1,0:T(8,128)S(1)}, f32[512,128]{1,0:T(8,128)S(1)}, u32[]{:S(2)}, u32[]{:S(2)}) %collective-permute-start.8) | collective-permute-done | bytes 262176 | tf_op jit(solution)/shard_map/ppermute | solution.py:429
  131.2 5.2 %collective-permute-start.10 = (f32[512,128]{1,0:T(8,128)S(1)}, f32[512,128]{1,0:T(8,128)S(1)}, u32[]{:S(2)}, u32[]{:S(2)}) collective-permute-start(f32[512,128]{1,0:T(8,128)S(1)} %get-tuple-element.78.refs_0_), channel_id=1, source_target_pairs={{0,2},{1,3},{2,0},{3,1},{4,6},{5,7},{6,4},{7,5},{8,10},{9,11},{10,... | collective-permute-start | bytes 786440 | tf_op jit(solution)/shard_map/ppermute | solution.py:429
  137.9 3.3 %collective-permute-done.10.refs_2_ = f32[512,128]{1,0:T(8,128)S(1)} collective-permute-done((f32[512,128]{1,0:T(8,128)S(1)}, f32[512,128]{1,0:T(8,128)S(1)}, u32[]{:S(2)}, u32[]{:S(2)}) %collective-permute-start.10) | collective-permute-done | bytes 262176 | tf_op jit(solution)/shard_map/ppermute | solution.py:429
  141.2 7.0 %collective-permute-done.11.refs_3_ = f32[512,128]{1,0:T(8,128)S(1)} collective-permute-done((f32[512,128]{1,0:T(8,128)S(1)}, f32[512,128]{1,0:T(8,128)S(1)}, u32[]{:S(2)}, u32[]{:S(2)}) %collective-permute-start.11) | collective-permute-done | bytes 262176 | tf_op jit(solution)/shard_map/ppermute | solution.py:429
  148.2 5.8 %field.3 = (f32[2048,128]{1,0:T(8,128)S(1)}, f32[32,96,128]{2,1,0:T(8,128)}) custom-call(s32[1]{0:T(128)} %bitcast.lane, s32[2176]{0:T(1024)S(1)} %get-tuple-element.53.rows_a, f32[2176]{0:T(1024)S(1)} %get-tuple-element.54.mass_a, s32[1]{0:T(128)} %get-tuple-element.55.size_a, s32[2176]{0:T(1024)S(1)} %get-tuple-element.57.rows_b, ...), custom_call_target="tpu_custom_call" | custom-call | bytes 4194304 | tf_op jit(solution)/shard_map/field/pallas_call | solution.py:534
  155.0 12.3 %all-to-all-start.2 = ((f32[32,96,128]{2,1,0:T(8,128)}), f32[32,96,128]{2,1,0:T(8,128)S(1)}, u32[]{:S(2)}, u32[]{:S(2)}) async-start(f32[32,96,128]{2,1,0:T(8,128)} %get-tuple-element.68), calls=%async_computation.2 | async-start | bytes 3145728 | tf_op jit(solution)/shard_map/all_to_all | solution.py:444
  171.6 17.9 %all-to-all-done.2.arrived = f32[32,96,128]{2,1,0:T(8,128)S(1)} async-done(((f32[32,96,128]{2,1,0:T(8,128)}), f32[32,96,128]{2,1,0:T(8,128)S(1)}, u32[]{:S(2)}, u32[]{:S(2)}) %all-to-all-start.2) | async-done | bytes 1572896 | tf_op jit(solution)/shard_map/all_to_all | solution.py:444
  189.5 4.4 %join_two.3 = (f32[512,128]{1,0:T(8,128)S(1)}, f32[2048,128]{1,0:T(8,128)S(1)}, bf16[1536,256]{1,0:T(8,128)(2,1)S(1)}) custom-call(s32[1]{0:T(128)} %bitcast.lane, s32[2176]{0:T(1024)S(1)} %get-tuple-element.53.rows_a, f32[2176]{0:T(1024)S(1)} %get-tuple-element.54.mass_a, s32[1]{0:T(128)} %get-tuple-element.55.size_a, s32[2176]{0:T(1024)S(1)} %get-tuple-element.57.rows_b, ...), custom_call_target="tpu_custom_call" | custom-call | bytes 4194304 | tf_op jit(solution)/shard_map/join_two/pallas_call | solution.py:552
  201.8 3.9 %collective-permute-done.13 = f32[512,128]{1,0:T(8,128)S(1)} collective-permute-done((f32[512,128]{1,0:T(8,128)S(1)}, f32[512,128]{1,0:T(8,128)S(1)}, u32[]{:S(2)}, u32[]{:S(2)}) %collective-permute-start.13) | collective-permute-done | bytes 262176 | tf_op jit(solution)/shard_map/ppermute | solution.py:429
  207.1 3.8 %collective-permute-start.16 = (f32[512,128]{1,0:T(8,128)S(1)}, f32[512,128]{1,0:T(8,128)S(1)}, u32[]{:S(2)}, u32[]{:S(2)}) collective-permute-start(f32[512,128]{1,0:T(8,128)S(1)} %add_add_fusion.1.refs_0_), channel_id=1, source_target_pairs={{0,2},{1,3},{2,0},{3,1},{4,6},{5,7},{6,4},{7,5},{8,10},{9,11},{10,... | collective-permute-start | bytes 786440 | tf_op jit(solution)/shard_map/ppermute | solution.py:429
  217.4 3.9 %solution_rows.1 = (f32[2048,128]{1,0:T(8,128)}, f32[32,48,128]{2,1,0:T(8,128)}) custom-call(s32[1]{0:T(128)} %bitcast.lane, s32[1536]{0:T(1024)S(1)} %reshape_squeeze.3.lists, f32[512,128]{1,0:T(8,128)S(1)} %add_add_fusion.1.refs_0_, f32[512,128]{1,0:T(8,128)S(1)} %collective-permute-done.15.refs_1_, f32[512,128]{1,0:T(8,128)S(1)} %collective-permute-done.16.refs_2_, ...), custom_call_target="tpu_custom_call" | custom-call | bytes 4194304 | tf_op jit(solution)/shard_map/solution_rows/pallas_call | solution.py:581
  221.3 17.6 %all-to-all-start.3 = ((f32[32,48,128]{2,1,0:T(8,128)}), f32[32,48,128]{2,1,0:T(8,128)S(1)}, u32[]{:S(2)}, u32[]{:S(2)}) async-start(f32[32,48,128]{2,1,0:T(8,128)} %get-tuple-element.75), calls=%async_computation.3 | async-start | bytes 1572864 | tf_op jit(solution)/shard_map/all_to_all | solution.py:444
  242.0 11.1 %all-to-all-done.3.arrived = f32[32,48,128]{2,1,0:T(8,128)S(1)} async-done(((f32[32,48,128]{2,1,0:T(8,128)}), f32[32,48,128]{2,1,0:T(8,128)S(1)}, u32[]{:S(2)}, u32[]{:S(2)}) %all-to-all-start.3) | async-done | bytes 786464 | tf_op jit(solution)/shard_map/all_to_all | solution.py:444
  (75 shorter events, 67.9 us)
Async XLA Ops:
  3.9 15.0 %copy-start.11 = (s32[1,32,48]{2,1,0:T(8,128)S(1)}, s32[1,32,48]{2,1,0:T(8,128)}, u32[]{:S(2)}) copy-start(s32[1,32,48]{2,1,0:T(8,128)} %param.12) | copy-start | bytes 18436
  3.9 15.1 %copy-start.7 = (s32[4096]{0:T(1024)S(1)}, s32[4096]{0:T(1024)}, u32[]{:S(2)}) copy-start(s32[4096]{0:T(1024)} %param.10) | copy-start | bytes 49156
  10.3 24.4 %all-to-all-start = ((f32[32,56,128]{2,1,0:T(8,128)}), f32[32,56,128]{2,1,0:T(8,128)S(1)}, u32[]{:S(2)}, u32[]{:S(2)}) async-start(f32[32,56,128]{2,1,0:T(8,128)} %copy-done.5), calls=%async_computation | async-start | bytes 1835008 | tf_op jit(solution)/shard_map/all_to_all | solution.py:444
  39.8 10.3 %collective-permute-start = (f32[520,128]{1,0:T(8,128)S(1)}, f32[520,128]{1,0:T(8,128)S(1)}, u32[]{:S(2)}, u32[]{:S(2)}) collective-permute-start(f32[520,128]{1,0:T(8,128)S(1)} %get-tuple-element.46), channel_id=1, source_target_pairs={{0,1},{1,2},{2,3},{3,0},{4,5},{5,6},{6,7},{7,4},{8,9},{9,10},{10,1... | collective-permute-start | bytes 798728 | tf_op jit(solution)/shard_map/ppermute | solution.py:429
  41.5 15.1 %collective-permute-start.1 = (f32[520,128]{1,0:T(8,128)S(1)}, f32[520,128]{1,0:T(8,128)S(1)}, u32[]{:S(2)}, u32[]{:S(2)}) collective-permute-start(f32[520,128]{1,0:T(8,128)S(1)} %get-tuple-element.47), channel_id=1, source_target_pairs={{0,2},{1,3},{2,0},{3,1},{4,6},{5,7},{6,4},{7,5},{8,10},{9,11},{10,... | collective-permute-start | bytes 798728 | tf_op jit(solution)/shard_map/ppermute | solution.py:429
  44.8 11.8 %collective-permute-start.2 = (f32[520,128]{1,0:T(8,128)S(1)}, f32[520,128]{1,0:T(8,128)S(1)}, u32[]{:S(2)}, u32[]{:S(2)}) collective-permute-start(f32[520,128]{1,0:T(8,128)S(1)} %get-tuple-element.48), channel_id=1, source_target_pairs={{0,3},{1,0},{2,1},{3,2},{4,7},{5,4},{6,5},{7,6},{8,11},{9,8},{10,9... | collective-permute-start | bytes 798728 | tf_op jit(solution)/shard_map/ppermute | solution.py:429
  57.7 7.9 %collective-permute-start.3 = (f32[512,128]{1,0:T(8,128)S(1)}, f32[512,128]{1,0:T(8,128)S(1)}, u32[]{:S(2)}, u32[]{:S(2)}) collective-permute-start(f32[512,128]{1,0:T(8,128)S(1)} %slice_multiply_fusion.refs_0_), channel_id=1, source_target_pairs={{0,1},{1,2},{2,3},{3,0},{4,5},{5,6},{6,7},{7,4},{8,9},{9,10},{10,1... | collective-permute-start | bytes 786440 | tf_op jit(solution)/shard_map/ppermute | solution.py:429
  59.0 14.0 %collective-permute-start.4 = (f32[512,128]{1,0:T(8,128)S(1)}, f32[512,128]{1,0:T(8,128)S(1)}, u32[]{:S(2)}, u32[]{:S(2)}) collective-permute-start(f32[512,128]{1,0:T(8,128)S(1)} %slice_multiply_fusion.refs_0_), channel_id=1, source_target_pairs={{0,2},{1,3},{2,0},{3,1},{4,6},{5,7},{6,4},{7,5},{8,10},{9,11},{10,... | collective-permute-start | bytes 786440 | tf_op jit(solution)/shard_map/ppermute | solution.py:429
  61.5 11.5 %collective-permute-start.5 = (f32[512,128]{1,0:T(8,128)S(1)}, f32[512,128]{1,0:T(8,128)S(1)}, u32[]{:S(2)}, u32[]{:S(2)}) collective-permute-start(f32[512,128]{1,0:T(8,128)S(1)} %slice_multiply_fusion.refs_0_), channel_id=1, source_target_pairs={{0,3},{1,0},{2,1},{3,2},{4,7},{5,4},{6,5},{7,6},{8,11},{9,8},{10,9... | collective-permute-start | bytes 786440 | tf_op jit(solution)/shard_map/ppermute | solution.py:429
  79.9 31.9 %all-to-all-start.1 = ((f32[32,96,128]{2,1,0:T(8,128)}), f32[32,96,128]{2,1,0:T(8,128)S(1)}, u32[]{:S(2)}, u32[]{:S(2)}) async-start(f32[32,96,128]{2,1,0:T(8,128)} %get-tuple-element.61), calls=%async_computation.1 | async-start | bytes 3145728 | tf_op jit(solution)/shard_map/all_to_all | solution.py:444
  117.6 6.5 %collective-permute-start.6 = (f32[512,128]{1,0:T(8,128)S(1)}, f32[512,128]{1,0:T(8,128)S(1)}, u32[]{:S(2)}, u32[]{:S(2)}) collective-permute-start(f32[512,128]{1,0:T(8,128)S(1)} %get-tuple-element.64), channel_id=1, source_target_pairs={{0,1},{1,2},{2,3},{3,0},{4,5},{5,6},{6,7},{7,4},{8,9},{9,10},{10,1... | collective-permute-start | bytes 786440 | tf_op jit(solution)/shard_map/ppermute | solution.py:429
  118.1 9.7 %collective-permute-start.8 = (f32[512,128]{1,0:T(8,128)S(1)}, f32[512,128]{1,0:T(8,128)S(1)}, u32[]{:S(2)}, u32[]{:S(2)}) collective-permute-start(f32[512,128]{1,0:T(8,128)S(1)} %get-tuple-element.66), channel_id=1, source_target_pairs={{0,3},{1,0},{2,1},{3,2},{4,7},{5,4},{6,5},{7,6},{8,11},{9,8},{10,9... | collective-permute-start | bytes 786440 | tf_op jit(solution)/shard_map/ppermute | solution.py:429
  120.4 9.9 %collective-permute-start.7 = (f32[512,128]{1,0:T(8,128)S(1)}, f32[512,128]{1,0:T(8,128)S(1)}, u32[]{:S(2)}, u32[]{:S(2)}) collective-permute-start(f32[512,128]{1,0:T(8,128)S(1)} %get-tuple-element.65), channel_id=1, source_target_pairs={{0,2},{1,3},{2,0},{3,1},{4,6},{5,7},{6,4},{7,5},{8,10},{9,11},{10,... | collective-permute-start | bytes 786440 | tf_op jit(solution)/shard_map/ppermute | solution.py:429
  131.2 10.0 %collective-permute-start.10 = (f32[512,128]{1,0:T(8,128)S(1)}, f32[512,128]{1,0:T(8,128)S(1)}, u32[]{:S(2)}, u32[]{:S(2)}) collective-permute-start(f32[512,128]{1,0:T(8,128)S(1)} %get-tuple-element.78.refs_0_), channel_id=1, source_target_pairs={{0,2},{1,3},{2,0},{3,1},{4,6},{5,7},{6,4},{7,5},{8,10},{9,11},{10,... | collective-permute-start | bytes 786440 | tf_op jit(solution)/shard_map/ppermute | solution.py:429
  136.4 11.8 %collective-permute-start.11 = (f32[512,128]{1,0:T(8,128)S(1)}, f32[512,128]{1,0:T(8,128)S(1)}, u32[]{:S(2)}, u32[]{:S(2)}) collective-permute-start(f32[512,128]{1,0:T(8,128)S(1)} %get-tuple-element.78.refs_0_), channel_id=1, source_target_pairs={{0,3},{1,0},{2,1},{3,2},{4,7},{5,4},{6,5},{7,6},{8,11},{9,8},{10,9... | collective-permute-start | bytes 786440 | tf_op jit(solution)/shard_map/ppermute | solution.py:429
  136.9 11.3 %collective-permute-start.9 = (f32[512,128]{1,0:T(8,128)S(1)}, f32[512,128]{1,0:T(8,128)S(1)}, u32[]{:S(2)}, u32[]{:S(2)}) collective-permute-start(f32[512,128]{1,0:T(8,128)S(1)} %get-tuple-element.78.refs_0_), channel_id=1, source_target_pairs={{0,1},{1,2},{2,3},{3,0},{4,5},{5,6},{6,7},{7,4},{8,9},{9,10},{10,1... | collective-permute-start | bytes 786440 | tf_op jit(solution)/shard_map/ppermute | solution.py:429
  155.0 34.5 %all-to-all-start.2 = ((f32[32,96,128]{2,1,0:T(8,128)}), f32[32,96,128]{2,1,0:T(8,128)S(1)}, u32[]{:S(2)}, u32[]{:S(2)}) async-start(f32[32,96,128]{2,1,0:T(8,128)} %get-tuple-element.68), calls=%async_computation.2 | async-start | bytes 3145728 | tf_op jit(solution)/shard_map/all_to_all | solution.py:444
  195.2 6.5 %collective-permute-start.12 = (f32[512,128]{1,0:T(8,128)S(1)}, f32[512,128]{1,0:T(8,128)S(1)}, u32[]{:S(2)}, u32[]{:S(2)}) collective-permute-start(f32[512,128]{1,0:T(8,128)S(1)} %get-tuple-element.71), channel_id=1, source_target_pairs={{0,1},{1,2},{2,3},{3,0},{4,5},{5,6},{6,7},{7,4},{8,9},{9,10},{10,1... | collective-permute-start | bytes 786440 | tf_op jit(solution)/shard_map/ppermute | solution.py:429
  195.3 6.5 %collective-permute-start.14 = (f32[512,128]{1,0:T(8,128)S(1)}, f32[512,128]{1,0:T(8,128)S(1)}, u32[]{:S(2)}, u32[]{:S(2)}) collective-permute-start(f32[512,128]{1,0:T(8,128)S(1)} %get-tuple-element.73), channel_id=1, source_target_pairs={{0,3},{1,0},{2,1},{3,2},{4,7},{5,4},{6,5},{7,6},{8,11},{9,8},{10,9... | collective-permute-start | bytes 786440 | tf_op jit(solution)/shard_map/ppermute | solution.py:429
  198.0 7.8 %collective-permute-start.13 = (f32[512,128]{1,0:T(8,128)S(1)}, f32[512,128]{1,0:T(8,128)S(1)}, u32[]{:S(2)}, u32[]{:S(2)}) collective-permute-start(f32[512,128]{1,0:T(8,128)S(1)} %get-tuple-element.72), channel_id=1, source_target_pairs={{0,2},{1,3},{2,0},{3,1},{4,6},{5,7},{6,4},{7,5},{8,10},{9,11},{10,... | collective-permute-start | bytes 786440 | tf_op jit(solution)/shard_map/ppermute | solution.py:429
  206.1 8.0 %collective-permute-start.15 = (f32[512,128]{1,0:T(8,128)S(1)}, f32[512,128]{1,0:T(8,128)S(1)}, u32[]{:S(2)}, u32[]{:S(2)}) collective-permute-start(f32[512,128]{1,0:T(8,128)S(1)} %add_add_fusion.1.refs_0_), channel_id=1, source_target_pairs={{0,1},{1,2},{2,3},{3,0},{4,5},{5,6},{6,7},{7,4},{8,9},{9,10},{10,1... | collective-permute-start | bytes 786440 | tf_op jit(solution)/shard_map/ppermute | solution.py:429
  207.1 10.3 %collective-permute-start.16 = (f32[512,128]{1,0:T(8,128)S(1)}, f32[512,128]{1,0:T(8,128)S(1)}, u32[]{:S(2)}, u32[]{:S(2)}) collective-permute-start(f32[512,128]{1,0:T(8,128)S(1)} %add_add_fusion.1.refs_0_), channel_id=1, source_target_pairs={{0,2},{1,3},{2,0},{3,1},{4,6},{5,7},{6,4},{7,5},{8,10},{9,11},{10,... | collective-permute-start | bytes 786440 | tf_op jit(solution)/shard_map/ppermute | solution.py:429
  210.8 6.6 %collective-permute-start.17 = (f32[512,128]{1,0:T(8,128)S(1)}, f32[512,128]{1,0:T(8,128)S(1)}, u32[]{:S(2)}, u32[]{:S(2)}) collective-permute-start(f32[512,128]{1,0:T(8,128)S(1)} %add_add_fusion.1.refs_0_), channel_id=1, source_target_pairs={{0,3},{1,0},{2,1},{3,2},{4,7},{5,4},{6,5},{7,6},{8,11},{9,8},{10,9... | collective-permute-start | bytes 786440 | tf_op jit(solution)/shard_map/ppermute | solution.py:429
  221.3 31.8 %all-to-all-start.3 = ((f32[32,48,128]{2,1,0:T(8,128)}), f32[32,48,128]{2,1,0:T(8,128)S(1)}, u32[]{:S(2)}, u32[]{:S(2)}) async-start(f32[32,48,128]{2,1,0:T(8,128)} %get-tuple-element.75), calls=%async_computation.3 | async-start | bytes 1572864 | tf_op jit(solution)/shard_map/all_to_all | solution.py:444
  (10 other events, 24.0 us)

commit v4 on v3

--- a/solution.py
+++ b/solution.py
@@ -11,13 +11,15 @@
 LANES = 128
 UNROLL = 16
 BANKS = 4
+QUARTERS = 4
+SPARE = 1536
 
 lam_low = 0.05
 lam_high = 2.0
 
 SMEM = pl.BlockSpec(memory_space=pltpu.SMEM)
 VMEM = pl.BlockSpec(memory_space=pltpu.VMEM)
-ANY = pl.BlockSpec(memory_space=pl.ANY)
+HBM = pl.BlockSpec(memory_space=pltpu.HBM)
 LIMIT = 24 * 2**20
 
 
@@ -37,7 +39,9 @@
 def call(kernel, outs, ins, scratch, name, flops=0, moved=2**22):
     return pl.pallas_call(
         kernel,
-        out_shape=[jax.ShapeDtypeStruct(shape, dtype) for shape, dtype, _ in outs],
+        out_shape=[
+            pltpu.HBM(shape, dtype) if space is HBM else jax.ShapeDtypeStruct(shape, dtype) for shape, dtype, space in outs
+        ],
         in_specs=ins,
         out_specs=[space for _, _, space in outs],
         scratch_shapes=scratch,
@@ -87,10 +91,28 @@
 
 def halo_side_kernel(rows, slots, width, terms, target, weight, sent, both, hot, out, leave):
     groups = target.shape[0]
-    edges = terms.shape[0]
-    put_split(both, slice(None), terms[...])
     tall = hot.shape[0]
     per = tall // width
+    blocks = slots // width
+    chunks = slots // tall
+
+    def slot(k):
+        return target[k : k + 1, :] - rows
+
+    def block_of(k):
+        return jnp.where(slot(k) < 0, -1, lax.shift_right_arithmetic(slot(k) * 1366, 16))
+
+    def within(k):
+        return slot(k) - block_of(k) * width
+
+    deg = factored(4, groups, block_of, within, lambda k: weight[k : k + 1, :], blocks)
+    for c in range(blocks):
+        out[c, width : width + 8, :] = jnp.broadcast_to(deg[c : c + 1, :], (8, LANES))
+    put_split(both, slice(None), terms[...])
+
+    def part(i):
+        at = pl.ds(i * per, per)
+        return pltpu.make_async_copy(out.at[at], sent.at[at], leave.at[i])
 
     def chunk(i, _):
         base = rows + i * tall
@@ -99,33 +121,23 @@
         got = halves(jnp.dot(hot[...], both[...], preferred_element_type=jnp.float32))
         for c in range(per):
             out[i * per + c, :width, :] = -got[c * width : (c + 1) * width]
+        part(i).start()
         return 0
 
-    lax.fori_loop(0, slots // tall, chunk, 0)
-    blocks = slots // width
-
-    def slot(k):
-        return target[k : k + 1, :] - rows
-
-    def block_of(k):
-        return jnp.where(slot(k) < 0, -1, lax.shift_right_arithmetic(slot(k) * 1366, 16))
-
-    def within(k):
-        return slot(k) - block_of(k) * width
-
-    deg = factored(4, groups, block_of, within, lambda k: weight[k : k + 1, :], blocks)
-    for c in range(blocks):
-        out[c, width : width + 8, :] = jnp.broadcast_to(deg[c : c + 1, :], (8, LANES))
-    go = pltpu.make_async_copy(out, sent, leave)
-    go.start()
-    go.wait()
-
-
-def own_side_kernel(terms, source, target, weight, out, degree, both, hot):
+    lax.fori_loop(0, chunks, chunk, 0)
+    for i in range(chunks):
+        part(i).wait()
+
+
+def own_side_kernel(terms, source, target, weight, kept, degree, both, hot, out, leave):
     groups = target.shape[0]
     rows = out.shape[0]
     put_split(both, slice(None), terms[...])
     tall = hot.shape[0]
+
+    def part(i):
+        at = pl.ds(pl.multiple_of(i * tall, tall), tall)
+        return pltpu.make_async_copy(out.at[at, :], kept.at[at, :], leave.at[i])
 
     def chunk(i, _):
         base = i * tall
@@ -136,6 +148,7 @@
         out[pl.ds(pl.multiple_of(i * tall, tall), tall), :] = halves(
             jnp.dot(hot[...], both[...], preferred_element_type=jnp.float32)
         )
+        part(i).start()
         return 0
 
     lax.fori_loop(0, rows // tall, chunk, 0)
@@ -151,6 +164,8 @@
         )
 
     degree[...] = total(source) + total(target)
+    for i in range(rows // tall):
+        part(i).wait()
 
 
 def scatter_back(ret_both, listed, hot, emit, rows):
@@ -169,9 +184,11 @@
 
 def side_join_kernel(lane, returned, listed, padded, own, own_degree, *refs):
     lanes = 4
-    outs, (acc, ret_both, hot, landed, arrival) = refs[:lanes], refs[lanes:]
+    outs, (acc, ret_both, hot, landed, arrival, arrival_own) = refs[:lanes], refs[lanes:]
     come = pltpu.make_async_copy(returned, landed, arrival)
     come.start()
+    mine = pltpu.make_async_copy(own, acc, arrival_own)
+    mine.start()
     blocks = returned.shape[0]
     rows = own.shape[0]
     width = listed.shape[0] * LANES // blocks
@@ -182,8 +199,9 @@
 
     def emit(i, got):
         at = pl.ds(pl.multiple_of(i * hot.shape[0], hot.shape[0]), hot.shape[0])
-        acc[at, :] = own[at, :] + got
-
+        acc[at, :] = acc[at, :] + got
+
+    mine.wait()
     scatter_back(ret_both, listed, hot, emit, rows)
     deg = own_degree[...] + factored(
         4,
@@ -206,23 +224,33 @@
         outs[s][share : share + 8, :] = row
 
 
-def far_list_kernel(begin, end, count, order, mass, code, heavy, size):
-    def step(i, at):
-        e = begin + i * 8
-        given = [order[e + u] for u in range(8)]
-        loads = [mass[e + u] for u in range(8)]
-        for u in range(8):
-            code[at] = given[u]
-            heavy[at] = loads[u]
-            at = at + 1 + lax.shift_right_arithmetic(given[u], 31)
-        return at
-
-    live = jnp.clip(count[0] - begin, 0, end - begin)
-    at = lax.fori_loop(0, lax.div(live + 7, 8), step, 0)
-    for u in range(UNROLL):
-        code[at + u] = 0
-        heavy[at + u] = 0.0
-    size[0] = at
+def far_list_kernel(first, room, count, lane, order, code, sizes):
+    quarter = order.shape[0] // QUARTERS
+    across = lax.rem(lane[0] + 2, 4)
+    for c in range(2):
+        begin = (first + c) * quarter
+        zero = 2 * c * room
+
+        def step(i, at):
+            e = begin + i * 8
+            given = [order[e + u] for u in range(8)]
+            early, late = at
+            for u in range(8):
+                far = jnp.where(lax.shift_right_arithmetic(given[u], 21) == -1, 0, 1)
+                after = (lax.shift_right_logical(given[u], 19) & 3) == across
+                code[jnp.where(after, late, early)] = given[u]
+                early = early + jnp.where(after, 0, far)
+                late = late + jnp.where(after, far, 0)
+            return early, late
+
+        live = jnp.clip(count[0] - begin, 0, quarter)
+        early, late = lax.fori_loop(0, lax.div(live + 7, 8), step, (zero, zero + room))
+        nothing = jnp.int32(SPARE - 2048) << 21
+        for u in range(UNROLL):
+            code[early + u] = nothing
+            code[late + u] = nothing
+        sizes[2 * c] = early - zero
+        sizes[2 * c + 1] = late - zero - room
 
 
 def trips(n):
@@ -234,21 +262,35 @@
         a[...] = jnp.zeros_like(a)
 
 
-def far_rows(lists, take, give, banks):
-    for code, heavy, size in lists:
-
-        def step(i, _):
-            for u in range(0, UNROLL, BANKS):
-                at = i * UNROLL + u
-                given = [code[at + k] for k in range(BANKS)]
-                rows = [take(given[k]) * heavy[at + k] for k in range(BANKS)]
-                to = [pl.ds(give(given[k]), 1) for k in range(BANKS)]
-                new = [banks[k][to[k], :] + rows[k] for k in range(BANKS)]
-                for k in range(BANKS):
-                    banks[k][to[k], :] = new[k]
-            return 0
-
-        lax.fori_loop(0, trips(size[0]), step, 0)
+def far_rows(kind, lists, mass, take, give, banks):
+    quarter = mass.shape[0] // QUARTERS
+    many = len(banks)
+    for h, (code, sizes) in enumerate(lists):
+        room = code.shape[0] // 4
+        for c in range(2):
+            start = (2 * c + kind) * room
+            base = (2 * h + c) * quarter
+
+            def step(i, _):
+                for u in range(0, UNROLL, many):
+                    at = start + i * UNROLL + u
+                    given = [code[at + k] for k in range(many)]
+                    rows = [take(given[k]) * mass[base + (given[k] & 1023)] for k in range(many)]
+                    to = [pl.ds(give(given[k]), 1) for k in range(many)]
+                    new = [banks[k][to[k], :] + rows[k] for k in range(many)]
+                    for k in range(many):
+                        banks[k][to[k], :] = new[k]
+                return 0
+
+            lax.fori_loop(0, trips(sizes[2 * c + kind]), step, 0)
+
+
+def far_source(given):
+    return lax.shift_right_logical(given, 10) & 2047
+
+
+def far_slot(given):
+    return lax.shift_right_logical(given, 21)
 
 
 def source_of(given):
@@ -259,11 +301,15 @@
     return lax.shift_right_logical(given, 12)
 
 
+def place(lane, lanes, shift, share, field):
+    q = lax.rem(lane[0] - shift + lanes, lanes)
+    rows = share.shape[0]
+    field[pl.ds(pl.multiple_of(q * rows, rows), rows), :] = share[...]
+
+
 def assemble(lane, lanes, shares, field):
-    share = shares[0].shape[0]
     for s in range(lanes):
-        q = lax.rem(lane[0] - s + lanes, lanes)
-        field[pl.ds(pl.multiple_of(q * share, share), share), :] = shares[s][...]
+        place(lane, lanes, s, shares[s], field)
 
 
 def pack(lists, field, out, width):
@@ -275,36 +321,63 @@
     lax.fori_loop(0, out.shape[0], step, 0)
 
 
-def field_kernel(lane, rows_a, mass_a, size_a, rows_b, mass_b, size_b, lists, *refs):
-    lanes = 4
-    shares, (field, sent), refs = refs[:lanes], refs[lanes : lanes + 2], refs[lanes + 2 :]
-    out, sums, leave, leave_more = refs[:4]
-    banks = refs[4:]
-    blocks, width, _ = out.shape
-    assemble(lane, lanes, shares, field)
-    pack(lists, field, out, width)
-    go = pltpu.make_async_copy(out, sent.at[:, :width, :], leave)
-    go.start()
+def early_field_kernel(lanes, lane, code_a, sizes_a, code_b, sizes_b, mass, home, one, three, out, field, *banks):
+    for s, share in ((0, home), (1, one), (3, three)):
+        place(lane, lanes, s, share, field)
     clear(banks)
     far_rows(
-        ((rows_a, mass_a, size_a), (rows_b, mass_b, size_b)),
-        lambda given: field[pl.ds(source_of(given), 1), :],
-        target_of,
+        0,
+        ((code_a, sizes_a), (code_b, sizes_b)),
+        mass,
+        lambda given: field[pl.ds(far_source(given), 1), :],
+        far_slot,
         banks,
     )
     total = banks[0][...]
     for a in banks[1:]:
         total = total + a[...]
+    out[...] = total
+
+
+def field_kernel(lanes, lane, code_a, sizes_a, code_b, sizes_b, mass, lists, part, *refs):
+    shares, (kept, sent), refs = refs[:lanes], refs[lanes : lanes + 2], refs[lanes + 2 :]
+    field, out, sums, leave_field, leave, leave_sums = refs[:6]
+    banks = refs[6:]
+    blocks, width, _ = out.shape
+    assemble(lane, lanes, shares, field)
+    keep = pltpu.make_async_copy(field, kept, leave_field)
+    keep.start()
+    banks[0][...] = part[...]
+    clear(banks[1:])
+    far_rows(
+        1,
+        ((code_a, sizes_a), (code_b, sizes_b)),
+        mass,
+        lambda given: field[pl.ds(far_source(given), 1), :],
+        far_slot,
+        banks,
+    )
     for c in range(blocks):
-        sums[c] = total[c * width : (c + 1) * width]
-    more = pltpu.make_async_copy(sums, sent.at[:, width:, :], leave_more)
+        at = slice(c * width, (c + 1) * width)
+        total = banks[0][at, :]
+        for a in banks[1:]:
+            total = total + a[at, :]
+        sums[c] = total
+    more = pltpu.make_async_copy(sums, sent.at[:, width:, :], leave_sums)
     more.start()
+    pack(lists, field, out, width)
+    go = pltpu.make_async_copy(out, sent.at[:, :width, :], leave)
+    go.start()
+    keep.wait()
+    more.wait()
     go.wait()
-    more.wait()
-
-
-def near_kernel(count, order, heavy, field, out, *banks):
+
+
+def near_kernel(count, order, heavy, kept, out, field, come, *banks):
+    bring = pltpu.make_async_copy(kept, field, come)
+    bring.start()
     clear(banks)
+    bring.wait()
 
     def step(i, _):
         for u in range(0, UNROLL, BANKS):
@@ -330,47 +403,63 @@
     out[...] = total
 
 
-def share_block(q, listed, far, ret_both, hot, out):
-    share = out.shape[0]
+def listed_rows(q, share, listed, ret_both, hot):
     for k in range(listed.shape[0]):
         hot[:, k * LANES : (k + 1) * LANES] = one_hot(listed[k : k + 1, :], share, q * share).astype(jnp.bfloat16)
-    got = halves(jnp.dot(hot[...], ret_both[...], preferred_element_type=jnp.float32))
-    out[...] = far[pl.ds(pl.multiple_of(q * share, share), share), :] + got
-
-
-def first_join_kernel(
-    shift, lanes, lane, rows_a, mass_a, size_a, rows_b, mass_b, size_b, listed, near, arrived, *refs
-):
-    out, far, ret_both, hot, halo, ret, come_halo, come_ret = refs[:8]
-    banks = refs[8:]
-    blocks, width, _ = halo.shape
-    first = pltpu.make_async_copy(arrived.at[:, :width, :], halo, come_halo)
+    return halves(jnp.dot(hot[...], ret_both[...], preferred_element_type=jnp.float32))
+
+
+def late_join_kernel(lanes, lane, code_a, sizes_a, code_b, sizes_b, mass, listed, near, arrived, *refs):
+    out, halo, ret_both, hot, ret, come_halo, come_ret = refs[:7]
+    banks = refs[7:]
+    blocks, width, _ = ret.shape
+    share = out.shape[0]
+    first = pltpu.make_async_copy(arrived.at[:, :width, :], halo.at[:blocks], come_halo)
     second = pltpu.make_async_copy(arrived.at[:, width:, :], ret, come_ret)
     first.start()
     second.start()
+    halo[blocks] = jnp.zeros((width, LANES), jnp.float32)
     clear(banks)
+    q = lax.rem(lane[0] + 2, lanes)
     first.wait()
-    flat = halo.reshape(blocks * width, LANES)
+    flat = halo.reshape((blocks + 1) * width, LANES)
     far_rows(
-        ((rows_a, mass_a, size_a), (rows_b, mass_b, size_b)),
-        lambda given: flat[pl.ds(target_of(given), 1), :],
-        source_of,
+        1,
+        ((code_a, sizes_a), (code_b, sizes_b)),
+        mass,
+        lambda given: flat[pl.ds(far_slot(given), 1), :],
+        lambda given: far_source(given) & (share - 1),
         banks,
     )
-    total = near[...]
-    for a in banks:
-        total = total + a[...]
-    far[...] = total
     second.wait()
     for c in range(blocks):
         put_split(ret_both, slice(c * width, (c + 1) * width), ret[c])
-    share_block(lax.rem(lane[0] + shift, lanes), listed, far, ret_both, hot, out)
-
-
-def join_kernel(shifts, lanes, lane, listed, far, ret_both, *refs):
-    outs, hot = refs[:-1], refs[-1]
-    for s, out in zip(shifts, outs):
-        share_block(lax.rem(lane[0] + s, lanes), listed, far, ret_both, hot, out)
+    total = near[pl.ds(pl.multiple_of(q * share, share), share), :]
+    for a in banks:
+        total = total + a[...]
+    out[...] = total + listed_rows(q, share, listed, ret_both, hot)
+
+
+def join_kernel(lanes, lane, code_a, sizes_a, code_b, sizes_b, mass, listed, near, halo, ret_both, *refs):
+    outs, hot, banks = refs[:3], refs[3], refs[4:]
+    share = outs[0].shape[0]
+    clear(banks)
+    flat = halo.reshape(halo.shape[0] * halo.shape[1], LANES)
+    far_rows(
+        0,
+        ((code_a, sizes_a), (code_b, sizes_b)),
+        mass,
+        lambda given: flat[pl.ds(far_slot(given), 1), :],
+        far_source,
+        banks,
+    )
+    for s, out in zip((1, 3, 0), outs):
+        q = lax.rem(lane[0] + s, lanes)
+        at = pl.ds(pl.multiple_of(q * share, share), share)
+        total = near[at, :]
+        for a in banks:
+            total = total + a[at, :]
+        out[...] = total + listed_rows(q, share, listed, ret_both, hot)
 
 
 def solution_kernel(lane, lists, *refs):
@@ -424,19 +513,21 @@
         out[k : k + 1, :] = jnp.where(alive > 0, total * (alive / LANES), 0.0)
 
 
-def passed_round(blocks, lanes, sign):
-    return [blocks[0]] + [
-        lax.ppermute(blocks[s], "edg", [(i, (i + sign * s) % lanes) for i in range(lanes)]) for s in (2, 1, 3)
-    ]
+def moved_by(x, shift, lanes):
+    return lax.ppermute(x, "edg", [(i, (i + shift) % lanes) for i in range(lanes)])
+
+
+def passed_round(blocks, lanes):
+    return [blocks[0]] + [moved_by(blocks[s], s, lanes) for s in (2, 1, 3)]
 
 
 def summed(blocks, lanes):
-    home, two, one, three = passed_round(blocks, lanes, 1)
+    home, two, one, three = passed_round(blocks, lanes)
     return (home + one) + (two + three)
 
 
 def to_all(mine, lanes):
-    home, two, one, three = passed_round([mine] * lanes, lanes, 1)
+    home, two, one, three = passed_round([mine] * lanes, lanes)
     return [home, one, two, three]
 
 
@@ -469,28 +560,30 @@
 
     outgoing = call(
         functools.partial(halo_side_kernel, rows, slots, width),
-        [((blocks, width + 8, LANES), f32, ANY)],
+        [((blocks, width + 8, LANES), f32, HBM)],
         [VMEM] * 3,
         [pltpu.VMEM((edges, 2 * LANES), bf16), pltpu.VMEM((8 * width, edges), bf16)]
-        + [pltpu.VMEM((blocks, width + 8, LANES), f32), pltpu.SemaphoreType.DMA],
+        + [pltpu.VMEM((blocks, width + 8, LANES), f32), pltpu.SemaphoreType.DMA((slots // (8 * width),))],
         "halo_side",
         flops=2 * slots * edges * 2 * LANES,
     )(terms, target_rows, weight_rows)[0]
     returned = across(outgoing)
     own, own_degree = call(
         own_side_kernel,
-        [((rows, LANES), f32, VMEM), ((rows // LANES, LANES), f32, VMEM)],
+        [((rows, LANES), f32, HBM), ((rows // LANES, LANES), f32, VMEM)],
         [VMEM] * 4,
-        [pltpu.VMEM((edges, 2 * LANES), bf16), pltpu.VMEM((256, edges), bf16)],
+        [pltpu.VMEM((edges, 2 * LANES), bf16), pltpu.VMEM((256, edges), bf16)]
+        + [pltpu.VMEM((rows, LANES), f32), pltpu.SemaphoreType.DMA((rows // 256,))],
         "own_side",
         flops=2 * rows * edges * 2 * LANES,
     )(terms, source_rows, target_rows, weight_rows)
     sides = call(
         side_join_kernel,
         [((share + 8, LANES), f32, VMEM)] * lanes,
-        [SMEM, ANY] + [VMEM] * 4,
+        [SMEM, HBM, VMEM, VMEM, HBM, VMEM],
         [pltpu.VMEM((rows, LANES), f32), pltpu.VMEM((slots, 2 * LANES), bf16), pltpu.VMEM((256, slots), bf16)]
-        + [pltpu.VMEM((blocks, width + 8, LANES), f32), pltpu.SemaphoreType.DMA],
+        + [pltpu.VMEM((blocks, width + 8, LANES), f32)]
+        + [pltpu.SemaphoreType.DMA] * 2,
         "side_join",
         flops=2 * rows * slots * 2 * LANES,
     )(lane, returned, listed, padded, own, own_degree)
@@ -500,26 +593,27 @@
     near_order = src_local | (jnp.where(away, 0, dst_index) << 12)
     gap_order = src_local | (jnp.minimum(dst_index, rows) << 12)
     gap_slot = jnp.where(away, dst_index - rows, slots)
-    far_order = jnp.where(away, src_local | ((dst_index - rows) << 12), -1)
-
-    def far_list(start, stop, count):
-        room = stop - start + LANES
+    quarter = edges // QUARTERS
+    number = jnp.arange(edges, dtype=i32) & (quarter - 1)
+    far_order = (jnp.where(away, dst_index - rows, 2047) << 21) | (src_local << 10) | number
+
+    def far_list(first, count):
+        room = quarter + LANES // 4
         return call(
-            functools.partial(far_list_kernel, start, stop),
-            [((room,), i32, SMEM), ((room,), f32, SMEM), ((1,), i32, SMEM)],
+            functools.partial(far_list_kernel, first, room),
+            [((4 * room,), i32, SMEM), ((4,), i32, SMEM)],
             [SMEM] * 3,
             [],
             "far_list",
             moved=2**25,
-        )(count, far_order, weight)
-
-    middle = edges // 2
-    list_a = far_list(0, middle, begin)
+        )(count, lane, far_order)
+
+    code_a, sizes_a = far_list(0, begin)
     side = summed(sides, lanes)
-    side, size_a = lax.optimization_barrier((side, list_a[2]))
+    side, sizes_a = lax.optimization_barrier((side, sizes_a))
     later, side = lax.optimization_barrier((edge_count, side))
-    list_b = far_list(middle, edges, later)
-    far = (list_a[0], list_a[1], size_a, *list_b)
+    code_b, sizes_b = far_list(2, later)
+    far = (code_a, sizes_a, code_b, sizes_b, weight)
     right_share = side[:share]
     degree_share = side[share : share + share // LANES].reshape(share)
     ground_share = lax.dynamic_slice_in_dim(ground, lane[0] * share, share)
@@ -531,56 +625,60 @@
     direction = first * inverse * right_share
     solution_share = direction
     for keep, push in pairs:
+        shares = to_all(direction, lanes)
+        early = call(
+            functools.partial(early_field_kernel, lanes),
+            [((slots + 8, LANES), f32, VMEM)],
+            [SMEM] * 6 + [VMEM] * 3,
+            [pltpu.VMEM((rows, LANES), f32)] + [pltpu.VMEM((slots + 8, LANES), f32)] * BANKS,
+            "early_field",
+            moved=2**25,
+        )(lane, *far, shares[0], shares[1], shares[3])[0]
         field, message = call(
-            field_kernel,
-            [((rows, LANES), f32, VMEM), ((blocks, 2 * width, LANES), f32, ANY)],
-            [SMEM] * 8 + [VMEM] * lanes,
-            [pltpu.VMEM((blocks, width, LANES), f32)] * 2
-            + [pltpu.SemaphoreType.DMA] * 2
-            + [pltpu.VMEM((slots, LANES), f32)] * BANKS,
+            functools.partial(field_kernel, lanes),
+            [((rows, LANES), f32, HBM), ((blocks, 2 * width, LANES), f32, HBM)],
+            [SMEM] * 7 + [VMEM] * (1 + lanes),
+            [pltpu.VMEM((rows, LANES), f32)]
+            + [pltpu.VMEM((blocks, width, LANES), f32)] * 2
+            + [pltpu.SemaphoreType.DMA] * 3
+            + [pltpu.VMEM((slots + 8, LANES), f32)] * 2,
             "field",
-        )(lane, *far, lists, *to_all(direction, lanes))
+        )(lane, *far, lists, early, *shares)
         arrived = across(message)
         near = call(
             near_kernel,
             [((rows, LANES), f32, VMEM)],
-            [SMEM] * 3 + [VMEM],
-            [pltpu.VMEM((rows, LANES), f32)] * BANKS,
+            [SMEM] * 3 + [HBM],
+            [pltpu.VMEM((rows, LANES), f32), pltpu.SemaphoreType.DMA] + [pltpu.VMEM((rows, LANES), f32)] * BANKS,
             "near",
             moved=2**25,
         )(edge_count, near_order, near_weight, field)[0]
-        two, sums, ret_both = call(
-            functools.partial(first_join_kernel, 2, lanes),
-            [((share, LANES), f32, VMEM), ((rows, LANES), f32, VMEM), ((slots, 2 * LANES), bf16, VMEM)],
-            [SMEM] * 7 + [VMEM, VMEM, ANY],
-            [pltpu.VMEM((share, slots), bf16)]
-            + [pltpu.VMEM((blocks, width, LANES), f32)] * 2
+        two, halo, ret_both = call(
+            functools.partial(late_join_kernel, lanes),
+            [((share, LANES), f32, VMEM), ((blocks + 1, width, LANES), f32, VMEM), ((slots, 2 * LANES), bf16, VMEM)],
+            [SMEM] * 6 + [VMEM, VMEM, HBM],
+            [pltpu.VMEM((share, slots), bf16), pltpu.VMEM((blocks, width, LANES), f32)]
             + [pltpu.SemaphoreType.DMA] * 2
-            + [pltpu.VMEM((rows, LANES), f32)] * BANKS,
-            "join_two",
+            + [pltpu.VMEM((share, LANES), f32)] * BANKS,
+            "late_join",
         )(lane, *far, listed, near, arrived)
-        one, three = call(
-            functools.partial(join_kernel, (1, 3), lanes),
-            [((share, LANES), f32, VMEM)] * 2,
-            [SMEM] + [VMEM] * 3,
-            [pltpu.VMEM((share, slots), bf16)],
-            "join_one_three",
-        )(lane, listed, sums, ret_both)
-        home = call(
-            functools.partial(join_kernel, (0,), lanes),
-            [((share, LANES), f32, VMEM)],
-            [SMEM] + [VMEM] * 3,
-            [pltpu.VMEM((share, slots), bf16)],
-            "join_home",
+        one, three, home = call(
+            functools.partial(join_kernel, lanes),
+            [((share, LANES), f32, VMEM)] * 3,
+            [SMEM] * 6 + [VMEM] * 4,
+            [pltpu.VMEM((share, slots), bf16)] + [pltpu.VMEM((rows, LANES), f32)] * BANKS,
+            "join",
             moved=2**25,
-        )(lane, listed, sums, ret_both)[0]
-        flows = summed((home, one, two, three), lanes)
+        )(lane, *far, listed, near, halo, ret_both)
+        two = moved_by(two, 2, lanes)
+        two, one, three = lax.optimization_barrier((two, one, three))
+        flows = (home + two) + (moved_by(one, 1, lanes) + moved_by(three, 3, lanes))
         residual = residual - (diagonal * direction - flows)
         direction = keep * direction + push * inverse * residual
         solution_share = solution_share + direction
     field, message = call(
         solution_kernel,
-        [((rows, LANES), f32, VMEM), ((blocks, width, LANES), f32, ANY)],
+        [((rows, LANES), f32, VMEM), ((blocks, width, LANES), f32, HBM)],
         [SMEM] * 2 + [VMEM] * lanes,
         [pltpu.VMEM((blocks, width, LANES), f32), pltpu.SemaphoreType.DMA],
         "solution_rows",
@@ -597,7 +695,7 @@
     resistance = call(
         far_gap_kernel,
         [((groups, LANES), f32, VMEM)],
-        [SMEM] * 2 + [VMEM, ANY, VMEM],
+        [SMEM] * 2 + [VMEM, HBM, VMEM],
         [pltpu.VMEM((blocks + 1, width, LANES), f32), pltpu.VMEM((edges, LANES), f32), pltpu.SemaphoreType.DMA],
         "far_gap",
     )(edge_count, gap_slot, gaps, halo, live_rows)[0]

time: 257 us -> 259 us (level)
  Pallas kernels: 66.4 us -> 78.5 us
  waiting for transfers between devices: 95.1 us -> 83.7 us
  starting transfers between devices: 78.8 us -> 85.8 us
  local copies, waits for them, and re-layouts: 8.93 us -> 5.07 us
    all_to_all x4, starting transfers between devices: 48.1 us -> 59.9 us  [across(): return lax.all_to_all(x, 'vtx', split_axis=0, concat_axis=0, tiled=True)]
    pallas_call x13, Pallas kernels: 48.7 us -> 58.8 us  [the longest x1 12.1 us: local(): call(own_side_kernel, [((rows, LANES), f32, HBM), ((rows // LANES, LANES)...]
    ppermute x18, waiting for transfers between devices: 45.5 us -> 37.3 us  [moved_by(): lax.ppermute(x, 'edg', [(i, (i + shift) % lanes) for i in range(lanes)])]
    ppermute x18, starting transfers between devices: 30.7 us -> 25.9 us  [moved_by(): lax.ppermute(x, 'edg', [(i, (i + shift) % lanes) for i in range(lanes)])]
    unnamed x24 -> x20, local copies, waits for them, and re-layouts: 8.77 us -> 4.92 us
    all_to_all x4, waiting for transfers between devices: 49.6 us -> 46.4 us  [across(): return lax.all_to_all(x, 'vtx', split_axis=0, concat_axis=0, tiled=True)]
  transfers between devices with their start and end apart: 22 -> 22, of which waited for: 18 -> 14; matrix products, arithmetic and copies ran while one was open for 0% -> 0% of each run, Pallas kernels for 11% -> 18%
where the time goes in v4:
time: 259 us; the launch traced here: 260 us
  starting transfers between devices  85.8 us (33%)
  waiting for transfers between devices  83.7 us (32%)
  Pallas kernels  78.5 us (30%)
  local copies, waits for them, and re-layouts  5.07 us (2%)
  other arithmetic  4.81 us (2%)
    all_to_all x4, starting transfers between devices, across(): return lax.all_to_all(x, 'vtx', split_axis=0, concat_axis=0, tiled=True)  59.9 us
    all_to_all x4, waiting for transfers between devices, across(): return lax.all_to_all(x, 'vtx', split_axis=0, concat_axis=0, tiled=True)  46.4 us
    ppermute x18, waiting for transfers between devices, moved_by(): lax.ppermute(x, 'edg', [(i, (i + shift) % lanes) for i in range(lanes)])  37.3 us
    ppermute x18, starting transfers between devices, moved_by(): lax.ppermute(x, 'edg', [(i, (i + shift) % lanes) for i in range(lanes)])  25.9 us
    pallas_call x1, Pallas kernels, local(): call(own_side_kernel, [((rows, LANES), f32, HBM), ((rows // LANES, LANES)...  12.1 us
    pallas_call x2, Pallas kernels, local(): call(near_kernel, [((rows, LANES), f32, VMEM)], [SMEM] * 3 + [HBM], [pltp...  9.35 us
    pallas_call x2, Pallas kernels, far_list(): call(functools.partial(far_list_kernel, first, room), [((4 * room,), i32,...  8.93 us
    pallas_call x2, Pallas kernels, local(): call(functools.partial(field_kernel, lanes), [((rows, LANES), f32, HBM),...  8.87 us
  transfers between devices with their start and end apart: 22, of which 14 were waited for; matrix products, arithmetic and copies ran while one was open for 0% of the time, Pallas kernels for 18%

profile of v4, /device:TPU:1, one launch (start us, length us, event | category | flops | bytes accessed | tf_op | source)
XLA Modules:
  0.0 259.7 jit_solution(4266673269173196484)
XLA Ops:
  4.5 6.0 %halo_side.1 = f32[32,56,128]{2,1,0:T(8,128)} custom-call(f32[4096,128]{1,0:T(8,128)S(1)} %convert_multiply_fusion.terms, s32[32,128]{1,0:T(8,128)S(1)} %bitcast.14, f32[32,128]{1,0:T(8,128)S(1)} %bitcast.12), custom_call_target="tpu_custom_call" | custom-call | flops 3221225472 | bytes 4194304 | tf_op jit(solution)/shard_map/halo_side/pallas_call | solution.py:561
  10.5 8.6 %all-to-all-start = ((f32[32,56,128]{2,1,0:T(8,128)}), f32[32,56,128]{2,1,0:T(8,128)S(1)}, u32[]{:S(2)}, u32[]{:S(2)}) async-start(f32[32,56,128]{2,1,0:T(8,128)} %halo_side.1), calls=%async_computation | async-start | bytes 1835008 | tf_op jit(solution)/shard_map/all_to_all | solution.py:535
  19.3 12.1 %own_side.1 = (f32[2048,128]{1,0:T(8,128)}, f32[16,128]{1,0:T(8,128)S(1)}) custom-call(f32[4096,128]{1,0:T(8,128)S(1)} %convert_multiply_fusion.terms, s32[32,128]{1,0:T(8,128)S(1)} %bitcast.16, s32[32,128]{1,0:T(8,128)S(1)} %bitcast.15, f32[32,128]{1,0:T(8,128)S(1)} %bitcast.13), custom_call_target="tpu_custom_call" | custom-call | flops 4294967296 | bytes 4194304 | tf_op jit(solution)/shard_map/own_side/pallas_call | solution.py:571
  36.1 4.0 %side_join.1 = (f32[520,128]{1,0:T(8,128)S(1)}, f32[520,128]{1,0:T(8,128)S(1)}, f32[520,128]{1,0:T(8,128)S(1)}, f32[520,128]{1,0:T(8,128)S(1)}) custom-call(s32[1]{0:T(128)} %bitcast.lane, f32[32,56,128]{2,1,0:T(8,128)S(1)} %all-to-all-done.returned, s32[12,128]{1,0:T(8,128)S(1)} %reshape_reshape_squeeze.3.listed, s32[32,128]{1,0:T(8,128)S(1)} %pad.4.padded, ...), custom_call_target="tpu_custom_call" | custom-call | flops 1610612736 | bytes 4194304 | tf_op jit(solution)/shard_map/side_join/pallas_call | solution.py:580
  45.9 7.2 %far_list.2 = (s32[4224]{0:T(1024)S(1)}, s32[4]{0:T(128)S(1)}) custom-call(s32[1]{0:T(128)} %copy.9.count, s32[1]{0:T(128)} %bitcast.lane, s32[4096]{0:T(1024)S(1)} %get-tuple-element.95.order), custom_call_target="tpu_custom_call" | custom-call | bytes 33554432 | tf_op jit(solution)/shard_map/far_list/pallas_call | solution.py:602
  53.1 3.9 %collective-permute-done.1 = f32[520,128]{1,0:T(8,128)S(1)} collective-permute-done((f32[520,128]{1,0:T(8,128)S(1)}, f32[520,128]{1,0:T(8,128)S(1)}, u32[]{:S(2)}, u32[]{:S(2)}) %collective-permute-start.1) | collective-permute-done | bytes 266272 | tf_op jit(solution)/shard_map/ppermute | solution.py:517
  67.3 6.0 %collective-permute-done.5.refs_2_ = f32[512,128]{1,0:T(8,128)S(1)} collective-permute-done((f32[512,128]{1,0:T(8,128)S(1)}, f32[512,128]{1,0:T(8,128)S(1)}, u32[]{:S(2)}, u32[]{:S(2)}) %collective-permute-start.5) | collective-permute-done | bytes 262176 | tf_op jit(solution)/shard_map/ppermute | solution.py:517
  73.3 4.4 %field.2 = (f32[2048,128]{1,0:T(8,128)}, f32[32,96,128]{2,1,0:T(8,128)}) custom-call(s32[1]{0:T(128)} %bitcast.lane, s32[4224]{0:T(1024)S(1)} %get-tuple-element.59.code_a, s32[4]{0:T(128)S(1)} %get-tuple-element.60.sizes_a, s32[4224]{0:T(1024)S(1)} %get-tuple-element.62.code_b, s32[4]{0:T(128)S(1)} %get-tuple-element.63.sizes_b, ...), custom_call_target="tpu_custom_call" | custom-call | bytes 4194304 | tf_op jit(solution)/shard_map/field/pallas_call | solution.py:637
  77.8 14.0 %all-to-all-start.1 = ((f32[32,96,128]{2,1,0:T(8,128)}), f32[32,96,128]{2,1,0:T(8,128)S(1)}, u32[]{:S(2)}, u32[]{:S(2)}) async-start(f32[32,96,128]{2,1,0:T(8,128)} %get-tuple-element.65), calls=%async_computation.1 | async-start | bytes 3145728 | tf_op jit(solution)/shard_map/all_to_all | solution.py:535
  93.1 4.7 %near.2 = f32[2048,128]{1,0:T(8,128)S(1)} custom-call(s32[1]{0:T(128)} %copy.9.count, s32[4096]{0:T(1024)S(1)} %get-tuple-element.96.order, f32[4096]{0:T(1024)S(1)} %copy-done.5, f32[2048,128]{1,0:T(8,128)S(1)} %copy-done.1), custom_call_target="tpu_custom_call" | custom-call | bytes 33554432 | tf_op jit(solution)/shard_map/near/pallas_call | solution.py:648
  97.8 16.3 %all-to-all-done.1.arrived = f32[32,96,128]{2,1,0:T(8,128)S(1)} async-done(((f32[32,96,128]{2,1,0:T(8,128)}), f32[32,96,128]{2,1,0:T(8,128)S(1)}, u32[]{:S(2)}, u32[]{:S(2)}) %all-to-all-start.1) | async-done | bytes 1572896 | tf_op jit(solution)/shard_map/all_to_all | solution.py:535
  120.3 4.4 %join.2 = (f32[512,128]{1,0:T(8,128)S(1)}, f32[512,128]{1,0:T(8,128)S(1)}, f32[512,128]{1,0:T(8,128)S(1)}) custom-call(s32[1]{0:T(128)} %bitcast.lane, s32[4224]{0:T(1024)S(1)} %get-tuple-element.59.code_a, s32[4]{0:T(128)S(1)} %get-tuple-element.60.sizes_a, s32[4224]{0:T(1024)S(1)} %get-tuple-element.62.code_b, s32[4]{0:T(128)S(1)} %get-tuple-element.63.sizes_b, ...), custom_call_target="tpu_custom_call" | custom-call | bytes 33554432 | tf_op jit(solution)/shard_map/join/pallas_call | solution.py:665
  127.5 3.8 %collective-permute-done.7 = f32[512,128]{1,0:T(8,128)S(1)} collective-permute-done((f32[512,128]{1,0:T(8,128)S(1)}, f32[512,128]{1,0:T(8,128)S(1)}, u32[]{:S(2)}, u32[]{:S(2)}) %collective-permute-start.7) | collective-permute-done | bytes 262176 | tf_op jit(solution)/shard_map/ppermute | solution.py:517
  135.6 7.0 %collective-permute-done.10.three.refs_3_ = f32[512,128]{1,0:T(8,128)S(1)} collective-permute-done((f32[512,128]{1,0:T(8,128)S(1)}, f32[512,128]{1,0:T(8,128)S(1)}, u32[]{:S(2)}, u32[]{:S(2)}) %collective-permute-start.10) | collective-permute-done | bytes 262176 | tf_op jit(solution)/shard_map/ppermute | solution.py:517
  146.6 4.4 %field.3 = (f32[2048,128]{1,0:T(8,128)}, f32[32,96,128]{2,1,0:T(8,128)}) custom-call(s32[1]{0:T(128)} %bitcast.lane, s32[4224]{0:T(1024)S(1)} %get-tuple-element.59.code_a, s32[4]{0:T(128)S(1)} %get-tuple-element.60.sizes_a, s32[4224]{0:T(1024)S(1)} %get-tuple-element.62.code_b, s32[4]{0:T(128)S(1)} %get-tuple-element.63.sizes_b, ...), custom_call_target="tpu_custom_call" | custom-call | bytes 4194304 | tf_op jit(solution)/shard_map/field/pallas_call | solution.py:637
  151.0 22.0 %all-to-all-start.2 = ((f32[32,96,128]{2,1,0:T(8,128)}), f32[32,96,128]{2,1,0:T(8,128)S(1)}, u32[]{:S(2)}, u32[]{:S(2)}) async-start(f32[32,96,128]{2,1,0:T(8,128)} %get-tuple-element.76), calls=%async_computation.2 | async-start | bytes 3145728 | tf_op jit(solution)/shard_map/all_to_all | solution.py:535
  174.2 4.7 %near.3 = f32[2048,128]{1,0:T(8,128)S(1)} custom-call(s32[1]{0:T(128)} %copy.9.count, s32[4096]{0:T(1024)S(1)} %get-tuple-element.96.order, f32[4096]{0:T(1024)S(1)} %copy-done.5, f32[2048,128]{1,0:T(8,128)S(1)} %copy-done), custom_call_target="tpu_custom_call" | custom-call | bytes 33554432 | tf_op jit(solution)/shard_map/near/pallas_call | solution.py:648
  178.9 16.4 %all-to-all-done.2.arrived = f32[32,96,128]{2,1,0:T(8,128)S(1)} async-done(((f32[32,96,128]{2,1,0:T(8,128)}), f32[32,96,128]{2,1,0:T(8,128)S(1)}, u32[]{:S(2)}, u32[]{:S(2)}) %all-to-all-start.2) | async-done | bytes 1572896 | tf_op jit(solution)/shard_map/all_to_all | solution.py:535
  198.0 4.4 %join.3 = (f32[512,128]{1,0:T(8,128)S(1)}, f32[512,128]{1,0:T(8,128)S(1)}, f32[512,128]{1,0:T(8,128)S(1)}) custom-call(s32[1]{0:T(128)} %bitcast.lane, s32[4224]{0:T(1024)S(1)} %get-tuple-element.59.code_a, s32[4]{0:T(128)S(1)} %get-tuple-element.60.sizes_a, s32[4224]{0:T(1024)S(1)} %get-tuple-element.62.code_b, s32[4]{0:T(128)S(1)} %get-tuple-element.63.sizes_b, ...), custom_call_target="tpu_custom_call" | custom-call | bytes 33554432 | tf_op jit(solution)/shard_map/join/pallas_call | solution.py:665
  207.4 4.5 %collective-permute-done.13 = f32[512,128]{1,0:T(8,128)S(1)} collective-permute-done((f32[512,128]{1,0:T(8,128)S(1)}, f32[512,128]{1,0:T(8,128)S(1)}, u32[]{:S(2)}, u32[]{:S(2)}) %collective-permute-start.13) | collective-permute-done | bytes 262176 | tf_op jit(solution)/shard_map/ppermute | solution.py:517
  215.5 7.7 %collective-permute-done.15.refs_1_ = f32[512,128]{1,0:T(8,128)S(1)} collective-permute-done((f32[512,128]{1,0:T(8,128)S(1)}, f32[512,128]{1,0:T(8,128)S(1)}, u32[]{:S(2)}, u32[]{:S(2)}) %collective-permute-start.15) | collective-permute-done | bytes 262176 | tf_op jit(solution)/shard_map/ppermute | solution.py:517
  223.1 3.9 %solution_rows.1 = (f32[2048,128]{1,0:T(8,128)}, f32[32,48,128]{2,1,0:T(8,128)}) custom-call(s32[1]{0:T(128)} %bitcast.lane, s32[1536]{0:T(1024)S(1)} %reshape_squeeze.3.lists, f32[512,128]{1,0:T(8,128)S(1)} %add_add_fusion.1.refs_0_, f32[512,128]{1,0:T(8,128)S(1)} %collective-permute-done.15.refs_1_, f32[512,128]{1,0:T(8,128)S(1)} %collective-permute-done.16.refs_2_, ...), custom_call_target="tpu_custom_call" | custom-call | bytes 4194304 | tf_op jit(solution)/shard_map/solution_rows/pallas_call | solution.py:679
  227.1 15.3 %all-to-all-start.3 = ((f32[32,48,128]{2,1,0:T(8,128)}), f32[32,48,128]{2,1,0:T(8,128)S(1)}, u32[]{:S(2)}, u32[]{:S(2)}) async-start(f32[32,48,128]{2,1,0:T(8,128)} %get-tuple-element.87), calls=%async_computation.3 | async-start | bytes 1572864 | tf_op jit(solution)/shard_map/all_to_all | solution.py:535
  246.5 10.1 %all-to-all-done.3.arrived = f32[32,48,128]{2,1,0:T(8,128)S(1)} async-done(((f32[32,48,128]{2,1,0:T(8,128)}), f32[32,48,128]{2,1,0:T(8,128)S(1)}, u32[]{:S(2)}, u32[]{:S(2)}) %all-to-all-start.3) | async-done | bytes 786464 | tf_op jit(solution)/shard_map/all_to_all | solution.py:535
  (71 shorter events, 62.1 us)
Async XLA Ops:
  10.5 24.4 %all-to-all-start = ((f32[32,56,128]{2,1,0:T(8,128)}), f32[32,56,128]{2,1,0:T(8,128)S(1)}, u32[]{:S(2)}, u32[]{:S(2)}) async-start(f32[32,56,128]{2,1,0:T(8,128)} %halo_side.1), calls=%async_computation | async-start | bytes 1835008 | tf_op jit(solution)/shard_map/all_to_all | solution.py:535
  40.1 13.0 %collective-permute-start = (f32[520,128]{1,0:T(8,128)S(1)}, f32[520,128]{1,0:T(8,128)S(1)}, u32[]{:S(2)}, u32[]{:S(2)}) collective-permute-start(f32[520,128]{1,0:T(8,128)S(1)} %get-tuple-element.52), channel_id=1, source_target_pairs={{0,1},{1,2},{2,3},{3,0},{4,5},{5,6},{6,7},{7,4},{8,9},{9,10},{10,1... | collective-permute-start | bytes 798728 | tf_op jit(solution)/shard_map/ppermute | solution.py:517
  41.8 15.1 %collective-permute-start.1 = (f32[520,128]{1,0:T(8,128)S(1)}, f32[520,128]{1,0:T(8,128)S(1)}, u32[]{:S(2)}, u32[]{:S(2)}) collective-permute-start(f32[520,128]{1,0:T(8,128)S(1)} %get-tuple-element.53), channel_id=1, source_target_pairs={{0,2},{1,3},{2,0},{3,1},{4,6},{5,7},{6,4},{7,5},{8,10},{9,11},{10,... | collective-permute-start | bytes 798728 | tf_op jit(solution)/shard_map/ppermute | solution.py:517
  45.1 11.8 %collective-permute-start.2 = (f32[520,128]{1,0:T(8,128)S(1)}, f32[520,128]{1,0:T(8,128)S(1)}, u32[]{:S(2)}, u32[]{:S(2)}) collective-permute-start(f32[520,128]{1,0:T(8,128)S(1)} %get-tuple-element.54), channel_id=1, source_target_pairs={{0,3},{1,0},{2,1},{3,2},{4,7},{5,4},{6,5},{7,6},{8,11},{9,8},{10,9... | collective-permute-start | bytes 798728 | tf_op jit(solution)/shard_map/ppermute | solution.py:517
  57.9 6.5 %collective-permute-start.3 = (f32[512,128]{1,0:T(8,128)S(1)}, f32[512,128]{1,0:T(8,128)S(1)}, u32[]{:S(2)}, u32[]{:S(2)}) collective-permute-start(f32[512,128]{1,0:T(8,128)S(1)} %slice_multiply_fusion.home.refs_0_), channel_id=1, source_target_pairs={{0,1},{1,2},{2,3},{3,0},{4,5},{5,6},{6,7},{7,4},{8,9},{9,10},{10,1... | collective-permute-start | bytes 786440 | tf_op jit(solution)/shard_map/ppermute | solution.py:517
  59.3 5.2 %collective-permute-start.4 = (f32[512,128]{1,0:T(8,128)S(1)}, f32[512,128]{1,0:T(8,128)S(1)}, u32[]{:S(2)}, u32[]{:S(2)}) collective-permute-start(f32[512,128]{1,0:T(8,128)S(1)} %slice_multiply_fusion.home.refs_0_), channel_id=1, source_target_pairs={{0,3},{1,0},{2,1},{3,2},{4,7},{5,4},{6,5},{7,6},{8,11},{9,8},{10,9... | collective-permute-start | bytes 786440 | tf_op jit(solution)/shard_map/ppermute | solution.py:517
  60.7 12.6 %collective-permute-start.5 = (f32[512,128]{1,0:T(8,128)S(1)}, f32[512,128]{1,0:T(8,128)S(1)}, u32[]{:S(2)}, u32[]{:S(2)}) collective-permute-start(f32[512,128]{1,0:T(8,128)S(1)} %slice_multiply_fusion.home.refs_0_), channel_id=1, source_target_pairs={{0,2},{1,3},{2,0},{3,1},{4,6},{5,7},{6,4},{7,5},{8,10},{9,11},{10,... | collective-permute-start | bytes 786440 | tf_op jit(solution)/shard_map/ppermute | solution.py:517
  67.3 24.5 %copy-start.5 = (f32[4096]{0:T(1024)S(1)}, f32[4096]{0:T(1024)}, u32[]{:S(2)}) copy-start(f32[4096]{0:T(1024)} %get-tuple-element.92.heavy) | copy-start | bytes 49156
  77.8 36.3 %copy-start.4 = (s32[12,128]{1,0:T(8,128)S(1)}, s32[12,128]{1,0:T(8,128)}, u32[]{:S(2)}) copy-start(s32[12,128]{1,0:T(8,128)} %copy-done.3) | copy-start | bytes 18436
  77.8 36.3 %all-to-all-start.1 = ((f32[32,96,128]{2,1,0:T(8,128)}), f32[32,96,128]{2,1,0:T(8,128)S(1)}, u32[]{:S(2)}, u32[]{:S(2)}) async-start(f32[32,96,128]{2,1,0:T(8,128)} %get-tuple-element.65), calls=%async_computation.1 | async-start | bytes 3145728 | tf_op jit(solution)/shard_map/all_to_all | solution.py:535
  116.8 7.9 %collective-permute-start.6 = (f32[512,128]{1,0:T(8,128)S(1)}, f32[512,128]{1,0:T(8,128)S(1)}, u32[]{:S(2)}, u32[]{:S(2)}) collective-permute-start(f32[512,128]{1,0:T(8,128)S(1)} %get-tuple-element.69), channel_id=1, source_target_pairs={{0,2},{1,3},{2,0},{3,1},{4,6},{5,7},{6,4},{7,5},{8,10},{9,11},{10,... | collective-permute-start | bytes 786440 | tf_op jit(solution)/shard_map/ppermute | solution.py:517
  124.7 6.5 %collective-permute-start.7 = (f32[512,128]{1,0:T(8,128)S(1)}, f32[512,128]{1,0:T(8,128)S(1)}, u32[]{:S(2)}, u32[]{:S(2)}) collective-permute-start(f32[512,128]{1,0:T(8,128)S(1)} %get-tuple-element.73), channel_id=1, source_target_pairs={{0,1},{1,2},{2,3},{3,0},{4,5},{5,6},{6,7},{7,4},{8,9},{9,10},{10,1... | collective-permute-start | bytes 786440 | tf_op jit(solution)/shard_map/ppermute | solution.py:517
  124.8 6.4 %collective-permute-start.8 = (f32[512,128]{1,0:T(8,128)S(1)}, f32[512,128]{1,0:T(8,128)S(1)}, u32[]{:S(2)}, u32[]{:S(2)}) collective-permute-start(f32[512,128]{1,0:T(8,128)S(1)} %get-tuple-element.74), channel_id=1, source_target_pairs={{0,3},{1,0},{2,1},{3,2},{4,7},{5,4},{6,5},{7,6},{8,11},{9,8},{10,9... | collective-permute-start | bytes 786440 | tf_op jit(solution)/shard_map/ppermute | solution.py:517
  131.5 11.1 %collective-permute-start.10 = (f32[512,128]{1,0:T(8,128)S(1)}, f32[512,128]{1,0:T(8,128)S(1)}, u32[]{:S(2)}, u32[]{:S(2)}) collective-permute-start(f32[512,128]{1,0:T(8,128)S(1)} %get-tuple-element.90.home.refs_0_), channel_id=1, source_target_pairs={{0,3},{1,0},{2,1},{3,2},{4,7},{5,4},{6,5},{7,6},{8,11},{9,8},{10,9... | collective-permute-start | bytes 786440 | tf_op jit(solution)/shard_map/ppermute | solution.py:517
  134.2 9.6 %collective-permute-start.9 = (f32[512,128]{1,0:T(8,128)S(1)}, f32[512,128]{1,0:T(8,128)S(1)}, u32[]{:S(2)}, u32[]{:S(2)}) collective-permute-start(f32[512,128]{1,0:T(8,128)S(1)} %get-tuple-element.90.home.refs_0_), channel_id=1, source_target_pairs={{0,1},{1,2},{2,3},{3,0},{4,5},{5,6},{6,7},{7,4},{8,9},{9,10},{10,1... | collective-permute-start | bytes 786440 | tf_op jit(solution)/shard_map/ppermute | solution.py:517
  134.2 12.3 %collective-permute-start.11 = (f32[512,128]{1,0:T(8,128)S(1)}, f32[512,128]{1,0:T(8,128)S(1)}, u32[]{:S(2)}, u32[]{:S(2)}) collective-permute-start(f32[512,128]{1,0:T(8,128)S(1)} %get-tuple-element.90.home.refs_0_), channel_id=1, source_target_pairs={{0,2},{1,3},{2,0},{3,1},{4,6},{5,7},{6,4},{7,5},{8,10},{9,11},{10,... | collective-permute-start | bytes 786440 | tf_op jit(solution)/shard_map/ppermute | solution.py:517
  151.0 44.2 %all-to-all-start.2 = ((f32[32,96,128]{2,1,0:T(8,128)}), f32[32,96,128]{2,1,0:T(8,128)S(1)}, u32[]{:S(2)}, u32[]{:S(2)}) async-start(f32[32,96,128]{2,1,0:T(8,128)} %get-tuple-element.76), calls=%async_computation.2 | async-start | bytes 3145728 | tf_op jit(solution)/shard_map/all_to_all | solution.py:535
  197.9 6.8 %collective-permute-start.12 = (f32[512,128]{1,0:T(8,128)S(1)}, f32[512,128]{1,0:T(8,128)S(1)}, u32[]{:S(2)}, u32[]{:S(2)}) collective-permute-start(f32[512,128]{1,0:T(8,128)S(1)} %get-tuple-element.80), channel_id=1, source_target_pairs={{0,2},{1,3},{2,0},{3,1},{4,6},{5,7},{6,4},{7,5},{8,10},{9,11},{10,... | collective-permute-start | bytes 786440 | tf_op jit(solution)/shard_map/ppermute | solution.py:517
  204.7 7.2 %collective-permute-start.13 = (f32[512,128]{1,0:T(8,128)S(1)}, f32[512,128]{1,0:T(8,128)S(1)}, u32[]{:S(2)}, u32[]{:S(2)}) collective-permute-start(f32[512,128]{1,0:T(8,128)S(1)} %get-tuple-element.84), channel_id=1, source_target_pairs={{0,1},{1,2},{2,3},{3,0},{4,5},{5,6},{6,7},{7,4},{8,9},{9,10},{10,1... | collective-permute-start | bytes 786440 | tf_op jit(solution)/shard_map/ppermute | solution.py:517
  204.7 7.2 %collective-permute-start.14 = (f32[512,128]{1,0:T(8,128)S(1)}, f32[512,128]{1,0:T(8,128)S(1)}, u32[]{:S(2)}, u32[]{:S(2)}) collective-permute-start(f32[512,128]{1,0:T(8,128)S(1)} %get-tuple-element.85), channel_id=1, source_target_pairs={{0,3},{1,0},{2,1},{3,2},{4,7},{5,4},{6,5},{7,6},{8,11},{9,8},{10,9... | collective-permute-start | bytes 786440 | tf_op jit(solution)/shard_map/ppermute | solution.py:517
  212.3 10.8 %collective-permute-start.15 = (f32[512,128]{1,0:T(8,128)S(1)}, f32[512,128]{1,0:T(8,128)S(1)}, u32[]{:S(2)}, u32[]{:S(2)}) collective-permute-start(f32[512,128]{1,0:T(8,128)S(1)} %add_add_fusion.1.refs_0_), channel_id=1, source_target_pairs={{0,1},{1,2},{2,3},{3,0},{4,5},{5,6},{6,7},{7,4},{8,9},{9,10},{10,1... | collective-permute-start | bytes 786440 | tf_op jit(solution)/shard_map/ppermute | solution.py:517
  212.4 10.7 %collective-permute-start.16 = (f32[512,128]{1,0:T(8,128)S(1)}, f32[512,128]{1,0:T(8,128)S(1)}, u32[]{:S(2)}, u32[]{:S(2)}) collective-permute-start(f32[512,128]{1,0:T(8,128)S(1)} %add_add_fusion.1.refs_0_), channel_id=1, source_target_pairs={{0,2},{1,3},{2,0},{3,1},{4,6},{5,7},{6,4},{7,5},{8,10},{9,11},{10,... | collective-permute-start | bytes 786440 | tf_op jit(solution)/shard_map/ppermute | solution.py:517
  215.5 7.7 %collective-permute-start.17 = (f32[512,128]{1,0:T(8,128)S(1)}, f32[512,128]{1,0:T(8,128)S(1)}, u32[]{:S(2)}, u32[]{:S(2)}) collective-permute-start(f32[512,128]{1,0:T(8,128)S(1)} %add_add_fusion.1.refs_0_), channel_id=1, source_target_pairs={{0,3},{1,0},{2,1},{3,2},{4,7},{5,4},{6,5},{7,6},{8,11},{9,8},{10,9... | collective-permute-start | bytes 786440 | tf_op jit(solution)/shard_map/ppermute | solution.py:517
  227.1 29.5 %all-to-all-start.3 = ((f32[32,48,128]{2,1,0:T(8,128)}), f32[32,48,128]{2,1,0:T(8,128)S(1)}, u32[]{:S(2)}, u32[]{:S(2)}) async-start(f32[32,48,128]{2,1,0:T(8,128)} %get-tuple-element.87), calls=%async_computation.3 | async-start | bytes 1572864 | tf_op jit(solution)/shard_map/all_to_all | solution.py:535
  (8 other events, 53.8 us)

commit v5 on v4

--- a/solution.py
+++ b/solution.py
@@ -224,33 +224,67 @@
         outs[s][share : share + 8, :] = row
 
 
-def far_list_kernel(first, room, count, lane, order, code, sizes):
-    quarter = order.shape[0] // QUARTERS
-    across = lax.rem(lane[0] + 2, 4)
+def edge_code_kernel(
+    rows, slots, room, count, lane, source, target, weight, far_code, spot, totals, mass, near_code, near_mass, gap_code, gap_slot
+):
+    groups = source.shape[0]
+    per = groups // QUARTERS
+    s, t = source[...], target[...]
+    row = lax.broadcasted_iota(jnp.int32, s.shape, 0)
+    number = row * LANES + lax.broadcasted_iota(jnp.int32, s.shape, 1)
+    live = number < count[0]
+    away = t >= rows
+    load = jnp.where(live, weight[...], 0.0)
+    mass[...] = load
+    near_mass[...] = jnp.where(away, 0.0, load)
+    near_code[...] = s | (jnp.where(away, 0, t) << 12)
+    gap_code[...] = s | (jnp.minimum(t, rows) << 12)
+    gap_slot[...] = jnp.where(away, t - rows, slots)
+    far_code[...] = (jnp.where(away, t - rows, 0) << 21) | (s << 10) | (number & (per * LANES - 1))
+    left = lax.broadcasted_iota(jnp.int32, (LANES, LANES), 0)
+    right = lax.broadcasted_iota(jnp.int32, (LANES, LANES), 1)
+    before = jnp.where(left < right, 1.0, 0.0).astype(jnp.bfloat16)
+    ones = jnp.ones((LANES, LANES), jnp.bfloat16)
+    down = lax.broadcasted_iota(jnp.int32, (groups, groups), 0)
+    over = lax.broadcasted_iota(jnp.int32, (groups, groups), 1)
+    same = lax.shift_right_logical(down, 3) == lax.shift_right_logical(over, 3)
+    above = jnp.where(same & (over < down), 1.0, 0.0).astype(jnp.bfloat16)
+    late = lax.shift_right_logical(s, 9) == lax.rem(lane[0] + 2, 4)
+    region = (lax.shift_right_logical(row, 3) & 1) * 2 * room
+    where = jnp.zeros_like(row) + 4 * room
+    for kind in range(2):
+        counted = away & live & (late if kind else ~late)
+        flags = jnp.where(counted, 1.0, 0.0).astype(jnp.bfloat16)
+        within = jnp.dot(flags, before, preferred_element_type=jnp.float32)
+        total = jnp.dot(flags, ones, preferred_element_type=jnp.float32)
+        base = jnp.dot(above, total.astype(jnp.bfloat16), preferred_element_type=jnp.float32)
+        where = jnp.where(counted, region + kind * room + (within + base).astype(jnp.int32), where)
+        through = (base + total).astype(jnp.int32)
+        for c in range(QUARTERS):
+            totals[kind * QUARTERS + c : kind * QUARTERS + c + 1, :] = through[(c + 1) * per - 1 : (c + 1) * per, :]
+    spot[...] = where
+
+
+def far_list_kernel(first, room, count, order, spot, totals, code):
+    half = order.shape[0] // 2
+    begin = first * order.shape[0] // QUARTERS
+
+    def step(i, _):
+        e = begin + i * 8
+        given = [order[e + u] for u in range(8)]
+        to = [spot[e + u] for u in range(8)]
+        for u in range(8):
+            code[to[u]] = given[u]
+        return 0
+
+    live = jnp.clip(count[0] - begin, 0, half)
+    lax.fori_loop(0, lax.div(live + 7, 8), step, 0)
+    nothing = jnp.int32(SPARE - 2048) << 21
     for c in range(2):
-        begin = (first + c) * quarter
-        zero = 2 * c * room
-
-        def step(i, at):
-            e = begin + i * 8
-            given = [order[e + u] for u in range(8)]
-            early, late = at
-            for u in range(8):
-                far = jnp.where(lax.shift_right_arithmetic(given[u], 21) == -1, 0, 1)
-                after = (lax.shift_right_logical(given[u], 19) & 3) == across
-                code[jnp.where(after, late, early)] = given[u]
-                early = early + jnp.where(after, 0, far)
-                late = late + jnp.where(after, far, 0)
-            return early, late
-
-        live = jnp.clip(count[0] - begin, 0, quarter)
-        early, late = lax.fori_loop(0, lax.div(live + 7, 8), step, (zero, zero + room))
-        nothing = jnp.int32(SPARE - 2048) << 21
-        for u in range(UNROLL):
-            code[early + u] = nothing
-            code[late + u] = nothing
-        sizes[2 * c] = early - zero
-        sizes[2 * c + 1] = late - zero - room
+        for kind in range(2):
+            end = (2 * c + kind) * room + totals[kind * QUARTERS + first + c, 0]
+            for u in range(UNROLL):
+                code[end + u] = nothing
 
 
 def trips(n):
@@ -262,11 +296,11 @@
         a[...] = jnp.zeros_like(a)
 
 
-def far_rows(kind, lists, mass, take, give, banks):
+def far_rows(kind, lists, totals, mass, take, give, banks):
     quarter = mass.shape[0] // QUARTERS
     many = len(banks)
-    for h, (code, sizes) in enumerate(lists):
-        room = code.shape[0] // 4
+    for h, code in enumerate(lists):
+        room = (code.shape[0] - LANES) // 4
         for c in range(2):
             start = (2 * c + kind) * room
             base = (2 * h + c) * quarter
@@ -282,7 +316,7 @@
                         banks[k][to[k], :] = new[k]
                 return 0
 
-            lax.fori_loop(0, trips(sizes[2 * c + kind]), step, 0)
+            lax.fori_loop(0, trips(totals[kind * QUARTERS + 2 * h + c, 0]), step, 0)
 
 
 def far_source(given):
@@ -321,25 +355,7 @@
     lax.fori_loop(0, out.shape[0], step, 0)
 
 
-def early_field_kernel(lanes, lane, code_a, sizes_a, code_b, sizes_b, mass, home, one, three, out, field, *banks):
-    for s, share in ((0, home), (1, one), (3, three)):
-        place(lane, lanes, s, share, field)
-    clear(banks)
-    far_rows(
-        0,
-        ((code_a, sizes_a), (code_b, sizes_b)),
-        mass,
-        lambda given: field[pl.ds(far_source(given), 1), :],
-        far_slot,
-        banks,
-    )
-    total = banks[0][...]
-    for a in banks[1:]:
-        total = total + a[...]
-    out[...] = total
-
-
-def field_kernel(lanes, lane, code_a, sizes_a, code_b, sizes_b, mass, lists, part, *refs):
+def field_kernel(lanes, lane, code_a, code_b, totals, mass, lists, *refs):
     shares, (kept, sent), refs = refs[:lanes], refs[lanes : lanes + 2], refs[lanes + 2 :]
     field, out, sums, leave_field, leave, leave_sums = refs[:6]
     banks = refs[6:]
@@ -347,16 +363,17 @@
     assemble(lane, lanes, shares, field)
     keep = pltpu.make_async_copy(field, kept, leave_field)
     keep.start()
-    banks[0][...] = part[...]
-    clear(banks[1:])
-    far_rows(
-        1,
-        ((code_a, sizes_a), (code_b, sizes_b)),
-        mass,
-        lambda given: field[pl.ds(far_source(given), 1), :],
-        far_slot,
-        banks,
-    )
+    clear(banks)
+    for kind in range(2):
+        far_rows(
+            kind,
+            (code_a, code_b),
+            totals,
+            mass,
+            lambda given: field[pl.ds(far_source(given), 1), :],
+            far_slot,
+            banks,
+        )
     for c in range(blocks):
         at = slice(c * width, (c + 1) * width)
         total = banks[0][at, :]
@@ -409,7 +426,7 @@
     return halves(jnp.dot(hot[...], ret_both[...], preferred_element_type=jnp.float32))
 
 
-def late_join_kernel(lanes, lane, code_a, sizes_a, code_b, sizes_b, mass, listed, near, arrived, *refs):
+def late_join_kernel(lanes, lane, code_a, code_b, totals, mass, listed, near, arrived, *refs):
     out, halo, ret_both, hot, ret, come_halo, come_ret = refs[:7]
     banks = refs[7:]
     blocks, width, _ = ret.shape
@@ -425,7 +442,8 @@
     flat = halo.reshape((blocks + 1) * width, LANES)
     far_rows(
         1,
-        ((code_a, sizes_a), (code_b, sizes_b)),
+        (code_a, code_b),
+        totals,
         mass,
         lambda given: flat[pl.ds(far_slot(given), 1), :],
         lambda given: far_source(given) & (share - 1),
@@ -440,14 +458,16 @@
     out[...] = total + listed_rows(q, share, listed, ret_both, hot)
 
 
-def join_kernel(lanes, lane, code_a, sizes_a, code_b, sizes_b, mass, listed, near, halo, ret_both, *refs):
+def join_kernel(lanes, lane, code_a, code_b, totals, mass, listed, near, halo, ret_both, *refs):
     outs, hot, banks = refs[:3], refs[3], refs[4:]
     share = outs[0].shape[0]
-    clear(banks)
+    banks[0][...] = near[...]
+    clear(banks[1:])
     flat = halo.reshape(halo.shape[0] * halo.shape[1], LANES)
     far_rows(
         0,
-        ((code_a, sizes_a), (code_b, sizes_b)),
+        (code_a, code_b),
+        totals,
         mass,
         lambda given: flat[pl.ds(far_slot(given), 1), :],
         far_source,
@@ -456,10 +476,14 @@
     for s, out in zip((1, 3, 0), outs):
         q = lax.rem(lane[0] + s, lanes)
         at = pl.ds(pl.multiple_of(q * share, share), share)
-        total = near[at, :]
-        for a in banks:
+        total = banks[0][at, :]
+        for a in banks[1:]:
             total = total + a[at, :]
-        out[...] = total + listed_rows(q, share, listed, ret_both, hot)
+        out[...] = total + listed_rows(q, share, listed, ret_both, hot) if s else total
+
+
+def home_kernel(lane, listed, part, ret_both, out, hot):
+    out[...] = part[...] + listed_rows(lane[0], out.shape[0], listed, ret_both, hot)
 
 
 def solution_kernel(lane, lists, *refs):
@@ -587,33 +611,38 @@
         "side_join",
         flops=2 * rows * slots * 2 * LANES,
     )(lane, returned, listed, padded, own, own_degree)
-    begin, *sides = lax.optimization_barrier((edge_count, *sides))
-    away = dst_index >= rows
-    near_weight = jnp.where(away, 0.0, weight)
-    near_order = src_local | (jnp.where(away, 0, dst_index) << 12)
-    gap_order = src_local | (jnp.minimum(dst_index, rows) << 12)
-    gap_slot = jnp.where(away, dst_index - rows, slots)
+    late = lax.optimization_barrier((edge_count, source_rows, target_rows, edge_weight, *sides))
+    begin, source_late, target_late, weight_late, *sides = late
     quarter = edges // QUARTERS
-    number = jnp.arange(edges, dtype=i32) & (quarter - 1)
-    far_order = (jnp.where(away, dst_index - rows, 2047) << 21) | (src_local << 10) | number
+    room = quarter + LANES // 4
+    per_edge = ((groups, LANES), i32, VMEM)
+    per_edge_f32 = ((groups, LANES), f32, VMEM)
+    coded = list(call(
+        functools.partial(edge_code_kernel, rows, slots, room),
+        [per_edge, per_edge, ((2 * QUARTERS, LANES), i32, VMEM), per_edge_f32, per_edge, per_edge_f32, per_edge, per_edge],
+        [SMEM] * 2 + [VMEM] * 3,
+        [],
+        "edge_code",
+    )(begin, lane, source_late, target_late, weight_late.reshape(groups, LANES)))
+    totals = coded.pop(2)
+    far_order, spot, mass, near_order, near_weight, gap_order, gap_slot = (x.reshape(edges) for x in coded)
 
     def far_list(first, count):
-        room = quarter + LANES // 4
         return call(
             functools.partial(far_list_kernel, first, room),
-            [((4 * room,), i32, SMEM), ((4,), i32, SMEM)],
-            [SMEM] * 3,
+            [((4 * room + LANES,), i32, SMEM)],
+            [SMEM] * 4,
             [],
             "far_list",
             moved=2**25,
-        )(count, lane, far_order)
-
-    code_a, sizes_a = far_list(0, begin)
+        )(count, far_order, spot, totals)[0]
+
+    code_a = far_list(0, begin)
     side = summed(sides, lanes)
-    side, sizes_a = lax.optimization_barrier((side, sizes_a))
-    later, side = lax.optimization_barrier((edge_count, side))
-    code_b, sizes_b = far_list(2, later)
-    far = (code_a, sizes_a, code_b, sizes_b, weight)
+    side, code_a = lax.optimization_barrier((side, code_a))
+    later, side = lax.optimization_barrier((begin, side))
+    code_b = far_list(2, later)
+    far = (code_a, code_b, totals, mass)
     right_share = side[:share]
     degree_share = side[share : share + share // LANES].reshape(share)
     ground_share = lax.dynamic_slice_in_dim(ground, lane[0] * share, share)
@@ -626,24 +655,16 @@
     solution_share = direction
     for keep, push in pairs:
         shares = to_all(direction, lanes)
-        early = call(
-            functools.partial(early_field_kernel, lanes),
-            [((slots + 8, LANES), f32, VMEM)],
-            [SMEM] * 6 + [VMEM] * 3,
-            [pltpu.VMEM((rows, LANES), f32)] + [pltpu.VMEM((slots + 8, LANES), f32)] * BANKS,
-            "early_field",
-            moved=2**25,
-        )(lane, *far, shares[0], shares[1], shares[3])[0]
         field, message = call(
             functools.partial(field_kernel, lanes),
             [((rows, LANES), f32, HBM), ((blocks, 2 * width, LANES), f32, HBM)],
-            [SMEM] * 7 + [VMEM] * (1 + lanes),
+            [SMEM] * 6 + [VMEM] * lanes,
             [pltpu.VMEM((rows, LANES), f32)]
             + [pltpu.VMEM((blocks, width, LANES), f32)] * 2
             + [pltpu.SemaphoreType.DMA] * 3
-            + [pltpu.VMEM((slots + 8, LANES), f32)] * 2,
+            + [pltpu.VMEM((slots + 8, LANES), f32)] * BANKS,
             "field",
-        )(lane, *far, lists, early, *shares)
+        )(lane, *far, lists, *shares)
         arrived = across(message)
         near = call(
             near_kernel,
@@ -656,7 +677,7 @@
         two, halo, ret_both = call(
             functools.partial(late_join_kernel, lanes),
             [((share, LANES), f32, VMEM), ((blocks + 1, width, LANES), f32, VMEM), ((slots, 2 * LANES), bf16, VMEM)],
-            [SMEM] * 6 + [VMEM, VMEM, HBM],
+            [SMEM] * 5 + [VMEM, VMEM, HBM],
             [pltpu.VMEM((share, slots), bf16), pltpu.VMEM((blocks, width, LANES), f32)]
             + [pltpu.SemaphoreType.DMA] * 2
             + [pltpu.VMEM((share, LANES), f32)] * BANKS,
@@ -665,11 +686,19 @@
         one, three, home = call(
             functools.partial(join_kernel, lanes),
             [((share, LANES), f32, VMEM)] * 3,
-            [SMEM] * 6 + [VMEM] * 4,
+            [SMEM] * 5 + [VMEM] * 4,
             [pltpu.VMEM((share, slots), bf16)] + [pltpu.VMEM((rows, LANES), f32)] * BANKS,
             "join",
             moved=2**25,
         )(lane, *far, listed, near, halo, ret_both)
+        home = call(
+            home_kernel,
+            [((share, LANES), f32, VMEM)],
+            [SMEM] + [VMEM] * 3,
+            [pltpu.VMEM((share, slots), bf16)],
+            "home",
+            moved=2**25,
+        )(lane, listed, home, ret_both)[0]
         two = moved_by(two, 2, lanes)
         two, one, three = lax.optimization_barrier((two, one, three))
         flows = (home + two) + (moved_by(one, 1, lanes) + moved_by(three, 3, lanes))

time: 259 us -> 249 us (0.961)
  starting transfers between devices: 85.8 us -> 76.6 us
  Pallas kernels: 78.5 us -> 73.1 us
  waiting for transfers between devices: 83.7 us -> 86.7 us
    all_to_all x4, starting transfers between devices: 59.9 us -> 49 us  [across(): return lax.all_to_all(x, 'vtx', split_axis=0, concat_axis=0, tiled=True)]
    pallas_call x4 -> x5, Pallas kernels: 14.4 us -> 7.46 us  [the longest x2 5.86 us: far_list(): call(functools.partial(far_list_kernel, first, room), [((4 * room + LANES...]
    ppermute x18, waiting for transfers between devices: 37.3 us -> 40.4 us  [moved_by(): lax.ppermute(x, 'edg', [(i, (i + shift) % lanes) for i in range(lanes)])]
  transfers between devices with their start and end apart: 22 -> 22, of which waited for: 14 -> 17; matrix products, arithmetic and copies ran while one was open for 0% -> 0% of each run, Pallas kernels for 18% -> 16%
where the time goes in v5:
time: 249 us; the launch traced here: 247 us
  waiting for transfers between devices  86.7 us (35%)
  starting transfers between devices  76.6 us (31%)
  Pallas kernels  73.1 us (29%)
  local copies, waits for them, and re-layouts  5.06 us (2%)
  other arithmetic  4.18 us (2%)
    all_to_all x4, starting transfers between devices, across(): return lax.all_to_all(x, 'vtx', split_axis=0, concat_axis=0, tiled=True)  49 us
    all_to_all x4, waiting for transfers between devices, across(): return lax.all_to_all(x, 'vtx', split_axis=0, concat_axis=0, tiled=True)  46.3 us
    ppermute x18, waiting for transfers between devices, moved_by(): lax.ppermute(x, 'edg', [(i, (i + shift) % lanes) for i in range(lanes)])  40.4 us
    ppermute x18, starting transfers between devices, moved_by(): lax.ppermute(x, 'edg', [(i, (i + shift) % lanes) for i in range(lanes)])  27.7 us
    pallas_call x1, Pallas kernels, local(): call(own_side_kernel, [((rows, LANES), f32, HBM), ((rows // LANES, LANES)...  12.1 us
    pallas_call x2, Pallas kernels, local(): call(functools.partial(field_kernel, lanes), [((rows, LANES), f32, HBM),...  11.1 us
    pallas_call x2, Pallas kernels, local(): call(near_kernel, [((rows, LANES), f32, VMEM)], [SMEM] * 3 + [HBM], [pltp...  9.35 us
    pallas_call x2, Pallas kernels, local(): call(functools.partial(join_kernel, lanes), [((share, LANES), f32, VMEM)]...  7.83 us
  transfers between devices with their start and end apart: 22, of which 17 were waited for; matrix products, arithmetic and copies ran while one was open for 0% of the time, Pallas kernels for 16%

profile of v5, /device:TPU:1, one launch (start us, length us, event | category | flops | bytes accessed | tf_op | source)
XLA Modules:
  0.0 247.4 jit_solution(3953977771079247521)
XLA Ops:
  3.9 6.0 %halo_side.1 = f32[32,56,128]{2,1,0:T(8,128)} custom-call(f32[4096,128]{1,0:T(8,128)S(1)} %convert_multiply_fusion.terms, s32[32,128]{1,0:T(8,128)S(1)} %bitcast.38, f32[32,128]{1,0:T(8,128)S(1)} %get-tuple-element.106.weight), custom_call_target="tpu_custom_call" | custom-call | flops 3221225472 | bytes 4194304 | tf_op jit(solution)/shard_map/halo_side/pallas_call | solution.py:585
  9.9 8.6 %all-to-all-start = ((f32[32,56,128]{2,1,0:T(8,128)}), f32[32,56,128]{2,1,0:T(8,128)S(1)}, u32[]{:S(2)}, u32[]{:S(2)}) async-start(f32[32,56,128]{2,1,0:T(8,128)} %halo_side.1), calls=%async_computation | async-start | bytes 1835008 | tf_op jit(solution)/shard_map/all_to_all | solution.py:559
  18.7 12.1 %own_side.1 = (f32[2048,128]{1,0:T(8,128)}, f32[16,128]{1,0:T(8,128)S(1)}) custom-call(f32[4096,128]{1,0:T(8,128)S(1)} %convert_multiply_fusion.terms, s32[32,128]{1,0:T(8,128)S(1)} %bitcast.41, s32[32,128]{1,0:T(8,128)S(1)} %bitcast.39, f32[32,128]{1,0:T(8,128)S(1)} %get-tuple-element.106.weight), custom_call_target="tpu_custom_call" | custom-call | flops 4294967296 | bytes 4194304 | tf_op jit(solution)/shard_map/own_side/pallas_call | solution.py:595
  30.7 3.6 %all-to-all-done.returned = f32[32,56,128]{2,1,0:T(8,128)S(1)} async-done(((f32[32,56,128]{2,1,0:T(8,128)}), f32[32,56,128]{2,1,0:T(8,128)S(1)}, u32[]{:S(2)}, u32[]{:S(2)}) %all-to-all-start) | async-done | bytes 917536 | tf_op jit(solution)/shard_map/all_to_all | solution.py:559
  35.5 4.0 %side_join.1 = (f32[520,128]{1,0:T(8,128)S(1)}, f32[520,128]{1,0:T(8,128)S(1)}, f32[520,128]{1,0:T(8,128)S(1)}, f32[520,128]{1,0:T(8,128)S(1)}) custom-call(s32[1]{0:T(128)} %bitcast.lane, f32[32,56,128]{2,1,0:T(8,128)S(1)} %all-to-all-done.returned, s32[12,128]{1,0:T(8,128)S(1)} %reshape_reshape_squeeze.3.listed, s32[32,128]{1,0:T(8,128)S(1)} %pad.4.padded, ...), custom_call_target="tpu_custom_call" | custom-call | flops 1610612736 | bytes 4194304 | tf_op jit(solution)/shard_map/side_join/pallas_call | solution.py:604
  45.7 3.8 %far_list.2.code_a = s32[4352]{0:T(1024)S(1)} custom-call(s32[1]{0:T(128)} %copy.9.count, s32[4096]{0:T(1024)S(1)} %bitcast.32, s32[4096]{0:T(1024)S(1)} %bitcast.34, s32[8,128]{1,0:T(8,128)S(1)} %get-tuple-element.68.totals), custom_call_target="tpu_custom_call" | custom-call | bytes 33554432 | tf_op jit(solution)/shard_map/far_list/pallas_call | solution.py:631
  49.9 6.6 %collective-permute-done.1 = f32[520,128]{1,0:T(8,128)S(1)} collective-permute-done((f32[520,128]{1,0:T(8,128)S(1)}, f32[520,128]{1,0:T(8,128)S(1)}, u32[]{:S(2)}, u32[]{:S(2)}) %collective-permute-start.1) | collective-permute-done | bytes 266272 | tf_op jit(solution)/shard_map/ppermute | solution.py:541
  65.3 7.5 %collective-permute-done.4.refs_2_ = f32[512,128]{1,0:T(8,128)S(1)} collective-permute-done((f32[512,128]{1,0:T(8,128)S(1)}, f32[512,128]{1,0:T(8,128)S(1)}, u32[]{:S(2)}, u32[]{:S(2)}) %collective-permute-start.4) | collective-permute-done | bytes 262176 | tf_op jit(solution)/shard_map/ppermute | solution.py:541
  72.8 5.5 %field.2 = (f32[2048,128]{1,0:T(8,128)}, f32[32,96,128]{2,1,0:T(8,128)}) custom-call(s32[1]{0:T(128)} %bitcast.lane, s32[4352]{0:T(1024)S(1)} %far_list.2.code_a, s32[4352]{0:T(1024)S(1)} %far_list.3.code_b, s32[8,128]{1,0:T(8,128)S(1)} %get-tuple-element.68.totals, f32[4096]{0:T(1024)S(1)} %bitcast.21, s32[1536]{0:T(1024)S(1)} %reshape_squeeze.3.lists, ...), custom_call_target="tpu_custom_call" | custom-call | bytes 4194304 | tf_op jit(solution)/shard_map/field/pallas_call | solution.py:658
  78.4 9.3 %all-to-all-start.1 = ((f32[32,96,128]{2,1,0:T(8,128)}), f32[32,96,128]{2,1,0:T(8,128)S(1)}, u32[]{:S(2)}, u32[]{:S(2)}) async-start(f32[32,96,128]{2,1,0:T(8,128)} %get-tuple-element.77), calls=%async_computation.1 | async-start | bytes 3145728 | tf_op jit(solution)/shard_map/all_to_all | solution.py:559
  88.9 4.7 %near.2 = f32[2048,128]{1,0:T(8,128)S(1)} custom-call(s32[1]{0:T(128)} %copy.9.count, s32[4096]{0:T(1024)S(1)} %bitcast.27, f32[4096]{0:T(1024)S(1)} %bitcast.29, f32[2048,128]{1,0:T(8,128)S(1)} %copy-done.1), custom_call_target="tpu_custom_call" | custom-call | bytes 33554432 | tf_op jit(solution)/shard_map/near/pallas_call | solution.py:669
  93.5 16.3 %all-to-all-done.1.arrived = f32[32,96,128]{2,1,0:T(8,128)S(1)} async-done(((f32[32,96,128]{2,1,0:T(8,128)}), f32[32,96,128]{2,1,0:T(8,128)S(1)}, u32[]{:S(2)}, u32[]{:S(2)}) %all-to-all-start.1) | async-done | bytes 1572896 | tf_op jit(solution)/shard_map/all_to_all | solution.py:559
  114.5 3.9 %join.2 = (f32[512,128]{1,0:T(8,128)S(1)}, f32[512,128]{1,0:T(8,128)S(1)}, f32[512,128]{1,0:T(8,128)S(1)}) custom-call(s32[1]{0:T(128)} %bitcast.lane, s32[4352]{0:T(1024)S(1)} %far_list.2.code_a, s32[4352]{0:T(1024)S(1)} %far_list.3.code_b, s32[8,128]{1,0:T(8,128)S(1)} %get-tuple-element.68.totals, f32[4096]{0:T(1024)S(1)} %bitcast.23, ...), custom_call_target="tpu_custom_call" | custom-call | bytes 33554432 | tf_op jit(solution)/shard_map/join/pallas_call | solution.py:686
  133.1 3.6 %collective-permute-done.11.refs_3_ = f32[512,128]{1,0:T(8,128)S(1)} collective-permute-done((f32[512,128]{1,0:T(8,128)S(1)}, f32[512,128]{1,0:T(8,128)S(1)}, u32[]{:S(2)}, u32[]{:S(2)}) %collective-permute-start.11) | collective-permute-done | bytes 262176 | tf_op jit(solution)/shard_map/ppermute | solution.py:541
  136.8 3.5 %collective-permute-done.9.refs_1_ = f32[512,128]{1,0:T(8,128)S(1)} collective-permute-done((f32[512,128]{1,0:T(8,128)S(1)}, f32[512,128]{1,0:T(8,128)S(1)}, u32[]{:S(2)}, u32[]{:S(2)}) %collective-permute-start.9) | collective-permute-done | bytes 262176 | tf_op jit(solution)/shard_map/ppermute | solution.py:541
  140.2 5.5 %field.3 = (f32[2048,128]{1,0:T(8,128)}, f32[32,96,128]{2,1,0:T(8,128)}) custom-call(s32[1]{0:T(128)} %bitcast.lane, s32[4352]{0:T(1024)S(1)} %far_list.2.code_a, s32[4352]{0:T(1024)S(1)} %far_list.3.code_b, s32[8,128]{1,0:T(8,128)S(1)} %get-tuple-element.68.totals, f32[4096]{0:T(1024)S(1)} %bitcast.24, s32[1536]{0:T(1024)S(1)} %reshape_squeeze.3.lists, ...), custom_call_target="tpu_custom_call" | custom-call | bytes 4194304 | tf_op jit(solution)/shard_map/field/pallas_call | solution.py:658
  145.8 16.1 %all-to-all-start.2 = ((f32[32,96,128]{2,1,0:T(8,128)}), f32[32,96,128]{2,1,0:T(8,128)S(1)}, u32[]{:S(2)}, u32[]{:S(2)}) async-start(f32[32,96,128]{2,1,0:T(8,128)} %get-tuple-element.88), calls=%async_computation.2 | async-start | bytes 3145728 | tf_op jit(solution)/shard_map/all_to_all | solution.py:559
  163.1 4.7 %near.3 = f32[2048,128]{1,0:T(8,128)S(1)} custom-call(s32[1]{0:T(128)} %copy.9.count, s32[4096]{0:T(1024)S(1)} %bitcast.28, f32[4096]{0:T(1024)S(1)} %bitcast.30, f32[2048,128]{1,0:T(8,128)S(1)} %copy-done), custom_call_target="tpu_custom_call" | custom-call | bytes 33554432 | tf_op jit(solution)/shard_map/near/pallas_call | solution.py:669
  167.8 16.3 %all-to-all-done.2.arrived = f32[32,96,128]{2,1,0:T(8,128)S(1)} async-done(((f32[32,96,128]{2,1,0:T(8,128)}), f32[32,96,128]{2,1,0:T(8,128)S(1)}, u32[]{:S(2)}, u32[]{:S(2)}) %all-to-all-start.2) | async-done | bytes 1572896 | tf_op jit(solution)/shard_map/all_to_all | solution.py:559
  188.9 3.9 %join.3 = (f32[512,128]{1,0:T(8,128)S(1)}, f32[512,128]{1,0:T(8,128)S(1)}, f32[512,128]{1,0:T(8,128)S(1)}) custom-call(s32[1]{0:T(128)} %bitcast.lane, s32[4352]{0:T(1024)S(1)} %far_list.2.code_a, s32[4352]{0:T(1024)S(1)} %far_list.3.code_b, s32[8,128]{1,0:T(8,128)S(1)} %get-tuple-element.68.totals, f32[4096]{0:T(1024)S(1)} %bitcast.26, ...), custom_call_target="tpu_custom_call" | custom-call | bytes 33554432 | tf_op jit(solution)/shard_map/join/pallas_call | solution.py:686
  206.9 4.2 %collective-permute-done.16.refs_2_ = f32[512,128]{1,0:T(8,128)S(1)} collective-permute-done((f32[512,128]{1,0:T(8,128)S(1)}, f32[512,128]{1,0:T(8,128)S(1)}, u32[]{:S(2)}, u32[]{:S(2)}) %collective-permute-start.16) | collective-permute-done | bytes 262176 | tf_op jit(solution)/shard_map/ppermute | solution.py:541
  211.1 3.9 %solution_rows.1 = (f32[2048,128]{1,0:T(8,128)}, f32[32,48,128]{2,1,0:T(8,128)}) custom-call(s32[1]{0:T(128)} %bitcast.lane, s32[1536]{0:T(1024)S(1)} %reshape_squeeze.3.lists, f32[512,128]{1,0:T(8,128)S(1)} %add_add_fusion.1.refs_0_, f32[512,128]{1,0:T(8,128)S(1)} %collective-permute-done.15.refs_1_, f32[512,128]{1,0:T(8,128)S(1)} %collective-permute-done.16.refs_2_, ...), custom_call_target="tpu_custom_call" | custom-call | bytes 4194304 | tf_op jit(solution)/shard_map/solution_rows/pallas_call | solution.py:708
  215.0 15.0 %all-to-all-start.3 = ((f32[32,48,128]{2,1,0:T(8,128)}), f32[32,48,128]{2,1,0:T(8,128)S(1)}, u32[]{:S(2)}, u32[]{:S(2)}) async-start(f32[32,48,128]{2,1,0:T(8,128)} %get-tuple-element.101), calls=%async_computation.3 | async-start | bytes 1572864 | tf_op jit(solution)/shard_map/all_to_all | solution.py:559
  234.1 10.1 %all-to-all-done.3.arrived = f32[32,48,128]{2,1,0:T(8,128)S(1)} async-done(((f32[32,48,128]{2,1,0:T(8,128)}), f32[32,48,128]{2,1,0:T(8,128)S(1)}, u32[]{:S(2)}, u32[]{:S(2)}) %all-to-all-start.3) | async-done | bytes 786464 | tf_op jit(solution)/shard_map/all_to_all | solution.py:559
  (67 shorter events, 66.9 us)
Async XLA Ops:
  3.9 14.7 %copy-start.7 = (s32[1,32,48]{2,1,0:T(8,128)S(1)}, s32[1,32,48]{2,1,0:T(8,128)}, u32[]{:S(2)}) copy-start(s32[1,32,48]{2,1,0:T(8,128)} %param.12) | copy-start | bytes 18436
  3.9 14.8 %copy-start.5 = (s32[4096]{0:T(1024)S(1)}, s32[4096]{0:T(1024)}, u32[]{:S(2)}) copy-start(s32[4096]{0:T(1024)} %param.10) | copy-start | bytes 49156
  9.9 24.4 %all-to-all-start = ((f32[32,56,128]{2,1,0:T(8,128)}), f32[32,56,128]{2,1,0:T(8,128)S(1)}, u32[]{:S(2)}, u32[]{:S(2)}) async-start(f32[32,56,128]{2,1,0:T(8,128)} %halo_side.1), calls=%async_computation | async-start | bytes 1835008 | tf_op jit(solution)/shard_map/all_to_all | solution.py:559
  39.6 10.3 %collective-permute-start = (f32[520,128]{1,0:T(8,128)S(1)}, f32[520,128]{1,0:T(8,128)S(1)}, u32[]{:S(2)}, u32[]{:S(2)}) collective-permute-start(f32[520,128]{1,0:T(8,128)S(1)} %get-tuple-element.60), channel_id=1, source_target_pairs={{0,1},{1,2},{2,3},{3,0},{4,5},{5,6},{6,7},{7,4},{8,9},{9,10},{10,1... | collective-permute-start | bytes 798728 | tf_op jit(solution)/shard_map/ppermute | solution.py:541
  41.3 15.1 %collective-permute-start.1 = (f32[520,128]{1,0:T(8,128)S(1)}, f32[520,128]{1,0:T(8,128)S(1)}, u32[]{:S(2)}, u32[]{:S(2)}) collective-permute-start(f32[520,128]{1,0:T(8,128)S(1)} %get-tuple-element.61), channel_id=1, source_target_pairs={{0,2},{1,3},{2,0},{3,1},{4,6},{5,7},{6,4},{7,5},{8,10},{9,11},{10,... | collective-permute-start | bytes 798728 | tf_op jit(solution)/shard_map/ppermute | solution.py:541
  44.6 11.8 %collective-permute-start.2 = (f32[520,128]{1,0:T(8,128)S(1)}, f32[520,128]{1,0:T(8,128)S(1)}, u32[]{:S(2)}, u32[]{:S(2)}) collective-permute-start(f32[520,128]{1,0:T(8,128)S(1)} %get-tuple-element.62), channel_id=1, source_target_pairs={{0,3},{1,0},{2,1},{3,2},{4,7},{5,4},{6,5},{7,6},{8,11},{9,8},{10,9... | collective-permute-start | bytes 798728 | tf_op jit(solution)/shard_map/ppermute | solution.py:541
  57.4 7.9 %collective-permute-start.3 = (f32[512,128]{1,0:T(8,128)S(1)}, f32[512,128]{1,0:T(8,128)S(1)}, u32[]{:S(2)}, u32[]{:S(2)}) collective-permute-start(f32[512,128]{1,0:T(8,128)S(1)} %slice_multiply_fusion.refs_0_), channel_id=1, source_target_pairs={{0,1},{1,2},{2,3},{3,0},{4,5},{5,6},{6,7},{7,4},{8,9},{9,10},{10,1... | collective-permute-start | bytes 786440 | tf_op jit(solution)/shard_map/ppermute | solution.py:541
  58.8 14.0 %collective-permute-start.4 = (f32[512,128]{1,0:T(8,128)S(1)}, f32[512,128]{1,0:T(8,128)S(1)}, u32[]{:S(2)}, u32[]{:S(2)}) collective-permute-start(f32[512,128]{1,0:T(8,128)S(1)} %slice_multiply_fusion.refs_0_), channel_id=1, source_target_pairs={{0,2},{1,3},{2,0},{3,1},{4,6},{5,7},{6,4},{7,5},{8,10},{9,11},{10,... | collective-permute-start | bytes 786440 | tf_op jit(solution)/shard_map/ppermute | solution.py:541
  61.3 11.5 %collective-permute-start.5 = (f32[512,128]{1,0:T(8,128)S(1)}, f32[512,128]{1,0:T(8,128)S(1)}, u32[]{:S(2)}, u32[]{:S(2)}) collective-permute-start(f32[512,128]{1,0:T(8,128)S(1)} %slice_multiply_fusion.refs_0_), channel_id=1, source_target_pairs={{0,3},{1,0},{2,1},{3,2},{4,7},{5,4},{6,5},{7,6},{8,11},{9,8},{10,9... | collective-permute-start | bytes 786440 | tf_op jit(solution)/shard_map/ppermute | solution.py:541
  78.4 31.5 %all-to-all-start.1 = ((f32[32,96,128]{2,1,0:T(8,128)}), f32[32,96,128]{2,1,0:T(8,128)S(1)}, u32[]{:S(2)}, u32[]{:S(2)}) async-start(f32[32,96,128]{2,1,0:T(8,128)} %get-tuple-element.77), calls=%async_computation.1 | async-start | bytes 3145728 | tf_op jit(solution)/shard_map/all_to_all | solution.py:559
  112.6 7.0 %collective-permute-start.6 = (f32[512,128]{1,0:T(8,128)S(1)}, f32[512,128]{1,0:T(8,128)S(1)}, u32[]{:S(2)}, u32[]{:S(2)}) collective-permute-start(f32[512,128]{1,0:T(8,128)S(1)} %get-tuple-element.81), channel_id=1, source_target_pairs={{0,2},{1,3},{2,0},{3,1},{4,6},{5,7},{6,4},{7,5},{8,10},{9,11},{10,... | collective-permute-start | bytes 786440 | tf_op jit(solution)/shard_map/ppermute | solution.py:541
  119.6 6.4 %collective-permute-start.7 = (f32[512,128]{1,0:T(8,128)S(1)}, f32[512,128]{1,0:T(8,128)S(1)}, u32[]{:S(2)}, u32[]{:S(2)}) collective-permute-start(f32[512,128]{1,0:T(8,128)S(1)} %get-tuple-element.85), channel_id=1, source_target_pairs={{0,1},{1,2},{2,3},{3,0},{4,5},{5,6},{6,7},{7,4},{8,9},{9,10},{10,1... | collective-permute-start | bytes 786440 | tf_op jit(solution)/shard_map/ppermute | solution.py:541
  120.1 6.0 %collective-permute-start.8 = (f32[512,128]{1,0:T(8,128)S(1)}, f32[512,128]{1,0:T(8,128)S(1)}, u32[]{:S(2)}, u32[]{:S(2)}) collective-permute-start(f32[512,128]{1,0:T(8,128)S(1)} %get-tuple-element.86), channel_id=1, source_target_pairs={{0,3},{1,0},{2,1},{3,2},{4,7},{5,4},{6,5},{7,6},{8,11},{9,8},{10,9... | collective-permute-start | bytes 786440 | tf_op jit(solution)/shard_map/ppermute | solution.py:541
  126.3 6.8 %collective-permute-start.10 = (f32[512,128]{1,0:T(8,128)S(1)}, f32[512,128]{1,0:T(8,128)S(1)}, u32[]{:S(2)}, u32[]{:S(2)}) collective-permute-start(f32[512,128]{1,0:T(8,128)S(1)} %get-tuple-element.104.refs_0_), channel_id=1, source_target_pairs={{0,2},{1,3},{2,0},{3,1},{4,6},{5,7},{6,4},{7,5},{8,10},{9,11},{10,... | collective-permute-start | bytes 786440 | tf_op jit(solution)/shard_map/ppermute | solution.py:541
  129.3 7.5 %collective-permute-start.11 = (f32[512,128]{1,0:T(8,128)S(1)}, f32[512,128]{1,0:T(8,128)S(1)}, u32[]{:S(2)}, u32[]{:S(2)}) collective-permute-start(f32[512,128]{1,0:T(8,128)S(1)} %get-tuple-element.104.refs_0_), channel_id=1, source_target_pairs={{0,3},{1,0},{2,1},{3,2},{4,7},{5,4},{6,5},{7,6},{8,11},{9,8},{10,9... | collective-permute-start | bytes 786440 | tf_op jit(solution)/shard_map/ppermute | solution.py:541
  130.2 10.1 %collective-permute-start.9 = (f32[512,128]{1,0:T(8,128)S(1)}, f32[512,128]{1,0:T(8,128)S(1)}, u32[]{:S(2)}, u32[]{:S(2)}) collective-permute-start(f32[512,128]{1,0:T(8,128)S(1)} %get-tuple-element.104.refs_0_), channel_id=1, source_target_pairs={{0,1},{1,2},{2,3},{3,0},{4,5},{5,6},{6,7},{7,4},{8,9},{9,10},{10,1... | collective-permute-start | bytes 786440 | tf_op jit(solution)/shard_map/ppermute | solution.py:541
  145.8 38.3 %all-to-all-start.2 = ((f32[32,96,128]{2,1,0:T(8,128)}), f32[32,96,128]{2,1,0:T(8,128)S(1)}, u32[]{:S(2)}, u32[]{:S(2)}) async-start(f32[32,96,128]{2,1,0:T(8,128)} %get-tuple-element.88), calls=%async_computation.2 | async-start | bytes 3145728 | tf_op jit(solution)/shard_map/all_to_all | solution.py:559
  186.8 6.8 %collective-permute-start.12 = (f32[512,128]{1,0:T(8,128)S(1)}, f32[512,128]{1,0:T(8,128)S(1)}, u32[]{:S(2)}, u32[]{:S(2)}) collective-permute-start(f32[512,128]{1,0:T(8,128)S(1)} %get-tuple-element.92), channel_id=1, source_target_pairs={{0,2},{1,3},{2,0},{3,1},{4,6},{5,7},{6,4},{7,5},{8,10},{9,11},{10,... | collective-permute-start | bytes 786440 | tf_op jit(solution)/shard_map/ppermute | solution.py:541
  193.7 6.4 %collective-permute-start.13 = (f32[512,128]{1,0:T(8,128)S(1)}, f32[512,128]{1,0:T(8,128)S(1)}, u32[]{:S(2)}, u32[]{:S(2)}) collective-permute-start(f32[512,128]{1,0:T(8,128)S(1)} %get-tuple-element.96), channel_id=1, source_target_pairs={{0,1},{1,2},{2,3},{3,0},{4,5},{5,6},{6,7},{7,4},{8,9},{9,10},{10,1... | collective-permute-start | bytes 786440 | tf_op jit(solution)/shard_map/ppermute | solution.py:541
  193.7 6.4 %collective-permute-start.14 = (f32[512,128]{1,0:T(8,128)S(1)}, f32[512,128]{1,0:T(8,128)S(1)}, u32[]{:S(2)}, u32[]{:S(2)}) collective-permute-start(f32[512,128]{1,0:T(8,128)S(1)} %get-tuple-element.97), channel_id=1, source_target_pairs={{0,3},{1,0},{2,1},{3,2},{4,7},{5,4},{6,5},{7,6},{8,11},{9,8},{10,9... | collective-permute-start | bytes 786440 | tf_op jit(solution)/shard_map/ppermute | solution.py:541
  200.4 6.5 %collective-permute-start.15 = (f32[512,128]{1,0:T(8,128)S(1)}, f32[512,128]{1,0:T(8,128)S(1)}, u32[]{:S(2)}, u32[]{:S(2)}) collective-permute-start(f32[512,128]{1,0:T(8,128)S(1)} %add_add_fusion.1.refs_0_), channel_id=1, source_target_pairs={{0,1},{1,2},{2,3},{3,0},{4,5},{5,6},{6,7},{7,4},{8,9},{9,10},{10,1... | collective-permute-start | bytes 786440 | tf_op jit(solution)/shard_map/ppermute | solution.py:541
  202.2 8.9 %collective-permute-start.16 = (f32[512,128]{1,0:T(8,128)S(1)}, f32[512,128]{1,0:T(8,128)S(1)}, u32[]{:S(2)}, u32[]{:S(2)}) collective-permute-start(f32[512,128]{1,0:T(8,128)S(1)} %add_add_fusion.1.refs_0_), channel_id=1, source_target_pairs={{0,2},{1,3},{2,0},{3,1},{4,6},{5,7},{6,4},{7,5},{8,10},{9,11},{10,... | collective-permute-start | bytes 786440 | tf_op jit(solution)/shard_map/ppermute | solution.py:541
  204.4 6.7 %collective-permute-start.17 = (f32[512,128]{1,0:T(8,128)S(1)}, f32[512,128]{1,0:T(8,128)S(1)}, u32[]{:S(2)}, u32[]{:S(2)}) collective-permute-start(f32[512,128]{1,0:T(8,128)S(1)} %add_add_fusion.1.refs_0_), channel_id=1, source_target_pairs={{0,3},{1,0},{2,1},{3,2},{4,7},{5,4},{6,5},{7,6},{8,11},{9,8},{10,9... | collective-permute-start | bytes 786440 | tf_op jit(solution)/shard_map/ppermute | solution.py:541
  215.0 29.2 %all-to-all-start.3 = ((f32[32,48,128]{2,1,0:T(8,128)}), f32[32,48,128]{2,1,0:T(8,128)S(1)}, u32[]{:S(2)}, u32[]{:S(2)}) async-start(f32[32,48,128]{2,1,0:T(8,128)} %get-tuple-element.101), calls=%async_computation.3 | async-start | bytes 1572864 | tf_op jit(solution)/shard_map/all_to_all | solution.py:559
  (6 other events, 17.9 us)

commit v6 on v5

--- a/solution.py
+++ b/solution.py
@@ -13,6 +13,9 @@
 BANKS = 4
 QUARTERS = 4
 SPARE = 1536
+BESIDE, OPPOSITE, HOME = range(3)
+KINDS = 3
+PARTS = 8
 
 lam_low = 0.05
 lam_high = 2.0
@@ -249,11 +252,12 @@
     over = lax.broadcasted_iota(jnp.int32, (groups, groups), 1)
     same = lax.shift_right_logical(down, 3) == lax.shift_right_logical(over, 3)
     above = jnp.where(same & (over < down), 1.0, 0.0).astype(jnp.bfloat16)
-    late = lax.shift_right_logical(s, 9) == lax.rem(lane[0] + 2, 4)
-    region = (lax.shift_right_logical(row, 3) & 1) * 2 * room
-    where = jnp.zeros_like(row) + 4 * room
-    for kind in range(2):
-        counted = away & live & (late if kind else ~late)
+    apart = (lax.shift_right_logical(s, 9) - lane[0]) & 3
+    kinds = jnp.where(apart == 0, HOME, jnp.where(apart == 2, OPPOSITE, BESIDE))
+    region = (lax.shift_right_logical(row, 3) & 1) * KINDS * room
+    where = jnp.zeros_like(row) + 2 * KINDS * room
+    for kind in range(KINDS):
+        counted = away & live & (kinds == kind)
         flags = jnp.where(counted, 1.0, 0.0).astype(jnp.bfloat16)
         within = jnp.dot(flags, before, preferred_element_type=jnp.float32)
         total = jnp.dot(flags, ones, preferred_element_type=jnp.float32)
@@ -281,8 +285,8 @@
     lax.fori_loop(0, lax.div(live + 7, 8), step, 0)
     nothing = jnp.int32(SPARE - 2048) << 21
     for c in range(2):
-        for kind in range(2):
-            end = (2 * c + kind) * room + totals[kind * QUARTERS + first + c, 0]
+        for kind in range(KINDS):
+            end = (KINDS * c + kind) * room + totals[kind * QUARTERS + first + c, 0]
             for u in range(UNROLL):
                 code[end + u] = nothing
 
@@ -300,9 +304,9 @@
     quarter = mass.shape[0] // QUARTERS
     many = len(banks)
     for h, code in enumerate(lists):
-        room = (code.shape[0] - LANES) // 4
+        room = (code.shape[0] - LANES) // (2 * KINDS)
         for c in range(2):
-            start = (2 * c + kind) * room
+            start = (KINDS * c + kind) * room
             base = (2 * h + c) * quarter
 
             def step(i, _):
@@ -346,25 +350,24 @@
         place(lane, lanes, s, shares[s], field)
 
 
-def pack(lists, field, out, width):
-    def step(c, _):
-        for r in range(width):
-            out[c, pl.ds(r, 1), :] = field[pl.ds(lists[c * width + r], 1), :]
+def pack(lists, field, out, width, part):
+    per = out.shape[0] // PARTS
+
+    def step(i, _):
+        for c in range(per):
+            for r in range(width):
+                out[i * per + c, pl.ds(r, 1), :] = field[pl.ds(lists[(i * per + c) * width + r], 1), :]
+        part(i).start()
         return 0
 
-    lax.fori_loop(0, out.shape[0], step, 0)
-
-
-def field_kernel(lanes, lane, code_a, code_b, totals, mass, lists, *refs):
-    shares, (kept, sent), refs = refs[:lanes], refs[lanes : lanes + 2], refs[lanes + 2 :]
-    field, out, sums, leave_field, leave, leave_sums = refs[:6]
-    banks = refs[6:]
-    blocks, width, _ = out.shape
-    assemble(lane, lanes, shares, field)
-    keep = pltpu.make_async_copy(field, kept, leave_field)
-    keep.start()
+    lax.fori_loop(0, PARTS, step, 0)
+
+
+def early_field_kernel(lanes, lane, code_a, code_b, totals, mass, home, opposite, out, field, *banks):
+    place(lane, lanes, 0, home, field)
+    place(lane, lanes, 2, opposite, field)
     clear(banks)
-    for kind in range(2):
+    for kind in (HOME, OPPOSITE):
         far_rows(
             kind,
             (code_a, code_b),
@@ -374,6 +377,31 @@
             far_slot,
             banks,
         )
+    total = banks[0][...]
+    for a in banks[1:]:
+        total = total + a[...]
+    out[...] = total
+
+
+def field_kernel(lanes, lane, code_a, code_b, totals, mass, lists, early, *refs):
+    shares, (kept, sent), refs = refs[:lanes], refs[lanes : lanes + 2], refs[lanes + 2 :]
+    field, out, sums, leave_field, leave, leave_sums = refs[:6]
+    banks = refs[6:]
+    blocks, width, _ = out.shape
+    assemble(lane, lanes, shares, field)
+    keep = pltpu.make_async_copy(field, kept, leave_field)
+    keep.start()
+    banks[0][...] = early[...]
+    clear(banks[1:])
+    far_rows(
+        BESIDE,
+        (code_a, code_b),
+        totals,
+        mass,
+        lambda given: field[pl.ds(far_source(given), 1), :],
+        far_slot,
+        banks,
+    )
     for c in range(blocks):
         at = slice(c * width, (c + 1) * width)
         total = banks[0][at, :]
@@ -382,12 +410,17 @@
         sums[c] = total
     more = pltpu.make_async_copy(sums, sent.at[:, width:, :], leave_sums)
     more.start()
-    pack(lists, field, out, width)
-    go = pltpu.make_async_copy(out, sent.at[:, :width, :], leave)
-    go.start()
+    per = blocks // PARTS
+
+    def part(i):
+        at = pl.ds(i * per, per)
+        return pltpu.make_async_copy(out.at[at], sent.at[at, :width, :], leave.at[i])
+
+    pack(lists, field, out, width, part)
     keep.wait()
     more.wait()
-    go.wait()
+    for i in range(PARTS):
+        part(i).wait()
 
 
 def near_kernel(count, order, heavy, kept, out, field, come, *banks):
@@ -441,7 +474,7 @@
     first.wait()
     flat = halo.reshape((blocks + 1) * width, LANES)
     far_rows(
-        1,
+        OPPOSITE,
         (code_a, code_b),
         totals,
         mass,
@@ -459,13 +492,19 @@
 
 
 def join_kernel(lanes, lane, code_a, code_b, totals, mass, listed, near, halo, ret_both, *refs):
-    outs, hot, banks = refs[:3], refs[3], refs[4:]
+    outs, hot, banks = refs[:2], refs[2], refs[3:]
     share = outs[0].shape[0]
-    banks[0][...] = near[...]
-    clear(banks[1:])
+    spots = []
+    for s in (1, 3):
+        q = lax.rem(lane[0] + s, lanes)
+        at = pl.ds(pl.multiple_of(q * share, share), share)
+        banks[0][at, :] = near[at, :]
+        for a in banks[1:]:
+            a[at, :] = jnp.zeros((share, LANES), jnp.float32)
+        spots.append((q, at))
     flat = halo.reshape(halo.shape[0] * halo.shape[1], LANES)
     far_rows(
-        0,
+        BESIDE,
         (code_a, code_b),
         totals,
         mass,
@@ -473,27 +512,45 @@
         far_source,
         banks,
     )
-    for s, out in zip((1, 3, 0), outs):
-        q = lax.rem(lane[0] + s, lanes)
-        at = pl.ds(pl.multiple_of(q * share, share), share)
+    for (q, at), out in zip(spots, outs):
         total = banks[0][at, :]
         for a in banks[1:]:
             total = total + a[at, :]
-        out[...] = total + listed_rows(q, share, listed, ret_both, hot) if s else total
-
-
-def home_kernel(lane, listed, part, ret_both, out, hot):
-    out[...] = part[...] + listed_rows(lane[0], out.shape[0], listed, ret_both, hot)
+        out[...] = total + listed_rows(q, share, listed, ret_both, hot)
+
+
+def home_kernel(lane, code_a, code_b, totals, mass, listed, near, halo, ret_both, out, hot, *banks):
+    share = out.shape[0]
+    clear(banks)
+    flat = halo.reshape(halo.shape[0] * halo.shape[1], LANES)
+    far_rows(
+        HOME,
+        (code_a, code_b),
+        totals,
+        mass,
+        lambda given: flat[pl.ds(far_slot(given), 1), :],
+        lambda given: far_source(given) & (share - 1),
+        banks,
+    )
+    total = near[pl.ds(pl.multiple_of(lane[0] * share, share), share), :]
+    for a in banks:
+        total = total + a[...]
+    out[...] = total + listed_rows(lane[0], share, listed, ret_both, hot)
 
 
 def solution_kernel(lane, lists, *refs):
     lanes = 4
     shares, (field, sent, out, leave) = refs[:lanes], refs[lanes:]
     assemble(lane, lanes, shares, field)
-    pack(lists, field, out, out.shape[1])
-    go = pltpu.make_async_copy(out, sent, leave)
-    go.start()
-    go.wait()
+    per = out.shape[0] // PARTS
+
+    def part(i):
+        at = pl.ds(i * per, per)
+        return pltpu.make_async_copy(out.at[at], sent.at[at], leave.at[i])
+
+    pack(lists, field, out, out.shape[1], part)
+    for i in range(PARTS):
+        part(i).wait()
 
 
 def near_gap_kernel(count, order, field, gaps, more):
@@ -614,12 +671,12 @@
     late = lax.optimization_barrier((edge_count, source_rows, target_rows, edge_weight, *sides))
     begin, source_late, target_late, weight_late, *sides = late
     quarter = edges // QUARTERS
-    room = quarter + LANES // 4
+    room = quarter + LANES // 2
     per_edge = ((groups, LANES), i32, VMEM)
     per_edge_f32 = ((groups, LANES), f32, VMEM)
     coded = list(call(
         functools.partial(edge_code_kernel, rows, slots, room),
-        [per_edge, per_edge, ((2 * QUARTERS, LANES), i32, VMEM), per_edge_f32, per_edge, per_edge_f32, per_edge, per_edge],
+        [per_edge, per_edge, ((4 * QUARTERS, LANES), i32, VMEM), per_edge_f32, per_edge, per_edge_f32, per_edge, per_edge],
         [SMEM] * 2 + [VMEM] * 3,
         [],
         "edge_code",
@@ -630,7 +687,7 @@
     def far_list(first, count):
         return call(
             functools.partial(far_list_kernel, first, room),
-            [((4 * room + LANES,), i32, SMEM)],
+            [((2 * KINDS * room + LANES,), i32, SMEM)],
             [SMEM] * 4,
             [],
             "far_list",
@@ -655,16 +712,24 @@
     solution_share = direction
     for keep, push in pairs:
         shares = to_all(direction, lanes)
+        early = call(
+            functools.partial(early_field_kernel, lanes),
+            [((slots + 8, LANES), f32, VMEM)],
+            [SMEM] * 5 + [VMEM] * 2,
+            [pltpu.VMEM((rows, LANES), f32)] + [pltpu.VMEM((slots + 8, LANES), f32)] * BANKS,
+            "early_field",
+            moved=2**25,
+        )(lane, *far, shares[0], shares[2])[0]
         field, message = call(
             functools.partial(field_kernel, lanes),
             [((rows, LANES), f32, HBM), ((blocks, 2 * width, LANES), f32, HBM)],
-            [SMEM] * 6 + [VMEM] * lanes,
+            [SMEM] * 6 + [VMEM] * (1 + lanes),
             [pltpu.VMEM((rows, LANES), f32)]
             + [pltpu.VMEM((blocks, width, LANES), f32)] * 2
-            + [pltpu.SemaphoreType.DMA] * 3
+            + [pltpu.SemaphoreType.DMA, pltpu.SemaphoreType.DMA((PARTS,)), pltpu.SemaphoreType.DMA]
             + [pltpu.VMEM((slots + 8, LANES), f32)] * BANKS,
             "field",
-        )(lane, *far, lists, *shares)
+        )(lane, *far, lists, early, *shares)
         arrived = across(message)
         near = call(
             near_kernel,
@@ -683,9 +748,9 @@
             + [pltpu.VMEM((share, LANES), f32)] * BANKS,
             "late_join",
         )(lane, *far, listed, near, arrived)
-        one, three, home = call(
+        one, three = call(
             functools.partial(join_kernel, lanes),
-            [((share, LANES), f32, VMEM)] * 3,
+            [((share, LANES), f32, VMEM)] * 2,
             [SMEM] * 5 + [VMEM] * 4,
             [pltpu.VMEM((share, slots), bf16)] + [pltpu.VMEM((rows, LANES), f32)] * BANKS,
             "join",
@@ -694,11 +759,11 @@
         home = call(
             home_kernel,
             [((share, LANES), f32, VMEM)],
-            [SMEM] + [VMEM] * 3,
-            [pltpu.VMEM((share, slots), bf16)],
+            [SMEM] * 5 + [VMEM] * 4,
+            [pltpu.VMEM((share, slots), bf16)] + [pltpu.VMEM((share, LANES), f32)] * BANKS,
             "home",
             moved=2**25,
-        )(lane, listed, home, ret_both)[0]
+        )(lane, *far, listed, near, halo, ret_both)[0]
         two = moved_by(two, 2, lanes)
         two, one, three = lax.optimization_barrier((two, one, three))
         flows = (home + two) + (moved_by(one, 1, lanes) + moved_by(three, 3, lanes))
@@ -709,7 +774,7 @@
         solution_kernel,
         [((rows, LANES), f32, VMEM), ((blocks, width, LANES), f32, HBM)],
         [SMEM] * 2 + [VMEM] * lanes,
-        [pltpu.VMEM((blocks, width, LANES), f32), pltpu.SemaphoreType.DMA],
+        [pltpu.VMEM((blocks, width, LANES), f32), pltpu.SemaphoreType.DMA((PARTS,))],
         "solution_rows",
     )(lane, lists, *to_all(solution_share, lanes))
     halo = across(message)

time: 249 us -> 247 us (level)
  Pallas kernels: 73.1 us -> 83.4 us
  waiting for transfers between devices: 86.7 us -> 80.2 us
  starting transfers between devices: 76.6 us -> 70.2 us
    pallas_call x4 -> x6, Pallas kernels: 7.06 us -> 18 us  [the longest x2 6.33 us: far_list(): call(functools.partial(far_list_kernel, first, room), [((2 * KINDS * room...]
    ppermute x18, waiting for transfers between devices: 40.4 us -> 33.9 us  [moved_by(): lax.ppermute(x, 'edg', [(i, (i + shift) % lanes) for i in range(lanes)])]
    all_to_all x4, starting transfers between devices: 49 us -> 45.6 us  [across(): return lax.all_to_all(x, 'vtx', split_axis=0, concat_axis=0, tiled=True)]
    ppermute x18, starting transfers between devices: 27.7 us -> 24.6 us  [moved_by(): lax.ppermute(x, 'edg', [(i, (i + shift) % lanes) for i in range(lanes)])]
  transfers between devices with their start and end apart: 22 -> 22, of which waited for: 17 -> 15; matrix products, arithmetic and copies ran while one was open for 0% -> 0% of each run, Pallas kernels for 16% -> 21%
where the time goes in v6:
time: 247 us; the launch traced here: 245 us
  Pallas kernels  83.4 us (34%)
  waiting for transfers between devices  80.2 us (32%)
  starting transfers between devices  70.2 us (28%)
  local copies, waits for them, and re-layouts  5.06 us (2%)
  other arithmetic  4.19 us (2%)
    all_to_all x4, waiting for transfers between devices, across(): return lax.all_to_all(x, 'vtx', split_axis=0, concat_axis=0, tiled=True)  46.3 us
    all_to_all x4, starting transfers between devices, across(): return lax.all_to_all(x, 'vtx', split_axis=0, concat_axis=0, tiled=True)  45.6 us
    ppermute x18, waiting for transfers between devices, moved_by(): lax.ppermute(x, 'edg', [(i, (i + shift) % lanes) for i in range(lanes)])  33.9 us
    ppermute x18, starting transfers between devices, moved_by(): lax.ppermute(x, 'edg', [(i, (i + shift) % lanes) for i in range(lanes)])  24.6 us
    pallas_call x1, Pallas kernels, local(): call(own_side_kernel, [((rows, LANES), f32, HBM), ((rows // LANES, LANES)...  12 us
    pallas_call x2, Pallas kernels, local(): call(functools.partial(field_kernel, lanes), [((rows, LANES), f32, HBM),...  9.9 us
    pallas_call x2, Pallas kernels, local(): call(near_kernel, [((rows, LANES), f32, VMEM)], [SMEM] * 3 + [HBM], [pltp...  9.35 us
    pallas_call x2, Pallas kernels, local(): call(functools.partial(join_kernel, lanes), [((share, LANES), f32, VMEM)]...  7.75 us
  transfers between devices with their start and end apart: 22, of which 15 were waited for; matrix products, arithmetic and copies ran while one was open for 0% of the time, Pallas kernels for 21%

profile of v6, /device:TPU:1, one launch (start us, length us, event | category | flops | bytes accessed | tf_op | source)
XLA Modules:
  0.0 244.9 jit_solution(1552605229543486801)
XLA Ops:
  3.9 6.0 %halo_side.1 = f32[32,56,128]{2,1,0:T(8,128)} custom-call(f32[4096,128]{1,0:T(8,128)S(1)} %convert_multiply_fusion.terms, s32[32,128]{1,0:T(8,128)S(1)} %bitcast.42, f32[32,128]{1,0:T(8,128)S(1)} %get-tuple-element.102.weight), custom_call_target="tpu_custom_call" | custom-call | flops 3221225472 | bytes 4194304 | tf_op jit(solution)/shard_map/halo_side/pallas_call | solution.py:642
  9.9 8.6 %all-to-all-start = ((f32[32,56,128]{2,1,0:T(8,128)}), f32[32,56,128]{2,1,0:T(8,128)S(1)}, u32[]{:S(2)}, u32[]{:S(2)}) async-start(f32[32,56,128]{2,1,0:T(8,128)} %halo_side.1), calls=%async_computation | async-start | bytes 1835008 | tf_op jit(solution)/shard_map/all_to_all | solution.py:616
  18.6 12.0 %own_side.1 = (f32[2048,128]{1,0:T(8,128)}, f32[16,128]{1,0:T(8,128)S(1)}) custom-call(f32[4096,128]{1,0:T(8,128)S(1)} %convert_multiply_fusion.terms, s32[32,128]{1,0:T(8,128)S(1)} %bitcast.45, s32[32,128]{1,0:T(8,128)S(1)} %bitcast.43, f32[32,128]{1,0:T(8,128)S(1)} %get-tuple-element.102.weight), custom_call_target="tpu_custom_call" | custom-call | flops 4294967296 | bytes 4194304 | tf_op jit(solution)/shard_map/own_side/pallas_call | solution.py:652
  30.7 3.6 %all-to-all-done.returned = f32[32,56,128]{2,1,0:T(8,128)S(1)} async-done(((f32[32,56,128]{2,1,0:T(8,128)}), f32[32,56,128]{2,1,0:T(8,128)S(1)}, u32[]{:S(2)}, u32[]{:S(2)}) %all-to-all-start) | async-done | bytes 917536 | tf_op jit(solution)/shard_map/all_to_all | solution.py:616
  35.5 4.0 %side_join.1 = (f32[520,128]{1,0:T(8,128)S(1)}, f32[520,128]{1,0:T(8,128)S(1)}, f32[520,128]{1,0:T(8,128)S(1)}, f32[520,128]{1,0:T(8,128)S(1)}) custom-call(s32[1]{0:T(128)} %bitcast.lane, f32[32,56,128]{2,1,0:T(8,128)S(1)} %all-to-all-done.returned, s32[12,128]{1,0:T(8,128)S(1)} %reshape_reshape_squeeze.3.listed, s32[32,128]{1,0:T(8,128)S(1)} %pad.4.padded, ...), custom_call_target="tpu_custom_call" | custom-call | flops 1610612736 | bytes 4194304 | tf_op jit(solution)/shard_map/side_join/pallas_call | solution.py:661
  45.7 4.0 %far_list.2.code_a = s32[6656]{0:T(1024)S(1)} custom-call(s32[1]{0:T(128)} %copy.9.count, s32[4096]{0:T(1024)S(1)} %bitcast.36, s32[4096]{0:T(1024)S(1)} %bitcast.38, s32[16,128]{1,0:T(8,128)S(1)} %get-tuple-element.66.totals), custom_call_target="tpu_custom_call" | custom-call | bytes 33554432 | tf_op jit(solution)/shard_map/far_list/pallas_call | solution.py:688
  49.8 6.6 %collective-permute-done.1 = f32[520,128]{1,0:T(8,128)S(1)} collective-permute-done((f32[520,128]{1,0:T(8,128)S(1)}, f32[520,128]{1,0:T(8,128)S(1)}, u32[]{:S(2)}, u32[]{:S(2)}) %collective-permute-start.1) | collective-permute-done | bytes 266272 | tf_op jit(solution)/shard_map/ppermute | solution.py:598
  68.5 4.3 %collective-permute-done.4.refs_1_ = f32[512,128]{1,0:T(8,128)S(1)} collective-permute-done((f32[512,128]{1,0:T(8,128)S(1)}, f32[512,128]{1,0:T(8,128)S(1)}, u32[]{:S(2)}, u32[]{:S(2)}) %collective-permute-start.4) | collective-permute-done | bytes 262176 | tf_op jit(solution)/shard_map/ppermute | solution.py:598
  72.8 5.0 %field.2 = (f32[2048,128]{1,0:T(8,128)}, f32[32,96,128]{2,1,0:T(8,128)}) custom-call(s32[1]{0:T(128)} %bitcast.lane, s32[6656]{0:T(1024)S(1)} %far_list.2.code_a, s32[6656]{0:T(1024)S(1)} %far_list.3.code_b, s32[16,128]{1,0:T(8,128)S(1)} %get-tuple-element.66.totals, f32[4096]{0:T(1024)S(1)} %bitcast.22, s32[1536]{0:T(1024)S(1)} %reshape_squeeze.3.lists, ...), custom_call_target="tpu_custom_call" | custom-call | bytes 4194304 | tf_op jit(solution)/shard_map/field/pallas_call | solution.py:723
  77.8 8.0 %all-to-all-start.1 = ((f32[32,96,128]{2,1,0:T(8,128)}), f32[32,96,128]{2,1,0:T(8,128)S(1)}, u32[]{:S(2)}, u32[]{:S(2)}) async-start(f32[32,96,128]{2,1,0:T(8,128)} %get-tuple-element.75), calls=%async_computation.1 | async-start | bytes 3145728 | tf_op jit(solution)/shard_map/all_to_all | solution.py:616
  87.0 4.7 %near.2 = f32[2048,128]{1,0:T(8,128)S(1)} custom-call(s32[1]{0:T(128)} %copy.9.count, s32[4096]{0:T(1024)S(1)} %bitcast.31, f32[4096]{0:T(1024)S(1)} %bitcast.33, f32[2048,128]{1,0:T(8,128)S(1)} %copy-done.1), custom_call_target="tpu_custom_call" | custom-call | bytes 33554432 | tf_op jit(solution)/shard_map/near/pallas_call | solution.py:734
  91.7 16.3 %all-to-all-done.1.arrived = f32[32,96,128]{2,1,0:T(8,128)S(1)} async-done(((f32[32,96,128]{2,1,0:T(8,128)}), f32[32,96,128]{2,1,0:T(8,128)S(1)}, u32[]{:S(2)}, u32[]{:S(2)}) %all-to-all-start.1) | async-done | bytes 1572896 | tf_op jit(solution)/shard_map/all_to_all | solution.py:616
  111.5 3.9 %join.2 = (f32[512,128]{1,0:T(8,128)S(1)}, f32[512,128]{1,0:T(8,128)S(1)}) custom-call(s32[1]{0:T(128)} %bitcast.lane, s32[6656]{0:T(1024)S(1)} %far_list.2.code_a, s32[6656]{0:T(1024)S(1)} %far_list.3.code_b, s32[16,128]{1,0:T(8,128)S(1)} %get-tuple-element.66.totals, f32[4096]{0:T(1024)S(1)} %bitcast.24, s32[12,128]{1,0:T(8,128)S(1)} %reshape_reshape_squeeze.3.listed, ...), custom_call_target="tpu_custom_call" | custom-call | bytes 33554432 | tf_op jit(solution)/shard_map/join/pallas_call | solution.py:751
  115.4 3.5 %collective-permute-done.6 = f32[512,128]{1,0:T(8,128)S(1)} collective-permute-done((f32[512,128]{1,0:T(8,128)S(1)}, f32[512,128]{1,0:T(8,128)S(1)}, u32[]{:S(2)}, u32[]{:S(2)}) %collective-permute-start.6) | collective-permute-done | bytes 262176 | tf_op jit(solution)/shard_map/ppermute | solution.py:598
  138.8 5.0 %field.3 = (f32[2048,128]{1,0:T(8,128)}, f32[32,96,128]{2,1,0:T(8,128)}) custom-call(s32[1]{0:T(128)} %bitcast.lane, s32[6656]{0:T(1024)S(1)} %far_list.2.code_a, s32[6656]{0:T(1024)S(1)} %far_list.3.code_b, s32[16,128]{1,0:T(8,128)S(1)} %get-tuple-element.66.totals, f32[4096]{0:T(1024)S(1)} %bitcast.27, s32[1536]{0:T(1024)S(1)} %reshape_squeeze.3.lists, ...), custom_call_target="tpu_custom_call" | custom-call | bytes 4194304 | tf_op jit(solution)/shard_map/field/pallas_call | solution.py:723
  143.7 14.7 %all-to-all-start.2 = ((f32[32,96,128]{2,1,0:T(8,128)}), f32[32,96,128]{2,1,0:T(8,128)S(1)}, u32[]{:S(2)}, u32[]{:S(2)}) async-start(f32[32,96,128]{2,1,0:T(8,128)} %get-tuple-element.85), calls=%async_computation.2 | async-start | bytes 3145728 | tf_op jit(solution)/shard_map/all_to_all | solution.py:616
  159.7 4.7 %near.3 = f32[2048,128]{1,0:T(8,128)S(1)} custom-call(s32[1]{0:T(128)} %copy.9.count, s32[4096]{0:T(1024)S(1)} %bitcast.32, f32[4096]{0:T(1024)S(1)} %bitcast.34, f32[2048,128]{1,0:T(8,128)S(1)} %copy-done), custom_call_target="tpu_custom_call" | custom-call | bytes 33554432 | tf_op jit(solution)/shard_map/near/pallas_call | solution.py:734
  164.4 16.3 %all-to-all-done.2.arrived = f32[32,96,128]{2,1,0:T(8,128)S(1)} async-done(((f32[32,96,128]{2,1,0:T(8,128)}), f32[32,96,128]{2,1,0:T(8,128)S(1)}, u32[]{:S(2)}, u32[]{:S(2)}) %all-to-all-start.2) | async-done | bytes 1572896 | tf_op jit(solution)/shard_map/all_to_all | solution.py:616
  184.6 3.9 %join.3 = (f32[512,128]{1,0:T(8,128)S(1)}, f32[512,128]{1,0:T(8,128)S(1)}) custom-call(s32[1]{0:T(128)} %bitcast.lane, s32[6656]{0:T(1024)S(1)} %far_list.2.code_a, s32[6656]{0:T(1024)S(1)} %far_list.3.code_b, s32[16,128]{1,0:T(8,128)S(1)} %get-tuple-element.66.totals, f32[4096]{0:T(1024)S(1)} %bitcast.29, s32[12,128]{1,0:T(8,128)S(1)} %reshape_reshape_squeeze.3.listed, ...), custom_call_target="tpu_custom_call" | custom-call | bytes 33554432 | tf_op jit(solution)/shard_map/join/pallas_call | solution.py:751
  198.4 3.7 %collective-permute-start.16 = (f32[512,128]{1,0:T(8,128)S(1)}, f32[512,128]{1,0:T(8,128)S(1)}, u32[]{:S(2)}, u32[]{:S(2)}) collective-permute-start(f32[512,128]{1,0:T(8,128)S(1)} %add_add_fusion.1.refs_0_), channel_id=1, source_target_pairs={{0,2},{1,3},{2,0},{3,1},{4,6},{5,7},{6,4},{7,5},{8,10},{9,11},{10,... | collective-permute-start | bytes 786440 | tf_op jit(solution)/shard_map/ppermute | solution.py:598
  204.7 4.9 %collective-permute-done.16.refs_2_ = f32[512,128]{1,0:T(8,128)S(1)} collective-permute-done((f32[512,128]{1,0:T(8,128)S(1)}, f32[512,128]{1,0:T(8,128)S(1)}, u32[]{:S(2)}, u32[]{:S(2)}) %collective-permute-start.16) | collective-permute-done | bytes 262176 | tf_op jit(solution)/shard_map/ppermute | solution.py:598
  209.6 3.6 %solution_rows.1 = (f32[2048,128]{1,0:T(8,128)}, f32[32,48,128]{2,1,0:T(8,128)}) custom-call(s32[1]{0:T(128)} %bitcast.lane, s32[1536]{0:T(1024)S(1)} %reshape_squeeze.3.lists, f32[512,128]{1,0:T(8,128)S(1)} %add_add_fusion.1.refs_0_, f32[512,128]{1,0:T(8,128)S(1)} %collective-permute-done.15.refs_1_, f32[512,128]{1,0:T(8,128)S(1)} %collective-permute-done.16.refs_2_, ...), custom_call_target="tpu_custom_call" | custom-call | bytes 4194304 | tf_op jit(solution)/shard_map/solution_rows/pallas_call | solution.py:773
  213.3 14.3 %all-to-all-start.3 = ((f32[32,48,128]{2,1,0:T(8,128)}), f32[32,48,128]{2,1,0:T(8,128)S(1)}, u32[]{:S(2)}, u32[]{:S(2)}) async-start(f32[32,48,128]{2,1,0:T(8,128)} %get-tuple-element.97), calls=%async_computation.3 | async-start | bytes 1572864 | tf_op jit(solution)/shard_map/all_to_all | solution.py:616
  231.6 10.1 %all-to-all-done.3.arrived = f32[32,48,128]{2,1,0:T(8,128)S(1)} async-done(((f32[32,48,128]{2,1,0:T(8,128)}), f32[32,48,128]{2,1,0:T(8,128)S(1)}, u32[]{:S(2)}, u32[]{:S(2)}) %all-to-all-start.3) | async-done | bytes 786464 | tf_op jit(solution)/shard_map/all_to_all | solution.py:616
  (69 shorter events, 71.4 us)
Async XLA Ops:
  3.9 14.6 %copy-start.7 = (s32[1,32,48]{2,1,0:T(8,128)S(1)}, s32[1,32,48]{2,1,0:T(8,128)}, u32[]{:S(2)}) copy-start(s32[1,32,48]{2,1,0:T(8,128)} %param.12) | copy-start | bytes 18436
  3.9 14.7 %copy-start.5 = (s32[4096]{0:T(1024)S(1)}, s32[4096]{0:T(1024)}, u32[]{:S(2)}) copy-start(s32[4096]{0:T(1024)} %param.10) | copy-start | bytes 49156
  9.9 24.4 %all-to-all-start = ((f32[32,56,128]{2,1,0:T(8,128)}), f32[32,56,128]{2,1,0:T(8,128)S(1)}, u32[]{:S(2)}, u32[]{:S(2)}) async-start(f32[32,56,128]{2,1,0:T(8,128)} %halo_side.1), calls=%async_computation | async-start | bytes 1835008 | tf_op jit(solution)/shard_map/all_to_all | solution.py:616
  39.6 10.3 %collective-permute-start = (f32[520,128]{1,0:T(8,128)S(1)}, f32[520,128]{1,0:T(8,128)S(1)}, u32[]{:S(2)}, u32[]{:S(2)}) collective-permute-start(f32[520,128]{1,0:T(8,128)S(1)} %get-tuple-element.58), channel_id=1, source_target_pairs={{0,1},{1,2},{2,3},{3,0},{4,5},{5,6},{6,7},{7,4},{8,9},{9,10},{10,1... | collective-permute-start | bytes 798728 | tf_op jit(solution)/shard_map/ppermute | solution.py:598
  41.3 15.1 %collective-permute-start.1 = (f32[520,128]{1,0:T(8,128)S(1)}, f32[520,128]{1,0:T(8,128)S(1)}, u32[]{:S(2)}, u32[]{:S(2)}) collective-permute-start(f32[520,128]{1,0:T(8,128)S(1)} %get-tuple-element.59), channel_id=1, source_target_pairs={{0,2},{1,3},{2,0},{3,1},{4,6},{5,7},{6,4},{7,5},{8,10},{9,11},{10,... | collective-permute-start | bytes 798728 | tf_op jit(solution)/shard_map/ppermute | solution.py:598
  44.5 11.8 %collective-permute-start.2 = (f32[520,128]{1,0:T(8,128)S(1)}, f32[520,128]{1,0:T(8,128)S(1)}, u32[]{:S(2)}, u32[]{:S(2)}) collective-permute-start(f32[520,128]{1,0:T(8,128)S(1)} %get-tuple-element.60), channel_id=1, source_target_pairs={{0,3},{1,0},{2,1},{3,2},{4,7},{5,4},{6,5},{7,6},{8,11},{9,8},{10,9... | collective-permute-start | bytes 798728 | tf_op jit(solution)/shard_map/ppermute | solution.py:598
  57.4 8.2 %collective-permute-start.3 = (f32[512,128]{1,0:T(8,128)S(1)}, f32[512,128]{1,0:T(8,128)S(1)}, u32[]{:S(2)}, u32[]{:S(2)}) collective-permute-start(f32[512,128]{1,0:T(8,128)S(1)} %slice_multiply_fusion.home.refs_0_), channel_id=1, source_target_pairs={{0,2},{1,3},{2,0},{3,1},{4,6},{5,7},{6,4},{7,5},{8,10},{9,11},{10,... | collective-permute-start | bytes 786440 | tf_op jit(solution)/shard_map/ppermute | solution.py:598
  59.1 13.7 %collective-permute-start.4 = (f32[512,128]{1,0:T(8,128)S(1)}, f32[512,128]{1,0:T(8,128)S(1)}, u32[]{:S(2)}, u32[]{:S(2)}) collective-permute-start(f32[512,128]{1,0:T(8,128)S(1)} %slice_multiply_fusion.home.refs_0_), channel_id=1, source_target_pairs={{0,1},{1,2},{2,3},{3,0},{4,5},{5,6},{6,7},{7,4},{8,9},{9,10},{10,1... | collective-permute-start | bytes 786440 | tf_op jit(solution)/shard_map/ppermute | solution.py:598
  60.6 12.2 %collective-permute-start.5 = (f32[512,128]{1,0:T(8,128)S(1)}, f32[512,128]{1,0:T(8,128)S(1)}, u32[]{:S(2)}, u32[]{:S(2)}) collective-permute-start(f32[512,128]{1,0:T(8,128)S(1)} %slice_multiply_fusion.home.refs_0_), channel_id=1, source_target_pairs={{0,3},{1,0},{2,1},{3,2},{4,7},{5,4},{6,5},{7,6},{8,11},{9,8},{10,9... | collective-permute-start | bytes 786440 | tf_op jit(solution)/shard_map/ppermute | solution.py:598
  77.8 30.2 %all-to-all-start.1 = ((f32[32,96,128]{2,1,0:T(8,128)}), f32[32,96,128]{2,1,0:T(8,128)S(1)}, u32[]{:S(2)}, u32[]{:S(2)}) async-start(f32[32,96,128]{2,1,0:T(8,128)} %get-tuple-element.75), calls=%async_computation.1 | async-start | bytes 3145728 | tf_op jit(solution)/shard_map/all_to_all | solution.py:616
  111.3 7.6 %collective-permute-start.6 = (f32[512,128]{1,0:T(8,128)S(1)}, f32[512,128]{1,0:T(8,128)S(1)}, u32[]{:S(2)}, u32[]{:S(2)}) collective-permute-start(f32[512,128]{1,0:T(8,128)S(1)} %get-tuple-element.78), channel_id=1, source_target_pairs={{0,2},{1,3},{2,0},{3,1},{4,6},{5,7},{6,4},{7,5},{8,10},{9,11},{10,... | collective-permute-start | bytes 786440 | tf_op jit(solution)/shard_map/ppermute | solution.py:598
  118.9 6.4 %collective-permute-start.7 = (f32[512,128]{1,0:T(8,128)S(1)}, f32[512,128]{1,0:T(8,128)S(1)}, u32[]{:S(2)}, u32[]{:S(2)}) collective-permute-start(f32[512,128]{1,0:T(8,128)S(1)} %get-tuple-element.82), channel_id=1, source_target_pairs={{0,1},{1,2},{2,3},{3,0},{4,5},{5,6},{6,7},{7,4},{8,9},{9,10},{10,1... | collective-permute-start | bytes 786440 | tf_op jit(solution)/shard_map/ppermute | solution.py:598
  119.9 5.5 %collective-permute-start.8 = (f32[512,128]{1,0:T(8,128)S(1)}, f32[512,128]{1,0:T(8,128)S(1)}, u32[]{:S(2)}, u32[]{:S(2)}) collective-permute-start(f32[512,128]{1,0:T(8,128)S(1)} %get-tuple-element.83), channel_id=1, source_target_pairs={{0,3},{1,0},{2,1},{3,2},{4,7},{5,4},{6,5},{7,6},{8,11},{9,8},{10,9... | collective-permute-start | bytes 786440 | tf_op jit(solution)/shard_map/ppermute | solution.py:598
  125.6 6.9 %collective-permute-start.9 = (f32[512,128]{1,0:T(8,128)S(1)}, f32[512,128]{1,0:T(8,128)S(1)}, u32[]{:S(2)}, u32[]{:S(2)}) collective-permute-start(f32[512,128]{1,0:T(8,128)S(1)} %get-tuple-element.100.home.refs_0_), channel_id=1, source_target_pairs={{0,2},{1,3},{2,0},{3,1},{4,6},{5,7},{6,4},{7,5},{8,10},{9,11},{10,... | collective-permute-start | bytes 786440 | tf_op jit(solution)/shard_map/ppermute | solution.py:598
  127.2 11.6 %collective-permute-start.10 = (f32[512,128]{1,0:T(8,128)S(1)}, f32[512,128]{1,0:T(8,128)S(1)}, u32[]{:S(2)}, u32[]{:S(2)}) collective-permute-start(f32[512,128]{1,0:T(8,128)S(1)} %get-tuple-element.100.home.refs_0_), channel_id=1, source_target_pairs={{0,1},{1,2},{2,3},{3,0},{4,5},{5,6},{6,7},{7,4},{8,9},{9,10},{10,1... | collective-permute-start | bytes 786440 | tf_op jit(solution)/shard_map/ppermute | solution.py:598
  129.0 9.8 %collective-permute-start.11 = (f32[512,128]{1,0:T(8,128)S(1)}, f32[512,128]{1,0:T(8,128)S(1)}, u32[]{:S(2)}, u32[]{:S(2)}) collective-permute-start(f32[512,128]{1,0:T(8,128)S(1)} %get-tuple-element.100.home.refs_0_), channel_id=1, source_target_pairs={{0,3},{1,0},{2,1},{3,2},{4,7},{5,4},{6,5},{7,6},{8,11},{9,8},{10,9... | collective-permute-start | bytes 786440 | tf_op jit(solution)/shard_map/ppermute | solution.py:598
  143.7 36.9 %all-to-all-start.2 = ((f32[32,96,128]{2,1,0:T(8,128)}), f32[32,96,128]{2,1,0:T(8,128)S(1)}, u32[]{:S(2)}, u32[]{:S(2)}) async-start(f32[32,96,128]{2,1,0:T(8,128)} %get-tuple-element.85), calls=%async_computation.2 | async-start | bytes 3145728 | tf_op jit(solution)/shard_map/all_to_all | solution.py:616
  183.8 7.6 %collective-permute-start.12 = (f32[512,128]{1,0:T(8,128)S(1)}, f32[512,128]{1,0:T(8,128)S(1)}, u32[]{:S(2)}, u32[]{:S(2)}) collective-permute-start(f32[512,128]{1,0:T(8,128)S(1)} %get-tuple-element.88), channel_id=1, source_target_pairs={{0,2},{1,3},{2,0},{3,1},{4,6},{5,7},{6,4},{7,5},{8,10},{9,11},{10,... | collective-permute-start | bytes 786440 | tf_op jit(solution)/shard_map/ppermute | solution.py:598
  191.4 6.4 %collective-permute-start.13 = (f32[512,128]{1,0:T(8,128)S(1)}, f32[512,128]{1,0:T(8,128)S(1)}, u32[]{:S(2)}, u32[]{:S(2)}) collective-permute-start(f32[512,128]{1,0:T(8,128)S(1)} %get-tuple-element.92), channel_id=1, source_target_pairs={{0,1},{1,2},{2,3},{3,0},{4,5},{5,6},{6,7},{7,4},{8,9},{9,10},{10,1... | collective-permute-start | bytes 786440 | tf_op jit(solution)/shard_map/ppermute | solution.py:598
  192.5 5.3 %collective-permute-start.14 = (f32[512,128]{1,0:T(8,128)S(1)}, f32[512,128]{1,0:T(8,128)S(1)}, u32[]{:S(2)}, u32[]{:S(2)}) collective-permute-start(f32[512,128]{1,0:T(8,128)S(1)} %get-tuple-element.93), channel_id=1, source_target_pairs={{0,3},{1,0},{2,1},{3,2},{4,7},{5,4},{6,5},{7,6},{8,11},{9,8},{10,9... | collective-permute-start | bytes 786440 | tf_op jit(solution)/shard_map/ppermute | solution.py:598
  198.2 6.5 %collective-permute-start.15 = (f32[512,128]{1,0:T(8,128)S(1)}, f32[512,128]{1,0:T(8,128)S(1)}, u32[]{:S(2)}, u32[]{:S(2)}) collective-permute-start(f32[512,128]{1,0:T(8,128)S(1)} %add_add_fusion.1.refs_0_), channel_id=1, source_target_pairs={{0,1},{1,2},{2,3},{3,0},{4,5},{5,6},{6,7},{7,4},{8,9},{9,10},{10,1... | collective-permute-start | bytes 786440 | tf_op jit(solution)/shard_map/ppermute | solution.py:598
  198.4 11.2 %collective-permute-start.16 = (f32[512,128]{1,0:T(8,128)S(1)}, f32[512,128]{1,0:T(8,128)S(1)}, u32[]{:S(2)}, u32[]{:S(2)}) collective-permute-start(f32[512,128]{1,0:T(8,128)S(1)} %add_add_fusion.1.refs_0_), channel_id=1, source_target_pairs={{0,2},{1,3},{2,0},{3,1},{4,6},{5,7},{6,4},{7,5},{8,10},{9,11},{10,... | collective-permute-start | bytes 786440 | tf_op jit(solution)/shard_map/ppermute | solution.py:598
  202.1 7.5 %collective-permute-start.17 = (f32[512,128]{1,0:T(8,128)S(1)}, f32[512,128]{1,0:T(8,128)S(1)}, u32[]{:S(2)}, u32[]{:S(2)}) collective-permute-start(f32[512,128]{1,0:T(8,128)S(1)} %add_add_fusion.1.refs_0_), channel_id=1, source_target_pairs={{0,3},{1,0},{2,1},{3,2},{4,7},{5,4},{6,5},{7,6},{8,11},{9,8},{10,9... | collective-permute-start | bytes 786440 | tf_op jit(solution)/shard_map/ppermute | solution.py:598
  213.3 28.5 %all-to-all-start.3 = ((f32[32,48,128]{2,1,0:T(8,128)}), f32[32,48,128]{2,1,0:T(8,128)S(1)}, u32[]{:S(2)}, u32[]{:S(2)}) async-start(f32[32,48,128]{2,1,0:T(8,128)} %get-tuple-element.97), calls=%async_computation.3 | async-start | bytes 1572864 | tf_op jit(solution)/shard_map/all_to_all | solution.py:616
  (6 other events, 17.9 us)

commit v7 on v6

--- a/solution.py
+++ b/solution.py
@@ -92,7 +92,7 @@
     return total[:height] + total[height:]
 
 
-def halo_side_kernel(rows, slots, width, terms, target, weight, sent, both, hot, out, leave):
+def halo_side_kernel(rows, slots, width, terms, target, weight, sent, both, hot, other, out, leave):
     groups = target.shape[0]
     tall = hot.shape[0]
     per = tall // width
@@ -117,17 +117,19 @@
         at = pl.ds(i * per, per)
         return pltpu.make_async_copy(out.at[at], sent.at[at], leave.at[i])
 
-    def chunk(i, _):
-        base = rows + i * tall
+    def build(i):
+        to = (hot, other)[i % 2]
         for k in range(groups):
-            hot[:, k * LANES : (k + 1) * LANES] = one_hot(target[k : k + 1, :], tall, base).astype(jnp.bfloat16)
-        got = halves(jnp.dot(hot[...], both[...], preferred_element_type=jnp.float32))
+            to[:, k * LANES : (k + 1) * LANES] = one_hot(target[k : k + 1, :], tall, rows + i * tall).astype(jnp.bfloat16)
+
+    build(0)
+    for i in range(chunks):
+        if i + 1 < chunks:
+            build(i + 1)
+        got = halves(jnp.dot((hot, other)[i % 2][...], both[...], preferred_element_type=jnp.float32))
         for c in range(per):
             out[i * per + c, :width, :] = -got[c * width : (c + 1) * width]
         part(i).start()
-        return 0
-
-    lax.fori_loop(0, chunks, chunk, 0)
     for i in range(chunks):
         part(i).wait()
 
@@ -171,23 +173,24 @@
         part(i).wait()
 
 
-def scatter_back(ret_both, listed, hot, emit, rows):
-    tall = hot.shape[0]
-    groups = listed.shape[0]
-
-    def chunk(i, _):
-        base = i * tall
-        for k in range(groups):
-            hot[:, k * LANES : (k + 1) * LANES] = one_hot(listed[k : k + 1, :], tall, base).astype(jnp.bfloat16)
-        emit(i, halves(jnp.dot(hot[...], ret_both[...], preferred_element_type=jnp.float32)))
-        return 0
-
-    lax.fori_loop(0, rows // tall, chunk, 0)
+def scatter_back(ret_both, listed, hots, emit, rows):
+    tall = hots[0].shape[0]
+
+    def build(i):
+        to = hots[i % 2]
+        for k in range(listed.shape[0]):
+            to[:, k * LANES : (k + 1) * LANES] = one_hot(listed[k : k + 1, :], tall, i * tall).astype(jnp.bfloat16)
+
+    build(0)
+    for i in range(rows // tall):
+        if (i + 1) * tall < rows:
+            build(i + 1)
+        emit(i, halves(jnp.dot(hots[i % 2][...], ret_both[...], preferred_element_type=jnp.float32)))
 
 
 def side_join_kernel(lane, returned, listed, padded, own, own_degree, *refs):
     lanes = 4
-    outs, (acc, ret_both, hot, landed, arrival, arrival_own) = refs[:lanes], refs[lanes:]
+    outs, (acc, ret_both, hot, other, landed, arrival, arrival_own) = refs[:lanes], refs[lanes:]
     come = pltpu.make_async_copy(returned, landed, arrival)
     come.start()
     mine = pltpu.make_async_copy(own, acc, arrival_own)
@@ -201,11 +204,11 @@
         put_split(ret_both, slice(c * width, (c + 1) * width), landed[c, :width, :])
 
     def emit(i, got):
-        at = pl.ds(pl.multiple_of(i * hot.shape[0], hot.shape[0]), hot.shape[0])
+        at = slice(i * hot.shape[0], (i + 1) * hot.shape[0])
         acc[at, :] = acc[at, :] + got
 
     mine.wait()
-    scatter_back(ret_both, listed, hot, emit, rows)
+    scatter_back(ret_both, listed, (hot, other), emit, rows)
     deg = own_degree[...] + factored(
         4,
         blocks,
@@ -466,11 +469,16 @@
     share = out.shape[0]
     first = pltpu.make_async_copy(arrived.at[:, :width, :], halo.at[:blocks], come_halo)
     second = pltpu.make_async_copy(arrived.at[:, width:, :], ret, come_ret)
+    second.start()
     first.start()
-    second.start()
     halo[blocks] = jnp.zeros((width, LANES), jnp.float32)
     clear(banks)
     q = lax.rem(lane[0] + 2, lanes)
+    second.wait()
+    for c in range(blocks):
+        put_split(ret_both, slice(c * width, (c + 1) * width), ret[c])
+    total = near[pl.ds(pl.multiple_of(q * share, share), share), :]
+    out[...] = total + listed_rows(q, share, listed, ret_both, hot)
     first.wait()
     flat = halo.reshape((blocks + 1) * width, LANES)
     far_rows(
@@ -482,13 +490,10 @@
         lambda given: far_source(given) & (share - 1),
         banks,
     )
-    second.wait()
-    for c in range(blocks):
-        put_split(ret_both, slice(c * width, (c + 1) * width), ret[c])
-    total = near[pl.ds(pl.multiple_of(q * share, share), share), :]
+    total = out[...]
     for a in banks:
         total = total + a[...]
-    out[...] = total + listed_rows(q, share, listed, ret_both, hot)
+    out[...] = total
 
 
 def join_kernel(lanes, lane, code_a, code_b, totals, mass, listed, near, halo, ret_both, *refs):
@@ -579,19 +584,28 @@
     first.wait()
     flat = halo.reshape((blocks + 1) * width, LANES)
 
-    def step(i, _):
-        for u in range(4 * UNROLL):
-            e = i * 4 * UNROLL + u
+    def gather(k):
+        for u in range(LANES):
+            e = k * LANES + u
             taken[pl.ds(e, 1), :] = flat[pl.ds(slot[e], 1), :]
-        return 0
-
-    lax.fori_loop(0, lax.div(count[0] + 4 * UNROLL - 1, 4 * UNROLL), step, 0)
-    for k in range(groups):
-        at = slice(k * LANES, (k + 1) * LANES)
+
+    def finish(k):
+        at = pl.ds(pl.multiple_of(k * LANES, LANES), LANES)
         gap = gaps[at, :] - taken[at, :]
         total = jnp.sum((gap * gap).T, axis=0, keepdims=True)
-        alive = live[k : k + 1, :]
-        out[k : k + 1, :] = jnp.where(alive > 0, total * (alive / LANES), 0.0)
+        alive = live[pl.ds(k, 1), :]
+        out[pl.ds(k, 1), :] = jnp.where(alive > 0, total * (alive / LANES), 0.0)
+
+    def step(k, _):
+        finish(k - 1)
+        gather(k)
+        return 0
+
+    out[...] = jnp.zeros((groups, LANES), jnp.float32)
+    many = lax.div(count[0] + LANES - 1, LANES)
+    gather(0)
+    lax.fori_loop(1, many, step, 0)
+    finish(many - 1)
 
 
 def moved_by(x, shift, lanes):
@@ -643,7 +657,8 @@
         functools.partial(halo_side_kernel, rows, slots, width),
         [((blocks, width + 8, LANES), f32, HBM)],
         [VMEM] * 3,
-        [pltpu.VMEM((edges, 2 * LANES), bf16), pltpu.VMEM((8 * width, edges), bf16)]
+        [pltpu.VMEM((edges, 2 * LANES), bf16)]
+        + [pltpu.VMEM((8 * width, edges), bf16)] * 2
         + [pltpu.VMEM((blocks, width + 8, LANES), f32), pltpu.SemaphoreType.DMA((slots // (8 * width),))],
         "halo_side",
         flops=2 * slots * edges * 2 * LANES,
@@ -662,7 +677,8 @@
         side_join_kernel,
         [((share + 8, LANES), f32, VMEM)] * lanes,
         [SMEM, HBM, VMEM, VMEM, HBM, VMEM],
-        [pltpu.VMEM((rows, LANES), f32), pltpu.VMEM((slots, 2 * LANES), bf16), pltpu.VMEM((256, slots), bf16)]
+        [pltpu.VMEM((rows, LANES), f32), pltpu.VMEM((slots, 2 * LANES), bf16)]
+        + [pltpu.VMEM((256, slots), bf16)] * 2
         + [pltpu.VMEM((blocks, width + 8, LANES), f32)]
         + [pltpu.SemaphoreType.DMA] * 2,
         "side_join",

time: 247 us -> 247 us (level)
  Pallas kernels: 83.4 us -> 131 us
  waiting for transfers between devices: 80.2 us -> 44.8 us
  starting transfers between devices: 70.2 us -> 59.3 us
    all_to_all x4, waiting for transfers between devices: 46.3 us -> 22 us  [across(): return lax.all_to_all(x, 'vtx', split_axis=0, concat_axis=0, tiled=True)]
    pallas_call x2, Pallas kernels: 9.35 us -> 27.7 us  [local(): call(near_kernel, [((rows, LANES), f32, VMEM)], [SMEM] * 3 + [HBM], [pltp...]
    ppermute x18, waiting for transfers between devices: 33.9 us -> 22.8 us  [moved_by(): lax.ppermute(x, 'edg', [(i, (i + shift) % lanes) for i in range(lanes)])]
    all_to_all x4, starting transfers between devices: 45.6 us -> 35.9 us  [across(): return lax.all_to_all(x, 'vtx', split_axis=0, concat_axis=0, tiled=True)]
    pallas_call x1, Pallas kernels: 2.82 us -> 8.68 us  [local(): call(near_gap_kernel, [((edges, LANES), f32, VMEM)], [SMEM] * 2 + [VMEM],...]
    pallas_call x2, Pallas kernels: 6.33 us -> 12 us  [far_list(): call(functools.partial(far_list_kernel, first, room), [((2 * KINDS * room...]
    pallas_call x2, Pallas kernels: 5.82 us -> 9.86 us  [local(): call(functools.partial(early_field_kernel, lanes), [((slots + 8, LANES),...]
    pallas_call x2, Pallas kernels: 9.9 us -> 13.7 us  [local(): call(functools.partial(field_kernel, lanes), [((rows, LANES), f32, HBM),...]
  transfers between devices with their start and end apart: 22 -> 22, of which waited for: 15 -> 13; matrix products, arithmetic and copies ran while one was open for 0% -> 0% of each run, Pallas kernels for 21% -> 36%
where the time goes in v7:
time: 247 us
  Pallas kernels  131 us (53%)
  starting transfers between devices  59.3 us (24%)
  waiting for transfers between devices  44.8 us (18%)
  local copies, waits for them, and re-layouts  5.06 us (2%)
  other arithmetic  4.2 us (2%)
    all_to_all x4, starting transfers between devices, across(): return lax.all_to_all(x, 'vtx', split_axis=0, concat_axis=0, tiled=True)  35.9 us
    pallas_call x2, Pallas kernels, local(): call(near_kernel, [((rows, LANES), f32, VMEM)], [SMEM] * 3 + [HBM], [pltp...  27.7 us
    ppermute x18, starting transfers between devices, moved_by(): lax.ppermute(x, 'edg', [(i, (i + shift) % lanes) for i in range(lanes)])  23.4 us
    ppermute x18, waiting for transfers between devices, moved_by(): lax.ppermute(x, 'edg', [(i, (i + shift) % lanes) for i in range(lanes)])  22.8 us
    all_to_all x4, waiting for transfers between devices, across(): return lax.all_to_all(x, 'vtx', split_axis=0, concat_axis=0, tiled=True)  22 us
    pallas_call x2, Pallas kernels, local(): call(functools.partial(field_kernel, lanes), [((rows, LANES), f32, HBM),...  13.7 us
    pallas_call x2, Pallas kernels, far_list(): call(functools.partial(far_list_kernel, first, room), [((2 * KINDS * room...  12 us
    pallas_call x1, Pallas kernels, local(): call(own_side_kernel, [((rows, LANES), f32, HBM), ((rows // LANES, LANES)...  12 us
  transfers between devices with their start and end apart: 22, of which 13 were waited for; matrix products, arithmetic and copies ran while one was open for 0% of the time, Pallas kernels for 36%

profile of v7, /device:TPU:1, one launch (start us, length us, event | category | flops | bytes accessed | tf_op | source)
XLA Modules:
  0.0 246.5 jit_solution(7643432944954455478)
XLA Ops:
  3.9 7.1 %halo_side.1 = f32[32,56,128]{2,1,0:T(8,128)} custom-call(f32[4096,128]{1,0:T(8,128)S(1)} %convert_multiply_fusion.terms, s32[32,128]{1,0:T(8,128)S(1)} %bitcast.42, f32[32,128]{1,0:T(8,128)S(1)} %get-tuple-element.102.weight), custom_call_target="tpu_custom_call" | custom-call | flops 3221225472 | bytes 4194304 | tf_op jit(solution)/shard_map/halo_side/pallas_call | solution.py:656
  11.0 8.6 %all-to-all-start = ((f32[32,56,128]{2,1,0:T(8,128)}), f32[32,56,128]{2,1,0:T(8,128)S(1)}, u32[]{:S(2)}, u32[]{:S(2)}) async-start(f32[32,56,128]{2,1,0:T(8,128)} %halo_side.1), calls=%async_computation | async-start | bytes 1835008 | tf_op jit(solution)/shard_map/all_to_all | solution.py:630
  19.8 12.0 %own_side.1 = (f32[2048,128]{1,0:T(8,128)}, f32[16,128]{1,0:T(8,128)S(1)}) custom-call(f32[4096,128]{1,0:T(8,128)S(1)} %convert_multiply_fusion.terms, s32[32,128]{1,0:T(8,128)S(1)} %bitcast.45, s32[32,128]{1,0:T(8,128)S(1)} %bitcast.43, f32[32,128]{1,0:T(8,128)S(1)} %get-tuple-element.102.weight), custom_call_target="tpu_custom_call" | custom-call | flops 4294967296 | bytes 4194304 | tf_op jit(solution)/shard_map/own_side/pallas_call | solution.py:667
  46.1 6.0 %far_list.2.code_a = s32[6656]{0:T(1024)S(1)} custom-call(s32[1]{0:T(128)} %copy.9.count, s32[4096]{0:T(1024)S(1)} %bitcast.36, s32[4096]{0:T(1024)S(1)} %bitcast.38, s32[16,128]{1,0:T(8,128)S(1)} %get-tuple-element.66.totals), custom_call_target="tpu_custom_call" | custom-call | bytes 33554432 | tf_op jit(solution)/shard_map/far_list/pallas_call | solution.py:704
  52.1 4.7 %collective-permute-done.1 = f32[520,128]{1,0:T(8,128)S(1)} collective-permute-done((f32[520,128]{1,0:T(8,128)S(1)}, f32[520,128]{1,0:T(8,128)S(1)}, u32[]{:S(2)}, u32[]{:S(2)}) %collective-permute-start.1) | collective-permute-done | bytes 266272 | tf_op jit(solution)/shard_map/ppermute | solution.py:612
  62.3 6.1 %far_list.3.code_b = s32[6656]{0:T(1024)S(1)} custom-call(s32[1]{0:T(128)} %copy.9.count, s32[4096]{0:T(1024)S(1)} %bitcast.37, s32[4096]{0:T(1024)S(1)} %bitcast.39, s32[16,128]{1,0:T(8,128)S(1)} %get-tuple-element.66.totals), custom_call_target="tpu_custom_call" | custom-call | bytes 33554432 | tf_op jit(solution)/shard_map/far_list/pallas_call | solution.py:704
  68.4 4.9 %early_field.2.early = f32[1544,128]{1,0:T(8,128)S(1)} custom-call(s32[1]{0:T(128)} %bitcast.lane, s32[6656]{0:T(1024)S(1)} %far_list.2.code_a, s32[6656]{0:T(1024)S(1)} %far_list.3.code_b, s32[16,128]{1,0:T(8,128)S(1)} %get-tuple-element.66.totals, f32[4096]{0:T(1024)S(1)} %bitcast.21, f32[512,128]{1,0:T(8,128)S(1)} %slice_multiply_fusion.home.refs_0_, ...), custom_call_target="tpu_custom_call" | custom-call | bytes 33554432 | tf_op jit(solution)/shard_map/early_field/pallas_call | solution.py:731
  73.3 6.8 %field.2 = (f32[2048,128]{1,0:T(8,128)}, f32[32,96,128]{2,1,0:T(8,128)}) custom-call(s32[1]{0:T(128)} %bitcast.lane, s32[6656]{0:T(1024)S(1)} %far_list.2.code_a, s32[6656]{0:T(1024)S(1)} %far_list.3.code_b, s32[16,128]{1,0:T(8,128)S(1)} %get-tuple-element.66.totals, f32[4096]{0:T(1024)S(1)} %bitcast.22, s32[1536]{0:T(1024)S(1)} %reshape_squeeze.3.lists, ...), custom_call_target="tpu_custom_call" | custom-call | bytes 4194304 | tf_op jit(solution)/shard_map/field/pallas_call | solution.py:739
  80.2 5.7 %all-to-all-start.1 = ((f32[32,96,128]{2,1,0:T(8,128)}), f32[32,96,128]{2,1,0:T(8,128)S(1)}, u32[]{:S(2)}, u32[]{:S(2)}) async-start(f32[32,96,128]{2,1,0:T(8,128)} %get-tuple-element.75), calls=%async_computation.1 | async-start | bytes 3145728 | tf_op jit(solution)/shard_map/all_to_all | solution.py:630
  87.1 13.9 %near.2 = f32[2048,128]{1,0:T(8,128)S(1)} custom-call(s32[1]{0:T(128)} %copy.9.count, s32[4096]{0:T(1024)S(1)} %bitcast.31, f32[4096]{0:T(1024)S(1)} %bitcast.33, f32[2048,128]{1,0:T(8,128)S(1)} %copy-done.1), custom_call_target="tpu_custom_call" | custom-call | bytes 33554432 | tf_op jit(solution)/shard_map/near/pallas_call | solution.py:750
  101.0 7.1 %all-to-all-done.1.arrived = f32[32,96,128]{2,1,0:T(8,128)S(1)} async-done(((f32[32,96,128]{2,1,0:T(8,128)}), f32[32,96,128]{2,1,0:T(8,128)S(1)}, u32[]{:S(2)}, u32[]{:S(2)}) %all-to-all-start.1) | async-done | bytes 1572896 | tf_op jit(solution)/shard_map/all_to_all | solution.py:630
  108.1 4.2 %late_join.2 = (f32[512,128]{1,0:T(8,128)S(1)}, f32[33,48,128]{2,1,0:T(8,128)S(1)}, bf16[1536,256]{1,0:T(8,128)(2,1)S(1)}) custom-call(s32[1]{0:T(128)} %bitcast.lane, s32[6656]{0:T(1024)S(1)} %far_list.2.code_a, s32[6656]{0:T(1024)S(1)} %far_list.3.code_b, s32[16,128]{1,0:T(8,128)S(1)} %get-tuple-element.66.totals, f32[4096]{0:T(1024)S(1)} %bitcast.23, ...), custom_call_target="tpu_custom_call" | custom-call | bytes 4194304 | tf_op jit(solution)/shard_map/late_join/pallas_call | solution.py:758
  112.4 5.7 %join.2 = (f32[512,128]{1,0:T(8,128)S(1)}, f32[512,128]{1,0:T(8,128)S(1)}) custom-call(s32[1]{0:T(128)} %bitcast.lane, s32[6656]{0:T(1024)S(1)} %far_list.2.code_a, s32[6656]{0:T(1024)S(1)} %far_list.3.code_b, s32[16,128]{1,0:T(8,128)S(1)} %get-tuple-element.66.totals, f32[4096]{0:T(1024)S(1)} %bitcast.24, s32[12,128]{1,0:T(8,128)S(1)} %reshape_reshape_squeeze.3.listed, ...), custom_call_target="tpu_custom_call" | custom-call | bytes 33554432 | tf_op jit(solution)/shard_map/join/pallas_call | solution.py:767
  134.3 4.9 %early_field.3.early = f32[1544,128]{1,0:T(8,128)S(1)} custom-call(s32[1]{0:T(128)} %bitcast.lane, s32[6656]{0:T(1024)S(1)} %far_list.2.code_a, s32[6656]{0:T(1024)S(1)} %far_list.3.code_b, s32[16,128]{1,0:T(8,128)S(1)} %get-tuple-element.66.totals, f32[4096]{0:T(1024)S(1)} %bitcast.26, f32[512,128]{1,0:T(8,128)S(1)} %get-tuple-element.100.home.refs_0_, ...), custom_call_target="tpu_custom_call" | custom-call | bytes 33554432 | tf_op jit(solution)/shard_map/early_field/pallas_call | solution.py:731
  141.2 6.8 %field.3 = (f32[2048,128]{1,0:T(8,128)}, f32[32,96,128]{2,1,0:T(8,128)}) custom-call(s32[1]{0:T(128)} %bitcast.lane, s32[6656]{0:T(1024)S(1)} %far_list.2.code_a, s32[6656]{0:T(1024)S(1)} %far_list.3.code_b, s32[16,128]{1,0:T(8,128)S(1)} %get-tuple-element.66.totals, f32[4096]{0:T(1024)S(1)} %bitcast.27, s32[1536]{0:T(1024)S(1)} %reshape_squeeze.3.lists, ...), custom_call_target="tpu_custom_call" | custom-call | bytes 4194304 | tf_op jit(solution)/shard_map/field/pallas_call | solution.py:739
  148.1 10.1 %all-to-all-start.2 = ((f32[32,96,128]{2,1,0:T(8,128)}), f32[32,96,128]{2,1,0:T(8,128)S(1)}, u32[]{:S(2)}, u32[]{:S(2)}) async-start(f32[32,96,128]{2,1,0:T(8,128)} %get-tuple-element.85), calls=%async_computation.2 | async-start | bytes 3145728 | tf_op jit(solution)/shard_map/all_to_all | solution.py:630
  159.4 13.9 %near.3 = f32[2048,128]{1,0:T(8,128)S(1)} custom-call(s32[1]{0:T(128)} %copy.9.count, s32[4096]{0:T(1024)S(1)} %bitcast.32, f32[4096]{0:T(1024)S(1)} %bitcast.34, f32[2048,128]{1,0:T(8,128)S(1)} %copy-done), custom_call_target="tpu_custom_call" | custom-call | bytes 33554432 | tf_op jit(solution)/shard_map/near/pallas_call | solution.py:750
  173.3 7.0 %all-to-all-done.2.arrived = f32[32,96,128]{2,1,0:T(8,128)S(1)} async-done(((f32[32,96,128]{2,1,0:T(8,128)}), f32[32,96,128]{2,1,0:T(8,128)S(1)}, u32[]{:S(2)}, u32[]{:S(2)}) %all-to-all-start.2) | async-done | bytes 1572896 | tf_op jit(solution)/shard_map/all_to_all | solution.py:630
  184.5 5.8 %join.3 = (f32[512,128]{1,0:T(8,128)S(1)}, f32[512,128]{1,0:T(8,128)S(1)}) custom-call(s32[1]{0:T(128)} %bitcast.lane, s32[6656]{0:T(1024)S(1)} %far_list.2.code_a, s32[6656]{0:T(1024)S(1)} %far_list.3.code_b, s32[16,128]{1,0:T(8,128)S(1)} %get-tuple-element.66.totals, f32[4096]{0:T(1024)S(1)} %bitcast.29, s32[12,128]{1,0:T(8,128)S(1)} %reshape_reshape_squeeze.3.listed, ...), custom_call_target="tpu_custom_call" | custom-call | bytes 33554432 | tf_op jit(solution)/shard_map/join/pallas_call | solution.py:767
  205.8 5.2 %collective-permute-done.16.refs_2_ = f32[512,128]{1,0:T(8,128)S(1)} collective-permute-done((f32[512,128]{1,0:T(8,128)S(1)}, f32[512,128]{1,0:T(8,128)S(1)}, u32[]{:S(2)}, u32[]{:S(2)}) %collective-permute-start.16) | collective-permute-done | bytes 262176 | tf_op jit(solution)/shard_map/ppermute | solution.py:612
  215.4 11.5 %all-to-all-start.3 = ((f32[32,48,128]{2,1,0:T(8,128)}), f32[32,48,128]{2,1,0:T(8,128)S(1)}, u32[]{:S(2)}, u32[]{:S(2)}) async-start(f32[32,48,128]{2,1,0:T(8,128)} %get-tuple-element.97), calls=%async_computation.3 | async-start | bytes 1572864 | tf_op jit(solution)/shard_map/all_to_all | solution.py:630
  228.2 8.7 %near_gap.1.gaps = f32[4096,128]{1,0:T(8,128)S(1)} custom-call(s32[1]{0:T(128)} %copy.9.count, s32[4096]{0:T(1024)S(1)} %bitcast.41, f32[2048,128]{1,0:T(8,128)S(1)} %copy-done.2), custom_call_target="tpu_custom_call" | custom-call | bytes 33554432 | tf_op jit(solution)/shard_map/near_gap/pallas_call | solution.py:797
  236.9 4.3 %all-to-all-done.3.arrived = f32[32,48,128]{2,1,0:T(8,128)S(1)} async-done(((f32[32,48,128]{2,1,0:T(8,128)}), f32[32,48,128]{2,1,0:T(8,128)S(1)}, u32[]{:S(2)}, u32[]{:S(2)}) %all-to-all-start.3) | async-done | bytes 786464 | tf_op jit(solution)/shard_map/all_to_all | solution.py:630
  241.2 5.2 %far_gap.1 = f32[32,128]{1,0:T(8,128)} custom-call(s32[1]{0:T(128)} %copy.9.count, s32[4096]{0:T(1024)S(1)} %bitcast.40, f32[4096,128]{1,0:T(8,128)S(1)} %near_gap.1.gaps, f32[32,48,128]{2,1,0:T(8,128)S(1)} %all-to-all-done.3.arrived, f32[32,128]{1,0:T(8,128)S(1)} %fusion.live), custom_call_target="tpu_custom_call" | custom-call | bytes 4194304 | tf_op jit(solution)/shard_map/far_gap/pallas_call | solution.py:805
  (69 shorter events, 68.6 us)
Async XLA Ops:
  3.9 15.8 %copy-start.7 = (s32[1,32,48]{2,1,0:T(8,128)S(1)}, s32[1,32,48]{2,1,0:T(8,128)}, u32[]{:S(2)}) copy-start(s32[1,32,48]{2,1,0:T(8,128)} %param.12) | copy-start | bytes 18436
  3.9 15.9 %copy-start.5 = (s32[4096]{0:T(1024)S(1)}, s32[4096]{0:T(1024)}, u32[]{:S(2)}) copy-start(s32[4096]{0:T(1024)} %param.10) | copy-start | bytes 49156
  11.0 24.4 %all-to-all-start = ((f32[32,56,128]{2,1,0:T(8,128)}), f32[32,56,128]{2,1,0:T(8,128)S(1)}, u32[]{:S(2)}, u32[]{:S(2)}) async-start(f32[32,56,128]{2,1,0:T(8,128)} %halo_side.1), calls=%async_computation | async-start | bytes 1835008 | tf_op jit(solution)/shard_map/all_to_all | solution.py:630
  40.0 12.2 %collective-permute-start = (f32[520,128]{1,0:T(8,128)S(1)}, f32[520,128]{1,0:T(8,128)S(1)}, u32[]{:S(2)}, u32[]{:S(2)}) collective-permute-start(f32[520,128]{1,0:T(8,128)S(1)} %get-tuple-element.58), channel_id=1, source_target_pairs={{0,1},{1,2},{2,3},{3,0},{4,5},{5,6},{6,7},{7,4},{8,9},{9,10},{10,1... | collective-permute-start | bytes 798728 | tf_op jit(solution)/shard_map/ppermute | solution.py:612
  41.7 15.1 %collective-permute-start.1 = (f32[520,128]{1,0:T(8,128)S(1)}, f32[520,128]{1,0:T(8,128)S(1)}, u32[]{:S(2)}, u32[]{:S(2)}) collective-permute-start(f32[520,128]{1,0:T(8,128)S(1)} %get-tuple-element.59), channel_id=1, source_target_pairs={{0,2},{1,3},{2,0},{3,1},{4,6},{5,7},{6,4},{7,5},{8,10},{9,11},{10,... | collective-permute-start | bytes 798728 | tf_op jit(solution)/shard_map/ppermute | solution.py:612
  45.0 11.8 %collective-permute-start.2 = (f32[520,128]{1,0:T(8,128)S(1)}, f32[520,128]{1,0:T(8,128)S(1)}, u32[]{:S(2)}, u32[]{:S(2)}) collective-permute-start(f32[520,128]{1,0:T(8,128)S(1)} %get-tuple-element.60), channel_id=1, source_target_pairs={{0,3},{1,0},{2,1},{3,2},{4,7},{5,4},{6,5},{7,6},{8,11},{9,8},{10,9... | collective-permute-start | bytes 798728 | tf_op jit(solution)/shard_map/ppermute | solution.py:612
  57.8 10.6 %collective-permute-start.3 = (f32[512,128]{1,0:T(8,128)S(1)}, f32[512,128]{1,0:T(8,128)S(1)}, u32[]{:S(2)}, u32[]{:S(2)}) collective-permute-start(f32[512,128]{1,0:T(8,128)S(1)} %slice_multiply_fusion.home.refs_0_), channel_id=1, source_target_pairs={{0,2},{1,3},{2,0},{3,1},{4,6},{5,7},{6,4},{7,5},{8,10},{9,11},{10,... | collective-permute-start | bytes 786440 | tf_op jit(solution)/shard_map/ppermute | solution.py:612
  59.5 13.8 %collective-permute-start.4 = (f32[512,128]{1,0:T(8,128)S(1)}, f32[512,128]{1,0:T(8,128)S(1)}, u32[]{:S(2)}, u32[]{:S(2)}) collective-permute-start(f32[512,128]{1,0:T(8,128)S(1)} %slice_multiply_fusion.home.refs_0_), channel_id=1, source_target_pairs={{0,1},{1,2},{2,3},{3,0},{4,5},{5,6},{6,7},{7,4},{8,9},{9,10},{10,1... | collective-permute-start | bytes 786440 | tf_op jit(solution)/shard_map/ppermute | solution.py:612
  61.1 12.3 %collective-permute-start.5 = (f32[512,128]{1,0:T(8,128)S(1)}, f32[512,128]{1,0:T(8,128)S(1)}, u32[]{:S(2)}, u32[]{:S(2)}) collective-permute-start(f32[512,128]{1,0:T(8,128)S(1)} %slice_multiply_fusion.home.refs_0_), channel_id=1, source_target_pairs={{0,3},{1,0},{2,1},{3,2},{4,7},{5,4},{6,5},{7,6},{8,11},{9,8},{10,9... | collective-permute-start | bytes 786440 | tf_op jit(solution)/shard_map/ppermute | solution.py:612
  80.2 27.9 %all-to-all-start.1 = ((f32[32,96,128]{2,1,0:T(8,128)}), f32[32,96,128]{2,1,0:T(8,128)S(1)}, u32[]{:S(2)}, u32[]{:S(2)}) async-start(f32[32,96,128]{2,1,0:T(8,128)} %get-tuple-element.75), calls=%async_computation.1 | async-start | bytes 3145728 | tf_op jit(solution)/shard_map/all_to_all | solution.py:630
  112.3 8.1 %collective-permute-start.6 = (f32[512,128]{1,0:T(8,128)S(1)}, f32[512,128]{1,0:T(8,128)S(1)}, u32[]{:S(2)}, u32[]{:S(2)}) collective-permute-start(f32[512,128]{1,0:T(8,128)S(1)} %get-tuple-element.78), channel_id=1, source_target_pairs={{0,2},{1,3},{2,0},{3,1},{4,6},{5,7},{6,4},{7,5},{8,10},{9,11},{10,... | collective-permute-start | bytes 786440 | tf_op jit(solution)/shard_map/ppermute | solution.py:612
  120.3 6.8 %collective-permute-start.7 = (f32[512,128]{1,0:T(8,128)S(1)}, f32[512,128]{1,0:T(8,128)S(1)}, u32[]{:S(2)}, u32[]{:S(2)}) collective-permute-start(f32[512,128]{1,0:T(8,128)S(1)} %get-tuple-element.82), channel_id=1, source_target_pairs={{0,1},{1,2},{2,3},{3,0},{4,5},{5,6},{6,7},{7,4},{8,9},{9,10},{10,1... | collective-permute-start | bytes 786440 | tf_op jit(solution)/shard_map/ppermute | solution.py:612
  120.3 6.8 %collective-permute-start.8 = (f32[512,128]{1,0:T(8,128)S(1)}, f32[512,128]{1,0:T(8,128)S(1)}, u32[]{:S(2)}, u32[]{:S(2)}) collective-permute-start(f32[512,128]{1,0:T(8,128)S(1)} %get-tuple-element.83), channel_id=1, source_target_pairs={{0,3},{1,0},{2,1},{3,2},{4,7},{5,4},{6,5},{7,6},{8,11},{9,8},{10,9... | collective-permute-start | bytes 786440 | tf_op jit(solution)/shard_map/ppermute | solution.py:612
  127.4 6.9 %collective-permute-start.9 = (f32[512,128]{1,0:T(8,128)S(1)}, f32[512,128]{1,0:T(8,128)S(1)}, u32[]{:S(2)}, u32[]{:S(2)}) collective-permute-start(f32[512,128]{1,0:T(8,128)S(1)} %get-tuple-element.100.home.refs_0_), channel_id=1, source_target_pairs={{0,2},{1,3},{2,0},{3,1},{4,6},{5,7},{6,4},{7,5},{8,10},{9,11},{10,... | collective-permute-start | bytes 786440 | tf_op jit(solution)/shard_map/ppermute | solution.py:612
  128.6 12.6 %collective-permute-start.10 = (f32[512,128]{1,0:T(8,128)S(1)}, f32[512,128]{1,0:T(8,128)S(1)}, u32[]{:S(2)}, u32[]{:S(2)}) collective-permute-start(f32[512,128]{1,0:T(8,128)S(1)} %get-tuple-element.100.home.refs_0_), channel_id=1, source_target_pairs={{0,1},{1,2},{2,3},{3,0},{4,5},{5,6},{6,7},{7,4},{8,9},{9,10},{10,1... | collective-permute-start | bytes 786440 | tf_op jit(solution)/shard_map/ppermute | solution.py:612
  130.4 10.8 %collective-permute-start.11 = (f32[512,128]{1,0:T(8,128)S(1)}, f32[512,128]{1,0:T(8,128)S(1)}, u32[]{:S(2)}, u32[]{:S(2)}) collective-permute-start(f32[512,128]{1,0:T(8,128)S(1)} %get-tuple-element.100.home.refs_0_), channel_id=1, source_target_pairs={{0,3},{1,0},{2,1},{3,2},{4,7},{5,4},{6,5},{7,6},{8,11},{9,8},{10,9... | collective-permute-start | bytes 786440 | tf_op jit(solution)/shard_map/ppermute | solution.py:612
  148.1 32.1 %all-to-all-start.2 = ((f32[32,96,128]{2,1,0:T(8,128)}), f32[32,96,128]{2,1,0:T(8,128)S(1)}, u32[]{:S(2)}, u32[]{:S(2)}) async-start(f32[32,96,128]{2,1,0:T(8,128)} %get-tuple-element.85), calls=%async_computation.2 | async-start | bytes 3145728 | tf_op jit(solution)/shard_map/all_to_all | solution.py:630
  184.4 7.9 %collective-permute-start.12 = (f32[512,128]{1,0:T(8,128)S(1)}, f32[512,128]{1,0:T(8,128)S(1)}, u32[]{:S(2)}, u32[]{:S(2)}) collective-permute-start(f32[512,128]{1,0:T(8,128)S(1)} %get-tuple-element.88), channel_id=1, source_target_pairs={{0,2},{1,3},{2,0},{3,1},{4,6},{5,7},{6,4},{7,5},{8,10},{9,11},{10,... | collective-permute-start | bytes 786440 | tf_op jit(solution)/shard_map/ppermute | solution.py:612
  192.4 6.5 %collective-permute-start.13 = (f32[512,128]{1,0:T(8,128)S(1)}, f32[512,128]{1,0:T(8,128)S(1)}, u32[]{:S(2)}, u32[]{:S(2)}) collective-permute-start(f32[512,128]{1,0:T(8,128)S(1)} %get-tuple-element.92), channel_id=1, source_target_pairs={{0,1},{1,2},{2,3},{3,0},{4,5},{5,6},{6,7},{7,4},{8,9},{9,10},{10,1... | collective-permute-start | bytes 786440 | tf_op jit(solution)/shard_map/ppermute | solution.py:612
  192.4 6.5 %collective-permute-start.14 = (f32[512,128]{1,0:T(8,128)S(1)}, f32[512,128]{1,0:T(8,128)S(1)}, u32[]{:S(2)}, u32[]{:S(2)}) collective-permute-start(f32[512,128]{1,0:T(8,128)S(1)} %get-tuple-element.93), channel_id=1, source_target_pairs={{0,3},{1,0},{2,1},{3,2},{4,7},{5,4},{6,5},{7,6},{8,11},{9,8},{10,9... | collective-permute-start | bytes 786440 | tf_op jit(solution)/shard_map/ppermute | solution.py:612
  199.3 6.5 %collective-permute-start.15 = (f32[512,128]{1,0:T(8,128)S(1)}, f32[512,128]{1,0:T(8,128)S(1)}, u32[]{:S(2)}, u32[]{:S(2)}) collective-permute-start(f32[512,128]{1,0:T(8,128)S(1)} %add_add_fusion.1.refs_0_), channel_id=1, source_target_pairs={{0,1},{1,2},{2,3},{3,0},{4,5},{5,6},{6,7},{7,4},{8,9},{9,10},{10,1... | collective-permute-start | bytes 786440 | tf_op jit(solution)/shard_map/ppermute | solution.py:612
  199.4 11.6 %collective-permute-start.16 = (f32[512,128]{1,0:T(8,128)S(1)}, f32[512,128]{1,0:T(8,128)S(1)}, u32[]{:S(2)}, u32[]{:S(2)}) collective-permute-start(f32[512,128]{1,0:T(8,128)S(1)} %add_add_fusion.1.refs_0_), channel_id=1, source_target_pairs={{0,2},{1,3},{2,0},{3,1},{4,6},{5,7},{6,4},{7,5},{8,10},{9,11},{10,... | collective-permute-start | bytes 786440 | tf_op jit(solution)/shard_map/ppermute | solution.py:612
  203.1 8.7 %collective-permute-start.17 = (f32[512,128]{1,0:T(8,128)S(1)}, f32[512,128]{1,0:T(8,128)S(1)}, u32[]{:S(2)}, u32[]{:S(2)}) collective-permute-start(f32[512,128]{1,0:T(8,128)S(1)} %add_add_fusion.1.refs_0_), channel_id=1, source_target_pairs={{0,3},{1,0},{2,1},{3,2},{4,7},{5,4},{6,5},{7,6},{8,11},{9,8},{10,9... | collective-permute-start | bytes 786440 | tf_op jit(solution)/shard_map/ppermute | solution.py:612
  215.4 25.7 %all-to-all-start.3 = ((f32[32,48,128]{2,1,0:T(8,128)}), f32[32,48,128]{2,1,0:T(8,128)S(1)}, u32[]{:S(2)}, u32[]{:S(2)}) async-start(f32[32,48,128]{2,1,0:T(8,128)} %get-tuple-element.97), calls=%async_computation.3 | async-start | bytes 1572864 | tf_op jit(solution)/shard_map/all_to_all | solution.py:630
  (6 other events, 17.2 us)

commit v8 on v7

--- a/solution.py
+++ b/solution.py
@@ -16,6 +16,7 @@
 BESIDE, OPPOSITE, HOME = range(3)
 KINDS = 3
 PARTS = 8
+ROOMY = 32
 
 lam_low = 0.05
 lam_high = 2.0
@@ -92,7 +93,7 @@
     return total[:height] + total[height:]
 
 
-def halo_side_kernel(rows, slots, width, terms, target, weight, sent, both, hot, other, out, leave):
+def halo_side_kernel(rows, slots, width, terms, target, weight, sent, both, hot, out, leave):
     groups = target.shape[0]
     tall = hot.shape[0]
     per = tall // width
@@ -117,19 +118,17 @@
         at = pl.ds(i * per, per)
         return pltpu.make_async_copy(out.at[at], sent.at[at], leave.at[i])
 
-    def build(i):
-        to = (hot, other)[i % 2]
+    def chunk(i, _):
+        base = rows + i * tall
         for k in range(groups):
-            to[:, k * LANES : (k + 1) * LANES] = one_hot(target[k : k + 1, :], tall, rows + i * tall).astype(jnp.bfloat16)
-
-    build(0)
-    for i in range(chunks):
-        if i + 1 < chunks:
-            build(i + 1)
-        got = halves(jnp.dot((hot, other)[i % 2][...], both[...], preferred_element_type=jnp.float32))
+            hot[:, k * LANES : (k + 1) * LANES] = one_hot(target[k : k + 1, :], tall, base).astype(jnp.bfloat16)
+        got = halves(jnp.dot(hot[...], both[...], preferred_element_type=jnp.float32))
         for c in range(per):
             out[i * per + c, :width, :] = -got[c * width : (c + 1) * width]
         part(i).start()
+        return 0
+
+    lax.fori_loop(0, chunks, chunk, 0)
     for i in range(chunks):
         part(i).wait()
 
@@ -142,7 +141,7 @@
 
     def part(i):
         at = pl.ds(pl.multiple_of(i * tall, tall), tall)
-        return pltpu.make_async_copy(out.at[at, :], kept.at[at, :], leave.at[i])
+        return pltpu.make_async_copy(out.at[at, :], kept.at[0, at, :], leave.at[i])
 
     def chunk(i, _):
         base = i * tall
@@ -193,10 +192,10 @@
     outs, (acc, ret_both, hot, other, landed, arrival, arrival_own) = refs[:lanes], refs[lanes:]
     come = pltpu.make_async_copy(returned, landed, arrival)
     come.start()
-    mine = pltpu.make_async_copy(own, acc, arrival_own)
+    mine = pltpu.make_async_copy(own.at[0], acc, arrival_own)
     mine.start()
     blocks = returned.shape[0]
-    rows = own.shape[0]
+    rows = own.shape[1]
     width = listed.shape[0] * LANES // blocks
     share = rows // lanes
     come.wait()
@@ -657,8 +656,7 @@
         functools.partial(halo_side_kernel, rows, slots, width),
         [((blocks, width + 8, LANES), f32, HBM)],
         [VMEM] * 3,
-        [pltpu.VMEM((edges, 2 * LANES), bf16)]
-        + [pltpu.VMEM((8 * width, edges), bf16)] * 2
+        [pltpu.VMEM((edges, 2 * LANES), bf16), pltpu.VMEM((8 * width, edges), bf16)]
         + [pltpu.VMEM((blocks, width + 8, LANES), f32), pltpu.SemaphoreType.DMA((slots // (8 * width),))],
         "halo_side",
         flops=2 * slots * edges * 2 * LANES,
@@ -666,7 +664,7 @@
     returned = across(outgoing)
     own, own_degree = call(
         own_side_kernel,
-        [((rows, LANES), f32, HBM), ((rows // LANES, LANES), f32, VMEM)],
+        [((ROOMY, rows, LANES), f32, HBM), ((rows // LANES, LANES), f32, VMEM)],
         [VMEM] * 4,
         [pltpu.VMEM((edges, 2 * LANES), bf16), pltpu.VMEM((256, edges), bf16)]
         + [pltpu.VMEM((rows, LANES), f32), pltpu.SemaphoreType.DMA((rows // 256,))],

time: 247 us -> 248 us (level)
  starting transfers between devices: 59.3 us -> 66.5 us
  waiting for transfers between devices: 44.8 us -> 39.6 us
    all_to_all x4, starting transfers between devices: 35.9 us -> 42.8 us  [across(): return lax.all_to_all(x, 'vtx', split_axis=0, concat_axis=0, tiled=True)]
    ppermute x18, waiting for transfers between devices: 22.8 us -> 17.5 us  [moved_by(): lax.ppermute(x, 'edg', [(i, (i + shift) % lanes) for i in range(lanes)])]
  transfers between devices with their start and end apart: 22 -> 22, of which waited for: 13 -> 10; matrix products, arithmetic and copies ran while one was open for 0% -> 0% of each run, Pallas kernels for 36% -> 36%
where the time goes in v8:
time: 248 us
  Pallas kernels  132 us (53%)
  starting transfers between devices  66.5 us (27%)
  waiting for transfers between devices  39.6 us (16%)
  other arithmetic  4.2 us (2%)
  local copies, waits for them, and re-layouts  3.83 us (2%)
    all_to_all x4, starting transfers between devices, across(): return lax.all_to_all(x, 'vtx', split_axis=0, concat_axis=0, tiled=True)  42.8 us
    pallas_call x2, Pallas kernels, local(): call(near_kernel, [((rows, LANES), f32, VMEM)], [SMEM] * 3 + [HBM], [pltp...  27.7 us
    ppermute x18, starting transfers between devices, moved_by(): lax.ppermute(x, 'edg', [(i, (i + shift) % lanes) for i in range(lanes)])  23.7 us
    all_to_all x4, waiting for transfers between devices, across(): return lax.all_to_all(x, 'vtx', split_axis=0, concat_axis=0, tiled=True)  22.2 us
    ppermute x18, waiting for transfers between devices, moved_by(): lax.ppermute(x, 'edg', [(i, (i + shift) % lanes) for i in range(lanes)])  17.5 us
    pallas_call x2, Pallas kernels, local(): call(functools.partial(field_kernel, lanes), [((rows, LANES), f32, HBM),...  13.9 us
    pallas_call x1, Pallas kernels, local(): call(own_side_kernel, [((ROOMY, rows, LANES), f32, HBM), ((rows // LANES,...  12 us
    pallas_call x2, Pallas kernels, local(): call(functools.partial(join_kernel, lanes), [((share, LANES), f32, VMEM)]...  11.9 us
  transfers between devices with their start and end apart: 22, of which 10 were waited for; matrix products, arithmetic and copies ran while one was open for 0% of the time, Pallas kernels for 36%

profile of v8, /device:TPU:1, one launch (start us, length us, event | category | flops | bytes accessed | tf_op | source)
XLA Modules:
  0.0 247.8 jit_solution(13338732832179736683)
XLA Ops:
  3.9 6.0 %halo_side.1 = f32[32,56,128]{2,1,0:T(8,128)} custom-call(f32[4096,128]{1,0:T(8,128)S(1)} %convert_multiply_fusion.terms, s32[32,128]{1,0:T(8,128)S(1)} %bitcast.42, f32[32,128]{1,0:T(8,128)S(1)} %get-tuple-element.102.weight), custom_call_target="tpu_custom_call" | custom-call | flops 3221225472 | bytes 4194304 | tf_op jit(solution)/shard_map/halo_side/pallas_call | solution.py:655
  9.9 8.6 %all-to-all-start = ((f32[32,56,128]{2,1,0:T(8,128)}), f32[32,56,128]{2,1,0:T(8,128)S(1)}, u32[]{:S(2)}, u32[]{:S(2)}) async-start(f32[32,56,128]{2,1,0:T(8,128)} %halo_side.1), calls=%async_computation | async-start | bytes 1835008 | tf_op jit(solution)/shard_map/all_to_all | solution.py:629
  18.6 12.0 %own_side.1 = (f32[32,2048,128]{2,1,0:T(8,128)}, f32[16,128]{1,0:T(8,128)S(1)}) custom-call(f32[4096,128]{1,0:T(8,128)S(1)} %convert_multiply_fusion.terms, s32[32,128]{1,0:T(8,128)S(1)} %bitcast.45, s32[32,128]{1,0:T(8,128)S(1)} %bitcast.43, f32[32,128]{1,0:T(8,128)S(1)} %get-tuple-element.102.weight), custom_call_target="tpu_custom_call" | custom-call | flops 4294967296 | bytes 4194304 | tf_op jit(solution)/shard_map/own_side/pallas_call | solution.py:665
  34.3 4.3 %side_join.1 = (f32[520,128]{1,0:T(8,128)S(1)}, f32[520,128]{1,0:T(8,128)S(1)}, f32[520,128]{1,0:T(8,128)S(1)}, f32[520,128]{1,0:T(8,128)S(1)}) custom-call(s32[1]{0:T(128)} %bitcast.lane, f32[32,56,128]{2,1,0:T(8,128)S(1)} %all-to-all-done.returned, s32[12,128]{1,0:T(8,128)S(1)} %reshape_reshape_squeeze.3.listed, s32[32,128]{1,0:T(8,128)S(1)} %pad.4.padded, ...), custom_call_target="tpu_custom_call" | custom-call | flops 1610612736 | bytes 4194304 | tf_op jit(solution)/shard_map/side_join/pallas_call | solution.py:674
  44.8 5.8 %far_list.2.code_a = s32[6656]{0:T(1024)S(1)} custom-call(s32[1]{0:T(128)} %copy.9.count, s32[4096]{0:T(1024)S(1)} %bitcast.36, s32[4096]{0:T(1024)S(1)} %bitcast.38, s32[16,128]{1,0:T(8,128)S(1)} %get-tuple-element.66.totals), custom_call_target="tpu_custom_call" | custom-call | bytes 33554432 | tf_op jit(solution)/shard_map/far_list/pallas_call | solution.py:702
  50.6 4.8 %collective-permute-done.1 = f32[520,128]{1,0:T(8,128)S(1)} collective-permute-done((f32[520,128]{1,0:T(8,128)S(1)}, f32[520,128]{1,0:T(8,128)S(1)}, u32[]{:S(2)}, u32[]{:S(2)}) %collective-permute-start.1) | collective-permute-done | bytes 266272 | tf_op jit(solution)/shard_map/ppermute | solution.py:611
  61.0 6.1 %far_list.3.code_b = s32[6656]{0:T(1024)S(1)} custom-call(s32[1]{0:T(128)} %copy.9.count, s32[4096]{0:T(1024)S(1)} %bitcast.37, s32[4096]{0:T(1024)S(1)} %bitcast.39, s32[16,128]{1,0:T(8,128)S(1)} %get-tuple-element.66.totals), custom_call_target="tpu_custom_call" | custom-call | bytes 33554432 | tf_op jit(solution)/shard_map/far_list/pallas_call | solution.py:702
  67.0 4.9 %early_field.2.early = f32[1544,128]{1,0:T(8,128)S(1)} custom-call(s32[1]{0:T(128)} %bitcast.lane, s32[6656]{0:T(1024)S(1)} %far_list.2.code_a, s32[6656]{0:T(1024)S(1)} %far_list.3.code_b, s32[16,128]{1,0:T(8,128)S(1)} %get-tuple-element.66.totals, f32[4096]{0:T(1024)S(1)} %bitcast.21, f32[512,128]{1,0:T(8,128)S(1)} %slice_multiply_fusion.home.refs_0_, ...), custom_call_target="tpu_custom_call" | custom-call | bytes 33554432 | tf_op jit(solution)/shard_map/early_field/pallas_call | solution.py:729
  72.0 6.9 %field.2 = (f32[2048,128]{1,0:T(8,128)}, f32[32,96,128]{2,1,0:T(8,128)}) custom-call(s32[1]{0:T(128)} %bitcast.lane, s32[6656]{0:T(1024)S(1)} %far_list.2.code_a, s32[6656]{0:T(1024)S(1)} %far_list.3.code_b, s32[16,128]{1,0:T(8,128)S(1)} %get-tuple-element.66.totals, f32[4096]{0:T(1024)S(1)} %bitcast.22, s32[1536]{0:T(1024)S(1)} %reshape_squeeze.3.lists, ...), custom_call_target="tpu_custom_call" | custom-call | bytes 4194304 | tf_op jit(solution)/shard_map/field/pallas_call | solution.py:737
  78.9 6.3 %all-to-all-start.1 = ((f32[32,96,128]{2,1,0:T(8,128)}), f32[32,96,128]{2,1,0:T(8,128)S(1)}, u32[]{:S(2)}, u32[]{:S(2)}) async-start(f32[32,96,128]{2,1,0:T(8,128)} %get-tuple-element.75), calls=%async_computation.1 | async-start | bytes 3145728 | tf_op jit(solution)/shard_map/all_to_all | solution.py:629
  86.4 13.9 %near.2 = f32[2048,128]{1,0:T(8,128)S(1)} custom-call(s32[1]{0:T(128)} %copy.9.count, s32[4096]{0:T(1024)S(1)} %bitcast.31, f32[4096]{0:T(1024)S(1)} %bitcast.33, f32[2048,128]{1,0:T(8,128)S(1)} %copy-done.1), custom_call_target="tpu_custom_call" | custom-call | bytes 33554432 | tf_op jit(solution)/shard_map/near/pallas_call | solution.py:748
  100.3 7.2 %all-to-all-done.1.arrived = f32[32,96,128]{2,1,0:T(8,128)S(1)} async-done(((f32[32,96,128]{2,1,0:T(8,128)}), f32[32,96,128]{2,1,0:T(8,128)S(1)}, u32[]{:S(2)}, u32[]{:S(2)}) %all-to-all-start.1) | async-done | bytes 1572896 | tf_op jit(solution)/shard_map/all_to_all | solution.py:629
  111.8 5.8 %join.2 = (f32[512,128]{1,0:T(8,128)S(1)}, f32[512,128]{1,0:T(8,128)S(1)}) custom-call(s32[1]{0:T(128)} %bitcast.lane, s32[6656]{0:T(1024)S(1)} %far_list.2.code_a, s32[6656]{0:T(1024)S(1)} %far_list.3.code_b, s32[16,128]{1,0:T(8,128)S(1)} %get-tuple-element.66.totals, f32[4096]{0:T(1024)S(1)} %bitcast.24, s32[12,128]{1,0:T(8,128)S(1)} %reshape_reshape_squeeze.3.listed, ...), custom_call_target="tpu_custom_call" | custom-call | bytes 33554432 | tf_op jit(solution)/shard_map/join/pallas_call | solution.py:765
  132.8 4.9 %early_field.3.early = f32[1544,128]{1,0:T(8,128)S(1)} custom-call(s32[1]{0:T(128)} %bitcast.lane, s32[6656]{0:T(1024)S(1)} %far_list.2.code_a, s32[6656]{0:T(1024)S(1)} %far_list.3.code_b, s32[16,128]{1,0:T(8,128)S(1)} %get-tuple-element.66.totals, f32[4096]{0:T(1024)S(1)} %bitcast.26, f32[512,128]{1,0:T(8,128)S(1)} %get-tuple-element.100.home.refs_0_, ...), custom_call_target="tpu_custom_call" | custom-call | bytes 33554432 | tf_op jit(solution)/shard_map/early_field/pallas_call | solution.py:729
  137.7 6.9 %field.3 = (f32[2048,128]{1,0:T(8,128)}, f32[32,96,128]{2,1,0:T(8,128)}) custom-call(s32[1]{0:T(128)} %bitcast.lane, s32[6656]{0:T(1024)S(1)} %far_list.2.code_a, s32[6656]{0:T(1024)S(1)} %far_list.3.code_b, s32[16,128]{1,0:T(8,128)S(1)} %get-tuple-element.66.totals, f32[4096]{0:T(1024)S(1)} %bitcast.27, s32[1536]{0:T(1024)S(1)} %reshape_squeeze.3.lists, ...), custom_call_target="tpu_custom_call" | custom-call | bytes 4194304 | tf_op jit(solution)/shard_map/field/pallas_call | solution.py:737
  144.7 13.1 %all-to-all-start.2 = ((f32[32,96,128]{2,1,0:T(8,128)}), f32[32,96,128]{2,1,0:T(8,128)S(1)}, u32[]{:S(2)}, u32[]{:S(2)}) async-start(f32[32,96,128]{2,1,0:T(8,128)} %get-tuple-element.85), calls=%async_computation.2 | async-start | bytes 3145728 | tf_op jit(solution)/shard_map/all_to_all | solution.py:629
  159.0 13.9 %near.3 = f32[2048,128]{1,0:T(8,128)S(1)} custom-call(s32[1]{0:T(128)} %copy.9.count, s32[4096]{0:T(1024)S(1)} %bitcast.32, f32[4096]{0:T(1024)S(1)} %bitcast.34, f32[2048,128]{1,0:T(8,128)S(1)} %copy-done), custom_call_target="tpu_custom_call" | custom-call | bytes 33554432 | tf_op jit(solution)/shard_map/near/pallas_call | solution.py:748
  172.9 7.1 %all-to-all-done.2.arrived = f32[32,96,128]{2,1,0:T(8,128)S(1)} async-done(((f32[32,96,128]{2,1,0:T(8,128)}), f32[32,96,128]{2,1,0:T(8,128)S(1)}, u32[]{:S(2)}, u32[]{:S(2)}) %all-to-all-start.2) | async-done | bytes 1572896 | tf_op jit(solution)/shard_map/all_to_all | solution.py:629
  184.3 6.1 %join.3 = (f32[512,128]{1,0:T(8,128)S(1)}, f32[512,128]{1,0:T(8,128)S(1)}) custom-call(s32[1]{0:T(128)} %bitcast.lane, s32[6656]{0:T(1024)S(1)} %far_list.2.code_a, s32[6656]{0:T(1024)S(1)} %far_list.3.code_b, s32[16,128]{1,0:T(8,128)S(1)} %get-tuple-element.66.totals, f32[4096]{0:T(1024)S(1)} %bitcast.29, s32[12,128]{1,0:T(8,128)S(1)} %reshape_reshape_squeeze.3.listed, ...), custom_call_target="tpu_custom_call" | custom-call | bytes 33554432 | tf_op jit(solution)/shard_map/join/pallas_call | solution.py:765
  205.0 4.6 %collective-permute-done.16.refs_2_ = f32[512,128]{1,0:T(8,128)S(1)} collective-permute-done((f32[512,128]{1,0:T(8,128)S(1)}, f32[512,128]{1,0:T(8,128)S(1)}, u32[]{:S(2)}, u32[]{:S(2)}) %collective-permute-start.16) | collective-permute-done | bytes 262176 | tf_op jit(solution)/shard_map/ppermute | solution.py:611
  213.3 14.9 %all-to-all-start.3 = ((f32[32,48,128]{2,1,0:T(8,128)}), f32[32,48,128]{2,1,0:T(8,128)S(1)}, u32[]{:S(2)}, u32[]{:S(2)}) async-start(f32[32,48,128]{2,1,0:T(8,128)} %get-tuple-element.97), calls=%async_computation.3 | async-start | bytes 1572864 | tf_op jit(solution)/shard_map/all_to_all | solution.py:629
  229.4 8.7 %near_gap.1.gaps = f32[4096,128]{1,0:T(8,128)S(1)} custom-call(s32[1]{0:T(128)} %copy.9.count, s32[4096]{0:T(1024)S(1)} %bitcast.41, f32[2048,128]{1,0:T(8,128)S(1)} %copy-done.2), custom_call_target="tpu_custom_call" | custom-call | bytes 33554432 | tf_op jit(solution)/shard_map/near_gap/pallas_call | solution.py:795
  238.1 4.3 %all-to-all-done.3.arrived = f32[32,48,128]{2,1,0:T(8,128)S(1)} async-done(((f32[32,48,128]{2,1,0:T(8,128)}), f32[32,48,128]{2,1,0:T(8,128)S(1)}, u32[]{:S(2)}, u32[]{:S(2)}) %all-to-all-start.3) | async-done | bytes 786464 | tf_op jit(solution)/shard_map/all_to_all | solution.py:629
  242.4 5.2 %far_gap.1 = f32[32,128]{1,0:T(8,128)} custom-call(s32[1]{0:T(128)} %copy.9.count, s32[4096]{0:T(1024)S(1)} %bitcast.40, f32[4096,128]{1,0:T(8,128)S(1)} %near_gap.1.gaps, f32[32,48,128]{2,1,0:T(8,128)S(1)} %all-to-all-done.3.arrived, f32[32,128]{1,0:T(8,128)S(1)} %fusion.live), custom_call_target="tpu_custom_call" | custom-call | bytes 4194304 | tf_op jit(solution)/shard_map/far_gap/pallas_call | solution.py:803
  (67 shorter events, 63.6 us)
Async XLA Ops:
  3.9 14.7 %copy-start.6 = (s32[1,32,48]{2,1,0:T(8,128)S(1)}, s32[1,32,48]{2,1,0:T(8,128)}, u32[]{:S(2)}) copy-start(s32[1,32,48]{2,1,0:T(8,128)} %param.12) | copy-start | bytes 18436
  3.9 14.7 %copy-start.5 = (s32[4096]{0:T(1024)S(1)}, s32[4096]{0:T(1024)}, u32[]{:S(2)}) copy-start(s32[4096]{0:T(1024)} %param.10) | copy-start | bytes 49156
  9.9 24.4 %all-to-all-start = ((f32[32,56,128]{2,1,0:T(8,128)}), f32[32,56,128]{2,1,0:T(8,128)S(1)}, u32[]{:S(2)}, u32[]{:S(2)}) async-start(f32[32,56,128]{2,1,0:T(8,128)} %halo_side.1), calls=%async_computation | async-start | bytes 1835008 | tf_op jit(solution)/shard_map/all_to_all | solution.py:629
  38.6 12.0 %collective-permute-start = (f32[520,128]{1,0:T(8,128)S(1)}, f32[520,128]{1,0:T(8,128)S(1)}, u32[]{:S(2)}, u32[]{:S(2)}) collective-permute-start(f32[520,128]{1,0:T(8,128)S(1)} %get-tuple-element.58), channel_id=1, source_target_pairs={{0,1},{1,2},{2,3},{3,0},{4,5},{5,6},{6,7},{7,4},{8,9},{9,10},{10,1... | collective-permute-start | bytes 798728 | tf_op jit(solution)/shard_map/ppermute | solution.py:611
  40.3 15.1 %collective-permute-start.1 = (f32[520,128]{1,0:T(8,128)S(1)}, f32[520,128]{1,0:T(8,128)S(1)}, u32[]{:S(2)}, u32[]{:S(2)}) collective-permute-start(f32[520,128]{1,0:T(8,128)S(1)} %get-tuple-element.59), channel_id=1, source_target_pairs={{0,2},{1,3},{2,0},{3,1},{4,6},{5,7},{6,4},{7,5},{8,10},{9,11},{10,... | collective-permute-start | bytes 798728 | tf_op jit(solution)/shard_map/ppermute | solution.py:611
  43.6 11.8 %collective-permute-start.2 = (f32[520,128]{1,0:T(8,128)S(1)}, f32[520,128]{1,0:T(8,128)S(1)}, u32[]{:S(2)}, u32[]{:S(2)}) collective-permute-start(f32[520,128]{1,0:T(8,128)S(1)} %get-tuple-element.60), channel_id=1, source_target_pairs={{0,3},{1,0},{2,1},{3,2},{4,7},{5,4},{6,5},{7,6},{8,11},{9,8},{10,9... | collective-permute-start | bytes 798728 | tf_op jit(solution)/shard_map/ppermute | solution.py:611
  56.5 10.6 %collective-permute-start.3 = (f32[512,128]{1,0:T(8,128)S(1)}, f32[512,128]{1,0:T(8,128)S(1)}, u32[]{:S(2)}, u32[]{:S(2)}) collective-permute-start(f32[512,128]{1,0:T(8,128)S(1)} %slice_multiply_fusion.home.refs_0_), channel_id=1, source_target_pairs={{0,2},{1,3},{2,0},{3,1},{4,6},{5,7},{6,4},{7,5},{8,10},{9,11},{10,... | collective-permute-start | bytes 786440 | tf_op jit(solution)/shard_map/ppermute | solution.py:611
  58.2 13.8 %collective-permute-start.4 = (f32[512,128]{1,0:T(8,128)S(1)}, f32[512,128]{1,0:T(8,128)S(1)}, u32[]{:S(2)}, u32[]{:S(2)}) collective-permute-start(f32[512,128]{1,0:T(8,128)S(1)} %slice_multiply_fusion.home.refs_0_), channel_id=1, source_target_pairs={{0,1},{1,2},{2,3},{3,0},{4,5},{5,6},{6,7},{7,4},{8,9},{9,10},{10,1... | collective-permute-start | bytes 786440 | tf_op jit(solution)/shard_map/ppermute | solution.py:611
  59.7 12.3 %collective-permute-start.5 = (f32[512,128]{1,0:T(8,128)S(1)}, f32[512,128]{1,0:T(8,128)S(1)}, u32[]{:S(2)}, u32[]{:S(2)}) collective-permute-start(f32[512,128]{1,0:T(8,128)S(1)} %slice_multiply_fusion.home.refs_0_), channel_id=1, source_target_pairs={{0,3},{1,0},{2,1},{3,2},{4,7},{5,4},{6,5},{7,6},{8,11},{9,8},{10,9... | collective-permute-start | bytes 786440 | tf_op jit(solution)/shard_map/ppermute | solution.py:611
  78.9 28.5 %all-to-all-start.1 = ((f32[32,96,128]{2,1,0:T(8,128)}), f32[32,96,128]{2,1,0:T(8,128)S(1)}, u32[]{:S(2)}, u32[]{:S(2)}) async-start(f32[32,96,128]{2,1,0:T(8,128)} %get-tuple-element.75), calls=%async_computation.1 | async-start | bytes 3145728 | tf_op jit(solution)/shard_map/all_to_all | solution.py:629
  111.8 7.3 %collective-permute-start.6 = (f32[512,128]{1,0:T(8,128)S(1)}, f32[512,128]{1,0:T(8,128)S(1)}, u32[]{:S(2)}, u32[]{:S(2)}) collective-permute-start(f32[512,128]{1,0:T(8,128)S(1)} %get-tuple-element.78), channel_id=1, source_target_pairs={{0,2},{1,3},{2,0},{3,1},{4,6},{5,7},{6,4},{7,5},{8,10},{9,11},{10,... | collective-permute-start | bytes 786440 | tf_op jit(solution)/shard_map/ppermute | solution.py:611
  119.1 6.5 %collective-permute-start.7 = (f32[512,128]{1,0:T(8,128)S(1)}, f32[512,128]{1,0:T(8,128)S(1)}, u32[]{:S(2)}, u32[]{:S(2)}) collective-permute-start(f32[512,128]{1,0:T(8,128)S(1)} %get-tuple-element.82), channel_id=1, source_target_pairs={{0,1},{1,2},{2,3},{3,0},{4,5},{5,6},{6,7},{7,4},{8,9},{9,10},{10,1... | collective-permute-start | bytes 786440 | tf_op jit(solution)/shard_map/ppermute | solution.py:611
  119.1 6.5 %collective-permute-start.8 = (f32[512,128]{1,0:T(8,128)S(1)}, f32[512,128]{1,0:T(8,128)S(1)}, u32[]{:S(2)}, u32[]{:S(2)}) collective-permute-start(f32[512,128]{1,0:T(8,128)S(1)} %get-tuple-element.83), channel_id=1, source_target_pairs={{0,3},{1,0},{2,1},{3,2},{4,7},{5,4},{6,5},{7,6},{8,11},{9,8},{10,9... | collective-permute-start | bytes 786440 | tf_op jit(solution)/shard_map/ppermute | solution.py:611
  125.9 6.9 %collective-permute-start.9 = (f32[512,128]{1,0:T(8,128)S(1)}, f32[512,128]{1,0:T(8,128)S(1)}, u32[]{:S(2)}, u32[]{:S(2)}) collective-permute-start(f32[512,128]{1,0:T(8,128)S(1)} %get-tuple-element.100.home.refs_0_), channel_id=1, source_target_pairs={{0,2},{1,3},{2,0},{3,1},{4,6},{5,7},{6,4},{7,5},{8,10},{9,11},{10,... | collective-permute-start | bytes 786440 | tf_op jit(solution)/shard_map/ppermute | solution.py:611
  127.4 10.4 %collective-permute-start.10 = (f32[512,128]{1,0:T(8,128)S(1)}, f32[512,128]{1,0:T(8,128)S(1)}, u32[]{:S(2)}, u32[]{:S(2)}) collective-permute-start(f32[512,128]{1,0:T(8,128)S(1)} %get-tuple-element.100.home.refs_0_), channel_id=1, source_target_pairs={{0,1},{1,2},{2,3},{3,0},{4,5},{5,6},{6,7},{7,4},{8,9},{9,10},{10,1... | collective-permute-start | bytes 786440 | tf_op jit(solution)/shard_map/ppermute | solution.py:611
  129.1 8.6 %collective-permute-start.11 = (f32[512,128]{1,0:T(8,128)S(1)}, f32[512,128]{1,0:T(8,128)S(1)}, u32[]{:S(2)}, u32[]{:S(2)}) collective-permute-start(f32[512,128]{1,0:T(8,128)S(1)} %get-tuple-element.100.home.refs_0_), channel_id=1, source_target_pairs={{0,3},{1,0},{2,1},{3,2},{4,7},{5,4},{6,5},{7,6},{8,11},{9,8},{10,9... | collective-permute-start | bytes 786440 | tf_op jit(solution)/shard_map/ppermute | solution.py:611
  144.7 35.3 %all-to-all-start.2 = ((f32[32,96,128]{2,1,0:T(8,128)}), f32[32,96,128]{2,1,0:T(8,128)S(1)}, u32[]{:S(2)}, u32[]{:S(2)}) async-start(f32[32,96,128]{2,1,0:T(8,128)} %get-tuple-element.85), calls=%async_computation.2 | async-start | bytes 3145728 | tf_op jit(solution)/shard_map/all_to_all | solution.py:629
  184.2 7.4 %collective-permute-start.12 = (f32[512,128]{1,0:T(8,128)S(1)}, f32[512,128]{1,0:T(8,128)S(1)}, u32[]{:S(2)}, u32[]{:S(2)}) collective-permute-start(f32[512,128]{1,0:T(8,128)S(1)} %get-tuple-element.88), channel_id=1, source_target_pairs={{0,2},{1,3},{2,0},{3,1},{4,6},{5,7},{6,4},{7,5},{8,10},{9,11},{10,... | collective-permute-start | bytes 786440 | tf_op jit(solution)/shard_map/ppermute | solution.py:611
  191.6 6.5 %collective-permute-start.13 = (f32[512,128]{1,0:T(8,128)S(1)}, f32[512,128]{1,0:T(8,128)S(1)}, u32[]{:S(2)}, u32[]{:S(2)}) collective-permute-start(f32[512,128]{1,0:T(8,128)S(1)} %get-tuple-element.92), channel_id=1, source_target_pairs={{0,1},{1,2},{2,3},{3,0},{4,5},{5,6},{6,7},{7,4},{8,9},{9,10},{10,1... | collective-permute-start | bytes 786440 | tf_op jit(solution)/shard_map/ppermute | solution.py:611
  191.6 6.5 %collective-permute-start.14 = (f32[512,128]{1,0:T(8,128)S(1)}, f32[512,128]{1,0:T(8,128)S(1)}, u32[]{:S(2)}, u32[]{:S(2)}) collective-permute-start(f32[512,128]{1,0:T(8,128)S(1)} %get-tuple-element.93), channel_id=1, source_target_pairs={{0,3},{1,0},{2,1},{3,2},{4,7},{5,4},{6,5},{7,6},{8,11},{9,8},{10,9... | collective-permute-start | bytes 786440 | tf_op jit(solution)/shard_map/ppermute | solution.py:611
  198.5 6.5 %collective-permute-start.15 = (f32[512,128]{1,0:T(8,128)S(1)}, f32[512,128]{1,0:T(8,128)S(1)}, u32[]{:S(2)}, u32[]{:S(2)}) collective-permute-start(f32[512,128]{1,0:T(8,128)S(1)} %add_add_fusion.1.refs_0_), channel_id=1, source_target_pairs={{0,1},{1,2},{2,3},{3,0},{4,5},{5,6},{6,7},{7,4},{8,9},{9,10},{10,1... | collective-permute-start | bytes 786440 | tf_op jit(solution)/shard_map/ppermute | solution.py:611
  198.6 11.1 %collective-permute-start.16 = (f32[512,128]{1,0:T(8,128)S(1)}, f32[512,128]{1,0:T(8,128)S(1)}, u32[]{:S(2)}, u32[]{:S(2)}) collective-permute-start(f32[512,128]{1,0:T(8,128)S(1)} %add_add_fusion.1.refs_0_), channel_id=1, source_target_pairs={{0,2},{1,3},{2,0},{3,1},{4,6},{5,7},{6,4},{7,5},{8,10},{9,11},{10,... | collective-permute-start | bytes 786440 | tf_op jit(solution)/shard_map/ppermute | solution.py:611
  202.3 7.3 %collective-permute-start.17 = (f32[512,128]{1,0:T(8,128)S(1)}, f32[512,128]{1,0:T(8,128)S(1)}, u32[]{:S(2)}, u32[]{:S(2)}) collective-permute-start(f32[512,128]{1,0:T(8,128)S(1)} %add_add_fusion.1.refs_0_), channel_id=1, source_target_pairs={{0,3},{1,0},{2,1},{3,2},{4,7},{5,4},{6,5},{7,6},{8,11},{9,8},{10,9... | collective-permute-start | bytes 786440 | tf_op jit(solution)/shard_map/ppermute | solution.py:611
  213.3 29.1 %all-to-all-start.3 = ((f32[32,48,128]{2,1,0:T(8,128)}), f32[32,48,128]{2,1,0:T(8,128)S(1)}, u32[]{:S(2)}, u32[]{:S(2)}) async-start(f32[32,48,128]{2,1,0:T(8,128)} %get-tuple-element.97), calls=%async_computation.3 | async-start | bytes 1572864 | tf_op jit(solution)/shard_map/all_to_all | solution.py:629
  (5 other events, 17.0 us)

commit v9 on v8

--- a/solution.py
+++ b/solution.py
@@ -203,10 +203,11 @@
         put_split(ret_both, slice(c * width, (c + 1) * width), landed[c, :width, :])
 
     def emit(i, got):
+        if i == 0:
+            mine.wait()
         at = slice(i * hot.shape[0], (i + 1) * hot.shape[0])
         acc[at, :] = acc[at, :] + got
 
-    mine.wait()
     scatter_back(ret_both, listed, (hot, other), emit, rows)
     deg = own_degree[...] + factored(
         4,

time: 248 us -> 247 us (level)
  Pallas kernels: 132 us -> 83 us
  waiting for transfers between devices: 39.6 us -> 71.7 us
  starting transfers between devices: 66.5 us -> 79.9 us
    all_to_all x4, waiting for transfers between devices: 22.2 us -> 46.3 us  [across(): return lax.all_to_all(x, 'vtx', split_axis=0, concat_axis=0, tiled=True)]
    pallas_call x2, Pallas kernels: 27.7 us -> 9.35 us  [local(): call(near_kernel, [((rows, LANES), f32, VMEM)], [SMEM] * 3 + [HBM], [pltp...]
    all_to_all x4, starting transfers between devices: 42.8 us -> 51.4 us  [across(): return lax.all_to_all(x, 'vtx', split_axis=0, concat_axis=0, tiled=True)]
    ppermute x18, waiting for transfers between devices: 17.5 us -> 25.3 us  [moved_by(): lax.ppermute(x, 'edg', [(i, (i + shift) % lanes) for i in range(lanes)])]
    pallas_call x1, Pallas kernels: 8.68 us -> 2.82 us  [local(): call(near_gap_kernel, [((edges, LANES), f32, VMEM)], [SMEM] * 2 + [VMEM],...]
    pallas_call x2, Pallas kernels: 11.9 us -> 6.33 us  [far_list(): call(functools.partial(far_list_kernel, first, room), [((2 * KINDS * room...]
    ppermute x18, starting transfers between devices: 23.7 us -> 28.5 us  [moved_by(): lax.ppermute(x, 'edg', [(i, (i + shift) % lanes) for i in range(lanes)])]
    pallas_call x2, Pallas kernels: 9.86 us -> 5.64 us  [local(): call(functools.partial(early_field_kernel, lanes), [((slots + 8, LANES),...]
  transfers between devices with their start and end apart: 22 -> 22, of which waited for: 10 -> 15; matrix products, arithmetic and copies ran while one was open for 0% -> 0% of each run, Pallas kernels for 36% -> 21%
where the time goes in v9:
time: 247 us; the launch traced here: 244 us
  Pallas kernels  83 us (34%)
  starting transfers between devices  79.9 us (32%)
  waiting for transfers between devices  71.7 us (29%)
  other arithmetic  4.19 us (2%)
  local copies, waits for them, and re-layouts  3.83 us (2%)
    all_to_all x4, starting transfers between devices, across(): return lax.all_to_all(x, 'vtx', split_axis=0, concat_axis=0, tiled=True)  51.4 us
    all_to_all x4, waiting for transfers between devices, across(): return lax.all_to_all(x, 'vtx', split_axis=0, concat_axis=0, tiled=True)  46.3 us
    ppermute x18, starting transfers between devices, moved_by(): lax.ppermute(x, 'edg', [(i, (i + shift) % lanes) for i in range(lanes)])  28.5 us
    ppermute x18, waiting for transfers between devices, moved_by(): lax.ppermute(x, 'edg', [(i, (i + shift) % lanes) for i in range(lanes)])  25.3 us
    pallas_call x1, Pallas kernels, local(): call(own_side_kernel, [((ROOMY, rows, LANES), f32, HBM), ((rows // LANES,...  12 us
    pallas_call x2, Pallas kernels, local(): call(functools.partial(field_kernel, lanes), [((rows, LANES), f32, HBM),...  10.1 us
    pallas_call x2, Pallas kernels, local(): call(near_kernel, [((rows, LANES), f32, VMEM)], [SMEM] * 3 + [HBM], [pltp...  9.35 us
    pallas_call x2, Pallas kernels, local(): call(functools.partial(join_kernel, lanes), [((share, LANES), f32, VMEM)]...  7.97 us
  transfers between devices with their start and end apart: 22, of which 15 were waited for; matrix products, arithmetic and copies ran while one was open for 0% of the time, Pallas kernels for 21%

profile of v9, /device:TPU:1, one launch (start us, length us, event | category | flops | bytes accessed | tf_op | source)
XLA Modules:
  0.0 244.4 jit_solution(8860025340917812493)
XLA Ops:
  3.9 6.0 %halo_side.1 = f32[32,56,128]{2,1,0:T(8,128)} custom-call(f32[4096,128]{1,0:T(8,128)S(1)} %convert_multiply_fusion.terms, s32[32,128]{1,0:T(8,128)S(1)} %bitcast.42, f32[32,128]{1,0:T(8,128)S(1)} %get-tuple-element.102.weight), custom_call_target="tpu_custom_call" | custom-call | flops 3221225472 | bytes 4194304 | tf_op jit(solution)/shard_map/halo_side/pallas_call | solution.py:656
  9.9 8.6 %all-to-all-start = ((f32[32,56,128]{2,1,0:T(8,128)}), f32[32,56,128]{2,1,0:T(8,128)S(1)}, u32[]{:S(2)}, u32[]{:S(2)}) async-start(f32[32,56,128]{2,1,0:T(8,128)} %halo_side.1), calls=%async_computation | async-start | bytes 1835008 | tf_op jit(solution)/shard_map/all_to_all | solution.py:630
  18.6 12.0 %own_side.1 = (f32[32,2048,128]{2,1,0:T(8,128)}, f32[16,128]{1,0:T(8,128)S(1)}) custom-call(f32[4096,128]{1,0:T(8,128)S(1)} %convert_multiply_fusion.terms, s32[32,128]{1,0:T(8,128)S(1)} %bitcast.45, s32[32,128]{1,0:T(8,128)S(1)} %bitcast.43, f32[32,128]{1,0:T(8,128)S(1)} %get-tuple-element.102.weight), custom_call_target="tpu_custom_call" | custom-call | flops 4294967296 | bytes 4194304 | tf_op jit(solution)/shard_map/own_side/pallas_call | solution.py:666
  30.7 3.6 %all-to-all-done.returned = f32[32,56,128]{2,1,0:T(8,128)S(1)} async-done(((f32[32,56,128]{2,1,0:T(8,128)}), f32[32,56,128]{2,1,0:T(8,128)S(1)}, u32[]{:S(2)}, u32[]{:S(2)}) %all-to-all-start) | async-done | bytes 917536 | tf_op jit(solution)/shard_map/all_to_all | solution.py:630
  34.3 4.2 %side_join.1 = (f32[520,128]{1,0:T(8,128)S(1)}, f32[520,128]{1,0:T(8,128)S(1)}, f32[520,128]{1,0:T(8,128)S(1)}, f32[520,128]{1,0:T(8,128)S(1)}) custom-call(s32[1]{0:T(128)} %bitcast.lane, f32[32,56,128]{2,1,0:T(8,128)S(1)} %all-to-all-done.returned, s32[12,128]{1,0:T(8,128)S(1)} %reshape_reshape_squeeze.3.listed, s32[32,128]{1,0:T(8,128)S(1)} %pad.4.padded, ...), custom_call_target="tpu_custom_call" | custom-call | flops 1610612736 | bytes 4194304 | tf_op jit(solution)/shard_map/side_join/pallas_call | solution.py:675
  40.3 3.3 %collective-permute-start.1 = (f32[520,128]{1,0:T(8,128)S(1)}, f32[520,128]{1,0:T(8,128)S(1)}, u32[]{:S(2)}, u32[]{:S(2)}) collective-permute-start(f32[520,128]{1,0:T(8,128)S(1)} %get-tuple-element.59), channel_id=1, source_target_pairs={{0,2},{1,3},{2,0},{3,1},{4,6},{5,7},{6,4},{7,5},{8,10},{9,11},{10,... | collective-permute-start | bytes 798728 | tf_op jit(solution)/shard_map/ppermute | solution.py:612
  44.7 4.0 %far_list.2.code_a = s32[6656]{0:T(1024)S(1)} custom-call(s32[1]{0:T(128)} %copy.9.count, s32[4096]{0:T(1024)S(1)} %bitcast.36, s32[4096]{0:T(1024)S(1)} %bitcast.38, s32[16,128]{1,0:T(8,128)S(1)} %get-tuple-element.66.totals), custom_call_target="tpu_custom_call" | custom-call | bytes 33554432 | tf_op jit(solution)/shard_map/far_list/pallas_call | solution.py:703
  48.8 6.6 %collective-permute-done.1 = f32[520,128]{1,0:T(8,128)S(1)} collective-permute-done((f32[520,128]{1,0:T(8,128)S(1)}, f32[520,128]{1,0:T(8,128)S(1)}, u32[]{:S(2)}, u32[]{:S(2)}) %collective-permute-start.1) | collective-permute-done | bytes 266272 | tf_op jit(solution)/shard_map/ppermute | solution.py:612
  67.4 4.4 %collective-permute-done.4.refs_1_ = f32[512,128]{1,0:T(8,128)S(1)} collective-permute-done((f32[512,128]{1,0:T(8,128)S(1)}, f32[512,128]{1,0:T(8,128)S(1)}, u32[]{:S(2)}, u32[]{:S(2)}) %collective-permute-start.4) | collective-permute-done | bytes 262176 | tf_op jit(solution)/shard_map/ppermute | solution.py:612
  71.8 5.1 %field.2 = (f32[2048,128]{1,0:T(8,128)}, f32[32,96,128]{2,1,0:T(8,128)}) custom-call(s32[1]{0:T(128)} %bitcast.lane, s32[6656]{0:T(1024)S(1)} %far_list.2.code_a, s32[6656]{0:T(1024)S(1)} %far_list.3.code_b, s32[16,128]{1,0:T(8,128)S(1)} %get-tuple-element.66.totals, f32[4096]{0:T(1024)S(1)} %bitcast.22, s32[1536]{0:T(1024)S(1)} %reshape_squeeze.3.lists, ...), custom_call_target="tpu_custom_call" | custom-call | bytes 4194304 | tf_op jit(solution)/shard_map/field/pallas_call | solution.py:738
  77.0 8.1 %all-to-all-start.1 = ((f32[32,96,128]{2,1,0:T(8,128)}), f32[32,96,128]{2,1,0:T(8,128)S(1)}, u32[]{:S(2)}, u32[]{:S(2)}) async-start(f32[32,96,128]{2,1,0:T(8,128)} %get-tuple-element.75), calls=%async_computation.1 | async-start | bytes 3145728 | tf_op jit(solution)/shard_map/all_to_all | solution.py:630
  86.3 4.7 %near.2 = f32[2048,128]{1,0:T(8,128)S(1)} custom-call(s32[1]{0:T(128)} %copy.9.count, s32[4096]{0:T(1024)S(1)} %bitcast.31, f32[4096]{0:T(1024)S(1)} %bitcast.33, f32[2048,128]{1,0:T(8,128)S(1)} %copy-done.1), custom_call_target="tpu_custom_call" | custom-call | bytes 33554432 | tf_op jit(solution)/shard_map/near/pallas_call | solution.py:749
  90.9 16.3 %all-to-all-done.1.arrived = f32[32,96,128]{2,1,0:T(8,128)S(1)} async-done(((f32[32,96,128]{2,1,0:T(8,128)}), f32[32,96,128]{2,1,0:T(8,128)S(1)}, u32[]{:S(2)}, u32[]{:S(2)}) %all-to-all-start.1) | async-done | bytes 1572896 | tf_op jit(solution)/shard_map/all_to_all | solution.py:630
  107.2 3.2 %late_join.2 = (f32[512,128]{1,0:T(8,128)S(1)}, f32[33,48,128]{2,1,0:T(8,128)S(1)}, bf16[1536,256]{1,0:T(8,128)(2,1)S(1)}) custom-call(s32[1]{0:T(128)} %bitcast.lane, s32[6656]{0:T(1024)S(1)} %far_list.2.code_a, s32[6656]{0:T(1024)S(1)} %far_list.3.code_b, s32[16,128]{1,0:T(8,128)S(1)} %get-tuple-element.66.totals, f32[4096]{0:T(1024)S(1)} %bitcast.23, ...), custom_call_target="tpu_custom_call" | custom-call | bytes 4194304 | tf_op jit(solution)/shard_map/late_join/pallas_call | solution.py:757
  112.2 3.9 %join.2 = (f32[512,128]{1,0:T(8,128)S(1)}, f32[512,128]{1,0:T(8,128)S(1)}) custom-call(s32[1]{0:T(128)} %bitcast.lane, s32[6656]{0:T(1024)S(1)} %far_list.2.code_a, s32[6656]{0:T(1024)S(1)} %far_list.3.code_b, s32[16,128]{1,0:T(8,128)S(1)} %get-tuple-element.66.totals, f32[4096]{0:T(1024)S(1)} %bitcast.24, s32[12,128]{1,0:T(8,128)S(1)} %reshape_reshape_squeeze.3.listed, ...), custom_call_target="tpu_custom_call" | custom-call | bytes 33554432 | tf_op jit(solution)/shard_map/join/pallas_call | solution.py:766
  133.9 5.0 %field.3 = (f32[2048,128]{1,0:T(8,128)}, f32[32,96,128]{2,1,0:T(8,128)}) custom-call(s32[1]{0:T(128)} %bitcast.lane, s32[6656]{0:T(1024)S(1)} %far_list.2.code_a, s32[6656]{0:T(1024)S(1)} %far_list.3.code_b, s32[16,128]{1,0:T(8,128)S(1)} %get-tuple-element.66.totals, f32[4096]{0:T(1024)S(1)} %bitcast.27, s32[1536]{0:T(1024)S(1)} %reshape_squeeze.3.lists, ...), custom_call_target="tpu_custom_call" | custom-call | bytes 4194304 | tf_op jit(solution)/shard_map/field/pallas_call | solution.py:738
  138.9 19.3 %all-to-all-start.2 = ((f32[32,96,128]{2,1,0:T(8,128)}), f32[32,96,128]{2,1,0:T(8,128)S(1)}, u32[]{:S(2)}, u32[]{:S(2)}) async-start(f32[32,96,128]{2,1,0:T(8,128)} %get-tuple-element.85), calls=%async_computation.2 | async-start | bytes 3145728 | tf_op jit(solution)/shard_map/all_to_all | solution.py:630
  159.5 4.7 %near.3 = f32[2048,128]{1,0:T(8,128)S(1)} custom-call(s32[1]{0:T(128)} %copy.9.count, s32[4096]{0:T(1024)S(1)} %bitcast.32, f32[4096]{0:T(1024)S(1)} %bitcast.34, f32[2048,128]{1,0:T(8,128)S(1)} %copy-done), custom_call_target="tpu_custom_call" | custom-call | bytes 33554432 | tf_op jit(solution)/shard_map/near/pallas_call | solution.py:749
  164.1 16.3 %all-to-all-done.2.arrived = f32[32,96,128]{2,1,0:T(8,128)S(1)} async-done(((f32[32,96,128]{2,1,0:T(8,128)}), f32[32,96,128]{2,1,0:T(8,128)S(1)}, u32[]{:S(2)}, u32[]{:S(2)}) %all-to-all-start.2) | async-done | bytes 1572896 | tf_op jit(solution)/shard_map/all_to_all | solution.py:630
  185.0 4.1 %join.3 = (f32[512,128]{1,0:T(8,128)S(1)}, f32[512,128]{1,0:T(8,128)S(1)}) custom-call(s32[1]{0:T(128)} %bitcast.lane, s32[6656]{0:T(1024)S(1)} %far_list.2.code_a, s32[6656]{0:T(1024)S(1)} %far_list.3.code_b, s32[16,128]{1,0:T(8,128)S(1)} %get-tuple-element.66.totals, f32[4096]{0:T(1024)S(1)} %bitcast.29, s32[12,128]{1,0:T(8,128)S(1)} %reshape_reshape_squeeze.3.listed, ...), custom_call_target="tpu_custom_call" | custom-call | bytes 33554432 | tf_op jit(solution)/shard_map/join/pallas_call | solution.py:766
  204.3 4.1 %collective-permute-done.16.refs_2_ = f32[512,128]{1,0:T(8,128)S(1)} collective-permute-done((f32[512,128]{1,0:T(8,128)S(1)}, f32[512,128]{1,0:T(8,128)S(1)}, u32[]{:S(2)}, u32[]{:S(2)}) %collective-permute-start.16) | collective-permute-done | bytes 262176 | tf_op jit(solution)/shard_map/ppermute | solution.py:612
  208.4 3.7 %solution_rows.1 = (f32[2048,128]{1,0:T(8,128)}, f32[32,48,128]{2,1,0:T(8,128)}) custom-call(s32[1]{0:T(128)} %bitcast.lane, s32[1536]{0:T(1024)S(1)} %reshape_squeeze.3.lists, f32[512,128]{1,0:T(8,128)S(1)} %add_add_fusion.1.refs_0_, f32[512,128]{1,0:T(8,128)S(1)} %collective-permute-done.15.refs_1_, f32[512,128]{1,0:T(8,128)S(1)} %collective-permute-done.16.refs_2_, ...), custom_call_target="tpu_custom_call" | custom-call | bytes 4194304 | tf_op jit(solution)/shard_map/solution_rows/pallas_call | solution.py:788
  212.1 15.4 %all-to-all-start.3 = ((f32[32,48,128]{2,1,0:T(8,128)}), f32[32,48,128]{2,1,0:T(8,128)S(1)}, u32[]{:S(2)}, u32[]{:S(2)}) async-start(f32[32,48,128]{2,1,0:T(8,128)} %get-tuple-element.97), calls=%async_computation.3 | async-start | bytes 1572864 | tf_op jit(solution)/shard_map/all_to_all | solution.py:630
  231.6 10.1 %all-to-all-done.3.arrived = f32[32,48,128]{2,1,0:T(8,128)S(1)} async-done(((f32[32,48,128]{2,1,0:T(8,128)}), f32[32,48,128]{2,1,0:T(8,128)S(1)}, u32[]{:S(2)}, u32[]{:S(2)}) %all-to-all-start.3) | async-done | bytes 786464 | tf_op jit(solution)/shard_map/all_to_all | solution.py:630
  (67 shorter events, 65.9 us)
Async XLA Ops:
  3.9 14.7 %copy-start.6 = (s32[1,32,48]{2,1,0:T(8,128)S(1)}, s32[1,32,48]{2,1,0:T(8,128)}, u32[]{:S(2)}) copy-start(s32[1,32,48]{2,1,0:T(8,128)} %param.12) | copy-start | bytes 18436
  3.9 14.7 %copy-start.5 = (s32[4096]{0:T(1024)S(1)}, s32[4096]{0:T(1024)}, u32[]{:S(2)}) copy-start(s32[4096]{0:T(1024)} %param.10) | copy-start | bytes 49156
  9.9 24.4 %all-to-all-start = ((f32[32,56,128]{2,1,0:T(8,128)}), f32[32,56,128]{2,1,0:T(8,128)S(1)}, u32[]{:S(2)}, u32[]{:S(2)}) async-start(f32[32,56,128]{2,1,0:T(8,128)} %halo_side.1), calls=%async_computation | async-start | bytes 1835008 | tf_op jit(solution)/shard_map/all_to_all | solution.py:630
  38.6 10.3 %collective-permute-start = (f32[520,128]{1,0:T(8,128)S(1)}, f32[520,128]{1,0:T(8,128)S(1)}, u32[]{:S(2)}, u32[]{:S(2)}) collective-permute-start(f32[520,128]{1,0:T(8,128)S(1)} %get-tuple-element.58), channel_id=1, source_target_pairs={{0,1},{1,2},{2,3},{3,0},{4,5},{5,6},{6,7},{7,4},{8,9},{9,10},{10,1... | collective-permute-start | bytes 798728 | tf_op jit(solution)/shard_map/ppermute | solution.py:612
  40.3 15.1 %collective-permute-start.1 = (f32[520,128]{1,0:T(8,128)S(1)}, f32[520,128]{1,0:T(8,128)S(1)}, u32[]{:S(2)}, u32[]{:S(2)}) collective-permute-start(f32[520,128]{1,0:T(8,128)S(1)} %get-tuple-element.59), channel_id=1, source_target_pairs={{0,2},{1,3},{2,0},{3,1},{4,6},{5,7},{6,4},{7,5},{8,10},{9,11},{10,... | collective-permute-start | bytes 798728 | tf_op jit(solution)/shard_map/ppermute | solution.py:612
  43.6 11.8 %collective-permute-start.2 = (f32[520,128]{1,0:T(8,128)S(1)}, f32[520,128]{1,0:T(8,128)S(1)}, u32[]{:S(2)}, u32[]{:S(2)}) collective-permute-start(f32[520,128]{1,0:T(8,128)S(1)} %get-tuple-element.60), channel_id=1, source_target_pairs={{0,3},{1,0},{2,1},{3,2},{4,7},{5,4},{6,5},{7,6},{8,11},{9,8},{10,9... | collective-permute-start | bytes 798728 | tf_op jit(solution)/shard_map/ppermute | solution.py:612
  56.4 8.2 %collective-permute-start.3 = (f32[512,128]{1,0:T(8,128)S(1)}, f32[512,128]{1,0:T(8,128)S(1)}, u32[]{:S(2)}, u32[]{:S(2)}) collective-permute-start(f32[512,128]{1,0:T(8,128)S(1)} %slice_multiply_fusion.home.refs_0_), channel_id=1, source_target_pairs={{0,2},{1,3},{2,0},{3,1},{4,6},{5,7},{6,4},{7,5},{8,10},{9,11},{10,... | collective-permute-start | bytes 786440 | tf_op jit(solution)/shard_map/ppermute | solution.py:612
  58.1 13.7 %collective-permute-start.4 = (f32[512,128]{1,0:T(8,128)S(1)}, f32[512,128]{1,0:T(8,128)S(1)}, u32[]{:S(2)}, u32[]{:S(2)}) collective-permute-start(f32[512,128]{1,0:T(8,128)S(1)} %slice_multiply_fusion.home.refs_0_), channel_id=1, source_target_pairs={{0,1},{1,2},{2,3},{3,0},{4,5},{5,6},{6,7},{7,4},{8,9},{9,10},{10,1... | collective-permute-start | bytes 786440 | tf_op jit(solution)/shard_map/ppermute | solution.py:612
  59.6 12.2 %collective-permute-start.5 = (f32[512,128]{1,0:T(8,128)S(1)}, f32[512,128]{1,0:T(8,128)S(1)}, u32[]{:S(2)}, u32[]{:S(2)}) collective-permute-start(f32[512,128]{1,0:T(8,128)S(1)} %slice_multiply_fusion.home.refs_0_), channel_id=1, source_target_pairs={{0,3},{1,0},{2,1},{3,2},{4,7},{5,4},{6,5},{7,6},{8,11},{9,8},{10,9... | collective-permute-start | bytes 786440 | tf_op jit(solution)/shard_map/ppermute | solution.py:612
  77.0 30.3 %all-to-all-start.1 = ((f32[32,96,128]{2,1,0:T(8,128)}), f32[32,96,128]{2,1,0:T(8,128)S(1)}, u32[]{:S(2)}, u32[]{:S(2)}) async-start(f32[32,96,128]{2,1,0:T(8,128)} %get-tuple-element.75), calls=%async_computation.1 | async-start | bytes 3145728 | tf_op jit(solution)/shard_map/all_to_all | solution.py:630
  110.4 6.8 %collective-permute-start.6 = (f32[512,128]{1,0:T(8,128)S(1)}, f32[512,128]{1,0:T(8,128)S(1)}, u32[]{:S(2)}, u32[]{:S(2)}) collective-permute-start(f32[512,128]{1,0:T(8,128)S(1)} %get-tuple-element.78), channel_id=1, source_target_pairs={{0,2},{1,3},{2,0},{3,1},{4,6},{5,7},{6,4},{7,5},{8,10},{9,11},{10,... | collective-permute-start | bytes 786440 | tf_op jit(solution)/shard_map/ppermute | solution.py:612
  117.2 6.4 %collective-permute-start.7 = (f32[512,128]{1,0:T(8,128)S(1)}, f32[512,128]{1,0:T(8,128)S(1)}, u32[]{:S(2)}, u32[]{:S(2)}) collective-permute-start(f32[512,128]{1,0:T(8,128)S(1)} %get-tuple-element.82), channel_id=1, source_target_pairs={{0,1},{1,2},{2,3},{3,0},{4,5},{5,6},{6,7},{7,4},{8,9},{9,10},{10,1... | collective-permute-start | bytes 786440 | tf_op jit(solution)/shard_map/ppermute | solution.py:612
  118.1 5.5 %collective-permute-start.8 = (f32[512,128]{1,0:T(8,128)S(1)}, f32[512,128]{1,0:T(8,128)S(1)}, u32[]{:S(2)}, u32[]{:S(2)}) collective-permute-start(f32[512,128]{1,0:T(8,128)S(1)} %get-tuple-element.83), channel_id=1, source_target_pairs={{0,3},{1,0},{2,1},{3,2},{4,7},{5,4},{6,5},{7,6},{8,11},{9,8},{10,9... | collective-permute-start | bytes 786440 | tf_op jit(solution)/shard_map/ppermute | solution.py:612
  123.9 6.9 %collective-permute-start.9 = (f32[512,128]{1,0:T(8,128)S(1)}, f32[512,128]{1,0:T(8,128)S(1)}, u32[]{:S(2)}, u32[]{:S(2)}) collective-permute-start(f32[512,128]{1,0:T(8,128)S(1)} %get-tuple-element.100.home.refs_0_), channel_id=1, source_target_pairs={{0,2},{1,3},{2,0},{3,1},{4,6},{5,7},{6,4},{7,5},{8,10},{9,11},{10,... | collective-permute-start | bytes 786440 | tf_op jit(solution)/shard_map/ppermute | solution.py:612
  125.3 8.6 %collective-permute-start.10 = (f32[512,128]{1,0:T(8,128)S(1)}, f32[512,128]{1,0:T(8,128)S(1)}, u32[]{:S(2)}, u32[]{:S(2)}) collective-permute-start(f32[512,128]{1,0:T(8,128)S(1)} %get-tuple-element.100.home.refs_0_), channel_id=1, source_target_pairs={{0,1},{1,2},{2,3},{3,0},{4,5},{5,6},{6,7},{7,4},{8,9},{9,10},{10,1... | collective-permute-start | bytes 786440 | tf_op jit(solution)/shard_map/ppermute | solution.py:612
  127.3 6.6 %collective-permute-start.11 = (f32[512,128]{1,0:T(8,128)S(1)}, f32[512,128]{1,0:T(8,128)S(1)}, u32[]{:S(2)}, u32[]{:S(2)}) collective-permute-start(f32[512,128]{1,0:T(8,128)S(1)} %get-tuple-element.100.home.refs_0_), channel_id=1, source_target_pairs={{0,3},{1,0},{2,1},{3,2},{4,7},{5,4},{6,5},{7,6},{8,11},{9,8},{10,9... | collective-permute-start | bytes 786440 | tf_op jit(solution)/shard_map/ppermute | solution.py:612
  138.9 41.5 %all-to-all-start.2 = ((f32[32,96,128]{2,1,0:T(8,128)}), f32[32,96,128]{2,1,0:T(8,128)S(1)}, u32[]{:S(2)}, u32[]{:S(2)}) async-start(f32[32,96,128]{2,1,0:T(8,128)} %get-tuple-element.85), calls=%async_computation.2 | async-start | bytes 3145728 | tf_op jit(solution)/shard_map/all_to_all | solution.py:630
  183.6 6.8 %collective-permute-start.12 = (f32[512,128]{1,0:T(8,128)S(1)}, f32[512,128]{1,0:T(8,128)S(1)}, u32[]{:S(2)}, u32[]{:S(2)}) collective-permute-start(f32[512,128]{1,0:T(8,128)S(1)} %get-tuple-element.88), channel_id=1, source_target_pairs={{0,2},{1,3},{2,0},{3,1},{4,6},{5,7},{6,4},{7,5},{8,10},{9,11},{10,... | collective-permute-start | bytes 786440 | tf_op jit(solution)/shard_map/ppermute | solution.py:612
  190.4 7.1 %collective-permute-start.13 = (f32[512,128]{1,0:T(8,128)S(1)}, f32[512,128]{1,0:T(8,128)S(1)}, u32[]{:S(2)}, u32[]{:S(2)}) collective-permute-start(f32[512,128]{1,0:T(8,128)S(1)} %get-tuple-element.92), channel_id=1, source_target_pairs={{0,1},{1,2},{2,3},{3,0},{4,5},{5,6},{6,7},{7,4},{8,9},{9,10},{10,1... | collective-permute-start | bytes 786440 | tf_op jit(solution)/shard_map/ppermute | solution.py:612
  191.7 5.8 %collective-permute-start.14 = (f32[512,128]{1,0:T(8,128)S(1)}, f32[512,128]{1,0:T(8,128)S(1)}, u32[]{:S(2)}, u32[]{:S(2)}) collective-permute-start(f32[512,128]{1,0:T(8,128)S(1)} %get-tuple-element.93), channel_id=1, source_target_pairs={{0,3},{1,0},{2,1},{3,2},{4,7},{5,4},{6,5},{7,6},{8,11},{9,8},{10,9... | collective-permute-start | bytes 786440 | tf_op jit(solution)/shard_map/ppermute | solution.py:612
  197.8 6.5 %collective-permute-start.15 = (f32[512,128]{1,0:T(8,128)S(1)}, f32[512,128]{1,0:T(8,128)S(1)}, u32[]{:S(2)}, u32[]{:S(2)}) collective-permute-start(f32[512,128]{1,0:T(8,128)S(1)} %add_add_fusion.1.refs_0_), channel_id=1, source_target_pairs={{0,1},{1,2},{2,3},{3,0},{4,5},{5,6},{6,7},{7,4},{8,9},{9,10},{10,1... | collective-permute-start | bytes 786440 | tf_op jit(solution)/shard_map/ppermute | solution.py:612
  199.0 9.4 %collective-permute-start.16 = (f32[512,128]{1,0:T(8,128)S(1)}, f32[512,128]{1,0:T(8,128)S(1)}, u32[]{:S(2)}, u32[]{:S(2)}) collective-permute-start(f32[512,128]{1,0:T(8,128)S(1)} %add_add_fusion.1.refs_0_), channel_id=1, source_target_pairs={{0,2},{1,3},{2,0},{3,1},{4,6},{5,7},{6,4},{7,5},{8,10},{9,11},{10,... | collective-permute-start | bytes 786440 | tf_op jit(solution)/shard_map/ppermute | solution.py:612
  201.7 6.7 %collective-permute-start.17 = (f32[512,128]{1,0:T(8,128)S(1)}, f32[512,128]{1,0:T(8,128)S(1)}, u32[]{:S(2)}, u32[]{:S(2)}) collective-permute-start(f32[512,128]{1,0:T(8,128)S(1)} %add_add_fusion.1.refs_0_), channel_id=1, source_target_pairs={{0,3},{1,0},{2,1},{3,2},{4,7},{5,4},{6,5},{7,6},{8,11},{9,8},{10,9... | collective-permute-start | bytes 786440 | tf_op jit(solution)/shard_map/ppermute | solution.py:612
  212.1 29.6 %all-to-all-start.3 = ((f32[32,48,128]{2,1,0:T(8,128)}), f32[32,48,128]{2,1,0:T(8,128)S(1)}, u32[]{:S(2)}, u32[]{:S(2)}) async-start(f32[32,48,128]{2,1,0:T(8,128)} %get-tuple-element.97), calls=%async_computation.3 | async-start | bytes 1572864 | tf_op jit(solution)/shard_map/all_to_all | solution.py:630
  (5 other events, 16.9 us)
